TPU v7x, 32 devices: a whole 2x2x4 slice. The times are simulated.
32 devices in a mesh: group: 8 (over y, x, core), shuf: 4 (over z).
Axes of the slice: x: 2, y: 2, z: 4, core: 2. Of those that a mesh axis runs over, the one named last changes fastest.
Arguments:
- inputs: bfloat16 [8, 1024, 512], P('group', 'shuf'), may hold values from -8 to 8
- cotangent: bfloat16 [8, 1024, 512], P('group', 'shuf'), may hold values from -8 to 8
- w_uvqk: bfloat16 [512, 2048], P('group'), may hold values from -0.25 to 0.25
- w_out: bfloat16 [512, 512], P('group'), may hold values from -0.25 to 0.25
- send_perm: int32 [8, 4, 32], P('group', 'shuf'), may hold values from 0 to 31, each once within a row
- recv_perm: int32 [8, 4, 32], P('group', 'shuf'), may hold values from 0 to 31, each once within a row
- lengths: int32 [8, 4, 8], P('group', 'shuf'), may hold values from 1 to 128, 256 in all within a row
- prefixes: int32 [8, 4, 8], P('group', 'shuf'), may hold values from 0 to 32
Outputs:
- layer_out: bfloat16 [8, 1024, 512], P('group', 'shuf')
- grad_input: bfloat16 [8, 1024, 512], P('group', 'shuf')
- grad_uvqk: float32 [512, 2048], P('group')
- grad_wout: float32 [512, 512], P('group')
All inputs are finite; a program needn't handle non-finite values.
Results may differ from a plain program's by a relative error of at most 0.03.
Values may be sent and summed in bfloat16 or wider, within the bound.
No kernel may reach another device: no remote copies, remote signals or barrier semaphores. Data moves between devices by JAX's collectives and lax.ppermute only.
A program may use at most 64 MiB of HBM per device.

v0:
```python
from functools import partial

import jax
import jax.numpy as jnp
from jax import lax
from jax.sharding import PartitionSpec as P

D = 512
HEADS = 8
ROWS = 256


norm_eps = 1e-05


def normalize(values):
    center = jnp.mean(values, axis=-1, keepdims=True)
    centred = values - center
    variance = jnp.mean(centred * centred, axis=-1, keepdims=True)
    inv_scale = lax.rsqrt(variance + norm_eps)
    return (centred * inv_scale, inv_scale)


def silu_slope(values):
    sigma = jax.nn.sigmoid(values)
    return sigma * (1.0 + values * (1.0 - sigma))


def visible(user_lengths, user_prefixes, row_count):
    user_ends = jnp.cumsum(user_lengths)
    row_index = jnp.arange(row_count, dtype=jnp.int32)
    user_index = jnp.sum((row_index[:, None] >= user_ends[None, :]).astype(jnp.int32), axis=1)
    member = user_index[:, None] == jnp.arange(user_lengths.shape[0], dtype=jnp.int32)[None, :]
    starts = user_ends - user_lengths
    position = row_index - jnp.sum(jnp.where(member, starts[None, :], 0), axis=1)
    prefix_len = jnp.sum(jnp.where(member, user_prefixes[None, :], 0), axis=1)
    same_user = user_index[:, None] == user_index[None, :]
    return same_user & (
        (row_index[None, :] <= row_index[:, None]) | (position[None, :] < prefix_len[:, None])
    )


def attention(activated, weight_out, residual, allowed):
    row_count = activated.shape[0]
    gate_u = activated[:, :D]
    values = activated[:, D : 2 * D].reshape(row_count, HEADS, D // HEADS)
    queries = activated[:, 2 * D : 3 * D].reshape(row_count, HEADS, D // HEADS)
    keys = activated[:, 3 * D :].reshape(row_count, HEADS, D // HEADS)
    scores = jnp.einsum("qhd,khd->hqk", queries, keys, preferred_element_type=jnp.float32)
    weights = (jnp.where(allowed[None], jax.nn.silu(scores), 0.0) / ROWS).astype(jnp.bfloat16)
    mixed = jnp.einsum("hqk,khd->qhd", weights, values, preferred_element_type=jnp.float32).reshape(
        row_count, D
    )
    normed, unused = normalize(mixed)
    gated = (normed * gate_u.astype(jnp.float32)).astype(jnp.bfloat16)
    return (jnp.dot(gated, weight_out, preferred_element_type=jnp.float32) + residual).astype(
        jnp.bfloat16
    )


def on_device(inputs, cotangent, w_uvqk, w_out, send_perm, recv_perm, lengths, prefixes):
    row_count = inputs.shape[1]
    feature_width = inputs.shape[2]
    send_order = send_perm[0, 0]
    recv_order = recv_perm[0, 0]
    blocks = send_order.shape[0]
    block_rows = row_count // blocks

    def regroup(array, order):
        return jnp.take(array.reshape(blocks, block_rows, feature_width), order, axis=0).reshape(
            row_count, feature_width
        )

    def inverse(order):
        return jnp.zeros_like(order).at[order].set(jnp.arange(blocks, dtype=jnp.int32))

    full_uvqk, full_out = (
        lax.all_gather(w_uvqk, "group", axis=0, tiled=True),
        lax.all_gather(w_out, "group", axis=0, tiled=True),
    )
    outgoing = (regroup(inputs[0], send_order), regroup(cotangent[0], send_order))
    arrived = (
        lax.all_to_all(outgoing[0], "shuf", split_axis=0, concat_axis=0, tiled=True),
        lax.all_to_all(outgoing[1], "shuf", split_axis=0, concat_axis=0, tiled=True),
    )
    local_x = regroup(arrived[0], recv_order)
    local_cot = regroup(arrived[1], recv_order)
    inputs_f32 = local_x.astype(jnp.float32)
    centred, inv_scale = normalize(inputs_f32)
    normed_x = centred.astype(jnp.bfloat16)
    projected = jnp.dot(normed_x, full_uvqk, preferred_element_type=jnp.float32)
    activated = jax.nn.silu(projected).astype(jnp.bfloat16)
    allowed = visible(lengths[0, 0], prefixes[0, 0], row_count)
    layer_value, pullback = jax.vjp(
        partial(attention, allowed=allowed), activated, full_out, inputs_f32
    )
    grad_act, grad_weight, grad_res = pullback(local_cot)
    grad_proj = (grad_act.astype(jnp.float32) * silu_slope(projected)).astype(jnp.bfloat16)
    grad_normed = lax.dot_general(
        grad_proj, full_uvqk, (((1,), (1,)), ((), ())), preferred_element_type=jnp.float32
    )
    grad_center = jnp.mean(grad_normed, axis=-1, keepdims=True)
    grad_proj_z = jnp.mean(grad_normed * centred, axis=-1, keepdims=True)
    grad_rows = (inv_scale * (grad_normed - grad_center - centred * grad_proj_z) + grad_res).astype(
        jnp.bfloat16
    )
    recv_back = inverse(recv_order)
    returned = (
        lax.all_to_all(
            regroup(layer_value, recv_back), "shuf", split_axis=0, concat_axis=0, tiled=True
        ),
        lax.all_to_all(
            regroup(grad_rows, recv_back), "shuf", split_axis=0, concat_axis=0, tiled=True
        ),
    )
    send_back = inverse(send_order)
    owner_out = regroup(returned[0], send_back)[None]
    owner_grad = regroup(returned[1], send_back)[None]
    part_uvqk = lax.dot_general(
        normed_x, grad_proj, (((0,), (0,)), ((), ())), preferred_element_type=jnp.float32
    )
    part_proj, part_out = (
        lax.psum_scatter(
            part_uvqk.astype(jnp.bfloat16), "group", scatter_dimension=0, tiled=True
        ).astype(jnp.float32),
        lax.psum_scatter(
            grad_weight.astype(jnp.float32).astype(jnp.bfloat16),
            "group",
            scatter_dimension=0,
            tiled=True,
        ).astype(jnp.float32),
    )
    grad_uvqk, grad_wout = (
        lax.psum(part_proj.astype(jnp.bfloat16), "shuf").astype(jnp.float32),
        lax.psum(part_out.astype(jnp.bfloat16), "shuf").astype(jnp.float32),
    )
    return (owner_out, owner_grad, grad_uvqk, grad_wout)


def solution(mesh):
    return jax.shard_map(
        on_device,
        mesh=mesh,
        in_specs=(
            P("group", "shuf", None),
            P("group", "shuf", None),
            P("group", None),
            P("group", None),
            P("group", "shuf", None),
            P("group", "shuf", None),
            P("group", "shuf", None),
            P("group", "shuf", None),
        ),
        out_specs=(
            P("group", "shuf", None),
            P("group", "shuf", None),
            P("group", None),
            P("group", None),
        ),
        check_vma=False,
    )
```

profile of v0, /device:TPU:0, one launch (start us, length us, event | category | flops | bytes accessed | tf_op | source)
XLA Modules:
  0.0 190.4 jit_solution(363195939239503938)
XLA Ops:
  7.3 0.7 all-gather.2.cloned.1.call-update
  8.0 0.7 compare_select_fusion.3
  8.6 0.6 gather_fusion.4
  9.2 1.5 gather_fusion
  10.7 0.7 compare_and_fusion.3
  11.4 0.9 broadcast_select_fusion.4
  12.3 6.3 %all-to-all-start = ((bf16[4,64,512]{2,1,0:T(8,128)(2,1)}), bf16[4,64,512]{2,1,0:T(8,128)(2,1)S(1)}, u32[]{:S(2)}, u32[]{:S(2)}) async-start(bf16[4,64,512]{2,1,0:T(8,128)(2,1)} %bitcast.7), calls=%async_computation | async-start | bytes 524288 | tf_op jit(solution)/shard_map/all_to_all | solution.py:83
  19.1 10.5 %all_gather.7 = bf16[512,512]{1,0:T(8,128)(2,1)S(1)} all-gather(bf16[64,512]{1,0:T(8,128)(2,1)S(1)} %copy-done.9), channel_id=1, replica_groups=mesh['group'=8,'shuf'=4] {'group'}, dimensions={0}, use_global_device_ids=true | all-gather | bytes 589824 | tf_op jit(solution)/shard_map/all_gather | solution.py:79
  29.7 5.1 %all-to-all-start.2 = ((bf16[4,64,512]{2,1,0:T(8,128)(2,1)}), bf16[4,64,512]{2,1,0:T(8,128)(2,1)S(1)}, u32[]{:S(2)}, u32[]{:S(2)}) async-start(bf16[4,64,512]{2,1,0:T(8,128)(2,1)} %bitcast.24), calls=%async_computation.2 | async-start | bytes 524288 | tf_op jit(solution)/shard_map/all_to_all | solution.py:84
  34.8 0.6 gather_fusion.1
  35.7 0.2 fusion.17
  36.0 8.2 %all-to-all-done.2 = bf16[4,64,512]{2,1,0:T(8,128)(2,1)S(1)} async-done(((bf16[4,64,512]{2,1,0:T(8,128)(2,1)}), bf16[4,64,512]{2,1,0:T(8,128)(2,1)S(1)}, u32[]{:S(2)}, u32[]{:S(2)}) %all-to-all-start.2) | async-done | bytes 262176 | tf_op jit(solution)/shard_map/all_to_all | solution.py:84
  44.2 0.6 gather_fusion.5
  44.8 3.7 %multiply_convert_fusion.2 = (bf16[256,2048]{1,0:T(8,128)(2,1)S(1)}, f32[256,2048]{1,0:T(8,128)}) fusion(bf16[512,2048]{1,0:T(8,128)(2,1)} %all-gather.2.cloned.1.call-done, f32[256]{0:T(256)S(1)} %rsqrt.22, f32[256]{0:T(256)S(1)} %div.48, bf16[32,8,512]{2,1,0:T(8,128)(2,1)S(1)} %gather_fusion.1, pred[32]{0:T(512)(128)(4,1)S(1)} %compare_and_fusion.2), kind=kOutput, calls=%fused_computation.17 | convolution fusion | flops 540147712 | bytes 5507104 | tf_op jit(solution)/shard_map/dot_general | solution.py:91
  48.5 1.0 copy-done.1
  50.0 2.1 %multiply_convert_fusion.1 = (bf16[8,256,256]{2,1,0:T(8,128)(2,1)S(1)}, f32[8,256,256]{2,1,0:T(8,128)}) fusion(pred[256,256]{1,0:T(8,128)(4,1)S(1)} %fusion.24, bf16[256,8,64]{0,2,1:T(8,128)(2,1)S(1)} %bitcast.129, bf16[256,8,64]{0,2,1:T(8,128)(2,1)S(1)} %bitcast.131), kind=kOutput, calls=%fused_computation.15 | convolution fusion | flops 70778880 | bytes 3735552 | tf_op jit(solution)/shard_map/jvp(qhd,khd->hqk)/dot_general | solution.py:49
  52.1 0.5 fusion.38
  52.6 0.2 copy.34
  52.9 1.4 multiply_reduce_fusion
  54.3 1.3 fusion.36
  55.8 0.8 copy.35
  56.6 2.0 %fusion.39 = bf16[8,64,256]{2,1,0:T(8,128)(2,1)} fusion(bf16[8,64,256]{2,1,0:T(8,128)(2,1)} %bitcast.134, bf16[8,256,256]{2,1,0:T(8,128)(2,1)S(1)} %get-tuple-element.28), kind=kOutput, calls=%fused_computation.109 | convolution fusion | flops 67108864 | bytes 1572864 | tf_op jit(solution)/shard_map/transpose(jvp(hqk,khd->qhd))/dot_general | solution.py:51
  58.6 2.8 %fusion.1 = bf16[8,256,256]{2,1,0:T(8,128)(2,1)S(1)} fusion(f32[8,256,256]{2,1,0:T(8,128)} %get-tuple-element.29, bf16[8,64,256]{2,1,0:T(8,128)(2,1)} %bitcast.135, bf16[256,8,64]{0,2,1:T(8,128)(2,1)S(1)} %bitcast.124, pred[256,256]{1,0:T(8,128)(4,1)S(1)} %fusion.24), kind=kOutput, calls=%fused_computation.13 | convolution fusion | flops 73924608 | bytes 3735552 | tf_op jit(solution)/shard_map/transpose(jvp(hqk,khd->qhd))/dot_general | solution.py:51
  61.4 0.4 fusion.40
  61.9 0.3 fusion.41
  62.7 0.8 copy.36
  63.5 1.2 convolution_convert_fusion.2
  64.7 2.4 %multiply_convert_fusion = bf16[256,2048]{1,0:T(8,128)(2,1)S(1)} fusion(f32[256,2048]{1,0:T(8,128)} %get-tuple-element.27, bf16[256,512]{1,0:T(8,128)(2,1)S(1)} %get-tuple-element.14, bf16[256,512]{1,0:T(8,128)(2,1)S(1)} %copy.38, bf16[256,512]{1,0:T(8,128)(2,1)S(1)} %copy.37, bf16[256,512]{1,0:T(8,128)(2,1)} %copy.36), kind=kLoop, calls=%fused_computation.14 | loop fusion | flops 8912896 | bytes 4194304 | tf_op jit(solution)/shard_map/convert_element_type | solution.py:98
  67.2 2.2 %convolution_convert_fusion = bf16[512,2048]{1,0:T(8,128)(2,1)} fusion(bf16[256,2048]{1,0:T(8,128)(2,1)S(1)} %multiply_convert_fusion, f32[256]{0:T(256)S(1)} %rsqrt.22, f32[256]{0:T(256)S(1)} %div.48, bf16[32,8,512]{2,1,0:T(8,128)(2,1)S(1)} %gather_fusion.1, pred[32]{0:T(512)(128)(4,1)S(1)} %compare_and_fusion.2), kind=kOutput, calls=%fused_computation.11 | convolution fusion | flops 538574848 | bytes 3409952 | tf_op jit(solution)/shard_map/dot_general | solution.py:119
  69.4 0.7 scatter_custom_fusion
  70.1 2.5 %fusion.35 = (f32[256]{0:T(256)S(1)}, f32[256]{0:T(256)S(1)}, f32[256,512]{1,0:T(8,128)S(1)}) fusion(f32[256]{0:T(256)S(1)} %rsqrt.22, f32[256]{0:T(256)S(1)} %div.48, bf16[32,8,512]{2,1,0:T(8,128)(2,1)S(1)} %gather_fusion.1, pred[32]{0:T(512)(128)(4,1)S(1)} %compare_and_fusion.2, bf16[256,2048]{1,0:T(8,128)(2,1)S(1)} %multiply_convert_fusion, ...), kind=kOutput, calls=%fused_computation.105 | convolution fusion | flops 537787904 | bytes 3936288 | tf_op jit(solution)/shard_map/dot_general | solution.py:99
  72.6 0.3 fusion.20
  72.9 0.6 gather_fusion.6
  73.5 0.3 fusion.4
  73.8 0.6 gather_fusion.2
  74.4 0.9 broadcast_select_fusion
  75.3 3.4 %all-to-all-start.3 = ((bf16[4,64,512]{2,1,0:T(8,128)(2,1)}), bf16[4,64,512]{2,1,0:T(8,128)(2,1)S(1)}, u32[]{:S(2)}, u32[]{:S(2)}) async-start(bf16[4,64,512]{2,1,0:T(8,128)(2,1)} %bitcast.37), calls=%async_computation.3 | async-start | bytes 524288 | tf_op jit(solution)/shard_map/all_to_all | solution.py:112
  78.8 0.7 scatter_custom_fusion.1
  79.4 6.2 %all-to-all-done.3 = bf16[4,64,512]{2,1,0:T(8,128)(2,1)S(1)} async-done(((bf16[4,64,512]{2,1,0:T(8,128)(2,1)}), bf16[4,64,512]{2,1,0:T(8,128)(2,1)S(1)}, u32[]{:S(2)}, u32[]{:S(2)}) %all-to-all-start.3) | async-done | bytes 262176 | tf_op jit(solution)/shard_map/all_to_all | solution.py:112
  85.7 3.4 %all-to-all-start.1 = ((bf16[4,64,512]{2,1,0:T(8,128)(2,1)}), bf16[4,64,512]{2,1,0:T(8,128)(2,1)S(1)}, u32[]{:S(2)}, u32[]{:S(2)}) async-start(bf16[4,64,512]{2,1,0:T(8,128)(2,1)} %bitcast.20), calls=%async_computation.1 | async-start | bytes 524288 | tf_op jit(solution)/shard_map/all_to_all | solution.py:109
  89.1 8.0 %reduce-scatter.5.cloned.1.call-done = bf16[64,512]{1,0:T(8,128)(2,1)} async-done(((bf16[512,512]{1,0:T(8,128)(2,1)}), bf16[64,512]{1,0:T(8,128)(2,1)}) %reduce-scatter.5.cloned.1.call-update) | async-done | bytes 65552 | tf_op jit(solution)/shard_map/reduce_scatter | solution.py:126
  97.1 44.9 %reduce-scatter.3.cloned.1.call-done = bf16[64,2048]{1,0:T(8,128)(2,1)} async-done(((bf16[512,2048]{1,0:T(8,128)(2,1)}), bf16[64,2048]{1,0:T(8,128)(2,1)}) %reduce-scatter.3.cloned.1.call-update) | async-done | bytes 262160 | tf_op jit(solution)/shard_map/reduce_scatter | solution.py:123
  142.0 0.6 gather_fusion.7
  142.6 0.6 gather_fusion.3
  143.2 0.9 select_bitcast_fusion
  144.1 36.5 %all-reduce.7.cloned.1.call-done = (bf16[64,2048]{1,0:T(8,128)(2,1)}, bf16[64,512]{1,0:T(8,128)(2,1)}) async-done(((bf16[64,2048]{1,0:T(8,128)(2,1)}, bf16[64,512]{1,0:T(8,128)(2,1)}), (bf16[64,2048]{1,0:T(8,128)(2,1)}, bf16[64,512]{1,0:T(8,128)(2,1)})) %all-reduce.7.cloned.1.call-update) | async-done | bytes 327696 | tf_op jit(solution)/shard_map/psum | solution.py:134
  180.6 1.8 convert_element_type.120
  182.4 1.5 convert_element_type.122
  (74 shorter events, 2.4 us)
Async XLA Ops:
  7.2 1.5 copy-start
  7.2 11.4 %copy-start.11 = (s32[1,1,8]{2,1,0:T(1,128)S(1)}, s32[1,1,8]{2,1,0:T(1,128)}, u32[]{:S(2)}) copy-start(s32[1,1,8]{2,1,0:T(1,128)} %param.16) | copy-start | bytes 100
  7.2 11.7 %copy-start.10 = (s32[1,1,8]{2,1,0:T(1,128)S(1)}, s32[1,1,8]{2,1,0:T(1,128)}, u32[]{:S(2)}) copy-start(s32[1,1,8]{2,1,0:T(1,128)} %param.17) | copy-start | bytes 100
  7.2 11.8 %copy-start.12 = (s32[1,1,32]{2,1,0:T(1,128)S(1)}, s32[1,1,32]{2,1,0:T(1,128)}, u32[]{:S(2)}) copy-start(s32[1,1,32]{2,1,0:T(1,128)} %param.15) | copy-start | bytes 388
  7.2 11.8 %copy-start.9 = (bf16[64,512]{1,0:T(8,128)(2,1)S(1)}, bf16[64,512]{1,0:T(8,128)(2,1)}, u32[]{:S(2)}) copy-start(bf16[64,512]{1,0:T(8,128)(2,1)} %param.13) | copy-start | bytes 196612
  7.2 37.6 %all-gather.2.cloned.1.call-start = ((), (), s32[]{:S(2)}) async-start(), calls=%async_computation.6 | async-start | bytes 2359296 | tf_op jit(solution)/shard_map/all_gather | solution.py:78
  12.3 17.4 %all-to-all-start = ((bf16[4,64,512]{2,1,0:T(8,128)(2,1)}), bf16[4,64,512]{2,1,0:T(8,128)(2,1)S(1)}, u32[]{:S(2)}, u32[]{:S(2)}) async-start(bf16[4,64,512]{2,1,0:T(8,128)(2,1)} %bitcast.7), calls=%async_computation | async-start | bytes 524288 | tf_op jit(solution)/shard_map/all_to_all | solution.py:83
  29.7 14.4 %all-to-all-start.2 = ((bf16[4,64,512]{2,1,0:T(8,128)(2,1)}), bf16[4,64,512]{2,1,0:T(8,128)(2,1)S(1)}, u32[]{:S(2)}, u32[]{:S(2)}) async-start(bf16[4,64,512]{2,1,0:T(8,128)(2,1)} %bitcast.24), calls=%async_computation.2 | async-start | bytes 524288 | tf_op jit(solution)/shard_map/all_to_all | solution.py:84
  34.8 62.3 %reduce-scatter.5.cloned.1.call-start = ((), (), s32[]{:S(2)}) async-start(), calls=%async_computation.8 | async-start | bytes 589824 | tf_op jit(solution)/shard_map/reduce_scatter | solution.py:126
  48.5 1.0 copy-start.1
  49.7 2.4 %copy-start.2 = (bf16[256,512]{0,1:T(8,128)(2,1)}, bf16[256,512]{0,1:T(8,128)(2,1)S(1)}, u32[]{:S(2)}) copy-start(bf16[256,512]{0,1:T(8,128)(2,1)S(1)} %copy.31) | copy-start | bytes 786436
  49.9 2.2 %copy-start.4 = (bf16[256,512]{0,1:T(8,128)(2,1)}, bf16[256,512]{0,1:T(8,128)(2,1)S(1)}, u32[]{:S(2)}) copy-start(bf16[256,512]{0,1:T(8,128)(2,1)S(1)} %copy.32) | copy-start | bytes 786436
  50.0 2.1 %copy-start.6 = (bf16[256,512]{0,1:T(8,128)(2,1)}, bf16[256,512]{0,1:T(8,128)(2,1)S(1)}, u32[]{:S(2)}) copy-start(bf16[256,512]{0,1:T(8,128)(2,1)S(1)} %copy.33) | copy-start | bytes 786436
  55.6 2.9 %copy-start.3 = (bf16[256,512]{0,1:T(8,128)(2,1)S(1)}, bf16[256,512]{0,1:T(8,128)(2,1)}, u32[]{:S(2)}) copy-start(bf16[256,512]{0,1:T(8,128)(2,1)} %copy-done.2) | copy-start | bytes 786436
  58.6 2.8 %copy-start.7 = (bf16[256,512]{0,1:T(8,128)(2,1)S(1)}, bf16[256,512]{0,1:T(8,128)(2,1)}, u32[]{:S(2)}) copy-start(bf16[256,512]{0,1:T(8,128)(2,1)} %copy-done.6) | copy-start | bytes 786436
  58.6 3.3 %copy-start.5 = (bf16[256,512]{0,1:T(8,128)(2,1)S(1)}, bf16[256,512]{0,1:T(8,128)(2,1)}, u32[]{:S(2)}) copy-start(bf16[256,512]{0,1:T(8,128)(2,1)} %copy-done.4) | copy-start | bytes 786436
  61.4 1.0 copy-start.8
  64.7 77.3 %reduce-scatter.3.cloned.1.call-start = ((), (), s32[]{:S(2)}) async-start(), calls=%async_computation.7 | async-start | bytes 2359296 | tf_op jit(solution)/shard_map/reduce_scatter | solution.py:123
  72.9 5.8 %copy-start.13 = (s32[1,1,32]{2,1,0:T(1,128)S(1)}, s32[1,1,32]{2,1,0:T(1,128)}, u32[]{:S(2)}) copy-start(s32[1,1,32]{2,1,0:T(1,128)} %param.14) | copy-start | bytes 388
  75.3 10.3 %all-to-all-start.3 = ((bf16[4,64,512]{2,1,0:T(8,128)(2,1)}), bf16[4,64,512]{2,1,0:T(8,128)(2,1)S(1)}, u32[]{:S(2)}, u32[]{:S(2)}) async-start(bf16[4,64,512]{2,1,0:T(8,128)(2,1)} %bitcast.37), calls=%async_computation.3 | async-start | bytes 524288 | tf_op jit(solution)/shard_map/all_to_all | solution.py:112
  85.7 57.0 %all-to-all-start.1 = ((bf16[4,64,512]{2,1,0:T(8,128)(2,1)}), bf16[4,64,512]{2,1,0:T(8,128)(2,1)S(1)}, u32[]{:S(2)}, u32[]{:S(2)}) async-start(bf16[4,64,512]{2,1,0:T(8,128)(2,1)} %bitcast.20), calls=%async_computation.1 | async-start | bytes 524288 | tf_op jit(solution)/shard_map/all_to_all | solution.py:109
  89.1 91.5 %all-reduce.7.cloned.1.call-start = ((), (), s32[]{:S(2)}) async-start(), calls=%async_computation.9 | async-start | bytes 655360 | tf_op jit(solution)/shard_map/psum | solution.py:134
Sparse Core Ops, SparseCore 0:
  9.9 31.5 all-gather.1
  64.8 32.2 reduce-scatter.4
  100.8 41.2 reduce-scatter.2
  144.3 36.2 all-reduce.6
where the time goes:
time: 191 us; the launch traced here: 190 us
  waiting for transfers between devices  104 us (54%)
  matrix products  19.3 us (10%)
  starting transfers between devices  18.3 us (10%)
  between operations  14.3 us (7%)
  other arithmetic  12.6 us (7%)
  local copies, waits for them, and re-layouts  10.9 us (6%)
  blocking collectives  10.5 us (5%)
    reduce_scatter x1, waiting for transfers between devices, on_device(): lax.psum_scatter(part_uvqk.astype(jnp.bfloat16), 'group', scatter_dimensi...  44.9 us
    psum x1, waiting for transfers between devices, on_device(): lax.psum(part_proj.astype(jnp.bfloat16), 'shuf').astype(jnp.float32)  36.5 us
    all_gather x1, blocking collectives, on_device(): lax.all_gather(w_out, 'group', axis=0, tiled=True)  10.5 us
    all_to_all x1, waiting for transfers between devices, on_device(): lax.all_to_all(outgoing[1], 'shuf', split_axis=0, concat_axis=0, tiled=True)  8.16 us
    reduce_scatter x1, waiting for transfers between devices, on_device(): lax.psum_scatter(grad_weight.astype(jnp.float32).astype(jnp.bfloat16), 'g...  7.97 us
    all_to_all x1, starting transfers between devices, on_device(): lax.all_to_all(outgoing[0], 'shuf', split_axis=0, concat_axis=0, tiled=True)  6.32 us
    all_to_all x1, waiting for transfers between devices, on_device(): lax.all_to_all(regroup(grad_rows, recv_back), 'shuf', split_axis=0, conca...  6.22 us
    gather x8, local copies, waits for them, and re-layouts, regroup(): jnp.take(array.reshape(blocks, block_rows, feature_width), order, axis=0)  5.5 us
  transfers between devices with their start and end apart: 8, of which 5 were waited for; matrix products, arithmetic and copies ran while one was open for 10% of the time, Pallas kernels for 0%

commit v1 on v0

v1 whole, which is shorter than its diff:
```python
from functools import partial

import jax
import jax.numpy as jnp
from jax import lax
from jax.experimental import pallas as pl
from jax.experimental.pallas import tpu as pltpu
from jax.sharding import PartitionSpec as P

HEADS = 8
norm_eps = 1e-05
F32 = jnp.float32
BF16 = jnp.bfloat16
VMEM = pl.BlockSpec(memory_space=pltpu.VMEM)
SMEM = pl.BlockSpec(memory_space=pltpu.SMEM)
NN = (((1,), (0,)), ((), ()))
NT = (((1,), (1,)), ((), ()))
TN = (((0,), (0,)), ((), ()))


def dot(a, b, dims=NN):
    return lax.dot_general(a, b, dims, preferred_element_type=F32)


def sigmoid(values):
    return 0.5 * jnp.tanh(0.5 * values) + 0.5


def normalize(values):
    center = jnp.mean(values, axis=-1, keepdims=True)
    centred = values - center
    variance = jnp.mean(centred * centred, axis=-1, keepdims=True)
    inv_scale = lax.rsqrt(variance + norm_eps)
    return (centred * inv_scale, inv_scale)


def exchange(value, axis, size, mask):
    return lax.ppermute(value, axis, [(i, i ^ mask) for i in range(size)])


def global_row(index, me, chunk):
    place = lax.div(index, chunk)
    return (me ^ place) * chunk + (index - place * chunk)


def looked_up(order_ref, row):
    blocks = order_ref.shape[1]
    block = row.shape[0] // blocks
    at = lax.div(row, block)
    lane = lax.broadcasted_iota(jnp.int32, (row.shape[0], blocks), 1)
    picked = jnp.where(at == lane, order_ref[...], 0).astype(F32)
    found = jnp.sum(picked, axis=1, keepdims=True).astype(jnp.int32)
    return found * block + (row - at * block)


def send_matrix(order_ref, me, rows, chunk):
    row = lax.broadcasted_iota(jnp.int32, (rows, 1), 0)
    source = looked_up(order_ref, global_row(row, me, chunk))
    lane = lax.broadcasted_iota(jnp.int32, (rows, rows), 1)
    return (source == lane).astype(F32).astype(BF16)


def recv_matrix(order_ref, me, rows, chunk):
    row = lax.broadcasted_iota(jnp.int32, (rows, 1), 0)
    source = looked_up(order_ref, row)
    lane = lax.broadcasted_iota(jnp.int32, (rows, rows), 1)
    return (source == global_row(lane, me, chunk)).astype(F32).astype(BF16)


def stacked(refs, which):
    return jnp.concatenate([ref[which] for ref in refs], axis=0)


def pre_kernel(parts, me_ref, order_ref, x_ref, cot_ref, uvqk_ref, out_ref, w_ref, *send_refs):
    rows = x_ref.shape[0]
    columns = uvqk_ref.shape[1]
    w_ref[:, :columns] = uvqk_ref[...]
    w_ref[:, columns:] = out_ref[...]
    matrix = send_matrix(order_ref, me_ref[0], rows, rows // parts)
    step = rows // len(send_refs)
    for which, ref in enumerate((x_ref, cot_ref)):
        ordered = dot(matrix, ref[...]).astype(BF16)
        for k, send in enumerate(send_refs):
            send[which] = ordered[k * step : (k + 1) * step]


def post_kernel(parts, me_ref, order_ref, *refs):
    back_refs, (out_ref, grad_ref) = refs[:-2], refs[-2:]
    rows = out_ref.shape[0]
    matrix = send_matrix(order_ref, me_ref[0], rows, rows // parts)
    for which, ref in enumerate((out_ref, grad_ref)):
        ref[...] = dot(matrix, stacked(back_refs, which), TN).astype(BF16)


def layer_kernel(
    parts,
    groups,
    n_rows,
    me_ref,
    lengths_ref,
    prefixes_ref,
    order_ref,
    *refs,
):
    row_refs, refs = refs[:n_rows], refs[n_rows:]
    weight_refs, refs = refs[:groups], refs[groups:]
    back_refs, refs = refs[:n_rows], refs[n_rows:]
    keep_ref, give_ref, refs = refs[0], refs[1], refs[2:]
    w_ref, xt_ref, gt_ref, act_ref, slope_ref, mix_ref, weights_ref, bend_ref, gproj_ref = refs
    rows, width = mix_ref.shape
    shard = width // groups
    group_me, shuf_me = me_ref[1], me_ref[0]

    matrix = recv_matrix(order_ref, shuf_me, rows, rows // parts)
    x = dot(matrix, stacked(row_refs, 0))
    cot = dot(matrix, stacked(row_refs, 1))
    cot_b = cot.astype(BF16)
    z, inv_scale = normalize(x)
    xn = z.astype(BF16)
    xt_ref[...] = xn.T

    def shard_rows(k):
        return pl.ds(pl.multiple_of((group_me ^ k) * shard, shard), shard)

    for k in range(groups):
        w_ref[shard_rows(k), :] = weight_refs[k][...]

    for c in range(4):
        cols = slice(c * width, (c + 1) * width)
        projected = dot(xn, w_ref[:, cols])
        s = sigmoid(projected)
        act = projected * s
        act_ref[:, cols] = act.astype(BF16)
        slope_ref[:, cols] = s + act * (1.0 - s)

    row = lax.broadcasted_iota(jnp.int32, (rows, 1), 0)
    low = jnp.zeros((rows, 1), jnp.int32)
    high = jnp.zeros((rows, 1), jnp.int32)
    start = jnp.int32(0)
    for u in range(lengths_ref.shape[0]):
        end = start + lengths_ref[u]
        mine = (row >= start) & (row < end)
        reach = jnp.minimum(end, jnp.maximum(row + 1, start + prefixes_ref[u]))
        low = jnp.where(mine, start, low)
        high = jnp.where(mine, reach, high)
        start = end
    lane = lax.broadcasted_iota(jnp.int32, (rows, rows), 1)
    scale = jnp.where((lane >= low) & (lane < high), 1.0 / rows, 0.0)

    head_width = width // HEADS
    per = max(1, 128 // head_width)
    wide = per * head_width
    place = lax.div(lax.broadcasted_iota(jnp.int32, (rows, wide), 1), head_width)

    def only(value, h):
        return jnp.where(place == h, value, jnp.zeros_like(value)) if per > 1 else value

    def cut(ref, block, g):
        return ref[:, block * width + g * wide : block * width + (g + 1) * wide]

    for g in range(HEADS // per):
        v, q, k = cut(act_ref, 1, g), cut(act_ref, 2, g), cut(act_ref, 3, g)
        mixed = jnp.zeros((rows, wide), F32)
        for h in range(per):
            scores = dot(only(q, h), k, NT)
            s = sigmoid(scores)
            value = scores * s
            weights = (value * scale).astype(BF16)
            weights_ref[g * per + h] = weights
            bend_ref[g * per + h] = (s + value * (1.0 - s)) * scale
            mixed += dot(weights, only(v, h))
        mix_ref[:, g * wide : (g + 1) * wide] = mixed

    normed, mix_inv = normalize(mix_ref[...])
    gate = act_ref[:, :width].astype(F32)
    gated = (normed * gate).astype(BF16)
    gt_ref[...] = gated.T
    w_out = w_ref[:, 4 * width :]
    out = (dot(gated, w_out) + x).astype(BF16)

    g_gated = dot(cot_b, w_out, NT).astype(BF16).astype(F32)
    gproj_ref[:, :width] = ((g_gated * normed).astype(BF16).astype(F32) * slope_ref[:, :width]).astype(BF16)
    g_normed = g_gated * gate
    g_mixed = mix_inv * (
        g_normed
        - jnp.mean(g_normed, axis=-1, keepdims=True)
        - normed * jnp.mean(g_normed * normed, axis=-1, keepdims=True)
    )
    mix_ref[...] = g_mixed

    for g in range(HEADS // per):
        v, q, k = cut(act_ref, 1, g), cut(act_ref, 2, g), cut(act_ref, 3, g)
        g_mix = mix_ref[:, g * wide : (g + 1) * wide].astype(BF16)
        g_v = jnp.zeros((rows, wide), F32)
        g_q = jnp.zeros((rows, wide), F32)
        g_k = jnp.zeros((rows, wide), F32)
        for h in range(per):
            mine = only(g_mix, h)
            g_weights = dot(mine, v, NT).astype(BF16).astype(F32)
            g_scores = (g_weights * bend_ref[g * per + h]).astype(BF16)
            g_v += dot(weights_ref[g * per + h], mine, TN)
            g_q += dot(g_scores, only(k, h))
            g_k += dot(g_scores, only(q, h), TN)
        for block, value in ((1, g_v), (2, g_q), (3, g_k)):
            at = slice(block * width + g * wide, block * width + (g + 1) * wide)
            gproj_ref[:, at] = (value.astype(BF16).astype(F32) * slope_ref[:, at]).astype(BF16)

    for which, ref in ((0, keep_ref), (1, give_ref)):
        picked = [2 * m + which for m in range(groups // 2)]
        lhs = jnp.concatenate([xt_ref[shard_rows(k), :] for k in picked], axis=0)
        lhs_out = jnp.concatenate([gt_ref[shard_rows(k), :] for k in picked], axis=0)
        for c in range(4):
            cols = slice(c * width, (c + 1) * width)
            ref[:, cols] = dot(lhs, gproj_ref[:, cols]).astype(BF16)
        ref[:, 4 * width :] = dot(lhs_out, cot_b).astype(BF16)

    g_xn = dot(gproj_ref[...], w_ref[:, : 4 * width], NT)
    g_x = (
        inv_scale
        * (
            g_xn
            - jnp.mean(g_xn, axis=-1, keepdims=True)
            - z * jnp.mean(g_xn * z, axis=-1, keepdims=True)
        )
        + cot
    ).astype(BF16)
    step = rows // n_rows
    for which, value in ((0, out), (1, g_x)):
        back = dot(matrix, value, TN).astype(BF16)
        for k, ref in enumerate(back_refs):
            ref[which] = back[k * step : (k + 1) * step]


def on_device(groups, parts, inputs, cotangent, w_uvqk, w_out, send_perm, recv_perm, lengths, prefixes):
    rows, width = inputs.shape[1:]
    shard = w_uvqk.shape[0]
    columns = w_uvqk.shape[1] + w_out.shape[1]
    chunk = rows // parts
    whole_tiles = chunk % 16 == 0
    n_rows = parts if whole_tiles else 1
    me = jnp.stack([lax.axis_index("shuf"), lax.axis_index("group")]).astype(jnp.int32)
    send_order, recv_order = send_perm[0], recv_perm[0]
    limit = pltpu.CompilerParams(vmem_limit_bytes=40 * 1024 * 1024)
    rows_shape = jax.ShapeDtypeStruct((2, rows // n_rows, width), BF16)

    def swap_rows(pieces):
        if not whole_tiles:
            cut = pieces[0].reshape(2, parts, chunk, width)
            pieces = [cut[:, k] for k in range(parts)]
        moved = [pieces[0]] + [exchange(pieces[k], "shuf", parts, k) for k in range(1, parts)]
        return moved if whole_tiles else [jnp.concatenate(moved, axis=1)]

    w_mine, *outgoing = pl.pallas_call(
        partial(pre_kernel, parts),
        out_shape=[jax.ShapeDtypeStruct((shard, columns), BF16)] + [rows_shape] * n_rows,
        in_specs=[SMEM] + [VMEM] * 5,
        out_specs=[VMEM] * (1 + n_rows),
        compiler_params=limit,
        name="pre",
    )(me, send_order, inputs[0], cotangent[0], w_uvqk, w_out)

    shards = [None] * groups
    for k in range(0, groups, 2):
        shards[k] = w_mine if k == 0 else exchange(w_mine, "group", groups, k)
    for k in range(0, groups, 2):
        shards[k + 1] = exchange(shards[k], "group", groups, 1)
    arrived = swap_rows(outgoing)

    half = groups // 2 * shard
    *returning, keep, give = pl.pallas_call(
        partial(layer_kernel, parts, groups, n_rows),
        out_shape=[rows_shape] * n_rows + [jax.ShapeDtypeStruct((half, columns), BF16)] * 2,
        in_specs=[SMEM] * 3 + [VMEM] * (1 + n_rows + groups),
        out_specs=[VMEM] * (n_rows + 2),
        scratch_shapes=[
            pltpu.VMEM((width, columns), BF16),
            pltpu.VMEM((width, rows), BF16),
            pltpu.VMEM((width, rows), BF16),
            pltpu.VMEM((rows, 4 * width), BF16),
            pltpu.VMEM((rows, 4 * width), F32),
            pltpu.VMEM((rows, width), F32),
            pltpu.VMEM((HEADS, rows, rows), BF16),
            pltpu.VMEM((HEADS, rows, rows), F32),
            pltpu.VMEM((rows, 4 * width), BF16),
        ],
        compiler_params=limit,
        name="layer",
    )(me, lengths[0, 0], prefixes[0, 0], recv_order, *arrived, *shards)

    taken = exchange(give, "group", groups, 1)
    chip = (keep.astype(F32) + taken.astype(F32)).astype(BF16).reshape(groups // 2, shard, columns)
    total = chip[0].astype(F32)
    for m in range(1, groups // 2):
        total = total + exchange(chip[m], "group", groups, 2 * m).astype(F32)
    masks = [2 ** (j + 1) - 1 for j in range(parts.bit_length() - 1)]
    first, second = total[: shard // 2].astype(BF16), total[shard // 2 :].astype(BF16)
    for mask_a, mask_b in zip(masks, reversed(masks)):
        first_f32 = first.astype(F32) + exchange(first, "shuf", parts, mask_a).astype(F32)
        second_f32 = second.astype(F32) + exchange(second, "shuf", parts, mask_b).astype(F32)
        first, second = first_f32.astype(BF16), second_f32.astype(BF16)
    total = jnp.concatenate([first_f32, second_f32], axis=0)
    grad_uvqk, grad_wout = total[:, : w_uvqk.shape[1]], total[:, w_uvqk.shape[1] :]

    owner_out, owner_grad = pl.pallas_call(
        partial(post_kernel, parts),
        out_shape=[jax.ShapeDtypeStruct((rows, width), BF16)] * 2,
        in_specs=[SMEM] + [VMEM] * (1 + n_rows),
        out_specs=[VMEM] * 2,
        compiler_params=limit,
        name="post",
    )(me, send_order, *swap_rows(returning))
    return (owner_out[None], owner_grad[None], grad_uvqk, grad_wout)


def solution(mesh):
    data, weight = P("group", "shuf", None), P("group", None)
    return jax.shard_map(
        partial(on_device, mesh.shape["group"], mesh.shape["shuf"]),
        mesh=mesh,
        in_specs=(data, data, weight, weight, data, data, data, data),
        out_specs=(data, data, weight, weight),
        check_vma=False,
    )
```

time: 191 us -> 106 us (0.55)
  waiting for transfers between devices: 104 us -> 57.2 us
  matrix products: 19.3 us -> 0 us
  between operations: 14.3 us -> 0.74 us
  starting transfers between devices: 18.3 us -> 29.5 us
  blocking collectives: 10.5 us -> 0 us
  other arithmetic: 12.6 us -> 2.27 us
  Pallas kernels: 0 us -> 10.1 us
  local copies, waits for them, and re-layouts: 10.9 us -> 6.39 us
    ppermute x0 -> x21, waiting for transfers between devices: none -> 57.2 us  [exchange(): return lax.ppermute(value, axis, [(i, i ^ mask) for i in range(size)])]
    reduce_scatter x2 -> x0, waiting for transfers between devices: 52.9 us -> none  [the longest x1 44.9 us: on_device(): lax.psum_scatter(part_uvqk.astype(jnp.bfloat16), 'group', scatter_dimensi...]
    psum x1 -> x0, waiting for transfers between devices: 36.5 us -> none  [on_device(): lax.psum(part_proj.astype(jnp.bfloat16), 'shuf').astype(jnp.float32)]
    ppermute x0 -> x21, starting transfers between devices: none -> 29.5 us  [exchange(): return lax.ppermute(value, axis, [(i, i ^ mask) for i in range(size)])]
    dot_general x12 -> x0, matrix products: 19.3 us -> none  [the longest x3 5.24 us: attention(): jnp.einsum('hqk,khd->qhd', weights, values, preferred_element_type=jnp.fl...]
    all_to_all x4 -> x0, starting transfers between devices: 18.2 us -> none  [the longest x1 6.32 us: on_device(): lax.all_to_all(outgoing[0], 'shuf', split_axis=0, concat_axis=0, tiled=True)]
    all_to_all x4 -> x0, waiting for transfers between devices: 14.4 us -> none  [the longest x1 8.16 us: on_device(): lax.all_to_all(outgoing[1], 'shuf', split_axis=0, concat_axis=0, tiled=True)]
    all_gather x1 -> x0, blocking collectives: 10.5 us -> none  [on_device(): lax.all_gather(w_out, 'group', axis=0, tiled=True)]
  transfers between devices with their start and end apart: 8 -> 21, of which waited for: 5 -> 14; matrix products, arithmetic and copies ran while one was open for 10% -> 0% of each run, Pallas kernels for 0% -> 2%
where the time goes in v1:
time: 106 us
  waiting for transfers between devices  57.2 us (54%)
  starting transfers between devices  29.5 us (28%)
  Pallas kernels  10.1 us (10%)
  local copies, waits for them, and re-layouts  6.39 us (6%)
  other arithmetic  2.27 us (2%)
    ppermute x21, waiting for transfers between devices, exchange(): return lax.ppermute(value, axis, [(i, i ^ mask) for i in range(size)])  57.2 us
    ppermute x21, starting transfers between devices, exchange(): return lax.ppermute(value, axis, [(i, i ^ mask) for i in range(size)])  29.5 us
    pallas_call x1, Pallas kernels, on_device(): pl.pallas_call(partial(layer_kernel, parts, groups, n_rows), out_shape=[r...  7.42 us
    unnamed x16, local copies, waits for them, and re-layouts  6.3 us
  transfers between devices with their start and end apart: 21, of which 14 were waited for; matrix products, arithmetic and copies ran while one was open for 0% of the time, Pallas kernels for 2%

profile of v1, /device:TPU:0, one launch (start us, length us, event | category | flops | bytes accessed | tf_op | source)
XLA Modules:
  0.0 106.2 jit_solution(13754074926268742207)
XLA Ops:
  0.6 0.1 pad_add_fusion.me_ref
  0.7 0.9 copy-done
  1.7 0.9 copy-done.1
  2.6 0.9 copy-done.2
  3.6 0.8 copy-done.3
  4.4 0.7 copy-done.4
  5.1 0.9 pre.1
  6.0 4.0 %collective-permute-start.8 = (bf16[64,2560]{1,0:T(8,128)(2,1)S(1)}, bf16[64,2560]{1,0:T(8,128)(2,1)S(1)}, u32[]{:S(2)}, u32[]{:S(2)}) collective-permute-start(bf16[64,2560]{1,0:T(8,128)(2,1)S(1)} %get-tuple-element.21.refs_4_), channel_id=1, source_target_pairs={{0,24},{4,28},{8,16},{12,20},{16,8},{20,12},{24,0},{28,4},{1,25},{... | collective-permute-start | bytes 983048 | tf_op jit(solution)/shard_map/ppermute | solution.py:38
  9.9 0.5 collective-permute-start.6
  10.4 0.1 collective-permute-start.4
  10.6 2.0 %collective-permute-start = (bf16[2,64,512]{2,1,0:T(8,128)(2,1)S(1)}, bf16[2,64,512]{2,1,0:T(8,128)(2,1)S(1)}, u32[]{:S(2)}, u32[]{:S(2)}) collective-permute-start(bf16[2,64,512]{2,1,0:T(8,128)(2,1)S(1)} %get-tuple-element.18), channel_id=1, source_target_pairs={{0,1},{1,0},{2,3},{3,2},{4,5},{5,4},{6,7},{7,6},{8,9},{9,8},{10,11... | collective-permute-start | bytes 393224 | tf_op jit(solution)/shard_map/ppermute | solution.py:38
  12.6 6.0 %collective-permute-done.8.refs_10_ = bf16[64,2560]{1,0:T(8,128)(2,1)S(1)} collective-permute-done((bf16[64,2560]{1,0:T(8,128)(2,1)S(1)}, bf16[64,2560]{1,0:T(8,128)(2,1)S(1)}, u32[]{:S(2)}, u32[]{:S(2)}) %collective-permute-start.8) | collective-permute-done | bytes 327712 | tf_op jit(solution)/shard_map/ppermute | solution.py:38
  18.5 6.1 %collective-permute-done.6.refs_8_ = bf16[64,2560]{1,0:T(8,128)(2,1)S(1)} collective-permute-done((bf16[64,2560]{1,0:T(8,128)(2,1)S(1)}, bf16[64,2560]{1,0:T(8,128)(2,1)S(1)}, u32[]{:S(2)}, u32[]{:S(2)}) %collective-permute-start.6) | collective-permute-done | bytes 327712 | tf_op jit(solution)/shard_map/ppermute | solution.py:38
  24.7 0.3 collective-permute-done.4.refs_6_
  25.0 0.2 collective-permute-start.5
  25.2 2.8 %collective-permute-start.1 = (bf16[2,64,512]{2,1,0:T(8,128)(2,1)S(1)}, bf16[2,64,512]{2,1,0:T(8,128)(2,1)S(1)}, u32[]{:S(2)}, u32[]{:S(2)}) collective-permute-start(bf16[2,64,512]{2,1,0:T(8,128)(2,1)S(1)} %get-tuple-element.19), channel_id=1, source_target_pairs={{0,2},{1,3},{2,0},{3,1},{4,6},{5,7},{6,4},{7,5},{8,10},{9,11},{10,... | collective-permute-start | bytes 393224 | tf_op jit(solution)/shard_map/ppermute | solution.py:38
  28.0 6.6 %collective-permute-done.1.refs_2_ = bf16[2,64,512]{2,1,0:T(8,128)(2,1)S(1)} collective-permute-done((bf16[2,64,512]{2,1,0:T(8,128)(2,1)S(1)}, bf16[2,64,512]{2,1,0:T(8,128)(2,1)S(1)}, u32[]{:S(2)}, u32[]{:S(2)}) %collective-permute-start.1) | collective-permute-done | bytes 131104 | tf_op jit(solution)/shard_map/ppermute | solution.py:38
  34.6 3.5 %collective-permute-start.2 = (bf16[2,64,512]{2,1,0:T(8,128)(2,1)S(1)}, bf16[2,64,512]{2,1,0:T(8,128)(2,1)S(1)}, u32[]{:S(2)}, u32[]{:S(2)}) collective-permute-start(bf16[2,64,512]{2,1,0:T(8,128)(2,1)S(1)} %get-tuple-element.20), channel_id=1, source_target_pairs={{0,3},{1,2},{2,1},{3,0},{4,7},{5,6},{6,5},{7,4},{8,11},{9,10},{10,... | collective-permute-start | bytes 393224 | tf_op jit(solution)/shard_map/ppermute | solution.py:38
  38.1 3.8 %collective-permute-done.2.refs_3_ = bf16[2,64,512]{2,1,0:T(8,128)(2,1)S(1)} collective-permute-done((bf16[2,64,512]{2,1,0:T(8,128)(2,1)S(1)}, bf16[2,64,512]{2,1,0:T(8,128)(2,1)S(1)}, u32[]{:S(2)}, u32[]{:S(2)}) %collective-permute-start.2) | collective-permute-done | bytes 131104 | tf_op jit(solution)/shard_map/ppermute | solution.py:38
  41.9 0.6 copy-done.5
  42.6 0.7 copy-done.6
  43.2 0.7 copy-done.7
  43.9 7.4 %layer.1 = (bf16[2,64,512]{2,1,0:T(8,128)(2,1)S(1)}, bf16[2,64,512]{2,1,0:T(8,128)(2,1)S(1)}, bf16[2,64,512]{2,1,0:T(8,128)(2,1)S(1)}, bf16[2,64,512]{2,1,0:T(8,...) custom-call(s32[2]{0:T(128)S(1)} %pad_add_fusion.me_ref, s32[8]{0:T(128)S(1)} %bitcast.14, ...), custom_call_target="tpu_custom_call" | custom-call | tf_op jit(solution)/shard_map/layer/pallas_call | solution.py:270
  51.3 0.1 collective-permute-start.13
  51.4 3.0 %collective-permute-done.13 = bf16[256,2560]{1,0:T(8,128)(2,1)S(1)} collective-permute-done((bf16[256,2560]{1,0:T(8,128)(2,1)S(1)}, bf16[256,2560]{1,0:T(8,128)(2,1)S(1)}, u32[]{:S(2)}, u32[]{:S(2)}) %collective-permute-start.13) | collective-permute-done | bytes 1310752 | tf_op jit(solution)/shard_map/ppermute | solution.py:38
  54.4 0.4 add_convert_fusion
  54.8 1.6 %collective-permute-start.14 = (bf16[64,2560]{1,0:T(8,128)(2,1)S(1)}, bf16[64,2560]{1,0:T(8,128)(2,1)S(1)}, u32[]{:S(2)}, u32[]{:S(2)}) collective-permute-start(bf16[64,2560]{1,0:T(8,128)(2,1)S(1)} %get-tuple-element.30), channel_id=1, source_target_pairs={{0,8},{4,12},{8,0},{12,4},{16,24},{20,28},{24,16},{28,20},{1,9},{5... | collective-permute-start | bytes 983048 | tf_op jit(solution)/shard_map/ppermute | solution.py:38
  56.4 1.5 %collective-permute-start.16 = (bf16[64,2560]{1,0:T(8,128)(2,1)S(1)}, bf16[64,2560]{1,0:T(8,128)(2,1)S(1)}, u32[]{:S(2)}, u32[]{:S(2)}) collective-permute-start(bf16[64,2560]{1,0:T(8,128)(2,1)S(1)} %get-tuple-element.31), channel_id=1, source_target_pairs={{0,24},{4,28},{8,16},{12,20},{16,8},{20,12},{24,0},{28,4},{1,25},{... | collective-permute-start | bytes 983048 | tf_op jit(solution)/shard_map/ppermute | solution.py:38
  57.9 0.5 collective-permute-start.15
  58.4 7.1 %collective-permute-done.14 = bf16[64,2560]{1,0:T(8,128)(2,1)S(1)} collective-permute-done((bf16[64,2560]{1,0:T(8,128)(2,1)S(1)}, bf16[64,2560]{1,0:T(8,128)(2,1)S(1)}, u32[]{:S(2)}, u32[]{:S(2)}) %collective-permute-start.14) | collective-permute-done | bytes 327712 | tf_op jit(solution)/shard_map/ppermute | solution.py:38
  65.5 7.3 %collective-permute-done.16 = bf16[64,2560]{1,0:T(8,128)(2,1)S(1)} collective-permute-done((bf16[64,2560]{1,0:T(8,128)(2,1)S(1)}, bf16[64,2560]{1,0:T(8,128)(2,1)S(1)}, u32[]{:S(2)}, u32[]{:S(2)}) %collective-permute-start.16) | collective-permute-done | bytes 327712 | tf_op jit(solution)/shard_map/ppermute | solution.py:38
  72.7 1.4 %collective-permute-done.15 = bf16[64,2560]{1,0:T(8,128)(2,1)S(1)} collective-permute-done((bf16[64,2560]{1,0:T(8,128)(2,1)S(1)}, bf16[64,2560]{1,0:T(8,128)(2,1)S(1)}, u32[]{:S(2)}, u32[]{:S(2)}) %collective-permute-start.15) | collective-permute-done | bytes 327712 | tf_op jit(solution)/shard_map/ppermute | solution.py:38
  74.1 0.2 add_convert_fusion.1
  74.3 3.5 %collective-permute-start.19 = (bf16[32,2560]{1,0:T(8,128)(2,1)S(1)}, bf16[32,2560]{1,0:T(8,128)(2,1)S(1)}, u32[]{:S(2)}, u32[]{:S(2)}) collective-permute-start(bf16[32,2560]{1,0:T(8,128)(2,1)S(1)} %get-tuple-element.35), channel_id=1, source_target_pairs={{0,3},{1,2},{2,1},{3,0},{4,7},{5,6},{6,5},{7,4},{8,11},{9,10},{10,... | collective-permute-start | bytes 491528 | tf_op jit(solution)/shard_map/ppermute | solution.py:38
  77.8 4.3 %collective-permute-done.19 = bf16[32,2560]{1,0:T(8,128)(2,1)S(1)} collective-permute-done((bf16[32,2560]{1,0:T(8,128)(2,1)S(1)}, bf16[32,2560]{1,0:T(8,128)(2,1)S(1)}, u32[]{:S(2)}, u32[]{:S(2)}) %collective-permute-start.19) | collective-permute-done | bytes 163872 | tf_op jit(solution)/shard_map/ppermute | solution.py:38
  82.1 1.9 %collective-permute-done.17 = bf16[32,2560]{1,0:T(8,128)(2,1)S(1)} collective-permute-done((bf16[32,2560]{1,0:T(8,128)(2,1)S(1)}, bf16[32,2560]{1,0:T(8,128)(2,1)S(1)}, u32[]{:S(2)}, u32[]{:S(2)}) %collective-permute-start.17) | collective-permute-done | bytes 163872 | tf_op jit(solution)/shard_map/ppermute | solution.py:38
  84.0 0.1 add_convert_fusion.2
  84.1 1.6 %collective-permute-start.20 = (bf16[32,2560]{1,0:T(8,128)(2,1)S(1)}, bf16[32,2560]{1,0:T(8,128)(2,1)S(1)}, u32[]{:S(2)}, u32[]{:S(2)}) collective-permute-start(bf16[32,2560]{1,0:T(8,128)(2,1)S(1)} %get-tuple-element.33), channel_id=1, source_target_pairs={{0,1},{1,0},{2,3},{3,2},{4,5},{5,4},{6,7},{7,6},{8,9},{9,8},{10,11... | collective-permute-start | bytes 491528 | tf_op jit(solution)/shard_map/ppermute | solution.py:38
  85.7 0.5 collective-permute-start.10
  86.2 0.5 collective-permute-start.11
  86.7 3.3 %collective-permute-start.12 = (bf16[2,64,512]{2,1,0:T(8,128)(2,1)S(1)}, bf16[2,64,512]{2,1,0:T(8,128)(2,1)S(1)}, u32[]{:S(2)}, u32[]{:S(2)}) collective-permute-start(bf16[2,64,512]{2,1,0:T(8,128)(2,1)S(1)} %get-tuple-element.25), channel_id=1, source_target_pairs={{0,3},{1,2},{2,1},{3,0},{4,7},{5,6},{6,5},{7,4},{8,11},{9,10},{10,... | collective-permute-start | bytes 393224 | tf_op jit(solution)/shard_map/ppermute | solution.py:38
  90.0 4.3 %collective-permute-done.10.refs_1_ = bf16[2,64,512]{2,1,0:T(8,128)(2,1)S(1)} collective-permute-done((bf16[2,64,512]{2,1,0:T(8,128)(2,1)S(1)}, bf16[2,64,512]{2,1,0:T(8,128)(2,1)S(1)}, u32[]{:S(2)}, u32[]{:S(2)}) %collective-permute-start.10) | collective-permute-done | bytes 131104 | tf_op jit(solution)/shard_map/ppermute | solution.py:38
  94.3 1.4 %collective-permute-done.12.refs_3_ = bf16[2,64,512]{2,1,0:T(8,128)(2,1)S(1)} collective-permute-done((bf16[2,64,512]{2,1,0:T(8,128)(2,1)S(1)}, bf16[2,64,512]{2,1,0:T(8,128)(2,1)S(1)}, u32[]{:S(2)}, u32[]{:S(2)}) %collective-permute-start.12) | collective-permute-done | bytes 131104 | tf_op jit(solution)/shard_map/ppermute | solution.py:38
  95.8 1.7 %post.1 = (bf16[256,512]{1,0:T(8,128)(2,1)}, bf16[256,512]{1,0:T(8,128)(2,1)}) custom-call(s32[2]{0:T(128)S(1)} %pad_add_fusion.me_ref, s32[1,32]{1,0:T(1,128)S(1)} %bitcast.13, bf16[2,64,512]{2,1,0:T(8,128)(2,1)S(1)} %get-tuple-element.22.refs_0_, bf16[2,64,512]{2,1,0:T(8,128)(2,1)S(1)} %collective-permute-done.10.refs_1_, ...), custom_call_target="tpu_custom_call" | custom-call | tf_op jit(solution)/shard_map/post/pallas_call | solution.py:304
  97.5 3.4 %collective-permute-start.18 = (bf16[32,2560]{1,0:T(8,128)(2,1)S(1)}, bf16[32,2560]{1,0:T(8,128)(2,1)S(1)}, u32[]{:S(2)}, u32[]{:S(2)}) collective-permute-start(bf16[32,2560]{1,0:T(8,128)(2,1)S(1)} %get-tuple-element.34), channel_id=1, source_target_pairs={{0,3},{1,2},{2,1},{3,0},{4,7},{5,6},{6,5},{7,4},{8,11},{9,10},{10,... | collective-permute-start | bytes 491528 | tf_op jit(solution)/shard_map/ppermute | solution.py:38
  100.9 3.7 %collective-permute-done.18 = bf16[32,2560]{1,0:T(8,128)(2,1)S(1)} collective-permute-done((bf16[32,2560]{1,0:T(8,128)(2,1)S(1)}, bf16[32,2560]{1,0:T(8,128)(2,1)S(1)}, u32[]{:S(2)}, u32[]{:S(2)}) %collective-permute-start.18) | collective-permute-done | bytes 163872 | tf_op jit(solution)/shard_map/ppermute | solution.py:38
  104.7 0.7 pad_maximum_fusion
  105.3 0.8 fusion
  (23 shorter events, 0.2 us)
Async XLA Ops:
  0.7 1.0 copy-start
  1.7 0.9 copy-start.1
  2.6 0.9 copy-start.2
  3.6 0.8 copy-start.3
  4.4 0.7 copy-start.4
  6.0 12.5 %collective-permute-start.8 = (bf16[64,2560]{1,0:T(8,128)(2,1)S(1)}, bf16[64,2560]{1,0:T(8,128)(2,1)S(1)}, u32[]{:S(2)}, u32[]{:S(2)}) collective-permute-start(bf16[64,2560]{1,0:T(8,128)(2,1)S(1)} %get-tuple-element.21.refs_4_), channel_id=1, source_target_pairs={{0,24},{4,28},{8,16},{12,20},{16,8},{20,12},{24,0},{28,4},{1,25},{... | collective-permute-start | bytes 983048 | tf_op jit(solution)/shard_map/ppermute | solution.py:38
  9.9 14.7 %collective-permute-start.6 = (bf16[64,2560]{1,0:T(8,128)(2,1)S(1)}, bf16[64,2560]{1,0:T(8,128)(2,1)S(1)}, u32[]{:S(2)}, u32[]{:S(2)}) collective-permute-start(bf16[64,2560]{1,0:T(8,128)(2,1)S(1)} %get-tuple-element.21.refs_4_), channel_id=1, source_target_pairs={{0,16},{4,20},{8,24},{12,28},{16,0},{20,4},{24,8},{28,12},{1,17},{... | collective-permute-start | bytes 983048 | tf_op jit(solution)/shard_map/ppermute | solution.py:38
  10.4 14.5 %collective-permute-start.4 = (bf16[64,2560]{1,0:T(8,128)(2,1)S(1)}, bf16[64,2560]{1,0:T(8,128)(2,1)S(1)}, u32[]{:S(2)}, u32[]{:S(2)}) collective-permute-start(bf16[64,2560]{1,0:T(8,128)(2,1)S(1)} %get-tuple-element.21.refs_4_), channel_id=1, source_target_pairs={{0,8},{4,12},{8,0},{12,4},{16,24},{20,28},{24,16},{28,20},{1,9},{5... | collective-permute-start | bytes 983048 | tf_op jit(solution)/shard_map/ppermute | solution.py:38
  10.6 14.6 %collective-permute-start = (bf16[2,64,512]{2,1,0:T(8,128)(2,1)S(1)}, bf16[2,64,512]{2,1,0:T(8,128)(2,1)S(1)}, u32[]{:S(2)}, u32[]{:S(2)}) collective-permute-start(bf16[2,64,512]{2,1,0:T(8,128)(2,1)S(1)} %get-tuple-element.18), channel_id=1, source_target_pairs={{0,1},{1,0},{2,3},{3,2},{4,5},{5,4},{6,7},{7,6},{8,9},{9,8},{10,11... | collective-permute-start | bytes 393224 | tf_op jit(solution)/shard_map/ppermute | solution.py:38
  12.5 29.3 %collective-permute-start.3 = (bf16[64,2560]{1,0:T(8,128)(2,1)S(1)}, bf16[64,2560]{1,0:T(8,128)(2,1)S(1)}, u32[]{:S(2)}, u32[]{:S(2)}) collective-permute-start(bf16[64,2560]{1,0:T(8,128)(2,1)S(1)} %get-tuple-element.21.refs_4_), channel_id=1, source_target_pairs={{0,4},{4,0},{8,12},{12,8},{16,20},{20,16},{24,28},{28,24},{1,5},{5... | collective-permute-start | bytes 983048 | tf_op jit(solution)/shard_map/ppermute | solution.py:38
  18.5 23.4 %collective-permute-start.9 = (bf16[64,2560]{1,0:T(8,128)(2,1)S(1)}, bf16[64,2560]{1,0:T(8,128)(2,1)S(1)}, u32[]{:S(2)}, u32[]{:S(2)}) collective-permute-start(bf16[64,2560]{1,0:T(8,128)(2,1)S(1)} %collective-permute-done.8.refs_10_), channel_id=1, source_target_pairs={{0,4},{4,0},{8,12},{12,8},{16,20},{20,16},{24,28},{28,24},{1,5},{5... | collective-permute-start | bytes 983048 | tf_op jit(solution)/shard_map/ppermute | solution.py:38
  24.7 17.2 %collective-permute-start.7 = (bf16[64,2560]{1,0:T(8,128)(2,1)S(1)}, bf16[64,2560]{1,0:T(8,128)(2,1)S(1)}, u32[]{:S(2)}, u32[]{:S(2)}) collective-permute-start(bf16[64,2560]{1,0:T(8,128)(2,1)S(1)} %collective-permute-done.6.refs_8_), channel_id=1, source_target_pairs={{0,4},{4,0},{8,12},{12,8},{16,20},{20,16},{24,28},{28,24},{1,5},{5... | collective-permute-start | bytes 983048 | tf_op jit(solution)/shard_map/ppermute | solution.py:38
  25.0 16.9 %collective-permute-start.5 = (bf16[64,2560]{1,0:T(8,128)(2,1)S(1)}, bf16[64,2560]{1,0:T(8,128)(2,1)S(1)}, u32[]{:S(2)}, u32[]{:S(2)}) collective-permute-start(bf16[64,2560]{1,0:T(8,128)(2,1)S(1)} %collective-permute-done.4.refs_6_), channel_id=1, source_target_pairs={{0,4},{4,0},{8,12},{12,8},{16,20},{20,16},{24,28},{28,24},{1,5},{5... | collective-permute-start | bytes 983048 | tf_op jit(solution)/shard_map/ppermute | solution.py:38
  25.2 9.4 %collective-permute-start.1 = (bf16[2,64,512]{2,1,0:T(8,128)(2,1)S(1)}, bf16[2,64,512]{2,1,0:T(8,128)(2,1)S(1)}, u32[]{:S(2)}, u32[]{:S(2)}) collective-permute-start(bf16[2,64,512]{2,1,0:T(8,128)(2,1)S(1)} %get-tuple-element.19), channel_id=1, source_target_pairs={{0,2},{1,3},{2,0},{3,1},{4,6},{5,7},{6,4},{7,5},{8,10},{9,11},{10,... | collective-permute-start | bytes 393224 | tf_op jit(solution)/shard_map/ppermute | solution.py:38
  34.6 7.3 %collective-permute-start.2 = (bf16[2,64,512]{2,1,0:T(8,128)(2,1)S(1)}, bf16[2,64,512]{2,1,0:T(8,128)(2,1)S(1)}, u32[]{:S(2)}, u32[]{:S(2)}) collective-permute-start(bf16[2,64,512]{2,1,0:T(8,128)(2,1)S(1)} %get-tuple-element.20), channel_id=1, source_target_pairs={{0,3},{1,2},{2,1},{3,0},{4,7},{5,6},{6,5},{7,4},{8,11},{9,10},{10,... | collective-permute-start | bytes 393224 | tf_op jit(solution)/shard_map/ppermute | solution.py:38
  41.9 0.7 copy-start.5
  42.5 0.7 copy-start.6
  43.2 0.7 copy-start.7
  51.3 3.1 %collective-permute-start.13 = (bf16[256,2560]{1,0:T(8,128)(2,1)S(1)}, bf16[256,2560]{1,0:T(8,128)(2,1)S(1)}, u32[]{:S(2)}, u32[]{:S(2)}) collective-permute-start(bf16[256,2560]{1,0:T(8,128)(2,1)S(1)} %get-tuple-element.29), channel_id=1, source_target_pairs={{0,4},{4,0},{8,12},{12,8},{16,20},{20,16},{24,28},{28,24},{1,5},{5... | collective-permute-start | bytes 3932168 | tf_op jit(solution)/shard_map/ppermute | solution.py:38
  54.8 10.6 %collective-permute-start.14 = (bf16[64,2560]{1,0:T(8,128)(2,1)S(1)}, bf16[64,2560]{1,0:T(8,128)(2,1)S(1)}, u32[]{:S(2)}, u32[]{:S(2)}) collective-permute-start(bf16[64,2560]{1,0:T(8,128)(2,1)S(1)} %get-tuple-element.30), channel_id=1, source_target_pairs={{0,8},{4,12},{8,0},{12,4},{16,24},{20,28},{24,16},{28,20},{1,9},{5... | collective-permute-start | bytes 983048 | tf_op jit(solution)/shard_map/ppermute | solution.py:38
  56.4 16.3 %collective-permute-start.16 = (bf16[64,2560]{1,0:T(8,128)(2,1)S(1)}, bf16[64,2560]{1,0:T(8,128)(2,1)S(1)}, u32[]{:S(2)}, u32[]{:S(2)}) collective-permute-start(bf16[64,2560]{1,0:T(8,128)(2,1)S(1)} %get-tuple-element.31), channel_id=1, source_target_pairs={{0,24},{4,28},{8,16},{12,20},{16,8},{20,12},{24,0},{28,4},{1,25},{... | collective-permute-start | bytes 983048 | tf_op jit(solution)/shard_map/ppermute | solution.py:38
  57.9 16.2 %collective-permute-start.15 = (bf16[64,2560]{1,0:T(8,128)(2,1)S(1)}, bf16[64,2560]{1,0:T(8,128)(2,1)S(1)}, u32[]{:S(2)}, u32[]{:S(2)}) collective-permute-start(bf16[64,2560]{1,0:T(8,128)(2,1)S(1)} %get-tuple-element.32), channel_id=1, source_target_pairs={{0,16},{4,20},{8,24},{12,28},{16,0},{20,4},{24,8},{28,12},{1,17},{... | collective-permute-start | bytes 983048 | tf_op jit(solution)/shard_map/ppermute | solution.py:38
  74.3 7.8 %collective-permute-start.19 = (bf16[32,2560]{1,0:T(8,128)(2,1)S(1)}, bf16[32,2560]{1,0:T(8,128)(2,1)S(1)}, u32[]{:S(2)}, u32[]{:S(2)}) collective-permute-start(bf16[32,2560]{1,0:T(8,128)(2,1)S(1)} %get-tuple-element.35), channel_id=1, source_target_pairs={{0,3},{1,2},{2,1},{3,0},{4,7},{5,6},{6,5},{7,4},{8,11},{9,10},{10,... | collective-permute-start | bytes 491528 | tf_op jit(solution)/shard_map/ppermute | solution.py:38
  77.8 6.2 %collective-permute-start.17 = (bf16[32,2560]{1,0:T(8,128)(2,1)S(1)}, bf16[32,2560]{1,0:T(8,128)(2,1)S(1)}, u32[]{:S(2)}, u32[]{:S(2)}) collective-permute-start(bf16[32,2560]{1,0:T(8,128)(2,1)S(1)} %get-tuple-element.36), channel_id=1, source_target_pairs={{0,1},{1,0},{2,3},{3,2},{4,5},{5,4},{6,7},{7,6},{8,9},{9,8},{10,11... | collective-permute-start | bytes 491528 | tf_op jit(solution)/shard_map/ppermute | solution.py:38
  84.1 16.8 %collective-permute-start.20 = (bf16[32,2560]{1,0:T(8,128)(2,1)S(1)}, bf16[32,2560]{1,0:T(8,128)(2,1)S(1)}, u32[]{:S(2)}, u32[]{:S(2)}) collective-permute-start(bf16[32,2560]{1,0:T(8,128)(2,1)S(1)} %get-tuple-element.33), channel_id=1, source_target_pairs={{0,1},{1,0},{2,3},{3,2},{4,5},{5,4},{6,7},{7,6},{8,9},{9,8},{10,11... | collective-permute-start | bytes 491528 | tf_op jit(solution)/shard_map/ppermute | solution.py:38
  85.7 8.7 %collective-permute-start.10 = (bf16[2,64,512]{2,1,0:T(8,128)(2,1)S(1)}, bf16[2,64,512]{2,1,0:T(8,128)(2,1)S(1)}, u32[]{:S(2)}, u32[]{:S(2)}) collective-permute-start(bf16[2,64,512]{2,1,0:T(8,128)(2,1)S(1)} %get-tuple-element.23), channel_id=1, source_target_pairs={{0,1},{1,0},{2,3},{3,2},{4,5},{5,4},{6,7},{7,6},{8,9},{9,8},{10,11... | collective-permute-start | bytes 393224 | tf_op jit(solution)/shard_map/ppermute | solution.py:38
  86.2 8.2 %collective-permute-start.11 = (bf16[2,64,512]{2,1,0:T(8,128)(2,1)S(1)}, bf16[2,64,512]{2,1,0:T(8,128)(2,1)S(1)}, u32[]{:S(2)}, u32[]{:S(2)}) collective-permute-start(bf16[2,64,512]{2,1,0:T(8,128)(2,1)S(1)} %get-tuple-element.24), channel_id=1, source_target_pairs={{0,2},{1,3},{2,0},{3,1},{4,6},{5,7},{6,4},{7,5},{8,10},{9,11},{10,... | collective-permute-start | bytes 393224 | tf_op jit(solution)/shard_map/ppermute | solution.py:38
  86.7 9.1 %collective-permute-start.12 = (bf16[2,64,512]{2,1,0:T(8,128)(2,1)S(1)}, bf16[2,64,512]{2,1,0:T(8,128)(2,1)S(1)}, u32[]{:S(2)}, u32[]{:S(2)}) collective-permute-start(bf16[2,64,512]{2,1,0:T(8,128)(2,1)S(1)} %get-tuple-element.25), channel_id=1, source_target_pairs={{0,3},{1,2},{2,1},{3,0},{4,7},{5,6},{6,5},{7,4},{8,11},{9,10},{10,... | collective-permute-start | bytes 393224 | tf_op jit(solution)/shard_map/ppermute | solution.py:38
  97.5 7.1 %collective-permute-start.18 = (bf16[32,2560]{1,0:T(8,128)(2,1)S(1)}, bf16[32,2560]{1,0:T(8,128)(2,1)S(1)}, u32[]{:S(2)}, u32[]{:S(2)}) collective-permute-start(bf16[32,2560]{1,0:T(8,128)(2,1)S(1)} %get-tuple-element.34), channel_id=1, source_target_pairs={{0,3},{1,2},{2,1},{3,0},{4,7},{5,6},{6,5},{7,4},{8,11},{9,10},{10,... | collective-permute-start | bytes 491528 | tf_op jit(solution)/shard_map/ppermute | solution.py:38

commit v2 on v1

--- a/solution.py
+++ b/solution.py
@@ -13,6 +13,7 @@
 BF16 = jnp.bfloat16
 VMEM = pl.BlockSpec(memory_space=pltpu.VMEM)
 SMEM = pl.BlockSpec(memory_space=pltpu.SMEM)
+HBM = pl.BlockSpec(memory_space=pltpu.HBM)
 NN = (((1,), (0,)), ((), ()))
 NT = (((1,), (1,)), ((), ()))
 TN = (((0,), (0,)), ((), ()))
@@ -71,11 +72,22 @@
     return jnp.concatenate([ref[which] for ref in refs], axis=0)
 
 
-def pre_kernel(parts, me_ref, order_ref, x_ref, cot_ref, uvqk_ref, out_ref, w_ref, *send_refs):
+def pre_kernel(parts, me_ref, order_in, x_in, cot_in, uvqk_in, out_in, w_ref, *refs):
+    send_refs, (order_ref, x_ref, cot_ref, sem) = refs[:-4], refs[-4:]
     rows = x_ref.shape[0]
-    columns = uvqk_ref.shape[1]
-    w_ref[:, :columns] = uvqk_ref[...]
-    w_ref[:, columns:] = out_ref[...]
+    columns = uvqk_in.shape[1]
+    moves = (
+        (order_in, order_ref),
+        (x_in, x_ref),
+        (cot_in, cot_ref),
+        (uvqk_in, w_ref.at[:, :columns]),
+        (out_in, w_ref.at[:, columns:]),
+    )
+    copies = [pltpu.make_async_copy(a, b, sem.at[n]) for n, (a, b) in enumerate(moves)]
+    for copy in copies:
+        copy.start()
+    for copy in copies:
+        copy.wait()
     matrix = send_matrix(order_ref, me_ref[0], rows, rows // parts)
     step = rows // len(send_refs)
     for which, ref in enumerate((x_ref, cot_ref)):
@@ -84,6 +96,31 @@
             send[which] = ordered[k * step : (k + 1) * step]
 
 
+def plan_kernel(parts, me_ref, order_in, lengths_in, prefixes_in, matrix_ref, scale_ref, *refs):
+    order_ref, lengths_ref, prefixes_ref, sem = refs
+    rows = matrix_ref.shape[0]
+    moves = ((order_in, order_ref), (lengths_in, lengths_ref), (prefixes_in, prefixes_ref))
+    copies = [pltpu.make_async_copy(a, b, sem.at[n]) for n, (a, b) in enumerate(moves)]
+    for copy in copies:
+        copy.start()
+    for copy in copies:
+        copy.wait()
+    matrix_ref[...] = recv_matrix(order_ref, me_ref[0], rows, rows // parts)
+    row = lax.broadcasted_iota(jnp.int32, (rows, 1), 0)
+    low = jnp.zeros((rows, 1), jnp.int32)
+    high = jnp.zeros((rows, 1), jnp.int32)
+    start = jnp.int32(0)
+    for u in range(lengths_ref.shape[1]):
+        end = start + lengths_ref[0, u]
+        mine = (row >= start) & (row < end)
+        reach = jnp.minimum(end, jnp.maximum(row + 1, start + prefixes_ref[0, u]))
+        low = jnp.where(mine, start, low)
+        high = jnp.where(mine, reach, high)
+        start = end
+    lane = lax.broadcasted_iota(jnp.int32, (rows, rows), 1)
+    scale_ref[...] = jnp.where((lane >= low) & (lane < high), 1.0 / rows, 0.0)
+
+
 def post_kernel(parts, me_ref, order_ref, *refs):
     back_refs, (out_ref, grad_ref) = refs[:-2], refs[-2:]
     rows = out_ref.shape[0]
@@ -97,9 +134,8 @@
     groups,
     n_rows,
     me_ref,
-    lengths_ref,
-    prefixes_ref,
-    order_ref,
+    matrix_ref,
+    scale_ref,
     *refs,
 ):
     row_refs, refs = refs[:n_rows], refs[n_rows:]
@@ -109,9 +145,9 @@
     w_ref, xt_ref, gt_ref, act_ref, slope_ref, mix_ref, weights_ref, bend_ref, gproj_ref = refs
     rows, width = mix_ref.shape
     shard = width // groups
-    group_me, shuf_me = me_ref[1], me_ref[0]
-
-    matrix = recv_matrix(order_ref, shuf_me, rows, rows // parts)
+    group_me = me_ref[1]
+
+    matrix = matrix_ref[...]
     x = dot(matrix, stacked(row_refs, 0))
     cot = dot(matrix, stacked(row_refs, 1))
     cot_b = cot.astype(BF16)
@@ -133,20 +169,7 @@
         act_ref[:, cols] = act.astype(BF16)
         slope_ref[:, cols] = s + act * (1.0 - s)
 
-    row = lax.broadcasted_iota(jnp.int32, (rows, 1), 0)
-    low = jnp.zeros((rows, 1), jnp.int32)
-    high = jnp.zeros((rows, 1), jnp.int32)
-    start = jnp.int32(0)
-    for u in range(lengths_ref.shape[0]):
-        end = start + lengths_ref[u]
-        mine = (row >= start) & (row < end)
-        reach = jnp.minimum(end, jnp.maximum(row + 1, start + prefixes_ref[u]))
-        low = jnp.where(mine, start, low)
-        high = jnp.where(mine, reach, high)
-        start = end
-    lane = lax.broadcasted_iota(jnp.int32, (rows, rows), 1)
-    scale = jnp.where((lane >= low) & (lane < high), 1.0 / rows, 0.0)
-
+    scale = scale_ref[...]
     head_width = width // HEADS
     per = max(1, 128 // head_width)
     wide = per * head_width
@@ -253,24 +276,42 @@
     w_mine, *outgoing = pl.pallas_call(
         partial(pre_kernel, parts),
         out_shape=[jax.ShapeDtypeStruct((shard, columns), BF16)] + [rows_shape] * n_rows,
-        in_specs=[SMEM] + [VMEM] * 5,
+        in_specs=[SMEM] + [HBM] * 5,
         out_specs=[VMEM] * (1 + n_rows),
+        scratch_shapes=[
+            pltpu.VMEM(send_order.shape, jnp.int32),
+            pltpu.VMEM((rows, width), BF16),
+            pltpu.VMEM((rows, width), BF16),
+            pltpu.SemaphoreType.DMA((5,)),
+        ],
         compiler_params=limit,
         name="pre",
     )(me, send_order, inputs[0], cotangent[0], w_uvqk, w_out)
 
-    shards = [None] * groups
-    for k in range(0, groups, 2):
-        shards[k] = w_mine if k == 0 else exchange(w_mine, "group", groups, k)
-    for k in range(0, groups, 2):
-        shards[k + 1] = exchange(shards[k], "group", groups, 1)
-    arrived = swap_rows(outgoing)
+    matrix, scale = pl.pallas_call(
+        partial(plan_kernel, parts),
+        out_shape=[jax.ShapeDtypeStruct((rows, rows), BF16), jax.ShapeDtypeStruct((rows, rows), F32)],
+        in_specs=[SMEM] + [HBM] * 3,
+        out_specs=[VMEM] * 2,
+        scratch_shapes=[
+            pltpu.VMEM(recv_order.shape, jnp.int32),
+            pltpu.SMEM(lengths[0].shape, jnp.int32),
+            pltpu.SMEM(prefixes[0].shape, jnp.int32),
+            pltpu.SemaphoreType.DMA((3,)),
+        ],
+        compiler_params=limit,
+        name="plan",
+    )(me, recv_order, lengths[0], prefixes[0])
+
+    near = [w_mine] + [exchange(w_mine, "group", groups, k) for k in range(2, groups, 2)]
+    near, arrived, matrix, scale = lax.optimization_barrier((near, swap_rows(outgoing), matrix, scale))
+    shards = [s for mine in near for s in (mine, exchange(mine, "group", groups, 1))]
 
     half = groups // 2 * shard
     *returning, keep, give = pl.pallas_call(
         partial(layer_kernel, parts, groups, n_rows),
         out_shape=[rows_shape] * n_rows + [jax.ShapeDtypeStruct((half, columns), BF16)] * 2,
-        in_specs=[SMEM] * 3 + [VMEM] * (1 + n_rows + groups),
+        in_specs=[SMEM] + [VMEM] * (2 + n_rows + groups),
         out_specs=[VMEM] * (n_rows + 2),
         scratch_shapes=[
             pltpu.VMEM((width, columns), BF16),
@@ -285,13 +326,13 @@
         ],
         compiler_params=limit,
         name="layer",
-    )(me, lengths[0, 0], prefixes[0, 0], recv_order, *arrived, *shards)
+    )(me, matrix, scale, *arrived, *shards)
 
     taken = exchange(give, "group", groups, 1)
     chip = (keep.astype(F32) + taken.astype(F32)).astype(BF16).reshape(groups // 2, shard, columns)
-    total = chip[0].astype(F32)
-    for m in range(1, groups // 2):
-        total = total + exchange(chip[m], "group", groups, 2 * m).astype(F32)
+    others = [exchange(chip[m], "group", groups, 2 * m) for m in range(1, groups // 2)]
+    others, returned = lax.optimization_barrier((others, swap_rows(returning)))
+    total = chip[0].astype(F32) + sum(other.astype(F32) for other in others)
     masks = [2 ** (j + 1) - 1 for j in range(parts.bit_length() - 1)]
     first, second = total[: shard // 2].astype(BF16), total[shard // 2 :].astype(BF16)
     for mask_a, mask_b in zip(masks, reversed(masks)):
@@ -308,7 +349,7 @@
         out_specs=[VMEM] * 2,
         compiler_params=limit,
         name="post",
-    )(me, send_order, *swap_rows(returning))
+    )(me, send_order, *returned)
     return (owner_out[None], owner_grad[None], grad_uvqk, grad_wout)
 
 

time: 106 us -> 80.9 us (0.76)
  waiting for transfers between devices: 57.2 us -> 28.3 us
  starting transfers between devices: 29.5 us -> 31.6 us
  Pallas kernels: 10.1 us -> 11.3 us
    ppermute x21, waiting for transfers between devices: 57.2 us -> 28.3 us  [exchange(): return lax.ppermute(value, axis, [(i, i ^ mask) for i in range(size)])]
    ppermute x21, starting transfers between devices: 29.5 us -> 31.6 us  [exchange(): return lax.ppermute(value, axis, [(i, i ^ mask) for i in range(size)])]
    pallas_call x0 -> x1, Pallas kernels: none -> 1.51 us  [on_device(): pl.pallas_call(partial(plan_kernel, parts), out_shape=[jax.ShapeDtypeStru...]
  transfers between devices with their start and end apart: 21 -> 21, of which waited for: 14 -> 15; matrix products, arithmetic and copies ran while one was open for 0% -> 0% of each run, Pallas kernels for 2% -> 4%
where the time goes in v2:
time: 80.9 us; the launch traced here: 80.6 us
  starting transfers between devices  31.6 us (39%)
  waiting for transfers between devices  28.3 us (35%)
  Pallas kernels  11.3 us (14%)
  local copies, waits for them, and re-layouts  6.4 us (8%)
  other arithmetic  2.2 us (3%)
    ppermute x21, starting transfers between devices, exchange(): return lax.ppermute(value, axis, [(i, i ^ mask) for i in range(size)])  31.6 us
    ppermute x21, waiting for transfers between devices, exchange(): return lax.ppermute(value, axis, [(i, i ^ mask) for i in range(size)])  28.3 us
    pallas_call x1, Pallas kernels, on_device(): pl.pallas_call(partial(layer_kernel, parts, groups, n_rows), out_shape=[r...  7.08 us
    unnamed x16, local copies, waits for them, and re-layouts  6.31 us
    pallas_call x1, Pallas kernels, on_device(): pl.pallas_call(partial(post_kernel, parts), out_shape=[jax.ShapeDtypeStru...  1.73 us
  transfers between devices with their start and end apart: 21, of which 15 were waited for; matrix products, arithmetic and copies ran while one was open for 0% of the time, Pallas kernels for 4%

profile of v2, /device:TPU:0, one launch (start us, length us, event | category | flops | bytes accessed | tf_op | source)
XLA Modules:
  0.0 80.6 jit_solution(11327096311148854720)
XLA Ops:
  0.7 0.9 %copy-done = bf16[1,256,512]{2,1,0:T(8,128)(2,1)S(1)} copy-done((bf16[1,256,512]{2,1,0:T(8,128)(2,1)S(1)}, bf16[1,256,512]{2,1,0:T(8,128)(2,1)}, u32[]{:S(2)}) %copy-start) | copy-done | bytes 262168
  1.7 0.9 %copy-done.1 = bf16[1,256,512]{2,1,0:T(8,128)(2,1)S(1)} copy-done((bf16[1,256,512]{2,1,0:T(8,128)(2,1)S(1)}, bf16[1,256,512]{2,1,0:T(8,128)(2,1)}, u32[]{:S(2)}) %copy-start.1) | copy-done | bytes 262168
  2.6 0.9 %copy-done.2 = bf16[64,2048]{1,0:T(8,128)(2,1)S(1)} copy-done((bf16[64,2048]{1,0:T(8,128)(2,1)S(1)}, bf16[64,2048]{1,0:T(8,128)(2,1)}, u32[]{:S(2)}) %copy-start.2) | copy-done | bytes 262168
  3.6 0.8 %copy-done.3 = bf16[64,512]{1,0:T(8,128)(2,1)S(1)} copy-done((bf16[64,512]{1,0:T(8,128)(2,1)S(1)}, bf16[64,512]{1,0:T(8,128)(2,1)}, u32[]{:S(2)}) %copy-start.3) | copy-done | bytes 65560
  4.4 0.7 copy-done.4
  5.1 1.0 %pre.1 = (bf16[64,2560]{1,0:T(8,128)(2,1)S(1)}, bf16[2,64,512]{2,1,0:T(8,128)(2,1)S(1)}, bf16[2,64,512]{2,1,0:T(8,128)(2,1)S(1)}, bf16[2,64,512]{2,1,0:T(8,128)(2,1)S(1)}, bf16[2,64,512]{2,1,0:T(8,128)(2,1)S(1)}) custom-call(s32[2]{0:T(128)S(1)} %pad_add_fusion.me_ref, s32[1,32]{1,0:T(1,128)S(1)} %bitcast.12, bf16[256,512]{1,0:T(8,128)(2,1)S(1)} %bitcast.10, ...), custom_call_target="tpu_custom_call" | custom-call | tf_op jit(solution)/shard_map/pre/pallas_call | solution.py:276
  6.1 4.0 %collective-permute-start.2 = (bf16[64,2560]{1,0:T(8,128)(2,1)S(1)}, bf16[64,2560]{1,0:T(8,128)(2,1)S(1)}, u32[]{:S(2)}, u32[]{:S(2)}) collective-permute-start(bf16[64,2560]{1,0:T(8,128)(2,1)S(1)} %get-tuple-element.49.refs_4_), channel_id=1, source_target_pairs={{0,24},{4,28},{8,16},{12,20},{16,8},{20,12},{24,0},{28,4},{1,25},{... | collective-permute-start | bytes 983048 | tf_op jit(solution)/shard_map/ppermute | solution.py:39
  10.1 0.5 collective-permute-start.1
  10.7 2.0 %collective-permute-start.3 = (bf16[2,64,512]{2,1,0:T(8,128)(2,1)S(1)}, bf16[2,64,512]{2,1,0:T(8,128)(2,1)S(1)}, u32[]{:S(2)}, u32[]{:S(2)}) collective-permute-start(bf16[2,64,512]{2,1,0:T(8,128)(2,1)S(1)} %get-tuple-element.38), channel_id=1, source_target_pairs={{0,1},{1,0},{2,3},{3,2},{4,5},{5,4},{6,7},{7,6},{8,9},{9,8},{10,11... | collective-permute-start | bytes 393224 | tf_op jit(solution)/shard_map/ppermute | solution.py:39
  12.7 2.6 %collective-permute-start.4 = (bf16[2,64,512]{2,1,0:T(8,128)(2,1)S(1)}, bf16[2,64,512]{2,1,0:T(8,128)(2,1)S(1)}, u32[]{:S(2)}, u32[]{:S(2)}) collective-permute-start(bf16[2,64,512]{2,1,0:T(8,128)(2,1)S(1)} %get-tuple-element.39), channel_id=1, source_target_pairs={{0,2},{1,3},{2,0},{3,1},{4,6},{5,7},{6,4},{7,5},{8,10},{9,11},{10,... | collective-permute-start | bytes 393224 | tf_op jit(solution)/shard_map/ppermute | solution.py:39
  15.3 1.7 %collective-permute-done.3.refs_1_ = bf16[2,64,512]{2,1,0:T(8,128)(2,1)S(1)} collective-permute-done((bf16[2,64,512]{2,1,0:T(8,128)(2,1)S(1)}, bf16[2,64,512]{2,1,0:T(8,128)(2,1)S(1)}, u32[]{:S(2)}, u32[]{:S(2)}) %collective-permute-start.3) | collective-permute-done | bytes 131104 | tf_op jit(solution)/shard_map/ppermute | solution.py:39
  17.0 4.0 %collective-permute-start.5 = (bf16[2,64,512]{2,1,0:T(8,128)(2,1)S(1)}, bf16[2,64,512]{2,1,0:T(8,128)(2,1)S(1)}, u32[]{:S(2)}, u32[]{:S(2)}) collective-permute-start(bf16[2,64,512]{2,1,0:T(8,128)(2,1)S(1)} %get-tuple-element.40), channel_id=1, source_target_pairs={{0,3},{1,2},{2,1},{3,0},{4,7},{5,6},{6,5},{7,4},{8,11},{9,10},{10,... | collective-permute-start | bytes 393224 | tf_op jit(solution)/shard_map/ppermute | solution.py:39
  21.0 0.7 copy-done.5
  21.6 0.7 copy-done.6
  22.3 0.7 copy-done.7
  23.0 1.5 %plan.1 = (bf16[256,256]{1,0:T(8,128)(2,1)S(1)}, f32[256,256]{1,0:T(8,128)S(1)}) custom-call(s32[2]{0:T(128)S(1)} %pad_add_fusion.me_ref, s32[1,32]{1,0:T(1,128)S(1)} %bitcast.14, s32[1,8]{1,0:T(1,128)S(1)} %bitcast.15, s32[1,8]{1,0:T(1,128)S(1)} %bitcast.16), custom_call_target="tpu_custom_call" | custom-call | tf_op jit(solution)/shard_map/plan/pallas_call | solution.py:291
  24.5 0.3 collective-permute-done.1.refs_8_
  24.8 0.3 collective-permute-done.refs_6_
  25.1 0.5 collective-permute-start.7
  25.6 0.5 collective-permute-start.9
  26.1 0.6 collective-permute-done.6.refs_5_
  26.7 0.5 collective-permute-done.7.refs_7_
  27.2 0.5 collective-permute-done.8.refs_9_
  27.6 0.5 collective-permute-done.9.refs_11_
  28.1 7.1 %layer.1 = (bf16[2,64,512]{2,1,0:T(8,128)(2,1)S(1)}, bf16[2,64,512]{2,1,0:T(8,128)(2,1)S(1)}, bf16[2,64,512]{2,1,0:T(8,128)(2,1)S(1)}, bf16[2,64,512]{2,1,0:T(8,...) custom-call(s32[2]{0:T(128)S(1)} %pad_add_fusion.me_ref, ...), custom_call_target="tpu_custom_call" | custom-call | tf_op jit(solution)/shard_map/layer/pallas_call | solution.py:311
  35.2 0.2 collective-permute-start.10
  35.4 2.9 %collective-permute-done.10 = bf16[256,2560]{1,0:T(8,128)(2,1)S(1)} collective-permute-done((bf16[256,2560]{1,0:T(8,128)(2,1)S(1)}, bf16[256,2560]{1,0:T(8,128)(2,1)S(1)}, u32[]{:S(2)}, u32[]{:S(2)}) %collective-permute-start.10) | collective-permute-done | bytes 1310752 | tf_op jit(solution)/shard_map/ppermute | solution.py:39
  38.3 0.3 add_convert_fusion
  38.7 2.1 %collective-permute-start.13 = (bf16[64,2560]{1,0:T(8,128)(2,1)S(1)}, bf16[64,2560]{1,0:T(8,128)(2,1)S(1)}, u32[]{:S(2)}, u32[]{:S(2)}) collective-permute-start(bf16[64,2560]{1,0:T(8,128)(2,1)S(1)} %get-tuple-element.68), channel_id=1, source_target_pairs={{0,24},{4,28},{8,16},{12,20},{16,8},{20,12},{24,0},{28,4},{1,25},{... | collective-permute-start | bytes 983048 | tf_op jit(solution)/shard_map/ppermute | solution.py:39
  40.8 0.9 %collective-permute-start.12 = (bf16[64,2560]{1,0:T(8,128)(2,1)S(1)}, bf16[64,2560]{1,0:T(8,128)(2,1)S(1)}, u32[]{:S(2)}, u32[]{:S(2)}) collective-permute-start(bf16[64,2560]{1,0:T(8,128)(2,1)S(1)} %get-tuple-element.69), channel_id=1, source_target_pairs={{0,16},{4,20},{8,24},{12,28},{16,0},{20,4},{24,8},{28,12},{1,17},{... | collective-permute-start | bytes 983048 | tf_op jit(solution)/shard_map/ppermute | solution.py:39
  41.7 0.5 collective-permute-start.11
  42.3 1.7 %collective-permute-start.14 = (bf16[2,64,512]{2,1,0:T(8,128)(2,1)S(1)}, bf16[2,64,512]{2,1,0:T(8,128)(2,1)S(1)}, u32[]{:S(2)}, u32[]{:S(2)}) collective-permute-start(bf16[2,64,512]{2,1,0:T(8,128)(2,1)S(1)} %get-tuple-element.56), channel_id=1, source_target_pairs={{0,1},{1,0},{2,3},{3,2},{4,5},{5,4},{6,7},{7,6},{8,9},{9,8},{10,11... | collective-permute-start | bytes 393224 | tf_op jit(solution)/shard_map/ppermute | solution.py:39
  44.0 2.5 %collective-permute-start.15 = (bf16[2,64,512]{2,1,0:T(8,128)(2,1)S(1)}, bf16[2,64,512]{2,1,0:T(8,128)(2,1)S(1)}, u32[]{:S(2)}, u32[]{:S(2)}) collective-permute-start(bf16[2,64,512]{2,1,0:T(8,128)(2,1)S(1)} %get-tuple-element.57), channel_id=1, source_target_pairs={{0,2},{1,3},{2,0},{3,1},{4,6},{5,7},{6,4},{7,5},{8,10},{9,11},{10,... | collective-permute-start | bytes 393224 | tf_op jit(solution)/shard_map/ppermute | solution.py:39
  46.4 2.4 %collective-permute-done.14.refs_1_ = bf16[2,64,512]{2,1,0:T(8,128)(2,1)S(1)} collective-permute-done((bf16[2,64,512]{2,1,0:T(8,128)(2,1)S(1)}, bf16[2,64,512]{2,1,0:T(8,128)(2,1)S(1)}, u32[]{:S(2)}, u32[]{:S(2)}) %collective-permute-start.14) | collective-permute-done | bytes 131104 | tf_op jit(solution)/shard_map/ppermute | solution.py:39
  48.8 3.3 %collective-permute-start.16 = (bf16[2,64,512]{2,1,0:T(8,128)(2,1)S(1)}, bf16[2,64,512]{2,1,0:T(8,128)(2,1)S(1)}, u32[]{:S(2)}, u32[]{:S(2)}) collective-permute-start(bf16[2,64,512]{2,1,0:T(8,128)(2,1)S(1)} %get-tuple-element.58), channel_id=1, source_target_pairs={{0,3},{1,2},{2,1},{3,0},{4,7},{5,6},{6,5},{7,4},{8,11},{9,10},{10,... | collective-permute-start | bytes 393224 | tf_op jit(solution)/shard_map/ppermute | solution.py:39
  52.1 3.8 %collective-permute-done.15.refs_2_ = bf16[2,64,512]{2,1,0:T(8,128)(2,1)S(1)} collective-permute-done((bf16[2,64,512]{2,1,0:T(8,128)(2,1)S(1)}, bf16[2,64,512]{2,1,0:T(8,128)(2,1)S(1)}, u32[]{:S(2)}, u32[]{:S(2)}) %collective-permute-start.15) | collective-permute-done | bytes 131104 | tf_op jit(solution)/shard_map/ppermute | solution.py:39
  55.9 0.5 collective-permute-done.12
  56.4 0.2 add_convert_fusion.1
  56.6 3.7 %collective-permute-start.19 = (bf16[32,2560]{1,0:T(8,128)(2,1)S(1)}, bf16[32,2560]{1,0:T(8,128)(2,1)S(1)}, u32[]{:S(2)}, u32[]{:S(2)}) collective-permute-start(bf16[32,2560]{1,0:T(8,128)(2,1)S(1)} %get-tuple-element.73), channel_id=1, source_target_pairs={{0,3},{1,2},{2,1},{3,0},{4,7},{5,6},{6,5},{7,4},{8,11},{9,10},{10,... | collective-permute-start | bytes 491528 | tf_op jit(solution)/shard_map/ppermute | solution.py:39
  60.3 5.3 %collective-permute-done.19 = bf16[32,2560]{1,0:T(8,128)(2,1)S(1)} collective-permute-done((bf16[32,2560]{1,0:T(8,128)(2,1)S(1)}, bf16[32,2560]{1,0:T(8,128)(2,1)S(1)}, u32[]{:S(2)}, u32[]{:S(2)}) %collective-permute-start.19) | collective-permute-done | bytes 163872 | tf_op jit(solution)/shard_map/ppermute | solution.py:39
  65.6 2.7 %collective-permute-done.17 = bf16[32,2560]{1,0:T(8,128)(2,1)S(1)} collective-permute-done((bf16[32,2560]{1,0:T(8,128)(2,1)S(1)}, bf16[32,2560]{1,0:T(8,128)(2,1)S(1)}, u32[]{:S(2)}, u32[]{:S(2)}) %collective-permute-start.17) | collective-permute-done | bytes 163872 | tf_op jit(solution)/shard_map/ppermute | solution.py:39
  68.4 1.8 %collective-permute-start.20 = (bf16[32,2560]{1,0:T(8,128)(2,1)S(1)}, bf16[32,2560]{1,0:T(8,128)(2,1)S(1)}, u32[]{:S(2)}, u32[]{:S(2)}) collective-permute-start(bf16[32,2560]{1,0:T(8,128)(2,1)S(1)} %get-tuple-element.71), channel_id=1, source_target_pairs={{0,1},{1,0},{2,3},{3,2},{4,5},{5,4},{6,7},{7,6},{8,9},{9,8},{10,11... | collective-permute-start | bytes 491528 | tf_op jit(solution)/shard_map/ppermute | solution.py:39
  70.1 1.7 %post.1 = (bf16[256,512]{1,0:T(8,128)(2,1)}, bf16[256,512]{1,0:T(8,128)(2,1)}) custom-call(s32[2]{0:T(128)S(1)} %pad_add_fusion.me_ref, s32[1,32]{1,0:T(1,128)S(1)} %bitcast.13, bf16[2,64,512]{2,1,0:T(8,128)(2,1)S(1)} %get-tuple-element.59.refs_0_, bf16[2,64,512]{2,1,0:T(8,128)(2,1)S(1)} %collective-permute-done.14.refs_1_, ...), custom_call_target="tpu_custom_call" | custom-call | tf_op jit(solution)/shard_map/post/pallas_call | solution.py:345
  71.8 0.7 collective-permute-start.18
  72.6 2.1 %collective-permute-done.20 = bf16[32,2560]{1,0:T(8,128)(2,1)S(1)} collective-permute-done((bf16[32,2560]{1,0:T(8,128)(2,1)S(1)}, bf16[32,2560]{1,0:T(8,128)(2,1)S(1)}, u32[]{:S(2)}, u32[]{:S(2)}) %collective-permute-start.20) | collective-permute-done | bytes 163872 | tf_op jit(solution)/shard_map/ppermute | solution.py:39
  74.7 4.3 %collective-permute-done.18 = bf16[32,2560]{1,0:T(8,128)(2,1)S(1)} collective-permute-done((bf16[32,2560]{1,0:T(8,128)(2,1)S(1)}, bf16[32,2560]{1,0:T(8,128)(2,1)S(1)}, u32[]{:S(2)}, u32[]{:S(2)}) %collective-permute-start.18) | collective-permute-done | bytes 163872 | tf_op jit(solution)/shard_map/ppermute | solution.py:39
  79.1 0.7 pad_maximum_fusion
  79.7 0.8 %fusion = f32[64,2048]{1,0:T(8,128)} fusion(f32[32,2560]{1,0:T(8,128)S(1)} %convert_add_fusion.1, f32[32,2560]{1,0:T(8,128)S(1)} %convert_add_fusion), kind=kLoop, calls=%fused_computation.4 | loop fusion | flops 131072 | bytes 1179648 | tf_op jit(solution)/shard_map/concatenate | solution.py:342
  (24 shorter events, 0.5 us)
Async XLA Ops:
  0.7 1.0 %copy-start = (bf16[1,256,512]{2,1,0:T(8,128)(2,1)S(1)}, bf16[1,256,512]{2,1,0:T(8,128)(2,1)}, u32[]{:S(2)}) copy-start(bf16[1,256,512]{2,1,0:T(8,128)(2,1)} %param.8) | copy-start | bytes 786436
  1.7 0.9 %copy-start.1 = (bf16[1,256,512]{2,1,0:T(8,128)(2,1)S(1)}, bf16[1,256,512]{2,1,0:T(8,128)(2,1)}, u32[]{:S(2)}) copy-start(bf16[1,256,512]{2,1,0:T(8,128)(2,1)} %param.9) | copy-start | bytes 786436
  2.6 0.9 %copy-start.2 = (bf16[64,2048]{1,0:T(8,128)(2,1)S(1)}, bf16[64,2048]{1,0:T(8,128)(2,1)}, u32[]{:S(2)}) copy-start(bf16[64,2048]{1,0:T(8,128)(2,1)} %uvqk_in.1) | copy-start | bytes 786436
  3.6 0.8 %copy-start.3 = (bf16[64,512]{1,0:T(8,128)(2,1)S(1)}, bf16[64,512]{1,0:T(8,128)(2,1)}, u32[]{:S(2)}) copy-start(bf16[64,512]{1,0:T(8,128)(2,1)} %out_in.1) | copy-start | bytes 196612
  4.4 0.7 copy-start.4
  6.1 18.4 %collective-permute-start.2 = (bf16[64,2560]{1,0:T(8,128)(2,1)S(1)}, bf16[64,2560]{1,0:T(8,128)(2,1)S(1)}, u32[]{:S(2)}, u32[]{:S(2)}) collective-permute-start(bf16[64,2560]{1,0:T(8,128)(2,1)S(1)} %get-tuple-element.49.refs_4_), channel_id=1, source_target_pairs={{0,24},{4,28},{8,16},{12,20},{16,8},{20,12},{24,0},{28,4},{1,25},{... | collective-permute-start | bytes 983048 | tf_op jit(solution)/shard_map/ppermute | solution.py:39
  10.1 14.7 %collective-permute-start.1 = (bf16[64,2560]{1,0:T(8,128)(2,1)S(1)}, bf16[64,2560]{1,0:T(8,128)(2,1)S(1)}, u32[]{:S(2)}, u32[]{:S(2)}) collective-permute-start(bf16[64,2560]{1,0:T(8,128)(2,1)S(1)} %get-tuple-element.49.refs_4_), channel_id=1, source_target_pairs={{0,16},{4,20},{8,24},{12,28},{16,0},{20,4},{24,8},{28,12},{1,17},{... | collective-permute-start | bytes 983048 | tf_op jit(solution)/shard_map/ppermute | solution.py:39
  10.6 14.5 %collective-permute-start = (bf16[64,2560]{1,0:T(8,128)(2,1)S(1)}, bf16[64,2560]{1,0:T(8,128)(2,1)S(1)}, u32[]{:S(2)}, u32[]{:S(2)}) collective-permute-start(bf16[64,2560]{1,0:T(8,128)(2,1)S(1)} %get-tuple-element.49.refs_4_), channel_id=1, source_target_pairs={{0,8},{4,12},{8,0},{12,4},{16,24},{20,28},{24,16},{28,20},{1,9},{5... | collective-permute-start | bytes 983048 | tf_op jit(solution)/shard_map/ppermute | solution.py:39
  10.7 6.3 %collective-permute-start.3 = (bf16[2,64,512]{2,1,0:T(8,128)(2,1)S(1)}, bf16[2,64,512]{2,1,0:T(8,128)(2,1)S(1)}, u32[]{:S(2)}, u32[]{:S(2)}) collective-permute-start(bf16[2,64,512]{2,1,0:T(8,128)(2,1)S(1)} %get-tuple-element.38), channel_id=1, source_target_pairs={{0,1},{1,0},{2,3},{3,2},{4,5},{5,4},{6,7},{7,6},{8,9},{9,8},{10,11... | collective-permute-start | bytes 393224 | tf_op jit(solution)/shard_map/ppermute | solution.py:39
  12.7 11.8 %collective-permute-start.4 = (bf16[2,64,512]{2,1,0:T(8,128)(2,1)S(1)}, bf16[2,64,512]{2,1,0:T(8,128)(2,1)S(1)}, u32[]{:S(2)}, u32[]{:S(2)}) collective-permute-start(bf16[2,64,512]{2,1,0:T(8,128)(2,1)S(1)} %get-tuple-element.39), channel_id=1, source_target_pairs={{0,2},{1,3},{2,0},{3,1},{4,6},{5,7},{6,4},{7,5},{8,10},{9,11},{10,... | collective-permute-start | bytes 393224 | tf_op jit(solution)/shard_map/ppermute | solution.py:39
  17.0 7.5 %collective-permute-start.5 = (bf16[2,64,512]{2,1,0:T(8,128)(2,1)S(1)}, bf16[2,64,512]{2,1,0:T(8,128)(2,1)S(1)}, u32[]{:S(2)}, u32[]{:S(2)}) collective-permute-start(bf16[2,64,512]{2,1,0:T(8,128)(2,1)S(1)} %get-tuple-element.40), channel_id=1, source_target_pairs={{0,3},{1,2},{2,1},{3,0},{4,7},{5,6},{6,5},{7,4},{8,11},{9,10},{10,... | collective-permute-start | bytes 393224 | tf_op jit(solution)/shard_map/ppermute | solution.py:39
  21.0 0.7 copy-start.5
  21.6 0.7 copy-start.6
  22.3 0.7 copy-start.7
  25.1 1.6 %collective-permute-start.6 = (bf16[64,2560]{1,0:T(8,128)(2,1)S(1)}, bf16[64,2560]{1,0:T(8,128)(2,1)S(1)}, u32[]{:S(2)}, u32[]{:S(2)}) collective-permute-start(bf16[64,2560]{1,0:T(8,128)(2,1)S(1)} %get-tuple-element.49.refs_4_), channel_id=1, source_target_pairs={{0,4},{4,0},{8,12},{12,8},{16,20},{20,16},{24,28},{28,24},{1,5},{5... | collective-permute-start | bytes 983048 | tf_op jit(solution)/shard_map/ppermute | solution.py:39
  25.1 2.1 %collective-permute-start.7 = (bf16[64,2560]{1,0:T(8,128)(2,1)S(1)}, bf16[64,2560]{1,0:T(8,128)(2,1)S(1)}, u32[]{:S(2)}, u32[]{:S(2)}) collective-permute-start(bf16[64,2560]{1,0:T(8,128)(2,1)S(1)} %collective-permute-done.refs_6_), channel_id=1, source_target_pairs={{0,4},{4,0},{8,12},{12,8},{16,20},{20,16},{24,28},{28,24},{1,5},{5... | collective-permute-start | bytes 983048 | tf_op jit(solution)/shard_map/ppermute | solution.py:39
  25.6 2.1 %collective-permute-start.8 = (bf16[64,2560]{1,0:T(8,128)(2,1)S(1)}, bf16[64,2560]{1,0:T(8,128)(2,1)S(1)}, u32[]{:S(2)}, u32[]{:S(2)}) collective-permute-start(bf16[64,2560]{1,0:T(8,128)(2,1)S(1)} %collective-permute-done.1.refs_8_), channel_id=1, source_target_pairs={{0,4},{4,0},{8,12},{12,8},{16,20},{20,16},{24,28},{28,24},{1,5},{5... | collective-permute-start | bytes 983048 | tf_op jit(solution)/shard_map/ppermute | solution.py:39
  25.6 2.5 %collective-permute-start.9 = (bf16[64,2560]{1,0:T(8,128)(2,1)S(1)}, bf16[64,2560]{1,0:T(8,128)(2,1)S(1)}, u32[]{:S(2)}, u32[]{:S(2)}) collective-permute-start(bf16[64,2560]{1,0:T(8,128)(2,1)S(1)} %collective-permute-done.2.refs_10_), channel_id=1, source_target_pairs={{0,4},{4,0},{8,12},{12,8},{16,20},{20,16},{24,28},{28,24},{1,5},{5... | collective-permute-start | bytes 983048 | tf_op jit(solution)/shard_map/ppermute | solution.py:39
  35.2 3.1 %collective-permute-start.10 = (bf16[256,2560]{1,0:T(8,128)(2,1)S(1)}, bf16[256,2560]{1,0:T(8,128)(2,1)S(1)}, u32[]{:S(2)}, u32[]{:S(2)}) collective-permute-start(bf16[256,2560]{1,0:T(8,128)(2,1)S(1)} %get-tuple-element.54), channel_id=1, source_target_pairs={{0,4},{4,0},{8,12},{12,8},{16,20},{20,16},{24,28},{28,24},{1,5},{5... | collective-permute-start | bytes 3932168 | tf_op jit(solution)/shard_map/ppermute | solution.py:39
  38.7 17.2 %collective-permute-start.13 = (bf16[64,2560]{1,0:T(8,128)(2,1)S(1)}, bf16[64,2560]{1,0:T(8,128)(2,1)S(1)}, u32[]{:S(2)}, u32[]{:S(2)}) collective-permute-start(bf16[64,2560]{1,0:T(8,128)(2,1)S(1)} %get-tuple-element.68), channel_id=1, source_target_pairs={{0,24},{4,28},{8,16},{12,20},{16,8},{20,12},{24,0},{28,4},{1,25},{... | collective-permute-start | bytes 983048 | tf_op jit(solution)/shard_map/ppermute | solution.py:39
  40.8 15.6 %collective-permute-start.12 = (bf16[64,2560]{1,0:T(8,128)(2,1)S(1)}, bf16[64,2560]{1,0:T(8,128)(2,1)S(1)}, u32[]{:S(2)}, u32[]{:S(2)}) collective-permute-start(bf16[64,2560]{1,0:T(8,128)(2,1)S(1)} %get-tuple-element.69), channel_id=1, source_target_pairs={{0,16},{4,20},{8,24},{12,28},{16,0},{20,4},{24,8},{28,12},{1,17},{... | collective-permute-start | bytes 983048 | tf_op jit(solution)/shard_map/ppermute | solution.py:39
  41.7 14.7 %collective-permute-start.11 = (bf16[64,2560]{1,0:T(8,128)(2,1)S(1)}, bf16[64,2560]{1,0:T(8,128)(2,1)S(1)}, u32[]{:S(2)}, u32[]{:S(2)}) collective-permute-start(bf16[64,2560]{1,0:T(8,128)(2,1)S(1)} %get-tuple-element.70), channel_id=1, source_target_pairs={{0,8},{4,12},{8,0},{12,4},{16,24},{20,28},{24,16},{28,20},{1,9},{5... | collective-permute-start | bytes 983048 | tf_op jit(solution)/shard_map/ppermute | solution.py:39
  42.3 6.6 %collective-permute-start.14 = (bf16[2,64,512]{2,1,0:T(8,128)(2,1)S(1)}, bf16[2,64,512]{2,1,0:T(8,128)(2,1)S(1)}, u32[]{:S(2)}, u32[]{:S(2)}) collective-permute-start(bf16[2,64,512]{2,1,0:T(8,128)(2,1)S(1)} %get-tuple-element.56), channel_id=1, source_target_pairs={{0,1},{1,0},{2,3},{3,2},{4,5},{5,4},{6,7},{7,6},{8,9},{9,8},{10,11... | collective-permute-start | bytes 393224 | tf_op jit(solution)/shard_map/ppermute | solution.py:39
  44.0 12.0 %collective-permute-start.15 = (bf16[2,64,512]{2,1,0:T(8,128)(2,1)S(1)}, bf16[2,64,512]{2,1,0:T(8,128)(2,1)S(1)}, u32[]{:S(2)}, u32[]{:S(2)}) collective-permute-start(bf16[2,64,512]{2,1,0:T(8,128)(2,1)S(1)} %get-tuple-element.57), channel_id=1, source_target_pairs={{0,2},{1,3},{2,0},{3,1},{4,6},{5,7},{6,4},{7,5},{8,10},{9,11},{10,... | collective-permute-start | bytes 393224 | tf_op jit(solution)/shard_map/ppermute | solution.py:39
  48.8 7.1 %collective-permute-start.16 = (bf16[2,64,512]{2,1,0:T(8,128)(2,1)S(1)}, bf16[2,64,512]{2,1,0:T(8,128)(2,1)S(1)}, u32[]{:S(2)}, u32[]{:S(2)}) collective-permute-start(bf16[2,64,512]{2,1,0:T(8,128)(2,1)S(1)} %get-tuple-element.58), channel_id=1, source_target_pairs={{0,3},{1,2},{2,1},{3,0},{4,7},{5,6},{6,5},{7,4},{8,11},{9,10},{10,... | collective-permute-start | bytes 393224 | tf_op jit(solution)/shard_map/ppermute | solution.py:39
  56.6 9.0 %collective-permute-start.19 = (bf16[32,2560]{1,0:T(8,128)(2,1)S(1)}, bf16[32,2560]{1,0:T(8,128)(2,1)S(1)}, u32[]{:S(2)}, u32[]{:S(2)}) collective-permute-start(bf16[32,2560]{1,0:T(8,128)(2,1)S(1)} %get-tuple-element.73), channel_id=1, source_target_pairs={{0,3},{1,2},{2,1},{3,0},{4,7},{5,6},{6,5},{7,4},{8,11},{9,10},{10,... | collective-permute-start | bytes 491528 | tf_op jit(solution)/shard_map/ppermute | solution.py:39
  60.3 8.0 %collective-permute-start.17 = (bf16[32,2560]{1,0:T(8,128)(2,1)S(1)}, bf16[32,2560]{1,0:T(8,128)(2,1)S(1)}, u32[]{:S(2)}, u32[]{:S(2)}) collective-permute-start(bf16[32,2560]{1,0:T(8,128)(2,1)S(1)} %get-tuple-element.74), channel_id=1, source_target_pairs={{0,1},{1,0},{2,3},{3,2},{4,5},{5,4},{6,7},{7,6},{8,9},{9,8},{10,11... | collective-permute-start | bytes 491528 | tf_op jit(solution)/shard_map/ppermute | solution.py:39
  68.4 6.3 %collective-permute-start.20 = (bf16[32,2560]{1,0:T(8,128)(2,1)S(1)}, bf16[32,2560]{1,0:T(8,128)(2,1)S(1)}, u32[]{:S(2)}, u32[]{:S(2)}) collective-permute-start(bf16[32,2560]{1,0:T(8,128)(2,1)S(1)} %get-tuple-element.71), channel_id=1, source_target_pairs={{0,1},{1,0},{2,3},{3,2},{4,5},{5,4},{6,7},{7,6},{8,9},{9,8},{10,11... | collective-permute-start | bytes 491528 | tf_op jit(solution)/shard_map/ppermute | solution.py:39
  71.8 7.2 %collective-permute-start.18 = (bf16[32,2560]{1,0:T(8,128)(2,1)S(1)}, bf16[32,2560]{1,0:T(8,128)(2,1)S(1)}, u32[]{:S(2)}, u32[]{:S(2)}) collective-permute-start(bf16[32,2560]{1,0:T(8,128)(2,1)S(1)} %get-tuple-element.72), channel_id=1, source_target_pairs={{0,3},{1,2},{2,1},{3,0},{4,7},{5,6},{6,5},{7,4},{8,11},{9,10},{10,... | collective-permute-start | bytes 491528 | tf_op jit(solution)/shard_map/ppermute | solution.py:39

commit v3 on v2

v3 whole, which is shorter than its diff:
```python
from functools import partial

import jax
import jax.numpy as jnp
from jax import lax
from jax.experimental import pallas as pl
from jax.experimental.pallas import tpu as pltpu
from jax.sharding import PartitionSpec as P

HEADS = 8
norm_eps = 1e-05
F32 = jnp.float32
BF16 = jnp.bfloat16
VMEM = pl.BlockSpec(memory_space=pltpu.VMEM)
SMEM = pl.BlockSpec(memory_space=pltpu.SMEM)
HBM = pl.BlockSpec(memory_space=pltpu.HBM)
NN = (((1,), (0,)), ((), ()))
NT = (((1,), (1,)), ((), ()))
TN = (((0,), (0,)), ((), ()))


def dot(a, b, dims=NN):
    return lax.dot_general(a, b, dims, preferred_element_type=F32)


def sigmoid(values):
    return 0.5 * jnp.tanh(0.5 * values) + 0.5


def normalize(values):
    center = jnp.mean(values, axis=-1, keepdims=True)
    centred = values - center
    variance = jnp.mean(centred * centred, axis=-1, keepdims=True)
    inv_scale = lax.rsqrt(variance + norm_eps)
    return (centred * inv_scale, inv_scale)


def exchange(value, axis, size, mask):
    return lax.ppermute(value, axis, [(i, i ^ mask) for i in range(size)])


def global_row(index, me, chunk):
    place = lax.div(index, chunk)
    return (me ^ place) * chunk + (index - place * chunk)


def looked_up(order, row):
    blocks = order.shape[1]
    block = row.shape[0] // blocks
    at = lax.div(row, block)
    lane = lax.broadcasted_iota(jnp.int32, (row.shape[0], blocks), 1)
    picked = jnp.where(at == lane, order, 0).astype(F32)
    found = jnp.sum(picked, axis=1, keepdims=True).astype(jnp.int32)
    return found * block + (row - at * block)


def send_matrix(order, me, rows, chunk):
    row = lax.broadcasted_iota(jnp.int32, (rows, 1), 0)
    source = looked_up(order, global_row(row, me, chunk))
    lane = lax.broadcasted_iota(jnp.int32, (rows, rows), 1)
    return (source == lane).astype(F32).astype(BF16)


def recv_matrix(order, me, rows, chunk):
    row = lax.broadcasted_iota(jnp.int32, (rows, 1), 0)
    source = looked_up(order, row)
    lane = lax.broadcasted_iota(jnp.int32, (rows, rows), 1)
    return (source == global_row(lane, me, chunk)).astype(F32).astype(BF16)


def stacked(refs, which):
    return jnp.concatenate([ref[which] for ref in refs], axis=0)


def copy_all(moves, sem):
    copies = [pltpu.make_async_copy(a, b, sem.at[n]) for n, (a, b) in enumerate(moves)]
    for copy in copies:
        copy.start()
    return copies


def pre_kernel(parts, send_in, recv_in, lengths_in, prefixes_in, x_in, cot_in, uvqk_in, out_in, *refs):
    w_out, small_out, piece_outs, refs = refs[0], refs[1], refs[2:-13], refs[-13:]
    send_ref, recv_ref, lengths_ref, prefixes_ref, x_ref, cot_ref, w_ref, small_ref, x_sent, cot_sent = refs[:10]
    sem, sent_sem, flat_sem = refs[10:]
    rows = x_ref.shape[0]
    columns = uvqk_in.shape[1]
    copies = copy_all(
        (
            (send_in, send_ref),
            (x_in, x_ref),
            (cot_in, cot_ref),
            (uvqk_in, w_ref.at[:, :columns]),
            (out_in, w_ref.at[:, columns:]),
            (recv_in, recv_ref),
            (lengths_in, lengths_ref),
            (prefixes_in, prefixes_ref),
        ),
        sem,
    )
    copies[0].wait()
    matrix = send_matrix(send_ref[...], lax.axis_index("shuf"), rows, rows // parts)
    step = rows // len(piece_outs)
    sent = []
    for which, (ref, sent_ref) in enumerate(((x_ref, x_sent), (cot_ref, cot_sent))):
        copies[1 + which].wait()
        sent_ref[...] = dot(matrix, ref[...]).astype(BF16)
        sent += copy_all(
            [(sent_ref.at[pl.ds(k * step, step)], out.at[which]) for k, out in enumerate(piece_outs)],
            sent_sem.at[which],
        )
        if which == 0:
            for copy in copies[3:]:
                copy.wait()
            for n, ref in enumerate((recv_ref, lengths_ref, prefixes_ref)):
                small_ref[n : n + 1, : ref.shape[1]] = ref[...]
            sent += copy_all(((w_ref, w_out), (small_ref, small_out)), flat_sem)
    for copy in sent:
        copy.wait()


def plan_kernel(parts, blocks, users, small_ref, w_ref, own_ref, matrix_ref, scale_ref, w_out, own_out):
    rows = matrix_ref.shape[0]
    w_out[...] = w_ref[...]
    own_out[...] = own_ref[...]
    matrix_ref[...] = recv_matrix(small_ref[0:1, :blocks], lax.axis_index("shuf"), rows, rows // parts)
    row = lax.broadcasted_iota(jnp.int32, (rows, 1), 0)
    low = jnp.zeros((rows, 1), jnp.int32)
    high = jnp.zeros((rows, 1), jnp.int32)
    start = jnp.zeros((1, 1), jnp.int32)
    for u in range(users):
        end = start + small_ref[1:2, u : u + 1]
        mine = (row >= start) & (row < end)
        reach = jnp.minimum(end, jnp.maximum(row + 1, start + small_ref[2:3, u : u + 1]))
        low = jnp.where(mine, start, low)
        high = jnp.where(mine, reach, high)
        start = end
    lane = lax.broadcasted_iota(jnp.int32, (rows, rows), 1)
    scale_ref[...] = jnp.where((lane >= low) & (lane < high), 1.0 / rows, 0.0)


def post_kernel(parts, order_ref, *refs):
    back_refs, (out_ref, grad_ref) = refs[:-2], refs[-2:]
    rows = out_ref.shape[0]
    matrix = send_matrix(order_ref[...], lax.axis_index("shuf"), rows, rows // parts)
    for which, ref in enumerate((out_ref, grad_ref)):
        ref[...] = dot(matrix, stacked(back_refs, which), TN).astype(BF16)


def only(value, h, head_width):
    place = lax.div(lax.broadcasted_iota(jnp.int32, value.shape, 1), head_width)
    return jnp.where(place == h, value, jnp.zeros_like(value))


def blocks_of(width):
    head_width = width // HEADS
    per = max(1, 128 // head_width)
    return head_width, per, per * head_width


def partner_order(masks):
    order = [0]
    for mask in reversed(masks):
        order = order + [mask ^ k for k in order]
    return order


def weight_gradient(keep_ref, give_ref, groups, masks, parts):
    group_me = lax.axis_index("group")
    for which, ref in ((0, keep_ref), (1, give_ref)):
        at = 0
        for lhs_ref, rhs in parts:
            shard = lhs_ref.shape[0] // groups
            lhs = jnp.concatenate(
                [
                    lhs_ref[pl.ds(pl.multiple_of((group_me ^ k ^ which) * shard, shard), shard), :]
                    for k in partner_order(masks)
                ],
                axis=0,
            )
            ref[:, at : at + rhs.shape[1]] = dot(lhs, rhs).astype(BF16)
            at += rhs.shape[1]


def forward_kernel(groups, masks, n_rows, places, matrix_ref, scale_ref, *refs):
    row_refs, refs = refs[:n_rows], refs[n_rows:]
    weight_refs, refs = refs[: len(places)], refs[len(places) :]
    (keep_ref, give_ref, out_ref, w_ref, xt_ref, z_ref, inv_ref, cot_ref, act_ref, slope_ref) = refs[:10]
    bend_ref, gmix_ref, gproj_ref, weights_ref, gt_ref, mix_ref = refs[10:]
    width = mix_ref.shape[1]
    shard = width // groups
    group_me = lax.axis_index("group")

    matrix = matrix_ref[...]
    x = dot(matrix, stacked(row_refs, 0))
    cot = dot(matrix, stacked(row_refs, 1)).astype(BF16)
    cot_ref[...] = cot
    z, inv_scale = normalize(x)
    z_ref[...] = z
    inv_ref[...] = inv_scale
    xn = z.astype(BF16)
    xt_ref[...] = xn.T

    for (k, at), ref in zip(places, weight_refs):
        w_ref[pl.ds(pl.multiple_of((group_me ^ k) * shard, shard), shard), at : at + ref.shape[1]] = ref[...]

    for c in range(4):
        cols = slice(c * width, (c + 1) * width)
        projected = dot(xn, w_ref[:, cols])
        s = sigmoid(projected)
        act = projected * s
        act_ref[:, cols] = act.astype(BF16)
        slope_ref[:, cols] = s + act * (1.0 - s)

    scale = scale_ref[...]
    head_width, per, wide = blocks_of(width)
    for g in range(HEADS // per):
        v, q, k = (act_ref[:, c * width + g * wide : c * width + (g + 1) * wide] for c in (1, 2, 3))
        mixed = 0.0
        for h in range(per):
            scores = dot(only(q, h, head_width), k, NT)
            s = sigmoid(scores)
            value = scores * s
            weights = (value * scale).astype(BF16)
            weights_ref[g * per + h] = weights
            bend_ref[g * per + h] = (s + value * (1.0 - s)) * scale
            mixed = mixed + dot(weights, only(v, h, head_width))
        mix_ref[:, g * wide : (g + 1) * wide] = mixed

    normed, mix_inv = normalize(mix_ref[...])
    gate = act_ref[:, :width].astype(F32)
    gated = (normed * gate).astype(BF16)
    gt_ref[...] = gated.T
    w_out = w_ref[:, 4 * width :]
    out_ref[...] = (dot(gated, w_out) + x).astype(BF16)

    g_gated = dot(cot, w_out, NT).astype(BF16).astype(F32)
    g_u = ((g_gated * normed).astype(BF16).astype(F32) * slope_ref[:, :width]).astype(BF16)
    gproj_ref[:, :width] = g_u
    g_normed = g_gated * gate
    g_mixed = (
        mix_inv
        * (
            g_normed
            - jnp.mean(g_normed, axis=-1, keepdims=True)
            - normed * jnp.mean(g_normed * normed, axis=-1, keepdims=True)
        )
    ).astype(BF16)
    gmix_ref[...] = g_mixed
    for g in range(HEADS // per):
        mine = g_mixed[:, g * wide : (g + 1) * wide]
        g_v = 0.0
        for h in range(per):
            g_v = g_v + dot(weights_ref[g * per + h], only(mine, h, head_width), TN)
        at = slice(width + g * wide, width + (g + 1) * wide)
        gproj_ref[:, at] = (g_v.astype(BF16).astype(F32) * slope_ref[:, at]).astype(BF16)
    early = gproj_ref[:, : keep_ref.shape[1] - width]
    weight_gradient(keep_ref, give_ref, groups, masks, ((gt_ref, cot), (xt_ref, early)))


def backward_kernel(groups, masks, n_rows, matrix_ref, *refs):
    (out_ref, w_ref, xt_ref, z_ref, inv_ref, cot_ref, act_ref, slope_ref) = refs[:8]
    bend_ref, gmix_ref, early_ref, keep_ref, give_ref = refs[8:13]
    back_refs, gproj_ref = refs[13:-1], refs[-1]
    rows, width = out_ref.shape
    head_width, per, wide = blocks_of(width)

    gproj_ref[:, : 2 * width] = early_ref[...]
    for g in range(HEADS // per):
        v, q, k = (act_ref[:, c * width + g * wide : c * width + (g + 1) * wide] for c in (1, 2, 3))
        g_mix = gmix_ref[:, g * wide : (g + 1) * wide]
        g_q = g_k = 0.0
        for h in range(per):
            g_weights = dot(only(g_mix, h, head_width), v, NT).astype(BF16).astype(F32)
            g_scores = (g_weights * bend_ref[g * per + h]).astype(BF16)
            g_q = g_q + dot(g_scores, only(k, h, head_width))
            g_k = g_k + dot(g_scores, only(q, h, head_width), TN)
        for c, value in ((2, g_q), (3, g_k)):
            at = slice(c * width + g * wide, c * width + (g + 1) * wide)
            gproj_ref[:, at] = (value.astype(BF16).astype(F32) * slope_ref[:, at]).astype(BF16)

    late = gproj_ref[:, 4 * width - keep_ref.shape[1] :]
    weight_gradient(keep_ref, give_ref, groups, masks, ((xt_ref, late),))

    z = z_ref[...]
    g_xn = dot(gproj_ref[...], w_ref[:, : 4 * width], NT)
    g_x = (
        inv_ref[...]
        * (
            g_xn
            - jnp.mean(g_xn, axis=-1, keepdims=True)
            - z * jnp.mean(g_xn * z, axis=-1, keepdims=True)
        )
        + cot_ref[...].astype(F32)
    ).astype(BF16)
    step = rows // n_rows
    matrix = matrix_ref[...]
    for which, value in ((0, out_ref[...]), (1, g_x)):
        back = dot(matrix, value, TN).astype(BF16)
        for k, ref in enumerate(back_refs):
            ref[which] = back[k * step : (k + 1) * step]


def on_device(groups, parts, inputs, cotangent, w_uvqk, w_out, send_perm, recv_perm, lengths, prefixes):
    rows, width = inputs.shape[1:]
    shard = w_uvqk.shape[0]
    columns = w_uvqk.shape[1] + w_out.shape[1]
    chunk = rows // parts
    whole_tiles = chunk % 16 == 0
    n_rows = parts if whole_tiles else 1
    send_order, recv_order = send_perm[0], recv_perm[0]
    limit = pltpu.CompilerParams(vmem_limit_bytes=24 * 1024 * 1024)
    rows_shape = jax.ShapeDtypeStruct((2, rows // n_rows, width), BF16)

    def swap_rows(own, pieces):
        if not whole_tiles:
            cut = own.reshape(2, parts, chunk, width)
            own, pieces = cut[:, 0], [cut[:, k] for k in range(1, parts)]
        moved = [own] + [exchange(piece, "shuf", parts, k) for k, piece in enumerate(pieces, 1)]
        return moved if whole_tiles else [jnp.concatenate(moved, axis=1)]

    def spec(shape, dtype=BF16):
        return jax.ShapeDtypeStruct(shape, dtype)

    small_shape = (8, 128)
    w_mine, small, own, *outgoing = pl.pallas_call(
        partial(pre_kernel, parts),
        out_shape=[spec((shard, columns)), spec(small_shape, jnp.int32)] + [rows_shape] * n_rows,
        in_specs=[HBM] * 8,
        out_specs=[HBM] * (2 + n_rows),
        scratch_shapes=[
            pltpu.VMEM(send_order.shape, jnp.int32),
            pltpu.VMEM(recv_order.shape, jnp.int32),
            pltpu.VMEM(lengths[0].shape, jnp.int32),
            pltpu.VMEM(prefixes[0].shape, jnp.int32),
            pltpu.VMEM((rows, width), BF16),
            pltpu.VMEM((rows, width), BF16),
            pltpu.VMEM((shard, columns), BF16),
            pltpu.VMEM(small_shape, jnp.int32),
            pltpu.VMEM((rows, width), BF16),
            pltpu.VMEM((rows, width), BF16),
            pltpu.SemaphoreType.DMA((8,)),
            pltpu.SemaphoreType.DMA((2, n_rows)),
            pltpu.SemaphoreType.DMA((2,)),
        ],
        name="pre",
    )(send_order, recv_order, lengths[0], prefixes[0], inputs[0], cotangent[0], w_uvqk, w_out)
    matrix, scale, w_own, own = pl.pallas_call(
        partial(plan_kernel, parts, recv_order.shape[1], lengths.shape[2]),
        out_shape=[spec((rows, rows)), spec((rows, rows), F32), spec((shard, columns)), rows_shape],
        in_specs=[VMEM] * 3,
        out_specs=[VMEM] * 4,
        compiler_params=limit,
        name="plan",
    )(small, w_mine, own)

    chips = [2**j for j in range(1, groups.bit_length() - 1)]
    middle = columns // 2
    pieces = {(k, 0): exchange(w_mine, "group", groups, k) for k in chips}
    near = list(pieces)
    for k in range(2, groups, 2):
        if k not in chips:
            for at, mask in ((0, k & -k), (middle, 2 ** (k.bit_length() - 1))):
                source = pieces.get((k ^ mask, at))
                if (k ^ mask) in chips:
                    source = pieces[k ^ mask, 0][:, at : at + middle]
                pieces[k, at] = exchange(source, "group", groups, mask)
    close = [w_own] + [pieces[place] for place in near]
    arrived = swap_rows(own, outgoing)
    close, arrived[1:2], matrix, scale = lax.optimization_barrier((close, arrived[1:2], matrix, scale))
    pieces.update(zip([(0, 0)] + near, close))
    for (k, at), piece in list(pieces.items()):
        pieces[k ^ 1, at] = exchange(piece, "group", groups, 1)
    places = sorted(pieces)
    shards = [pieces[place] for place in places]

    half = groups // 2 * shard
    early_width = columns // 2
    keep, give, *saved, _ = pl.pallas_call(
        partial(forward_kernel, groups, chips, n_rows, places),
        out_shape=[
            spec((half, early_width)),
            spec((half, early_width)),
            spec((rows, width)),
            spec((width, columns)),
            spec((width, rows)),
            spec((rows, width), F32),
            spec((rows, 1), F32),
            spec((rows, width)),
            spec((rows, 4 * width)),
            spec((rows, 4 * width), F32),
            spec((HEADS, rows, rows), F32),
            spec((rows, width)),
            spec((rows, 2 * width)),
            spec((HEADS, rows, rows)),
        ],
        in_specs=[VMEM] * (2 + n_rows + len(shards)),
        out_specs=[VMEM] * 14,
        scratch_shapes=[pltpu.VMEM((width, rows), BF16), pltpu.VMEM((rows, width), F32)],
        compiler_params=limit,
        name="forward",
    )(matrix, scale, *arrived, *shards)
    taken = exchange(give, "group", groups, 1)
    keep_late, give_late, *returning = pl.pallas_call(
        partial(backward_kernel, groups, chips[::-1], n_rows),
        out_shape=[spec((half, columns - early_width))] * 2 + [rows_shape] * n_rows,
        in_specs=[VMEM] * (1 + len(saved)),
        out_specs=[VMEM] * (2 + n_rows),
        scratch_shapes=[pltpu.VMEM((rows, 4 * width), BF16)],
        compiler_params=limit,
        name="backward",
    )(matrix, *saved)

    far = [2**j for j in range(parts.bit_length() - 1)]

    def add(mine, other):
        return mine.astype(F32) + other.astype(F32)

    def both_cores(mine, other, beside):
        return lax.optimization_barrier((add(mine, other).astype(BF16), beside))

    def over_chips(total, masks, beside=()):
        for n, mask in enumerate(masks):
            middle = total.shape[0] // 2
            other = exchange(total[middle:], "group", groups, mask)
            if n == 0:
                other, beside = lax.optimization_barrier((other, beside))
            total = add(total[:middle], other).astype(BF16)
        return total, beside

    def over_shuf(total, masks, beside=()):
        for mask in masks[:-1]:
            total = add(total, exchange(total, "shuf", parts, mask)).astype(BF16)
        total, beside = lax.optimization_barrier((total, beside))
        return add(total, exchange(total, "shuf", parts, masks[-1])), beside

    taken, give_late = lax.optimization_barrier((taken, give_late))
    taken_late = exchange(give_late, "group", groups, 1)
    late, returning = both_cores(keep_late, taken_late, returning)
    returned = swap_rows(returning[0], returning[1:])
    early, returned[1:2] = over_chips(add(keep, taken).astype(BF16), chips, returned[1:2])
    early, returned = lax.optimization_barrier((early, returned))
    owner = pl.pallas_call(
        partial(post_kernel, parts),
        out_shape=[spec((rows, width))] * 2,
        in_specs=[VMEM] * (1 + n_rows),
        out_specs=[VMEM] * 2,
        compiler_params=limit,
        name="post",
    )(send_order, *returned)
    early, (owner_out, owner_grad) = over_shuf(early, far[::-1], owner)
    late, _ = over_chips(late, chips[::-1])
    late, _ = over_shuf(late, far)
    grad_uvqk = jnp.concatenate([early[:, width:], late], axis=1)
    grad_wout = early[:, :width]
    return (owner_out[None], owner_grad[None], grad_uvqk, grad_wout)


def solution(mesh):
    data, weight = P("group", "shuf", None), P("group", None)
    return jax.shard_map(
        partial(on_device, mesh.shape["group"], mesh.shape["shuf"]),
        mesh=mesh,
        in_specs=(data, data, weight, weight, data, data, data, data),
        out_specs=(data, data, weight, weight),
        check_vma=False,
    )
```

time: 80.9 us -> 72.3 us (0.89)
  starting transfers between devices: 31.6 us -> 23.9 us
  local copies, waits for them, and re-layouts: 6.4 us -> 3.32 us
  waiting for transfers between devices: 28.3 us -> 31.1 us
    ppermute x21 -> x25, starting transfers between devices: 31.6 us -> 23.9 us  [exchange(): return lax.ppermute(value, axis, [(i, i ^ mask) for i in range(size)])]
    unnamed x16 -> x8, local copies, waits for them, and re-layouts: 6.31 us -> 2.55 us
    ppermute x21 -> x25, waiting for transfers between devices: 28.3 us -> 31.1 us  [exchange(): return lax.ppermute(value, axis, [(i, i ^ mask) for i in range(size)])]
    pallas_call x4 -> x5, Pallas kernels: 11.3 us -> 11.4 us  [the longest x1 4.42 us: on_device(): pl.pallas_call(partial(forward_kernel, groups, chips, n_rows, places), ou...]
  transfers between devices with their start and end apart: 21 -> 25, of which waited for: 15 -> 12; matrix products, arithmetic and copies ran while one was open for 0% -> 2% of each run, Pallas kernels for 4% -> 6%
where the time goes in v3:
time: 72.3 us; the launch traced here: 72.1 us
  waiting for transfers between devices  31.1 us (43%)
  starting transfers between devices  23.9 us (33%)
  Pallas kernels  11.4 us (16%)
  local copies, waits for them, and re-layouts  3.32 us (5%)
  other arithmetic  1.59 us (2%)
  between operations  0.81 us (1%)
    ppermute x25, waiting for transfers between devices, exchange(): return lax.ppermute(value, axis, [(i, i ^ mask) for i in range(size)])  31.1 us
    ppermute x25, starting transfers between devices, exchange(): return lax.ppermute(value, axis, [(i, i ^ mask) for i in range(size)])  23.9 us
    pallas_call x1, Pallas kernels, on_device(): pl.pallas_call(partial(forward_kernel, groups, chips, n_rows, places), ou...  4.42 us
    pallas_call x1, Pallas kernels, on_device(): pl.pallas_call(partial(backward_kernel, groups, chips[::-1], n_rows), out...  2.75 us
    unnamed x8, local copies, waits for them, and re-layouts  2.55 us
    pallas_call x1, Pallas kernels, on_device(): pl.pallas_call(partial(pre_kernel, parts), out_shape=[spec((shard, column...  2.28 us
  transfers between devices with their start and end apart: 25, of which 12 were waited for; matrix products, arithmetic and copies ran while one was open for 2% of the time, Pallas kernels for 6%

profile of v3, /device:TPU:0, one launch (start us, length us, event | category | flops | bytes accessed | tf_op | source)
XLA Modules:
  0.0 72.1 jit_solution(12526312569440217410)
XLA Ops:
  0.6 2.3 %pre.1 = (bf16[64,2560]{1,0:T(8,128)(2,1)}, s32[8,128]{1,0:T(8,128)}, bf16[2,64,512]{2,1,0:T(8,128)(2,1)}, bf16[2,64,512]{2,1,0:T(8,128)(2,1)}, bf16[2,64,512]{2...) custom-call(s32[1,32]{1,0:T(1,128)} %bitcast.8, s32[1,32]{1,0:T(1,128)} %bitcast.12, s32[1,8]{1,0:T(1,128)} %bitcast.13, ...), custom_call_target="tpu_custom_call" | custom-call | tf_op jit(solution)/shard_map/pre/pallas_call | solution.py:326
  2.9 3.0 %collective-permute-start.1 = (bf16[64,2560]{1,0:T(8,128)(2,1)}, bf16[64,2560]{1,0:T(8,128)(2,1)S(1)}, u32[]{:S(2)}, u32[]{:S(2)}) collective-permute-start(bf16[64,2560]{1,0:T(8,128)(2,1)} %get-tuple-element.59.w_ref), channel_id=1, source_target_pairs={{0,16},{4,20},{8,24},{12,28},{16,0},{20,4},{24,8},{28,12},{1,17},{... | collective-permute-start | bytes 983048 | tf_op jit(solution)/shard_map/ppermute | solution.py:39
  6.0 1.5 %collective-permute-start = (bf16[64,2560]{1,0:T(8,128)(2,1)}, bf16[64,2560]{1,0:T(8,128)(2,1)S(1)}, u32[]{:S(2)}, u32[]{:S(2)}) collective-permute-start(bf16[64,2560]{1,0:T(8,128)(2,1)} %get-tuple-element.59.w_ref), channel_id=1, source_target_pairs={{0,8},{4,12},{8,0},{12,4},{16,24},{20,28},{24,16},{28,20},{1,9},{5... | collective-permute-start | bytes 983048 | tf_op jit(solution)/shard_map/ppermute | solution.py:39
  7.5 1.6 %collective-permute-start.2 = (bf16[2,64,512]{2,1,0:T(8,128)(2,1)}, bf16[2,64,512]{2,1,0:T(8,128)(2,1)S(1)}, u32[]{:S(2)}, u32[]{:S(2)}) collective-permute-start(bf16[2,64,512]{2,1,0:T(8,128)(2,1)} %get-tuple-element.62), channel_id=1, source_target_pairs={{0,1},{1,0},{2,3},{3,2},{4,5},{5,4},{6,7},{7,6},{8,9},{9,8},{10,11... | collective-permute-start | bytes 393224 | tf_op jit(solution)/shard_map/ppermute | solution.py:39
  9.0 2.6 %collective-permute-start.3 = (bf16[2,64,512]{2,1,0:T(8,128)(2,1)}, bf16[2,64,512]{2,1,0:T(8,128)(2,1)S(1)}, u32[]{:S(2)}, u32[]{:S(2)}) collective-permute-start(bf16[2,64,512]{2,1,0:T(8,128)(2,1)} %get-tuple-element.69), channel_id=1, source_target_pairs={{0,2},{1,3},{2,0},{3,1},{4,6},{5,7},{6,4},{7,5},{8,10},{9,11},{10,... | collective-permute-start | bytes 393224 | tf_op jit(solution)/shard_map/ppermute | solution.py:39
  11.6 0.2 collective-permute-start.4
  11.8 1.0 %copy-done = bf16[64,2560]{1,0:T(8,128)(2,1)S(1)} copy-done((bf16[64,2560]{1,0:T(8,128)(2,1)S(1)}, bf16[64,2560]{1,0:T(8,128)(2,1)}, u32[]{:S(2)}) %copy-start) | copy-done | bytes 327704
  12.8 0.9 %copy-done.1 = bf16[2,64,512]{2,1,0:T(8,128)(2,1)S(1)} copy-done((bf16[2,64,512]{2,1,0:T(8,128)(2,1)S(1)}, bf16[2,64,512]{2,1,0:T(8,128)(2,1)}, u32[]{:S(2)}) %copy-start.1) | copy-done | bytes 131096
  13.7 0.7 copy-done.2
  14.4 0.7 %plan.1 = (bf16[256,256]{1,0:T(8,128)(2,1)S(1)}, f32[256,256]{1,0:T(8,128)S(1)}, bf16[64,2560]{1,0:T(8,128)(2,1)S(1)}, bf16[2,64,512]{2,1,0:T(8,128)(2,1)S(1)}) custom-call(s32[8,128]{1,0:T(8,128)S(1)} %copy-done.2, bf16[64,2560]{1,0:T(8,128)(2,1)S(1)} %copy-done, bf16[2,64,512]{2,1,0:T(8,128)(2,1)S(1)} %copy-done.1), custom_call_target="tpu_custom_call" | custom-call | tf_op jit(solution)/shard_map/plan/pallas_call | solution.py:348
  15.1 0.6 collective-permute-start.8
  15.8 1.5 %collective-permute-start.9 = (bf16[64,1280]{1,0:T(8,128)(2,1)S(1)}, bf16[64,1280]{1,0:T(8,128)(2,1)S(1)}, u32[]{:S(2)}, u32[]{:S(2)}) collective-permute-start(bf16[64,1280]{1,0:T(8,128)(2,1)S(1)} %slice.49), channel_id=1, source_target_pairs={{0,16},{4,20},{8,24},{12,28},{16,0},{20,4},{24,8},{28,12},{1,17},{... | collective-permute-start | bytes 491528 | tf_op jit(solution)/shard_map/ppermute | solution.py:39
  17.3 4.3 %collective-permute-done.3.refs_2_ = bf16[2,64,512]{2,1,0:T(8,128)(2,1)S(1)} collective-permute-done((bf16[2,64,512]{2,1,0:T(8,128)(2,1)}, bf16[2,64,512]{2,1,0:T(8,128)(2,1)S(1)}, u32[]{:S(2)}, u32[]{:S(2)}) %collective-permute-start.3) | collective-permute-done | bytes 131104 | tf_op jit(solution)/shard_map/ppermute | solution.py:39
  21.6 0.5 collective-permute-start.7
  22.2 0.4 collective-permute-start.11
  22.6 1.3 %collective-permute-done.10.refs_12_ = bf16[64,1280]{1,0:T(8,128)(2,1)S(1)} collective-permute-done((bf16[64,1280]{1,0:T(8,128)(2,1)S(1)}, bf16[64,1280]{1,0:T(8,128)(2,1)S(1)}, u32[]{:S(2)}, u32[]{:S(2)}) %collective-permute-start.10) | collective-permute-done | bytes 163872 | tf_op jit(solution)/shard_map/ppermute | solution.py:39
  23.9 0.2 collective-permute-done.11.refs_13_
  24.2 4.4 %forward.1 = (bf16[256,1280]{1,0:T(8,128)(2,1)S(1)}, bf16[256,1280]{1,0:T(8,128)(2,1)S(1)}, bf16[256,512]{1,0:T(8,128)(2,1)S(1)}, bf16[512,2560]{1,0:T(8,128)(2,...) custom-call(bf16[256,256]{1,0:T(8,128)(2,1)S(1)} %get-tuple-element., ...), custom_call_target="tpu_custom_call" | custom-call | tf_op jit(solution)/shard_map/forward/pallas_call | solution.py:379
  28.6 0.2 collective-permute-start.12
  28.8 2.7 %backward.1 = (bf16[256,1280]{1,0:T(8,128)(2,1)S(1)}, bf16[256,1280]{1,0:T(8,128)(2,1)S(1)}, bf16[2,64,512]{2,1,0:T(8,128)(2,1)S(1)}, bf16[2,64,512]{2,1,0:T(8,1...) custom-call(bf16[256,256]{1,0:T(8,128)(2,1)S(1)} %get-tuple-element.65.matrix_ref, ...), custom_call_target="tpu_custom_call" | custom-call | tf_op jit(solution)/shard_map/backward/pallas_call | solution.py:404
  31.6 0.4 collective-permute-start.14
  32.0 0.2 add_convert_fusion.1
  32.2 0.6 collective-permute-start.13
  32.8 0.9 %collective-permute-done.14 = bf16[256,1280]{1,0:T(8,128)(2,1)S(1)} collective-permute-done((bf16[256,1280]{1,0:T(8,128)(2,1)S(1)}, bf16[256,1280]{1,0:T(8,128)(2,1)S(1)}, u32[]{:S(2)}, u32[]{:S(2)}) %collective-permute-start.14) | collective-permute-done | bytes 655392 | tf_op jit(solution)/shard_map/ppermute | solution.py:39
  33.7 0.2 add_convert_fusion
  33.9 1.6 %collective-permute-start.15 = (bf16[2,64,512]{2,1,0:T(8,128)(2,1)S(1)}, bf16[2,64,512]{2,1,0:T(8,128)(2,1)S(1)}, u32[]{:S(2)}, u32[]{:S(2)}) collective-permute-start(bf16[2,64,512]{2,1,0:T(8,128)(2,1)S(1)} %get-tuple-element.95), channel_id=1, source_target_pairs={{0,1},{1,0},{2,3},{3,2},{4,5},{5,4},{6,7},{7,6},{8,9},{9,8},{10,11... | collective-permute-start | bytes 393224 | tf_op jit(solution)/shard_map/ppermute | solution.py:39
  35.5 1.5 %collective-permute-start.17 = (bf16[2,64,512]{2,1,0:T(8,128)(2,1)S(1)}, bf16[2,64,512]{2,1,0:T(8,128)(2,1)S(1)}, u32[]{:S(2)}, u32[]{:S(2)}) collective-permute-start(bf16[2,64,512]{2,1,0:T(8,128)(2,1)S(1)} %get-tuple-element.99), channel_id=1, source_target_pairs={{0,2},{1,3},{2,0},{3,1},{4,6},{5,7},{6,4},{7,5},{8,10},{9,11},{10,... | collective-permute-start | bytes 393224 | tf_op jit(solution)/shard_map/ppermute | solution.py:39
  37.0 1.3 %collective-permute-start.18 = (bf16[2,64,512]{2,1,0:T(8,128)(2,1)S(1)}, bf16[2,64,512]{2,1,0:T(8,128)(2,1)S(1)}, u32[]{:S(2)}, u32[]{:S(2)}) collective-permute-start(bf16[2,64,512]{2,1,0:T(8,128)(2,1)S(1)} %get-tuple-element.100), channel_id=1, source_target_pairs={{0,3},{1,2},{2,1},{3,0},{4,7},{5,6},{6,5},{7,4},{8,11},{9,10},{10,... | collective-permute-start | bytes 393224 | tf_op jit(solution)/shard_map/ppermute | solution.py:39
  38.4 0.6 collective-permute-start.21
  39.0 3.0 %collective-permute-done.13 = bf16[128,1280]{1,0:T(8,128)(2,1)S(1)} collective-permute-done((bf16[128,1280]{1,0:T(8,128)(2,1)S(1)}, bf16[128,1280]{1,0:T(8,128)(2,1)S(1)}, u32[]{:S(2)}, u32[]{:S(2)}) %collective-permute-start.13) | collective-permute-done | bytes 327712 | tf_op jit(solution)/shard_map/ppermute | solution.py:39
  42.0 0.1 add_convert_fusion.3
  42.1 0.6 collective-permute-start.16
  42.7 6.4 %collective-permute-done.21 = bf16[128,1280]{1,0:T(8,128)(2,1)S(1)} collective-permute-done((bf16[128,1280]{1,0:T(8,128)(2,1)S(1)}, bf16[128,1280]{1,0:T(8,128)(2,1)S(1)}, u32[]{:S(2)}, u32[]{:S(2)}) %collective-permute-start.21) | collective-permute-done | bytes 327712 | tf_op jit(solution)/shard_map/ppermute | solution.py:39
  49.1 0.1 add_convert_fusion.2
  49.2 0.6 collective-permute-start.22
  49.8 1.3 %collective-permute-done.16 = bf16[64,1280]{1,0:T(8,128)(2,1)S(1)} collective-permute-done((bf16[64,1280]{1,0:T(8,128)(2,1)S(1)}, bf16[64,1280]{1,0:T(8,128)(2,1)S(1)}, u32[]{:S(2)}, u32[]{:S(2)}) %collective-permute-start.16) | collective-permute-done | bytes 163872 | tf_op jit(solution)/shard_map/ppermute | solution.py:39
  51.2 1.7 %collective-permute-start.19 = (bf16[64,1280]{1,0:T(8,128)(2,1)S(1)}, bf16[64,1280]{1,0:T(8,128)(2,1)S(1)}, u32[]{:S(2)}, u32[]{:S(2)}) collective-permute-start(bf16[64,1280]{1,0:T(8,128)(2,1)S(1)} %add_convert_fusion.7), channel_id=1, source_target_pairs={{0,2},{1,3},{2,0},{3,1},{4,6},{5,7},{6,4},{7,5},{8,10},{9,11},{10,... | collective-permute-start | bytes 491528 | tf_op jit(solution)/shard_map/ppermute | solution.py:39
  52.8 1.2 %post.1 = (bf16[256,512]{1,0:T(8,128)(2,1)}, bf16[256,512]{1,0:T(8,128)(2,1)}) custom-call(s32[1,32]{1,0:T(1,128)S(1)} %bitcast.9, bf16[2,64,512]{2,1,0:T(8,128)(2,1)S(1)} %get-tuple-element.102.refs_0_, bf16[2,64,512]{2,1,0:T(8,128)(2,1)S(1)} %collective-permute-done.15.refs_1_, bf16[2,64,512]{2,1,0:T(8,128)(2,1)S(1)} %collective-permute-done.17.refs_2_, ...), custom_call_target="tpu_custom_call" | custom-call | tf_op jit(solution)/shard_map/post/pallas_call | solution.py:443
  54.0 0.6 collective-permute-done.22
  54.7 0.9 %collective-permute-start.23 = (bf16[64,1280]{1,0:T(8,128)(2,1)S(1)}, bf16[64,1280]{1,0:T(8,128)(2,1)S(1)}, u32[]{:S(2)}, u32[]{:S(2)}) collective-permute-start(bf16[64,1280]{1,0:T(8,128)(2,1)S(1)} %add_convert_fusion.5), channel_id=1, source_target_pairs={{0,1},{1,0},{2,3},{3,2},{4,5},{5,4},{6,7},{7,6},{8,9},{9,8},{10,11... | collective-permute-start | bytes 491528 | tf_op jit(solution)/shard_map/ppermute | solution.py:39
  55.6 4.8 %collective-permute-done.19 = bf16[64,1280]{1,0:T(8,128)(2,1)S(1)} collective-permute-done((bf16[64,1280]{1,0:T(8,128)(2,1)S(1)}, bf16[64,1280]{1,0:T(8,128)(2,1)S(1)}, u32[]{:S(2)}, u32[]{:S(2)}) %collective-permute-start.19) | collective-permute-done | bytes 163872 | tf_op jit(solution)/shard_map/ppermute | solution.py:39
  60.5 0.1 collective-permute-start.20
  60.5 1.4 %collective-permute-done.23 = bf16[64,1280]{1,0:T(8,128)(2,1)S(1)} collective-permute-done((bf16[64,1280]{1,0:T(8,128)(2,1)S(1)}, bf16[64,1280]{1,0:T(8,128)(2,1)S(1)}, u32[]{:S(2)}, u32[]{:S(2)}) %collective-permute-start.23) | collective-permute-done | bytes 163872 | tf_op jit(solution)/shard_map/ppermute | solution.py:39
  62.0 1.7 %collective-permute-start.24 = (bf16[64,1280]{1,0:T(8,128)(2,1)S(1)}, bf16[64,1280]{1,0:T(8,128)(2,1)S(1)}, u32[]{:S(2)}, u32[]{:S(2)}) collective-permute-start(bf16[64,1280]{1,0:T(8,128)(2,1)S(1)} %add_convert_fusion.4), channel_id=1, source_target_pairs={{0,2},{1,3},{2,0},{3,1},{4,6},{5,7},{6,4},{7,5},{8,10},{9,11},{10,... | collective-permute-start | bytes 491528 | tf_op jit(solution)/shard_map/ppermute | solution.py:39
  63.7 5.0 %collective-permute-done.20 = bf16[64,1280]{1,0:T(8,128)(2,1)S(1)} collective-permute-done((bf16[64,1280]{1,0:T(8,128)(2,1)S(1)}, bf16[64,1280]{1,0:T(8,128)(2,1)S(1)}, u32[]{:S(2)}, u32[]{:S(2)}) %collective-permute-start.20) | collective-permute-done | bytes 163872 | tf_op jit(solution)/shard_map/ppermute | solution.py:39
  68.7 0.7 slice.57
  69.4 1.9 %collective-permute-done.24 = bf16[64,1280]{1,0:T(8,128)(2,1)S(1)} collective-permute-done((bf16[64,1280]{1,0:T(8,128)(2,1)S(1)}, bf16[64,1280]{1,0:T(8,128)(2,1)S(1)}, u32[]{:S(2)}, u32[]{:S(2)}) %collective-permute-start.24) | collective-permute-done | bytes 163872 | tf_op jit(solution)/shard_map/ppermute | solution.py:39
  71.3 0.8 %pad_maximum_fusion = f32[64,2048]{1,0:T(8,128)} fusion(f32[64,1280]{1,0:T(8,128)S(1)} %convert_add_fusion, f32[64,768]{1,0:T(8,128)S(1)} %slice.54), kind=kLoop, calls=%fused_computation.4 | loop fusion | flops 131072 | bytes 1048576 | tf_op jit(solution)/shard_map/concatenate | solution.py:454
  (34 shorter events, 0.5 us)
Async XLA Ops:
  2.9 12.2 %collective-permute-start.1 = (bf16[64,2560]{1,0:T(8,128)(2,1)}, bf16[64,2560]{1,0:T(8,128)(2,1)S(1)}, u32[]{:S(2)}, u32[]{:S(2)}) collective-permute-start(bf16[64,2560]{1,0:T(8,128)(2,1)} %get-tuple-element.59.w_ref), channel_id=1, source_target_pairs={{0,16},{4,20},{8,24},{12,28},{16,0},{20,4},{24,8},{28,12},{1,17},{... | collective-permute-start | bytes 983048 | tf_op jit(solution)/shard_map/ppermute | solution.py:39
  6.0 9.8 %collective-permute-start = (bf16[64,2560]{1,0:T(8,128)(2,1)}, bf16[64,2560]{1,0:T(8,128)(2,1)S(1)}, u32[]{:S(2)}, u32[]{:S(2)}) collective-permute-start(bf16[64,2560]{1,0:T(8,128)(2,1)} %get-tuple-element.59.w_ref), channel_id=1, source_target_pairs={{0,8},{4,12},{8,0},{12,4},{16,24},{20,28},{24,16},{28,20},{1,9},{5... | collective-permute-start | bytes 983048 | tf_op jit(solution)/shard_map/ppermute | solution.py:39
  7.5 9.8 %collective-permute-start.2 = (bf16[2,64,512]{2,1,0:T(8,128)(2,1)}, bf16[2,64,512]{2,1,0:T(8,128)(2,1)S(1)}, u32[]{:S(2)}, u32[]{:S(2)}) collective-permute-start(bf16[2,64,512]{2,1,0:T(8,128)(2,1)} %get-tuple-element.62), channel_id=1, source_target_pairs={{0,1},{1,0},{2,3},{3,2},{4,5},{5,4},{6,7},{7,6},{8,9},{9,8},{10,11... | collective-permute-start | bytes 393224 | tf_op jit(solution)/shard_map/ppermute | solution.py:39
  9.0 12.6 %collective-permute-start.3 = (bf16[2,64,512]{2,1,0:T(8,128)(2,1)}, bf16[2,64,512]{2,1,0:T(8,128)(2,1)S(1)}, u32[]{:S(2)}, u32[]{:S(2)}) collective-permute-start(bf16[2,64,512]{2,1,0:T(8,128)(2,1)} %get-tuple-element.69), channel_id=1, source_target_pairs={{0,2},{1,3},{2,0},{3,1},{4,6},{5,7},{6,4},{7,5},{8,10},{9,11},{10,... | collective-permute-start | bytes 393224 | tf_op jit(solution)/shard_map/ppermute | solution.py:39
  11.6 10.0 %collective-permute-start.4 = (bf16[2,64,512]{2,1,0:T(8,128)(2,1)}, bf16[2,64,512]{2,1,0:T(8,128)(2,1)S(1)}, u32[]{:S(2)}, u32[]{:S(2)}) collective-permute-start(bf16[2,64,512]{2,1,0:T(8,128)(2,1)} %get-tuple-element.70), channel_id=1, source_target_pairs={{0,3},{1,2},{2,1},{3,0},{4,7},{5,6},{6,5},{7,4},{8,11},{9,10},{10,... | collective-permute-start | bytes 393224 | tf_op jit(solution)/shard_map/ppermute | solution.py:39
  11.8 1.0 %copy-start = (bf16[64,2560]{1,0:T(8,128)(2,1)S(1)}, bf16[64,2560]{1,0:T(8,128)(2,1)}, u32[]{:S(2)}) copy-start(bf16[64,2560]{1,0:T(8,128)(2,1)} %get-tuple-element.59.w_ref) | copy-start | bytes 983044
  12.8 0.9 %copy-start.1 = (bf16[2,64,512]{2,1,0:T(8,128)(2,1)S(1)}, bf16[2,64,512]{2,1,0:T(8,128)(2,1)}, u32[]{:S(2)}) copy-start(bf16[2,64,512]{2,1,0:T(8,128)(2,1)} %get-tuple-element.60.own_ref) | copy-start | bytes 393220
  13.7 0.7 copy-start.2
  15.1 7.0 %collective-permute-start.8 = (bf16[64,1280]{1,0:T(8,128)(2,1)S(1)}, bf16[64,1280]{1,0:T(8,128)(2,1)S(1)}, u32[]{:S(2)}, u32[]{:S(2)}) collective-permute-start(bf16[64,1280]{1,0:T(8,128)(2,1)S(1)} %slice.48), channel_id=1, source_target_pairs={{0,8},{4,12},{8,0},{12,4},{16,24},{20,28},{24,16},{28,20},{1,9},{5... | collective-permute-start | bytes 491528 | tf_op jit(solution)/shard_map/ppermute | solution.py:39
  15.8 6.4 %collective-permute-start.9 = (bf16[64,1280]{1,0:T(8,128)(2,1)S(1)}, bf16[64,1280]{1,0:T(8,128)(2,1)S(1)}, u32[]{:S(2)}, u32[]{:S(2)}) collective-permute-start(bf16[64,1280]{1,0:T(8,128)(2,1)S(1)} %slice.49), channel_id=1, source_target_pairs={{0,16},{4,20},{8,24},{12,28},{16,0},{20,4},{24,8},{28,12},{1,17},{... | collective-permute-start | bytes 491528 | tf_op jit(solution)/shard_map/ppermute | solution.py:39
  17.3 6.9 %collective-permute-start.5 = (bf16[64,2560]{1,0:T(8,128)(2,1)S(1)}, bf16[64,2560]{1,0:T(8,128)(2,1)S(1)}, u32[]{:S(2)}, u32[]{:S(2)}) collective-permute-start(bf16[64,2560]{1,0:T(8,128)(2,1)S(1)} %get-tuple-element.71.refs_4_), channel_id=1, source_target_pairs={{0,4},{4,0},{8,12},{12,8},{16,20},{20,16},{24,28},{28,24},{1,5},{5... | collective-permute-start | bytes 983048 | tf_op jit(solution)/shard_map/ppermute | solution.py:39
  21.6 2.6 %collective-permute-start.6 = (bf16[64,2560]{1,0:T(8,128)(2,1)S(1)}, bf16[64,2560]{1,0:T(8,128)(2,1)S(1)}, u32[]{:S(2)}, u32[]{:S(2)}) collective-permute-start(bf16[64,2560]{1,0:T(8,128)(2,1)S(1)} %collective-permute-done.refs_6_), channel_id=1, source_target_pairs={{0,4},{4,0},{8,12},{12,8},{16,20},{20,16},{24,28},{28,24},{1,5},{5... | collective-permute-start | bytes 983048 | tf_op jit(solution)/shard_map/ppermute | solution.py:39
  21.6 2.6 %collective-permute-start.7 = (bf16[64,2560]{1,0:T(8,128)(2,1)S(1)}, bf16[64,2560]{1,0:T(8,128)(2,1)S(1)}, u32[]{:S(2)}, u32[]{:S(2)}) collective-permute-start(bf16[64,2560]{1,0:T(8,128)(2,1)S(1)} %collective-permute-done.1.refs_8_), channel_id=1, source_target_pairs={{0,4},{4,0},{8,12},{12,8},{16,20},{20,16},{24,28},{28,24},{1,5},{5... | collective-permute-start | bytes 983048 | tf_op jit(solution)/shard_map/ppermute | solution.py:39
  22.1 1.8 %collective-permute-start.10 = (bf16[64,1280]{1,0:T(8,128)(2,1)S(1)}, bf16[64,1280]{1,0:T(8,128)(2,1)S(1)}, u32[]{:S(2)}, u32[]{:S(2)}) collective-permute-start(bf16[64,1280]{1,0:T(8,128)(2,1)S(1)} %collective-permute-done.8.refs_10_), channel_id=1, source_target_pairs={{0,4},{4,0},{8,12},{12,8},{16,20},{20,16},{24,28},{28,24},{1,5},{5... | collective-permute-start | bytes 491528 | tf_op jit(solution)/shard_map/ppermute | solution.py:39
  22.2 2.0 %collective-permute-start.11 = (bf16[64,1280]{1,0:T(8,128)(2,1)S(1)}, bf16[64,1280]{1,0:T(8,128)(2,1)S(1)}, u32[]{:S(2)}, u32[]{:S(2)}) collective-permute-start(bf16[64,1280]{1,0:T(8,128)(2,1)S(1)} %collective-permute-done.9.refs_11_), channel_id=1, source_target_pairs={{0,4},{4,0},{8,12},{12,8},{16,20},{20,16},{24,28},{28,24},{1,5},{5... | collective-permute-start | bytes 491528 | tf_op jit(solution)/shard_map/ppermute | solution.py:39
  28.6 3.0 %collective-permute-start.12 = (bf16[256,1280]{1,0:T(8,128)(2,1)S(1)}, bf16[256,1280]{1,0:T(8,128)(2,1)S(1)}, u32[]{:S(2)}, u32[]{:S(2)}) collective-permute-start(bf16[256,1280]{1,0:T(8,128)(2,1)S(1)} %get-tuple-element.75), channel_id=1, source_target_pairs={{0,4},{4,0},{8,12},{12,8},{16,20},{20,16},{24,28},{28,24},{1,5},{5... | collective-permute-start | bytes 1966088 | tf_op jit(solution)/shard_map/ppermute | solution.py:39
  31.6 2.2 %collective-permute-start.14 = (bf16[256,1280]{1,0:T(8,128)(2,1)S(1)}, bf16[256,1280]{1,0:T(8,128)(2,1)S(1)}, u32[]{:S(2)}, u32[]{:S(2)}) collective-permute-start(bf16[256,1280]{1,0:T(8,128)(2,1)S(1)} %get-tuple-element.90), channel_id=1, source_target_pairs={{0,4},{4,0},{8,12},{12,8},{16,20},{20,16},{24,28},{28,24},{1,5},{5... | collective-permute-start | bytes 1966088 | tf_op jit(solution)/shard_map/ppermute | solution.py:39
  32.2 9.8 %collective-permute-start.13 = (bf16[128,1280]{1,0:T(8,128)(2,1)S(1)}, bf16[128,1280]{1,0:T(8,128)(2,1)S(1)}, u32[]{:S(2)}, u32[]{:S(2)}) collective-permute-start(bf16[128,1280]{1,0:T(8,128)(2,1)S(1)} %slice.51), channel_id=1, source_target_pairs={{0,8},{4,12},{8,0},{12,4},{16,24},{20,28},{24,16},{28,20},{1,9},{5... | collective-permute-start | bytes 983048 | tf_op jit(solution)/shard_map/ppermute | solution.py:39
  33.9 8.1 %collective-permute-start.15 = (bf16[2,64,512]{2,1,0:T(8,128)(2,1)S(1)}, bf16[2,64,512]{2,1,0:T(8,128)(2,1)S(1)}, u32[]{:S(2)}, u32[]{:S(2)}) collective-permute-start(bf16[2,64,512]{2,1,0:T(8,128)(2,1)S(1)} %get-tuple-element.95), channel_id=1, source_target_pairs={{0,1},{1,0},{2,3},{3,2},{4,5},{5,4},{6,7},{7,6},{8,9},{9,8},{10,11... | collective-permute-start | bytes 393224 | tf_op jit(solution)/shard_map/ppermute | solution.py:39
  35.5 15.7 %collective-permute-start.17 = (bf16[2,64,512]{2,1,0:T(8,128)(2,1)S(1)}, bf16[2,64,512]{2,1,0:T(8,128)(2,1)S(1)}, u32[]{:S(2)}, u32[]{:S(2)}) collective-permute-start(bf16[2,64,512]{2,1,0:T(8,128)(2,1)S(1)} %get-tuple-element.99), channel_id=1, source_target_pairs={{0,2},{1,3},{2,0},{3,1},{4,6},{5,7},{6,4},{7,5},{8,10},{9,11},{10,... | collective-permute-start | bytes 393224 | tf_op jit(solution)/shard_map/ppermute | solution.py:39
  37.0 14.1 %collective-permute-start.18 = (bf16[2,64,512]{2,1,0:T(8,128)(2,1)S(1)}, bf16[2,64,512]{2,1,0:T(8,128)(2,1)S(1)}, u32[]{:S(2)}, u32[]{:S(2)}) collective-permute-start(bf16[2,64,512]{2,1,0:T(8,128)(2,1)S(1)} %get-tuple-element.100), channel_id=1, source_target_pairs={{0,3},{1,2},{2,1},{3,0},{4,7},{5,6},{6,5},{7,4},{8,11},{9,10},{10,... | collective-permute-start | bytes 393224 | tf_op jit(solution)/shard_map/ppermute | solution.py:39
  38.4 10.7 %collective-permute-start.21 = (bf16[128,1280]{1,0:T(8,128)(2,1)S(1)}, bf16[128,1280]{1,0:T(8,128)(2,1)S(1)}, u32[]{:S(2)}, u32[]{:S(2)}) collective-permute-start(bf16[128,1280]{1,0:T(8,128)(2,1)S(1)} %slice.44), channel_id=1, source_target_pairs={{0,16},{4,20},{8,24},{12,28},{16,0},{20,4},{24,8},{28,12},{1,17},{... | collective-permute-start | bytes 983048 | tf_op jit(solution)/shard_map/ppermute | solution.py:39
  42.1 10.7 %copy-start.3 = (s32[1,1,32]{2,1,0:T(1,128)S(1)}, s32[1,1,32]{2,1,0:T(1,128)}, u32[]{:S(2)}) copy-start(s32[1,1,32]{2,1,0:T(1,128)} %param.12) | copy-start | bytes 388
  42.1 9.0 %collective-permute-start.16 = (bf16[64,1280]{1,0:T(8,128)(2,1)S(1)}, bf16[64,1280]{1,0:T(8,128)(2,1)S(1)}, u32[]{:S(2)}, u32[]{:S(2)}) collective-permute-start(bf16[64,1280]{1,0:T(8,128)(2,1)S(1)} %slice.53), channel_id=1, source_target_pairs={{0,16},{4,20},{8,24},{12,28},{16,0},{20,4},{24,8},{28,12},{1,17},{... | collective-permute-start | bytes 491528 | tf_op jit(solution)/shard_map/ppermute | solution.py:39
  49.2 5.4 %collective-permute-start.22 = (bf16[64,1280]{1,0:T(8,128)(2,1)S(1)}, bf16[64,1280]{1,0:T(8,128)(2,1)S(1)}, u32[]{:S(2)}, u32[]{:S(2)}) collective-permute-start(bf16[64,1280]{1,0:T(8,128)(2,1)S(1)} %slice.56), channel_id=1, source_target_pairs={{0,8},{4,12},{8,0},{12,4},{16,24},{20,28},{24,16},{28,20},{1,9},{5... | collective-permute-start | bytes 491528 | tf_op jit(solution)/shard_map/ppermute | solution.py:39
  51.2 9.2 %collective-permute-start.19 = (bf16[64,1280]{1,0:T(8,128)(2,1)S(1)}, bf16[64,1280]{1,0:T(8,128)(2,1)S(1)}, u32[]{:S(2)}, u32[]{:S(2)}) collective-permute-start(bf16[64,1280]{1,0:T(8,128)(2,1)S(1)} %add_convert_fusion.7), channel_id=1, source_target_pairs={{0,2},{1,3},{2,0},{3,1},{4,6},{5,7},{6,4},{7,5},{8,10},{9,11},{10,... | collective-permute-start | bytes 491528 | tf_op jit(solution)/shard_map/ppermute | solution.py:39
  54.7 7.3 %collective-permute-start.23 = (bf16[64,1280]{1,0:T(8,128)(2,1)S(1)}, bf16[64,1280]{1,0:T(8,128)(2,1)S(1)}, u32[]{:S(2)}, u32[]{:S(2)}) collective-permute-start(bf16[64,1280]{1,0:T(8,128)(2,1)S(1)} %add_convert_fusion.5), channel_id=1, source_target_pairs={{0,1},{1,0},{2,3},{3,2},{4,5},{5,4},{6,7},{7,6},{8,9},{9,8},{10,11... | collective-permute-start | bytes 491528 | tf_op jit(solution)/shard_map/ppermute | solution.py:39
  60.5 8.2 %collective-permute-start.20 = (bf16[64,1280]{1,0:T(8,128)(2,1)S(1)}, bf16[64,1280]{1,0:T(8,128)(2,1)S(1)}, u32[]{:S(2)}, u32[]{:S(2)}) collective-permute-start(bf16[64,1280]{1,0:T(8,128)(2,1)S(1)} %add_convert_fusion.6), channel_id=1, source_target_pairs={{0,1},{1,0},{2,3},{3,2},{4,5},{5,4},{6,7},{7,6},{8,9},{9,8},{10,11... | collective-permute-start | bytes 491528 | tf_op jit(solution)/shard_map/ppermute | solution.py:39
  62.0 9.2 %collective-permute-start.24 = (bf16[64,1280]{1,0:T(8,128)(2,1)S(1)}, bf16[64,1280]{1,0:T(8,128)(2,1)S(1)}, u32[]{:S(2)}, u32[]{:S(2)}) collective-permute-start(bf16[64,1280]{1,0:T(8,128)(2,1)S(1)} %add_convert_fusion.4), channel_id=1, source_target_pairs={{0,2},{1,3},{2,0},{3,1},{4,6},{5,7},{6,4},{7,5},{8,10},{9,11},{10,... | collective-permute-start | bytes 491528 | tf_op jit(solution)/shard_map/ppermute | solution.py:39

commit v4 on v3

--- a/solution.py
+++ b/solution.py
@@ -147,6 +147,18 @@
         ref[...] = dot(matrix, stacked(back_refs, which), TN).astype(BF16)
 
 
+def finish_kernel(early_own, early_other, late_own, late_other, uvqk_ref, out_ref):
+    rows = early_own.shape[0]
+    width = out_ref.shape[1]
+    split = early_own.shape[1] - width
+    side = lax.axis_index("shuf") & 1
+    for place, early, late in ((side, early_own, late_own), (1 - side, early_other, late_other)):
+        at = pl.ds(pl.multiple_of(place * rows, rows), rows)
+        out_ref[at, :] = early[:, :width].astype(F32)
+        uvqk_ref[at, :split] = early[:, width:].astype(F32)
+        uvqk_ref[at, split:] = late[...].astype(F32)
+
+
 def only(value, h, head_width):
     place = lax.div(lax.broadcasted_iota(jnp.int32, value.shape, 1), head_width)
     return jnp.where(place == h, value, jnp.zeros_like(value))
@@ -368,14 +380,16 @@
     close = [w_own] + [pieces[place] for place in near]
     arrived = swap_rows(own, outgoing)
     close, arrived[1:2], matrix, scale = lax.optimization_barrier((close, arrived[1:2], matrix, scale))
-    pieces.update(zip([(0, 0)] + near, close))
+    distant = [place for place in pieces if place not in near]
+    last, arrived[2:] = lax.optimization_barrier(([pieces[place] for place in distant], arrived[2:]))
+    pieces.update(zip([(0, 0)] + near + distant, close + last))
     for (k, at), piece in list(pieces.items()):
         pieces[k ^ 1, at] = exchange(piece, "group", groups, 1)
     places = sorted(pieces)
     shards = [pieces[place] for place in places]
 
     half = groups // 2 * shard
-    early_width = columns // 2
+    early_width = 3 * width
     keep, give, *saved, _ = pl.pallas_call(
         partial(forward_kernel, groups, chips, n_rows, places),
         out_shape=[
@@ -428,11 +442,16 @@
             total = add(total[:middle], other).astype(BF16)
         return total, beside
 
-    def over_shuf(total, masks, beside=()):
-        for mask in masks[:-1]:
+    side = lax.axis_index("shuf") & 1
+
+    def over_shuf(total):
+        middle = shard // 2
+        kept = lax.dynamic_slice_in_dim(total, side * middle, middle)
+        sent = lax.dynamic_slice_in_dim(total, (1 - side) * middle, middle)
+        total = add(kept, exchange(sent, "shuf", parts, 1)).astype(BF16)
+        for mask in far[1:]:
             total = add(total, exchange(total, "shuf", parts, mask)).astype(BF16)
-        total, beside = lax.optimization_barrier((total, beside))
-        return add(total, exchange(total, "shuf", parts, masks[-1])), beside
+        return total, exchange(total, "shuf", parts, 1)
 
     taken, give_late = lax.optimization_barrier((taken, give_late))
     taken_late = exchange(give_late, "group", groups, 1)
@@ -448,11 +467,18 @@
         compiler_params=limit,
         name="post",
     )(send_order, *returned)
-    early, (owner_out, owner_grad) = over_shuf(early, far[::-1], owner)
+    owner_out, owner_grad = owner
+    early = over_shuf(early)
     late, _ = over_chips(late, chips[::-1])
-    late, _ = over_shuf(late, far)
-    grad_uvqk = jnp.concatenate([early[:, width:], late], axis=1)
-    grad_wout = early[:, :width]
+    late = over_shuf(late)
+    grad_uvqk, grad_wout = pl.pallas_call(
+        finish_kernel,
+        out_shape=[spec((shard, 4 * width), F32), spec((shard, width), F32)],
+        in_specs=[VMEM] * 4,
+        out_specs=[VMEM] * 2,
+        compiler_params=limit,
+        name="finish",
+    )(*early, *late)
     return (owner_out[None], owner_grad[None], grad_uvqk, grad_wout)
 
 

time: 72.3 us -> 69.3 us (0.959)
  waiting for transfers between devices: 31.1 us -> 21.6 us
  starting transfers between devices: 23.9 us -> 30.9 us
  Pallas kernels: 11.4 us -> 12.4 us
  other arithmetic: 1.59 us -> 0.72 us
    ppermute x25 -> x27, waiting for transfers between devices: 31.1 us -> 21.6 us  [exchange(): return lax.ppermute(value, axis, [(i, i ^ mask) for i in range(size)])]
    ppermute x25 -> x27, starting transfers between devices: 23.9 us -> 30.9 us  [exchange(): return lax.ppermute(value, axis, [(i, i ^ mask) for i in range(size)])]
    pallas_call x0 -> x1, Pallas kernels: none -> 0.87 us  [on_device(): pl.pallas_call(finish_kernel, out_shape=[spec((shard, 4 * width), F32), s...]
    concatenate x1 -> x0, other arithmetic: 0.83 us -> none  [on_device(): grad_uvqk = jnp.concatenate([early[:, width:], late], axis=1)]
  transfers between devices with their start and end apart: 25 -> 27, of which waited for: 12 -> 13; matrix products, arithmetic and copies ran while one was open for 2% -> 1% of each run, Pallas kernels for 6% -> 7%
where the time goes in v4:
time: 69.3 us; the launch traced here: 69.1 us
  starting transfers between devices  30.9 us (45%)
  waiting for transfers between devices  21.6 us (31%)
  Pallas kernels  12.4 us (18%)
  local copies, waits for them, and re-layouts  2.69 us (4%)
  between operations  0.83 us (1%)
  other arithmetic  0.72 us (1%)
    ppermute x27, starting transfers between devices, exchange(): return lax.ppermute(value, axis, [(i, i ^ mask) for i in range(size)])  30.9 us
    ppermute x27, waiting for transfers between devices, exchange(): return lax.ppermute(value, axis, [(i, i ^ mask) for i in range(size)])  21.6 us
    pallas_call x1, Pallas kernels, on_device(): pl.pallas_call(partial(forward_kernel, groups, chips, n_rows, places), ou...  4.46 us
    pallas_call x1, Pallas kernels, on_device(): pl.pallas_call(partial(backward_kernel, groups, chips[::-1], n_rows), out...  2.85 us
    unnamed x8, local copies, waits for them, and re-layouts  2.57 us
    pallas_call x1, Pallas kernels, on_device(): pl.pallas_call(partial(pre_kernel, parts), out_shape=[spec((shard, column...  2.28 us
  transfers between devices with their start and end apart: 27, of which 13 were waited for; matrix products, arithmetic and copies ran while one was open for 1% of the time, Pallas kernels for 7%

profile of v4, /device:TPU:0, one launch (start us, length us, event | category | flops | bytes accessed | tf_op | source)
XLA Modules:
  0.0 69.1 jit_solution(11452756935504715523)
XLA Ops:
  0.6 2.3 %pre.1 = (bf16[64,2560]{1,0:T(8,128)(2,1)}, s32[8,128]{1,0:T(8,128)}, bf16[2,64,512]{2,1,0:T(8,128)(2,1)}, bf16[2,64,512]{2,1,0:T(8,128)(2,1)}, bf16[2,64,512]{2...) custom-call(s32[1,32]{1,0:T(1,128)} %bitcast.8, s32[1,32]{1,0:T(1,128)} %bitcast.12, s32[1,8]{1,0:T(1,128)} %bitcast.13, ...), custom_call_target="tpu_custom_call" | custom-call | tf_op jit(solution)/shard_map/pre/pallas_call | solution.py:338
  2.9 3.0 %collective-permute-start = (bf16[64,2560]{1,0:T(8,128)(2,1)}, bf16[64,2560]{1,0:T(8,128)(2,1)S(1)}, u32[]{:S(2)}, u32[]{:S(2)}) collective-permute-start(bf16[64,2560]{1,0:T(8,128)(2,1)} %get-tuple-element.62.w_ref), channel_id=1, source_target_pairs={{0,8},{4,12},{8,0},{12,4},{16,24},{20,28},{24,16},{28,20},{1,9},{5... | collective-permute-start | bytes 983048 | tf_op jit(solution)/shard_map/ppermute | solution.py:39
  5.9 1.5 %collective-permute-start.1 = (bf16[64,2560]{1,0:T(8,128)(2,1)}, bf16[64,2560]{1,0:T(8,128)(2,1)S(1)}, u32[]{:S(2)}, u32[]{:S(2)}) collective-permute-start(bf16[64,2560]{1,0:T(8,128)(2,1)} %get-tuple-element.62.w_ref), channel_id=1, source_target_pairs={{0,16},{4,20},{8,24},{12,28},{16,0},{20,4},{24,8},{28,12},{1,17},{... | collective-permute-start | bytes 983048 | tf_op jit(solution)/shard_map/ppermute | solution.py:39
  7.5 1.6 %collective-permute-start.2 = (bf16[2,64,512]{2,1,0:T(8,128)(2,1)}, bf16[2,64,512]{2,1,0:T(8,128)(2,1)S(1)}, u32[]{:S(2)}, u32[]{:S(2)}) collective-permute-start(bf16[2,64,512]{2,1,0:T(8,128)(2,1)} %get-tuple-element.65), channel_id=1, source_target_pairs={{0,1},{1,0},{2,3},{3,2},{4,5},{5,4},{6,7},{7,6},{8,9},{9,8},{10,11... | collective-permute-start | bytes 393224 | tf_op jit(solution)/shard_map/ppermute | solution.py:39
  9.0 2.6 %collective-permute-start.5 = (bf16[2,64,512]{2,1,0:T(8,128)(2,1)}, bf16[2,64,512]{2,1,0:T(8,128)(2,1)S(1)}, u32[]{:S(2)}, u32[]{:S(2)}) collective-permute-start(bf16[2,64,512]{2,1,0:T(8,128)(2,1)} %get-tuple-element.72), channel_id=1, source_target_pairs={{0,2},{1,3},{2,0},{3,1},{4,6},{5,7},{6,4},{7,5},{8,10},{9,11},{10,... | collective-permute-start | bytes 393224 | tf_op jit(solution)/shard_map/ppermute | solution.py:39
  11.6 0.2 collective-permute-start.6
  11.8 1.0 %copy-done = bf16[64,2560]{1,0:T(8,128)(2,1)S(1)} copy-done((bf16[64,2560]{1,0:T(8,128)(2,1)S(1)}, bf16[64,2560]{1,0:T(8,128)(2,1)}, u32[]{:S(2)}) %copy-start) | copy-done | bytes 327704
  12.8 0.9 %copy-done.1 = bf16[2,64,512]{2,1,0:T(8,128)(2,1)S(1)} copy-done((bf16[2,64,512]{2,1,0:T(8,128)(2,1)S(1)}, bf16[2,64,512]{2,1,0:T(8,128)(2,1)}, u32[]{:S(2)}) %copy-start.1) | copy-done | bytes 131096
  13.7 0.7 copy-done.2
  14.4 0.7 %plan.1 = (bf16[256,256]{1,0:T(8,128)(2,1)S(1)}, f32[256,256]{1,0:T(8,128)S(1)}, bf16[64,2560]{1,0:T(8,128)(2,1)S(1)}, bf16[2,64,512]{2,1,0:T(8,128)(2,1)S(1)}) custom-call(s32[8,128]{1,0:T(8,128)S(1)} %copy-done.2, bf16[64,2560]{1,0:T(8,128)(2,1)S(1)} %copy-done, bf16[2,64,512]{2,1,0:T(8,128)(2,1)S(1)} %copy-done.1), custom_call_target="tpu_custom_call" | custom-call | tf_op jit(solution)/shard_map/plan/pallas_call | solution.py:360
  15.2 0.1 collective-permute-done.1.refs_8_
  15.3 0.5 collective-permute-start.3
  15.9 1.6 %collective-permute-start.4 = (bf16[64,1280]{1,0:T(8,128)(2,1)S(1)}, bf16[64,1280]{1,0:T(8,128)(2,1)S(1)}, u32[]{:S(2)}, u32[]{:S(2)}) collective-permute-start(bf16[64,1280]{1,0:T(8,128)(2,1)S(1)} %slice.41), channel_id=1, source_target_pairs={{0,16},{4,20},{8,24},{12,28},{16,0},{20,4},{24,8},{28,12},{1,17},{... | collective-permute-start | bytes 491528 | tf_op jit(solution)/shard_map/ppermute | solution.py:39
  17.5 4.1 %collective-permute-done.5.refs_2_ = bf16[2,64,512]{2,1,0:T(8,128)(2,1)S(1)} collective-permute-done((bf16[2,64,512]{2,1,0:T(8,128)(2,1)}, bf16[2,64,512]{2,1,0:T(8,128)(2,1)S(1)}, u32[]{:S(2)}, u32[]{:S(2)}) %collective-permute-start.5) | collective-permute-done | bytes 131104 | tf_op jit(solution)/shard_map/ppermute | solution.py:39
  21.6 0.5 collective-permute-start.9
  22.1 0.1 collective-permute-done.4.refs_11_
  22.3 0.5 collective-permute-start.11
  22.8 0.4 collective-permute-done.8.refs_7_
  23.2 0.5 collective-permute-done.9.refs_9_
  23.7 0.2 collective-permute-done.10.refs_12_
  23.9 0.2 collective-permute-done.11.refs_13_
  24.2 4.5 %forward.1 = (bf16[256,1536]{1,0:T(8,128)(2,1)S(1)}, bf16[256,1536]{1,0:T(8,128)(2,1)S(1)}, bf16[256,512]{1,0:T(8,128)(2,1)S(1)}, bf16[512,2560]{1,0:T(8,128)(2,...) custom-call(bf16[256,256]{1,0:T(8,128)(2,1)S(1)} %get-tuple-element., ...), custom_call_target="tpu_custom_call" | custom-call | tf_op jit(solution)/shard_map/forward/pallas_call | solution.py:393
  28.6 0.2 collective-permute-start.12
  28.8 2.9 %backward.1 = (bf16[256,1024]{1,0:T(8,128)(2,1)S(1)}, bf16[256,1024]{1,0:T(8,128)(2,1)S(1)}, bf16[2,64,512]{2,1,0:T(8,128)(2,1)S(1)}, bf16[2,64,512]{2,1,0:T(8,1...) custom-call(bf16[256,256]{1,0:T(8,128)(2,1)S(1)} %get-tuple-element.68.matrix_ref, ...), custom_call_target="tpu_custom_call" | custom-call | tf_op jit(solution)/shard_map/backward/pallas_call | solution.py:418
  31.7 0.4 collective-permute-start.14
  32.1 0.2 add_convert_fusion
  32.4 1.4 %collective-permute-start.13 = (bf16[128,1536]{1,0:T(8,128)(2,1)S(1)}, bf16[128,1536]{1,0:T(8,128)(2,1)S(1)}, u32[]{:S(2)}, u32[]{:S(2)}) collective-permute-start(bf16[128,1536]{1,0:T(8,128)(2,1)S(1)} %slice.43), channel_id=1, source_target_pairs={{0,8},{4,12},{8,0},{12,4},{16,24},{20,28},{24,16},{28,20},{1,9},{5... | collective-permute-start | bytes 1179656 | tf_op jit(solution)/shard_map/ppermute | solution.py:39
  33.7 0.2 add_convert_fusion.1
  33.9 1.6 %collective-permute-start.15 = (bf16[2,64,512]{2,1,0:T(8,128)(2,1)S(1)}, bf16[2,64,512]{2,1,0:T(8,128)(2,1)S(1)}, u32[]{:S(2)}, u32[]{:S(2)}) collective-permute-start(bf16[2,64,512]{2,1,0:T(8,128)(2,1)S(1)} %get-tuple-element.102), channel_id=1, source_target_pairs={{0,1},{1,0},{2,3},{3,2},{4,5},{5,4},{6,7},{7,6},{8,9},{9,8},{10,11... | collective-permute-start | bytes 393224 | tf_op jit(solution)/shard_map/ppermute | solution.py:39
  35.6 1.6 %collective-permute-start.22 = (bf16[128,1024]{1,0:T(8,128)(2,1)S(1)}, bf16[128,1024]{1,0:T(8,128)(2,1)S(1)}, u32[]{:S(2)}, u32[]{:S(2)}) collective-permute-start(bf16[128,1024]{1,0:T(8,128)(2,1)S(1)} %slice.37), channel_id=1, source_target_pairs={{0,16},{4,20},{8,24},{12,28},{16,0},{20,4},{24,8},{28,12},{1,17},{... | collective-permute-start | bytes 786440 | tf_op jit(solution)/shard_map/ppermute | solution.py:39
  37.2 2.6 %collective-permute-start.17 = (bf16[2,64,512]{2,1,0:T(8,128)(2,1)S(1)}, bf16[2,64,512]{2,1,0:T(8,128)(2,1)S(1)}, u32[]{:S(2)}, u32[]{:S(2)}) collective-permute-start(bf16[2,64,512]{2,1,0:T(8,128)(2,1)S(1)} %get-tuple-element.106), channel_id=1, source_target_pairs={{0,2},{1,3},{2,0},{3,1},{4,6},{5,7},{6,4},{7,5},{8,10},{9,11},{10,... | collective-permute-start | bytes 393224 | tf_op jit(solution)/shard_map/ppermute | solution.py:39
  39.8 0.2 collective-permute-start.18
  40.0 3.6 %collective-permute-done.13 = bf16[128,1536]{1,0:T(8,128)(2,1)S(1)} collective-permute-done((bf16[128,1536]{1,0:T(8,128)(2,1)S(1)}, bf16[128,1536]{1,0:T(8,128)(2,1)S(1)}, u32[]{:S(2)}, u32[]{:S(2)}) %collective-permute-start.13) | collective-permute-done | bytes 393248 | tf_op jit(solution)/shard_map/ppermute | solution.py:39
  43.6 0.1 add_convert_fusion.2
  43.7 1.5 %collective-permute-start.16 = (bf16[64,1536]{1,0:T(8,128)(2,1)S(1)}, bf16[64,1536]{1,0:T(8,128)(2,1)S(1)}, u32[]{:S(2)}, u32[]{:S(2)}) collective-permute-start(bf16[64,1536]{1,0:T(8,128)(2,1)S(1)} %slice.45), channel_id=1, source_target_pairs={{0,16},{4,20},{8,24},{12,28},{16,0},{20,4},{24,8},{28,12},{1,17},{... | collective-permute-start | bytes 589832 | tf_op jit(solution)/shard_map/ppermute | solution.py:39
  45.4 1.6 %collective-permute-start.23 = (bf16[64,1024]{1,0:T(8,128)(2,1)S(1)}, bf16[64,1024]{1,0:T(8,128)(2,1)S(1)}, u32[]{:S(2)}, u32[]{:S(2)}) collective-permute-start(bf16[64,1024]{1,0:T(8,128)(2,1)S(1)} %slice.47), channel_id=1, source_target_pairs={{0,8},{4,12},{8,0},{12,4},{16,24},{20,28},{24,16},{28,20},{1,9},{5... | collective-permute-start | bytes 393224 | tf_op jit(solution)/shard_map/ppermute | solution.py:39
  46.9 3.0 %collective-permute-done.16 = bf16[64,1536]{1,0:T(8,128)(2,1)S(1)} collective-permute-done((bf16[64,1536]{1,0:T(8,128)(2,1)S(1)}, bf16[64,1536]{1,0:T(8,128)(2,1)S(1)}, u32[]{:S(2)}, u32[]{:S(2)}) %collective-permute-start.16) | collective-permute-done | bytes 196640 | tf_op jit(solution)/shard_map/ppermute | solution.py:39
  50.0 2.1 %collective-permute-start.19 = (bf16[32,1536]{1,0:T(8,128)(2,1)S(1)}, bf16[32,1536]{1,0:T(8,128)(2,1)S(1)}, u32[]{:S(2)}, u32[]{:S(2)}) collective-permute-start(bf16[32,1536]{1,0:T(8,128)(2,1)S(1)} %constant_dynamic-slice_fusion.1), channel_id=1, source_target_pairs={{0,1},{1,0},{2,3},{3,2},{4,5},{5,4},{6,7},{7,6},{8,9},{9,8},{10,11... | collective-permute-start | bytes 294920 | tf_op jit(solution)/shard_map/ppermute | solution.py:39
  52.2 0.1 collective-permute-start.24
  52.3 3.0 %collective-permute-done.19 = bf16[32,1536]{1,0:T(8,128)(2,1)S(1)} collective-permute-done((bf16[32,1536]{1,0:T(8,128)(2,1)S(1)}, bf16[32,1536]{1,0:T(8,128)(2,1)S(1)}, u32[]{:S(2)}, u32[]{:S(2)}) %collective-permute-start.19) | collective-permute-done | bytes 98336 | tf_op jit(solution)/shard_map/ppermute | solution.py:39
  55.3 2.6 %collective-permute-start.20 = (bf16[32,1536]{1,0:T(8,128)(2,1)S(1)}, bf16[32,1536]{1,0:T(8,128)(2,1)S(1)}, u32[]{:S(2)}, u32[]{:S(2)}) collective-permute-start(bf16[32,1536]{1,0:T(8,128)(2,1)S(1)} %add_convert_fusion.7), channel_id=1, source_target_pairs={{0,2},{1,3},{2,0},{3,1},{4,6},{5,7},{6,4},{7,5},{8,10},{9,11},{10,... | collective-permute-start | bytes 294920 | tf_op jit(solution)/shard_map/ppermute | solution.py:39
  57.9 1.5 %collective-permute-start.25 = (bf16[32,1024]{1,0:T(8,128)(2,1)S(1)}, bf16[32,1024]{1,0:T(8,128)(2,1)S(1)}, u32[]{:S(2)}, u32[]{:S(2)}) collective-permute-start(bf16[32,1024]{1,0:T(8,128)(2,1)S(1)} %add_convert_fusion.9), channel_id=1, source_target_pairs={{0,2},{1,3},{2,0},{3,1},{4,6},{5,7},{6,4},{7,5},{8,10},{9,11},{10,... | collective-permute-start | bytes 196616 | tf_op jit(solution)/shard_map/ppermute | solution.py:39
  59.4 3.3 %collective-permute-done.20 = bf16[32,1536]{1,0:T(8,128)(2,1)S(1)} collective-permute-done((bf16[32,1536]{1,0:T(8,128)(2,1)S(1)}, bf16[32,1536]{1,0:T(8,128)(2,1)S(1)}, u32[]{:S(2)}, u32[]{:S(2)}) %collective-permute-start.20) | collective-permute-done | bytes 98336 | tf_op jit(solution)/shard_map/ppermute | solution.py:39
  62.9 1.0 %collective-permute-done.25 = bf16[32,1024]{1,0:T(8,128)(2,1)S(1)} collective-permute-done((bf16[32,1024]{1,0:T(8,128)(2,1)S(1)}, bf16[32,1024]{1,0:T(8,128)(2,1)S(1)}, u32[]{:S(2)}, u32[]{:S(2)}) %collective-permute-start.25) | collective-permute-done | bytes 65568 | tf_op jit(solution)/shard_map/ppermute | solution.py:39
  63.9 1.2 %collective-permute-start.26 = (bf16[32,1024]{1,0:T(8,128)(2,1)S(1)}, bf16[32,1024]{1,0:T(8,128)(2,1)S(1)}, u32[]{:S(2)}, u32[]{:S(2)}) collective-permute-start(bf16[32,1024]{1,0:T(8,128)(2,1)S(1)} %add_convert_fusion.8.late_own), channel_id=1, source_target_pairs={{0,1},{1,0},{2,3},{3,2},{4,5},{5,4},{6,7},{7,6},{8,9},{9,8},{10,11... | collective-permute-start | bytes 196616 | tf_op jit(solution)/shard_map/ppermute | solution.py:39
  65.1 1.2 %post.1 = (bf16[256,512]{1,0:T(8,128)(2,1)}, bf16[256,512]{1,0:T(8,128)(2,1)}) custom-call(s32[1,32]{1,0:T(1,128)S(1)} %bitcast.9, bf16[2,64,512]{2,1,0:T(8,128)(2,1)S(1)} %get-tuple-element.108.refs_0_, bf16[2,64,512]{2,1,0:T(8,128)(2,1)S(1)} %collective-permute-done.15.refs_1_, bf16[2,64,512]{2,1,0:T(8,128)(2,1)S(1)} %collective-permute-done.17.refs_2_, ...), custom_call_target="tpu_custom_call" | custom-call | tf_op jit(solution)/shard_map/post/pallas_call | solution.py:462
  66.3 1.9 %collective-permute-done.26.late_other = bf16[32,1024]{1,0:T(8,128)(2,1)S(1)} collective-permute-done((bf16[32,1024]{1,0:T(8,128)(2,1)S(1)}, bf16[32,1024]{1,0:T(8,128)(2,1)S(1)}, u32[]{:S(2)}, u32[]{:S(2)}) %collective-permute-start.26) | collective-permute-done | bytes 65568 | tf_op jit(solution)/shard_map/ppermute | solution.py:39
  68.2 0.9 %finish.1 = (f32[64,2048]{1,0:T(8,128)}, f32[64,512]{1,0:T(8,128)}) custom-call(bf16[32,1536]{1,0:T(8,128)(2,1)S(1)} %add_convert_fusion.6.early_own, bf16[32,1536]{1,0:T(8,128)(2,1)S(1)} %collective-permute-done.21.early_other, bf16[32,1024]{1,0:T(8,128)(2,1)S(1)} %add_convert_fusion.8.late_own, bf16[32,1024]{1,0:T(8,128)(2,1)S(1)} %collective-permute-done.26.late_other), custom_call_target="tpu_custom_call" | custom-call | tf_op jit(solution)/shard_map/finish/pallas_call | solution.py:474
  (38 shorter events, 0.5 us)
Async XLA Ops:
  2.9 12.2 %collective-permute-start = (bf16[64,2560]{1,0:T(8,128)(2,1)}, bf16[64,2560]{1,0:T(8,128)(2,1)S(1)}, u32[]{:S(2)}, u32[]{:S(2)}) collective-permute-start(bf16[64,2560]{1,0:T(8,128)(2,1)} %get-tuple-element.62.w_ref), channel_id=1, source_target_pairs={{0,8},{4,12},{8,0},{12,4},{16,24},{20,28},{24,16},{28,20},{1,9},{5... | collective-permute-start | bytes 983048 | tf_op jit(solution)/shard_map/ppermute | solution.py:39
  5.9 9.4 %collective-permute-start.1 = (bf16[64,2560]{1,0:T(8,128)(2,1)}, bf16[64,2560]{1,0:T(8,128)(2,1)S(1)}, u32[]{:S(2)}, u32[]{:S(2)}) collective-permute-start(bf16[64,2560]{1,0:T(8,128)(2,1)} %get-tuple-element.62.w_ref), channel_id=1, source_target_pairs={{0,16},{4,20},{8,24},{12,28},{16,0},{20,4},{24,8},{28,12},{1,17},{... | collective-permute-start | bytes 983048 | tf_op jit(solution)/shard_map/ppermute | solution.py:39
  7.5 7.7 %collective-permute-start.2 = (bf16[2,64,512]{2,1,0:T(8,128)(2,1)}, bf16[2,64,512]{2,1,0:T(8,128)(2,1)S(1)}, u32[]{:S(2)}, u32[]{:S(2)}) collective-permute-start(bf16[2,64,512]{2,1,0:T(8,128)(2,1)} %get-tuple-element.65), channel_id=1, source_target_pairs={{0,1},{1,0},{2,3},{3,2},{4,5},{5,4},{6,7},{7,6},{8,9},{9,8},{10,11... | collective-permute-start | bytes 393224 | tf_op jit(solution)/shard_map/ppermute | solution.py:39
  9.0 12.6 %collective-permute-start.5 = (bf16[2,64,512]{2,1,0:T(8,128)(2,1)}, bf16[2,64,512]{2,1,0:T(8,128)(2,1)S(1)}, u32[]{:S(2)}, u32[]{:S(2)}) collective-permute-start(bf16[2,64,512]{2,1,0:T(8,128)(2,1)} %get-tuple-element.72), channel_id=1, source_target_pairs={{0,2},{1,3},{2,0},{3,1},{4,6},{5,7},{6,4},{7,5},{8,10},{9,11},{10,... | collective-permute-start | bytes 393224 | tf_op jit(solution)/shard_map/ppermute | solution.py:39
  11.6 10.0 %collective-permute-start.6 = (bf16[2,64,512]{2,1,0:T(8,128)(2,1)}, bf16[2,64,512]{2,1,0:T(8,128)(2,1)S(1)}, u32[]{:S(2)}, u32[]{:S(2)}) collective-permute-start(bf16[2,64,512]{2,1,0:T(8,128)(2,1)} %get-tuple-element.73), channel_id=1, source_target_pairs={{0,3},{1,2},{2,1},{3,0},{4,7},{5,6},{6,5},{7,4},{8,11},{9,10},{10,... | collective-permute-start | bytes 393224 | tf_op jit(solution)/shard_map/ppermute | solution.py:39
  11.8 1.0 %copy-start = (bf16[64,2560]{1,0:T(8,128)(2,1)S(1)}, bf16[64,2560]{1,0:T(8,128)(2,1)}, u32[]{:S(2)}) copy-start(bf16[64,2560]{1,0:T(8,128)(2,1)} %get-tuple-element.62.w_ref) | copy-start | bytes 983044
  12.8 0.9 %copy-start.1 = (bf16[2,64,512]{2,1,0:T(8,128)(2,1)S(1)}, bf16[2,64,512]{2,1,0:T(8,128)(2,1)}, u32[]{:S(2)}) copy-start(bf16[2,64,512]{2,1,0:T(8,128)(2,1)} %get-tuple-element.63.own_ref) | copy-start | bytes 393220
  13.7 0.7 copy-start.2
  15.3 7.5 %collective-permute-start.7 = (bf16[64,2560]{1,0:T(8,128)(2,1)S(1)}, bf16[64,2560]{1,0:T(8,128)(2,1)S(1)}, u32[]{:S(2)}, u32[]{:S(2)}) collective-permute-start(bf16[64,2560]{1,0:T(8,128)(2,1)S(1)} %get-tuple-element.76.refs_4_), channel_id=1, source_target_pairs={{0,4},{4,0},{8,12},{12,8},{16,20},{20,16},{24,28},{28,24},{1,5},{5... | collective-permute-start | bytes 983048 | tf_op jit(solution)/shard_map/ppermute | solution.py:39
  15.3 6.8 %collective-permute-start.3 = (bf16[64,1280]{1,0:T(8,128)(2,1)S(1)}, bf16[64,1280]{1,0:T(8,128)(2,1)S(1)}, u32[]{:S(2)}, u32[]{:S(2)}) collective-permute-start(bf16[64,1280]{1,0:T(8,128)(2,1)S(1)} %slice.40), channel_id=1, source_target_pairs={{0,8},{4,12},{8,0},{12,4},{16,24},{20,28},{24,16},{28,20},{1,9},{5... | collective-permute-start | bytes 491528 | tf_op jit(solution)/shard_map/ppermute | solution.py:39
  15.9 6.4 %collective-permute-start.4 = (bf16[64,1280]{1,0:T(8,128)(2,1)S(1)}, bf16[64,1280]{1,0:T(8,128)(2,1)S(1)}, u32[]{:S(2)}, u32[]{:S(2)}) collective-permute-start(bf16[64,1280]{1,0:T(8,128)(2,1)S(1)} %slice.41), channel_id=1, source_target_pairs={{0,16},{4,20},{8,24},{12,28},{16,0},{20,4},{24,8},{28,12},{1,17},{... | collective-permute-start | bytes 491528 | tf_op jit(solution)/shard_map/ppermute | solution.py:39
  21.6 1.6 %collective-permute-start.8 = (bf16[64,2560]{1,0:T(8,128)(2,1)S(1)}, bf16[64,2560]{1,0:T(8,128)(2,1)S(1)}, u32[]{:S(2)}, u32[]{:S(2)}) collective-permute-start(bf16[64,2560]{1,0:T(8,128)(2,1)S(1)} %collective-permute-done.refs_6_), channel_id=1, source_target_pairs={{0,4},{4,0},{8,12},{12,8},{16,20},{20,16},{24,28},{28,24},{1,5},{5... | collective-permute-start | bytes 983048 | tf_op jit(solution)/shard_map/ppermute | solution.py:39
  21.6 2.1 %collective-permute-start.9 = (bf16[64,2560]{1,0:T(8,128)(2,1)S(1)}, bf16[64,2560]{1,0:T(8,128)(2,1)S(1)}, u32[]{:S(2)}, u32[]{:S(2)}) collective-permute-start(bf16[64,2560]{1,0:T(8,128)(2,1)S(1)} %collective-permute-done.1.refs_8_), channel_id=1, source_target_pairs={{0,4},{4,0},{8,12},{12,8},{16,20},{20,16},{24,28},{28,24},{1,5},{5... | collective-permute-start | bytes 983048 | tf_op jit(solution)/shard_map/ppermute | solution.py:39
  22.3 1.7 %collective-permute-start.10 = (bf16[64,1280]{1,0:T(8,128)(2,1)S(1)}, bf16[64,1280]{1,0:T(8,128)(2,1)S(1)}, u32[]{:S(2)}, u32[]{:S(2)}) collective-permute-start(bf16[64,1280]{1,0:T(8,128)(2,1)S(1)} %collective-permute-done.3.refs_10_), channel_id=1, source_target_pairs={{0,4},{4,0},{8,12},{12,8},{16,20},{20,16},{24,28},{28,24},{1,5},{5... | collective-permute-start | bytes 491528 | tf_op jit(solution)/shard_map/ppermute | solution.py:39
  22.3 1.9 %collective-permute-start.11 = (bf16[64,1280]{1,0:T(8,128)(2,1)S(1)}, bf16[64,1280]{1,0:T(8,128)(2,1)S(1)}, u32[]{:S(2)}, u32[]{:S(2)}) collective-permute-start(bf16[64,1280]{1,0:T(8,128)(2,1)S(1)} %collective-permute-done.4.refs_11_), channel_id=1, source_target_pairs={{0,4},{4,0},{8,12},{12,8},{16,20},{20,16},{24,28},{28,24},{1,5},{5... | collective-permute-start | bytes 491528 | tf_op jit(solution)/shard_map/ppermute | solution.py:39
  28.6 3.1 %collective-permute-start.12 = (bf16[256,1536]{1,0:T(8,128)(2,1)S(1)}, bf16[256,1536]{1,0:T(8,128)(2,1)S(1)}, u32[]{:S(2)}, u32[]{:S(2)}) collective-permute-start(bf16[256,1536]{1,0:T(8,128)(2,1)S(1)} %get-tuple-element.82), channel_id=1, source_target_pairs={{0,4},{4,0},{8,12},{12,8},{16,20},{20,16},{24,28},{28,24},{1,5},{5... | collective-permute-start | bytes 2359304 | tf_op jit(solution)/shard_map/ppermute | solution.py:39
  31.7 2.0 %collective-permute-start.14 = (bf16[256,1024]{1,0:T(8,128)(2,1)S(1)}, bf16[256,1024]{1,0:T(8,128)(2,1)S(1)}, u32[]{:S(2)}, u32[]{:S(2)}) collective-permute-start(bf16[256,1024]{1,0:T(8,128)(2,1)S(1)} %get-tuple-element.97), channel_id=1, source_target_pairs={{0,4},{4,0},{8,12},{12,8},{16,20},{20,16},{24,28},{28,24},{1,5},{5... | collective-permute-start | bytes 1572872 | tf_op jit(solution)/shard_map/ppermute | solution.py:39
  32.4 11.2 %collective-permute-start.13 = (bf16[128,1536]{1,0:T(8,128)(2,1)S(1)}, bf16[128,1536]{1,0:T(8,128)(2,1)S(1)}, u32[]{:S(2)}, u32[]{:S(2)}) collective-permute-start(bf16[128,1536]{1,0:T(8,128)(2,1)S(1)} %slice.43), channel_id=1, source_target_pairs={{0,8},{4,12},{8,0},{12,4},{16,24},{20,28},{24,16},{28,20},{1,9},{5... | collective-permute-start | bytes 1179656 | tf_op jit(solution)/shard_map/ppermute | solution.py:39
  33.9 9.7 %collective-permute-start.15 = (bf16[2,64,512]{2,1,0:T(8,128)(2,1)S(1)}, bf16[2,64,512]{2,1,0:T(8,128)(2,1)S(1)}, u32[]{:S(2)}, u32[]{:S(2)}) collective-permute-start(bf16[2,64,512]{2,1,0:T(8,128)(2,1)S(1)} %get-tuple-element.102), channel_id=1, source_target_pairs={{0,1},{1,0},{2,3},{3,2},{4,5},{5,4},{6,7},{7,6},{8,9},{9,8},{10,11... | collective-permute-start | bytes 393224 | tf_op jit(solution)/shard_map/ppermute | solution.py:39
  35.6 9.7 %collective-permute-start.22 = (bf16[128,1024]{1,0:T(8,128)(2,1)S(1)}, bf16[128,1024]{1,0:T(8,128)(2,1)S(1)}, u32[]{:S(2)}, u32[]{:S(2)}) collective-permute-start(bf16[128,1024]{1,0:T(8,128)(2,1)S(1)} %slice.37), channel_id=1, source_target_pairs={{0,16},{4,20},{8,24},{12,28},{16,0},{20,4},{24,8},{28,12},{1,17},{... | collective-permute-start | bytes 786440 | tf_op jit(solution)/shard_map/ppermute | solution.py:39
  37.2 12.8 %collective-permute-start.17 = (bf16[2,64,512]{2,1,0:T(8,128)(2,1)S(1)}, bf16[2,64,512]{2,1,0:T(8,128)(2,1)S(1)}, u32[]{:S(2)}, u32[]{:S(2)}) collective-permute-start(bf16[2,64,512]{2,1,0:T(8,128)(2,1)S(1)} %get-tuple-element.106), channel_id=1, source_target_pairs={{0,2},{1,3},{2,0},{3,1},{4,6},{5,7},{6,4},{7,5},{8,10},{9,11},{10,... | collective-permute-start | bytes 393224 | tf_op jit(solution)/shard_map/ppermute | solution.py:39
  39.8 10.2 %collective-permute-start.18 = (bf16[2,64,512]{2,1,0:T(8,128)(2,1)S(1)}, bf16[2,64,512]{2,1,0:T(8,128)(2,1)S(1)}, u32[]{:S(2)}, u32[]{:S(2)}) collective-permute-start(bf16[2,64,512]{2,1,0:T(8,128)(2,1)S(1)} %get-tuple-element.107), channel_id=1, source_target_pairs={{0,3},{1,2},{2,1},{3,0},{4,7},{5,6},{6,5},{7,4},{8,11},{9,10},{10,... | collective-permute-start | bytes 393224 | tf_op jit(solution)/shard_map/ppermute | solution.py:39
  43.7 21.4 %copy-start.3 = (s32[1,1,32]{2,1,0:T(1,128)S(1)}, s32[1,1,32]{2,1,0:T(1,128)}, u32[]{:S(2)}) copy-start(s32[1,1,32]{2,1,0:T(1,128)} %param.12) | copy-start | bytes 388
  43.7 6.2 %collective-permute-start.16 = (bf16[64,1536]{1,0:T(8,128)(2,1)S(1)}, bf16[64,1536]{1,0:T(8,128)(2,1)S(1)}, u32[]{:S(2)}, u32[]{:S(2)}) collective-permute-start(bf16[64,1536]{1,0:T(8,128)(2,1)S(1)} %slice.45), channel_id=1, source_target_pairs={{0,16},{4,20},{8,24},{12,28},{16,0},{20,4},{24,8},{28,12},{1,17},{... | collective-permute-start | bytes 589832 | tf_op jit(solution)/shard_map/ppermute | solution.py:39
  45.4 6.8 %collective-permute-start.23 = (bf16[64,1024]{1,0:T(8,128)(2,1)S(1)}, bf16[64,1024]{1,0:T(8,128)(2,1)S(1)}, u32[]{:S(2)}, u32[]{:S(2)}) collective-permute-start(bf16[64,1024]{1,0:T(8,128)(2,1)S(1)} %slice.47), channel_id=1, source_target_pairs={{0,8},{4,12},{8,0},{12,4},{16,24},{20,28},{24,16},{28,20},{1,9},{5... | collective-permute-start | bytes 393224 | tf_op jit(solution)/shard_map/ppermute | solution.py:39
  50.0 5.3 %collective-permute-start.19 = (bf16[32,1536]{1,0:T(8,128)(2,1)S(1)}, bf16[32,1536]{1,0:T(8,128)(2,1)S(1)}, u32[]{:S(2)}, u32[]{:S(2)}) collective-permute-start(bf16[32,1536]{1,0:T(8,128)(2,1)S(1)} %constant_dynamic-slice_fusion.1), channel_id=1, source_target_pairs={{0,1},{1,0},{2,3},{3,2},{4,5},{5,4},{6,7},{7,6},{8,9},{9,8},{10,11... | collective-permute-start | bytes 294920 | tf_op jit(solution)/shard_map/ppermute | solution.py:39
  52.2 5.7 %collective-permute-start.24 = (bf16[32,1024]{1,0:T(8,128)(2,1)S(1)}, bf16[32,1024]{1,0:T(8,128)(2,1)S(1)}, u32[]{:S(2)}, u32[]{:S(2)}) collective-permute-start(bf16[32,1024]{1,0:T(8,128)(2,1)S(1)} %constant_dynamic-slice_fusion), channel_id=1, source_target_pairs={{0,1},{1,0},{2,3},{3,2},{4,5},{5,4},{6,7},{7,6},{8,9},{9,8},{10,11... | collective-permute-start | bytes 196616 | tf_op jit(solution)/shard_map/ppermute | solution.py:39
  55.3 7.4 %collective-permute-start.20 = (bf16[32,1536]{1,0:T(8,128)(2,1)S(1)}, bf16[32,1536]{1,0:T(8,128)(2,1)S(1)}, u32[]{:S(2)}, u32[]{:S(2)}) collective-permute-start(bf16[32,1536]{1,0:T(8,128)(2,1)S(1)} %add_convert_fusion.7), channel_id=1, source_target_pairs={{0,2},{1,3},{2,0},{3,1},{4,6},{5,7},{6,4},{7,5},{8,10},{9,11},{10,... | collective-permute-start | bytes 294920 | tf_op jit(solution)/shard_map/ppermute | solution.py:39
  57.9 5.9 %collective-permute-start.25 = (bf16[32,1024]{1,0:T(8,128)(2,1)S(1)}, bf16[32,1024]{1,0:T(8,128)(2,1)S(1)}, u32[]{:S(2)}, u32[]{:S(2)}) collective-permute-start(bf16[32,1024]{1,0:T(8,128)(2,1)S(1)} %add_convert_fusion.9), channel_id=1, source_target_pairs={{0,2},{1,3},{2,0},{3,1},{4,6},{5,7},{6,4},{7,5},{8,10},{9,11},{10,... | collective-permute-start | bytes 196616 | tf_op jit(solution)/shard_map/ppermute | solution.py:39
  62.8 5.4 %collective-permute-start.21 = (bf16[32,1536]{1,0:T(8,128)(2,1)S(1)}, bf16[32,1536]{1,0:T(8,128)(2,1)S(1)}, u32[]{:S(2)}, u32[]{:S(2)}) collective-permute-start(bf16[32,1536]{1,0:T(8,128)(2,1)S(1)} %add_convert_fusion.6.early_own), channel_id=1, source_target_pairs={{0,1},{1,0},{2,3},{3,2},{4,5},{5,4},{6,7},{7,6},{8,9},{9,8},{10,11... | collective-permute-start | bytes 294920 | tf_op jit(solution)/shard_map/ppermute | solution.py:39
  63.9 4.3 %collective-permute-start.26 = (bf16[32,1024]{1,0:T(8,128)(2,1)S(1)}, bf16[32,1024]{1,0:T(8,128)(2,1)S(1)}, u32[]{:S(2)}, u32[]{:S(2)}) collective-permute-start(bf16[32,1024]{1,0:T(8,128)(2,1)S(1)} %add_convert_fusion.8.late_own), channel_id=1, source_target_pairs={{0,1},{1,0},{2,3},{3,2},{4,5},{5,4},{6,7},{7,6},{8,9},{9,8},{10,11... | collective-permute-start | bytes 196616 | tf_op jit(solution)/shard_map/ppermute | solution.py:39

commit v5 on v4

--- a/solution.py
+++ b/solution.py
@@ -194,25 +194,28 @@
             at += rhs.shape[1]
 
 
-def forward_kernel(groups, masks, n_rows, places, matrix_ref, scale_ref, *refs):
-    row_refs, refs = refs[:n_rows], refs[n_rows:]
+def norm_kernel(matrix_ref, *refs):
+    row_refs, (x_ref, cot_ref, z_ref, inv_ref, xt_ref) = refs[:-5], refs[-5:]
+    matrix = matrix_ref[...]
+    x = dot(matrix, stacked(row_refs, 0))
+    x_ref[...] = x
+    cot_ref[...] = dot(matrix, stacked(row_refs, 1)).astype(BF16)
+    z, inv_scale = normalize(x)
+    z_ref[...] = z
+    inv_ref[...] = inv_scale
+    xt_ref[...] = z.astype(BF16).T
+
+
+def forward_kernel(groups, masks, places, scale_ref, x_ref, cot_ref, z_ref, xt_ref, *refs):
     weight_refs, refs = refs[: len(places)], refs[len(places) :]
-    (keep_ref, give_ref, out_ref, w_ref, xt_ref, z_ref, inv_ref, cot_ref, act_ref, slope_ref) = refs[:10]
-    bend_ref, gmix_ref, gproj_ref, weights_ref, gt_ref, mix_ref = refs[10:]
+    (keep_ref, give_ref, out_ref, w_ref, act_ref, slope_ref) = refs[:6]
+    bend_ref, gmix_ref, gproj_ref, weights_ref, gt_ref, mix_ref, ggate_ref = refs[6:]
     width = mix_ref.shape[1]
     shard = width // groups
     group_me = lax.axis_index("group")
 
-    matrix = matrix_ref[...]
-    x = dot(matrix, stacked(row_refs, 0))
-    cot = dot(matrix, stacked(row_refs, 1)).astype(BF16)
-    cot_ref[...] = cot
-    z, inv_scale = normalize(x)
-    z_ref[...] = z
-    inv_ref[...] = inv_scale
-    xn = z.astype(BF16)
-    xt_ref[...] = xn.T
-
+    xn = z_ref[...].astype(BF16)
+    cot = cot_ref[...]
     for (k, at), ref in zip(places, weight_refs):
         w_ref[pl.ds(pl.multiple_of((group_me ^ k) * shard, shard), shard), at : at + ref.shape[1]] = ref[...]
 
@@ -223,6 +226,9 @@
         act = projected * s
         act_ref[:, cols] = act.astype(BF16)
         slope_ref[:, cols] = s + act * (1.0 - s)
+
+    w_out = w_ref[:, 4 * width :]
+    ggate_ref[...] = dot(cot, w_out, NT).astype(BF16)
 
     scale = scale_ref[...]
     head_width, per, wide = blocks_of(width)
@@ -243,10 +249,9 @@
     gate = act_ref[:, :width].astype(F32)
     gated = (normed * gate).astype(BF16)
     gt_ref[...] = gated.T
-    w_out = w_ref[:, 4 * width :]
-    out_ref[...] = (dot(gated, w_out) + x).astype(BF16)
-
-    g_gated = dot(cot, w_out, NT).astype(BF16).astype(F32)
+    out_ref[...] = (dot(gated, w_out) + x_ref[...]).astype(BF16)
+
+    g_gated = ggate_ref[...].astype(F32)
     g_u = ((g_gated * normed).astype(BF16).astype(F32) * slope_ref[:, :width]).astype(BF16)
     gproj_ref[:, :width] = g_u
     g_normed = g_gated * gate
@@ -270,11 +275,10 @@
     weight_gradient(keep_ref, give_ref, groups, masks, ((gt_ref, cot), (xt_ref, early)))
 
 
-def backward_kernel(groups, masks, n_rows, matrix_ref, *refs):
-    (out_ref, w_ref, xt_ref, z_ref, inv_ref, cot_ref, act_ref, slope_ref) = refs[:8]
-    bend_ref, gmix_ref, early_ref, keep_ref, give_ref = refs[8:13]
-    back_refs, gproj_ref = refs[13:-1], refs[-1]
-    rows, width = out_ref.shape
+def backward_kernel(
+    groups, masks, xt_ref, act_ref, slope_ref, bend_ref, gmix_ref, early_ref, keep_ref, give_ref, gproj_ref
+):
+    width = gmix_ref.shape[1]
     head_width, per, wide = blocks_of(width)
 
     gproj_ref[:, : 2 * width] = early_ref[...]
@@ -294,6 +298,9 @@
     late = gproj_ref[:, 4 * width - keep_ref.shape[1] :]
     weight_gradient(keep_ref, give_ref, groups, masks, ((xt_ref, late),))
 
+
+def rows_kernel(matrix_ref, gproj_ref, w_ref, out_ref, z_ref, inv_ref, cot_ref, *back_refs):
+    rows, width = out_ref.shape
     z = z_ref[...]
     g_xn = dot(gproj_ref[...], w_ref[:, : 4 * width], NT)
     g_x = (
@@ -305,7 +312,7 @@
         )
         + cot_ref[...].astype(F32)
     ).astype(BF16)
-    step = rows // n_rows
+    step = rows // len(back_refs)
     matrix = matrix_ref[...]
     for which, value in ((0, out_ref[...]), (1, g_x)):
         back = dot(matrix, value, TN).astype(BF16)
@@ -390,41 +397,53 @@
 
     half = groups // 2 * shard
     early_width = 3 * width
-    keep, give, *saved, _ = pl.pallas_call(
-        partial(forward_kernel, groups, chips, n_rows, places),
+    x, cot, z, inv_scale, xt = pl.pallas_call(
+        norm_kernel,
+        out_shape=[
+            spec((rows, width), F32),
+            spec((rows, width)),
+            spec((rows, width), F32),
+            spec((rows, 1), F32),
+            spec((width, rows)),
+        ],
+        in_specs=[VMEM] * (1 + n_rows),
+        out_specs=[VMEM] * 5,
+        compiler_params=limit,
+        name="norm",
+    )(matrix, *arrived)
+    keep, give, out, full, act, slope, bend, g_mixed, g_early = pl.pallas_call(
+        partial(forward_kernel, groups, chips, places),
         out_shape=[
             spec((half, early_width)),
             spec((half, early_width)),
             spec((rows, width)),
             spec((width, columns)),
-            spec((width, rows)),
-            spec((rows, width), F32),
-            spec((rows, 1), F32),
-            spec((rows, width)),
             spec((rows, 4 * width)),
             spec((rows, 4 * width), F32),
             spec((HEADS, rows, rows), F32),
             spec((rows, width)),
             spec((rows, 2 * width)),
-            spec((HEADS, rows, rows)),
         ],
-        in_specs=[VMEM] * (2 + n_rows + len(shards)),
-        out_specs=[VMEM] * 14,
-        scratch_shapes=[pltpu.VMEM((width, rows), BF16), pltpu.VMEM((rows, width), F32)],
+        in_specs=[VMEM] * (5 + len(shards)),
+        out_specs=[VMEM] * 9,
+        scratch_shapes=[
+            pltpu.VMEM((HEADS, rows, rows), BF16),
+            pltpu.VMEM((width, rows), BF16),
+            pltpu.VMEM((rows, width), F32),
+            pltpu.VMEM((rows, width), BF16),
+        ],
         compiler_params=limit,
         name="forward",
-    )(matrix, scale, *arrived, *shards)
+    )(scale, x, cot, z, xt, *shards)
     taken = exchange(give, "group", groups, 1)
-    keep_late, give_late, *returning = pl.pallas_call(
-        partial(backward_kernel, groups, chips[::-1], n_rows),
-        out_shape=[spec((half, columns - early_width))] * 2 + [rows_shape] * n_rows,
-        in_specs=[VMEM] * (1 + len(saved)),
-        out_specs=[VMEM] * (2 + n_rows),
-        scratch_shapes=[pltpu.VMEM((rows, 4 * width), BF16)],
+    keep_late, give_late, g_proj = pl.pallas_call(
+        partial(backward_kernel, groups, chips[::-1]),
+        out_shape=[spec((half, columns - early_width))] * 2 + [spec((rows, 4 * width))],
+        in_specs=[VMEM] * 6,
+        out_specs=[VMEM] * 3,
         compiler_params=limit,
         name="backward",
-    )(matrix, *saved)
-
+    )(xt, act, slope, bend, g_mixed, g_early)
     far = [2**j for j in range(parts.bit_length() - 1)]
 
     def add(mine, other):
@@ -455,9 +474,18 @@
 
     taken, give_late = lax.optimization_barrier((taken, give_late))
     taken_late = exchange(give_late, "group", groups, 1)
+    early, g_proj = both_cores(keep, taken, g_proj)
+    returning = pl.pallas_call(
+        rows_kernel,
+        out_shape=[rows_shape] * n_rows,
+        in_specs=[VMEM] * 7,
+        out_specs=[VMEM] * n_rows,
+        compiler_params=limit,
+        name="rows",
+    )(matrix, g_proj, full, out, z, inv_scale, cot)
     late, returning = both_cores(keep_late, taken_late, returning)
     returned = swap_rows(returning[0], returning[1:])
-    early, returned[1:2] = over_chips(add(keep, taken).astype(BF16), chips, returned[1:2])
+    early, returned[1:2] = over_chips(early, chips, returned[1:2])
     early, returned = lax.optimization_barrier((early, returned))
     owner = pl.pallas_call(
         partial(post_kernel, parts),

time: 69.3 us -> 67.9 us (0.980)
  starting transfers between devices: 30.9 us -> 27.4 us
  waiting for transfers between devices: 21.6 us -> 23.4 us
    ppermute x27, starting transfers between devices: 30.9 us -> 27.4 us  [exchange(): return lax.ppermute(value, axis, [(i, i ^ mask) for i in range(size)])]
    ppermute x27, waiting for transfers between devices: 21.6 us -> 23.4 us  [exchange(): return lax.ppermute(value, axis, [(i, i ^ mask) for i in range(size)])]
    pallas_call x2 -> x4, Pallas kernels: 7.31 us -> 7.5 us  [the longest x1 3.93 us: on_device(): pl.pallas_call(partial(forward_kernel, groups, chips, places), out_shape=...]
  transfers between devices with their start and end apart: 27 -> 27, of which waited for: 13 -> 13; matrix products, arithmetic and copies ran while one was open for 1% -> 1% of each run, Pallas kernels for 7% -> 8%
where the time goes in v5:
time: 67.9 us; the launch traced here: 67.7 us
  starting transfers between devices  27.4 us (40%)
  waiting for transfers between devices  23.4 us (34%)
  Pallas kernels  12.6 us (19%)
  local copies, waits for them, and re-layouts  2.68 us (4%)
  between operations  0.85 us (1%)
  other arithmetic  0.72 us (1%)
    ppermute x27, starting transfers between devices, exchange(): return lax.ppermute(value, axis, [(i, i ^ mask) for i in range(size)])  27.4 us
    ppermute x27, waiting for transfers between devices, exchange(): return lax.ppermute(value, axis, [(i, i ^ mask) for i in range(size)])  23.4 us
    pallas_call x1, Pallas kernels, on_device(): pl.pallas_call(partial(forward_kernel, groups, chips, places), out_shape=...  3.93 us
    unnamed x8, local copies, waits for them, and re-layouts  2.56 us
    pallas_call x1, Pallas kernels, on_device(): pl.pallas_call(partial(pre_kernel, parts), out_shape=[spec((shard, column...  2.29 us
    pallas_call x1, Pallas kernels, on_device(): pl.pallas_call(partial(backward_kernel, groups, chips[::-1]), out_shape=[...  2.01 us
  transfers between devices with their start and end apart: 27, of which 13 were waited for; matrix products, arithmetic and copies ran while one was open for 1% of the time, Pallas kernels for 8%

profile of v5, /device:TPU:0, one launch (start us, length us, event | category | flops | bytes accessed | tf_op | source)
XLA Modules:
  0.0 67.7 jit_solution(13758976184137373922)
XLA Ops:
  0.6 2.3 %pre.1 = (bf16[64,2560]{1,0:T(8,128)(2,1)}, s32[8,128]{1,0:T(8,128)}, bf16[2,64,512]{2,1,0:T(8,128)(2,1)}, bf16[2,64,512]{2,1,0:T(8,128)(2,1)}, bf16[2,64,512]{2...) custom-call(s32[1,32]{1,0:T(1,128)} %bitcast.8, s32[1,32]{1,0:T(1,128)} %bitcast.12, s32[1,8]{1,0:T(1,128)} %bitcast.13, ...), custom_call_target="tpu_custom_call" | custom-call | tf_op jit(solution)/shard_map/pre/pallas_call | solution.py:345
  2.9 3.0 %collective-permute-start = (bf16[64,2560]{1,0:T(8,128)(2,1)}, bf16[64,2560]{1,0:T(8,128)(2,1)S(1)}, u32[]{:S(2)}, u32[]{:S(2)}) collective-permute-start(bf16[64,2560]{1,0:T(8,128)(2,1)} %get-tuple-element.66.w_ref), channel_id=1, source_target_pairs={{0,8},{4,12},{8,0},{12,4},{16,24},{20,28},{24,16},{28,20},{1,9},{5... | collective-permute-start | bytes 983048 | tf_op jit(solution)/shard_map/ppermute | solution.py:39
  5.9 1.5 %collective-permute-start.1 = (bf16[64,2560]{1,0:T(8,128)(2,1)}, bf16[64,2560]{1,0:T(8,128)(2,1)S(1)}, u32[]{:S(2)}, u32[]{:S(2)}) collective-permute-start(bf16[64,2560]{1,0:T(8,128)(2,1)} %get-tuple-element.66.w_ref), channel_id=1, source_target_pairs={{0,16},{4,20},{8,24},{12,28},{16,0},{20,4},{24,8},{28,12},{1,17},{... | collective-permute-start | bytes 983048 | tf_op jit(solution)/shard_map/ppermute | solution.py:39
  7.5 1.6 %collective-permute-start.2 = (bf16[2,64,512]{2,1,0:T(8,128)(2,1)}, bf16[2,64,512]{2,1,0:T(8,128)(2,1)S(1)}, u32[]{:S(2)}, u32[]{:S(2)}) collective-permute-start(bf16[2,64,512]{2,1,0:T(8,128)(2,1)} %get-tuple-element.69), channel_id=1, source_target_pairs={{0,1},{1,0},{2,3},{3,2},{4,5},{5,4},{6,7},{7,6},{8,9},{9,8},{10,11... | collective-permute-start | bytes 393224 | tf_op jit(solution)/shard_map/ppermute | solution.py:39
  9.0 2.6 %collective-permute-start.5 = (bf16[2,64,512]{2,1,0:T(8,128)(2,1)}, bf16[2,64,512]{2,1,0:T(8,128)(2,1)S(1)}, u32[]{:S(2)}, u32[]{:S(2)}) collective-permute-start(bf16[2,64,512]{2,1,0:T(8,128)(2,1)} %get-tuple-element.76), channel_id=1, source_target_pairs={{0,2},{1,3},{2,0},{3,1},{4,6},{5,7},{6,4},{7,5},{8,10},{9,11},{10,... | collective-permute-start | bytes 393224 | tf_op jit(solution)/shard_map/ppermute | solution.py:39
  11.6 0.2 collective-permute-start.6
  11.8 1.0 %copy-done = bf16[64,2560]{1,0:T(8,128)(2,1)S(1)} copy-done((bf16[64,2560]{1,0:T(8,128)(2,1)S(1)}, bf16[64,2560]{1,0:T(8,128)(2,1)}, u32[]{:S(2)}) %copy-start) | copy-done | bytes 327704
  12.8 0.9 %copy-done.1 = bf16[2,64,512]{2,1,0:T(8,128)(2,1)S(1)} copy-done((bf16[2,64,512]{2,1,0:T(8,128)(2,1)S(1)}, bf16[2,64,512]{2,1,0:T(8,128)(2,1)}, u32[]{:S(2)}) %copy-start.1) | copy-done | bytes 131096
  13.7 0.7 copy-done.2
  14.4 0.7 %plan.1 = (bf16[256,256]{1,0:T(8,128)(2,1)S(1)}, f32[256,256]{1,0:T(8,128)S(1)}, bf16[64,2560]{1,0:T(8,128)(2,1)S(1)}, bf16[2,64,512]{2,1,0:T(8,128)(2,1)S(1)}) custom-call(s32[8,128]{1,0:T(8,128)S(1)} %copy-done.2, bf16[64,2560]{1,0:T(8,128)(2,1)S(1)} %copy-done, bf16[2,64,512]{2,1,0:T(8,128)(2,1)S(1)} %copy-done.1), custom_call_target="tpu_custom_call" | custom-call | tf_op jit(solution)/shard_map/plan/pallas_call | solution.py:367
  15.2 0.2 collective-permute-done.1.refs_4_
  15.3 0.5 collective-permute-start.3
  15.8 1.7 %collective-permute-start.4 = (bf16[64,1280]{1,0:T(8,128)(2,1)S(1)}, bf16[64,1280]{1,0:T(8,128)(2,1)S(1)}, u32[]{:S(2)}, u32[]{:S(2)}) collective-permute-start(bf16[64,1280]{1,0:T(8,128)(2,1)S(1)} %slice.41), channel_id=1, source_target_pairs={{0,16},{4,20},{8,24},{12,28},{16,0},{20,4},{24,8},{28,12},{1,17},{... | collective-permute-start | bytes 491528 | tf_op jit(solution)/shard_map/ppermute | solution.py:39
  17.5 4.1 %collective-permute-done.5.refs_2_ = bf16[2,64,512]{2,1,0:T(8,128)(2,1)S(1)} collective-permute-done((bf16[2,64,512]{2,1,0:T(8,128)(2,1)}, bf16[2,64,512]{2,1,0:T(8,128)(2,1)S(1)}, u32[]{:S(2)}, u32[]{:S(2)}) %collective-permute-start.5) | collective-permute-done | bytes 131104 | tf_op jit(solution)/shard_map/ppermute | solution.py:39
  21.6 0.5 collective-permute-start.9
  22.2 0.4 collective-permute-start.11
  22.6 0.5 norm.1
  23.2 0.5 collective-permute-done.9.refs_5_
  23.7 0.2 collective-permute-done.10.refs_8_
  23.9 0.2 collective-permute-done.11.refs_9_
  24.2 3.9 %forward.1 = (bf16[256,1536]{1,0:T(8,128)(2,1)S(1)}, bf16[256,1536]{1,0:T(8,128)(2,1)S(1)}, bf16[256,512]{1,0:T(8,128)(2,1)S(1)}, bf16[512,2560]{1,0:T(8,128)(2,...) custom-call(f32[256,256]{1,0:T(8,128)S(1)} %get-tuple-element.72.sca, ...), custom_call_target="tpu_custom_call" | custom-call | tf_op jit(solution)/shard_map/forward/pallas_call | solution.py:414
  28.1 0.2 collective-permute-start.12
  28.3 2.0 %backward.1 = (bf16[256,1024]{1,0:T(8,128)(2,1)S(1)}, bf16[256,1024]{1,0:T(8,128)(2,1)S(1)}, bf16[256,2048]{1,0:T(8,128)(2,1)S(1)}) custom-call(bf16[512,256]{1,0:T(8,128)(2,1)S(1)} %get-tuple-element.83.xt_ref, bf16[256,2048]{1,0:T(8,128)(2,1)S(1)} %get-tuple-element.91.act_ref, f32[256,2048]{1,0:T(8,128)S(1)} %get-tuple-element.92.slope_ref, ...), custom_call_target="tpu_custom_call" | custom-call | tf_op jit(solution)/shard_map/backward/pallas_call | solution.py:439
  30.3 0.2 collective-permute-done.12
  30.5 0.3 collective-permute-start.14
  30.8 0.2 add_convert_fusion
  31.0 0.6 collective-permute-start.13
  31.6 1.1 %rows.1 = (bf16[2,64,512]{2,1,0:T(8,128)(2,1)S(1)}, bf16[2,64,512]{2,1,0:T(8,128)(2,1)S(1)}, bf16[2,64,512]{2,1,0:T(8,128)(2,1)S(1)}, bf16[2,64,512]{2,1,0:T(8,128)(2,1)S(1)}) custom-call(bf16[256,256]{1,0:T(8,128)(2,1)S(1)} %get-tuple-element.73.matrix_ref, bf16[256,2048]{1,0:T(8,128)(2,1)S(1)} %get-tuple-element.102.gproj_ref, ...), custom_call_target="tpu_custom_call" | custom-call | tf_op jit(solution)/shard_map/rows/pallas_call | solution.py:478
  32.7 0.2 add_convert_fusion.1
  32.9 1.6 %collective-permute-start.15 = (bf16[2,64,512]{2,1,0:T(8,128)(2,1)S(1)}, bf16[2,64,512]{2,1,0:T(8,128)(2,1)S(1)}, u32[]{:S(2)}, u32[]{:S(2)}) collective-permute-start(bf16[2,64,512]{2,1,0:T(8,128)(2,1)S(1)} %get-tuple-element.110), channel_id=1, source_target_pairs={{0,1},{1,0},{2,3},{3,2},{4,5},{5,4},{6,7},{7,6},{8,9},{9,8},{10,11... | collective-permute-start | bytes 393224 | tf_op jit(solution)/shard_map/ppermute | solution.py:39
  34.5 1.4 %collective-permute-start.22 = (bf16[128,1024]{1,0:T(8,128)(2,1)S(1)}, bf16[128,1024]{1,0:T(8,128)(2,1)S(1)}, u32[]{:S(2)}, u32[]{:S(2)}) collective-permute-start(bf16[128,1024]{1,0:T(8,128)(2,1)S(1)} %slice.37), channel_id=1, source_target_pairs={{0,16},{4,20},{8,24},{12,28},{16,0},{20,4},{24,8},{28,12},{1,17},{... | collective-permute-start | bytes 786440 | tf_op jit(solution)/shard_map/ppermute | solution.py:39
  35.9 2.6 %collective-permute-start.17 = (bf16[2,64,512]{2,1,0:T(8,128)(2,1)S(1)}, bf16[2,64,512]{2,1,0:T(8,128)(2,1)S(1)}, u32[]{:S(2)}, u32[]{:S(2)}) collective-permute-start(bf16[2,64,512]{2,1,0:T(8,128)(2,1)S(1)} %get-tuple-element.114), channel_id=1, source_target_pairs={{0,2},{1,3},{2,0},{3,1},{4,6},{5,7},{6,4},{7,5},{8,10},{9,11},{10,... | collective-permute-start | bytes 393224 | tf_op jit(solution)/shard_map/ppermute | solution.py:39
  38.5 0.2 collective-permute-start.18
  38.7 3.6 %collective-permute-done.13 = bf16[128,1536]{1,0:T(8,128)(2,1)S(1)} collective-permute-done((bf16[128,1536]{1,0:T(8,128)(2,1)S(1)}, bf16[128,1536]{1,0:T(8,128)(2,1)S(1)}, u32[]{:S(2)}, u32[]{:S(2)}) %collective-permute-start.13) | collective-permute-done | bytes 393248 | tf_op jit(solution)/shard_map/ppermute | solution.py:39
  42.4 0.6 collective-permute-start.16
  43.1 1.4 %collective-permute-start.23 = (bf16[64,1024]{1,0:T(8,128)(2,1)S(1)}, bf16[64,1024]{1,0:T(8,128)(2,1)S(1)}, u32[]{:S(2)}, u32[]{:S(2)}) collective-permute-start(bf16[64,1024]{1,0:T(8,128)(2,1)S(1)} %slice.45), channel_id=1, source_target_pairs={{0,8},{4,12},{8,0},{12,4},{16,24},{20,28},{24,16},{28,20},{1,9},{5... | collective-permute-start | bytes 393224 | tf_op jit(solution)/shard_map/ppermute | solution.py:39
  44.5 4.1 %collective-permute-done.16 = bf16[64,1536]{1,0:T(8,128)(2,1)S(1)} collective-permute-done((bf16[64,1536]{1,0:T(8,128)(2,1)S(1)}, bf16[64,1536]{1,0:T(8,128)(2,1)S(1)}, u32[]{:S(2)}, u32[]{:S(2)}) %collective-permute-start.16) | collective-permute-done | bytes 196640 | tf_op jit(solution)/shard_map/ppermute | solution.py:39
  48.8 1.9 %collective-permute-start.19 = (bf16[32,1536]{1,0:T(8,128)(2,1)S(1)}, bf16[32,1536]{1,0:T(8,128)(2,1)S(1)}, u32[]{:S(2)}, u32[]{:S(2)}) collective-permute-start(bf16[32,1536]{1,0:T(8,128)(2,1)S(1)} %constant_dynamic-slice_fusion.1), channel_id=1, source_target_pairs={{0,1},{1,0},{2,3},{3,2},{4,5},{5,4},{6,7},{7,6},{8,9},{9,8},{10,11... | collective-permute-start | bytes 294920 | tf_op jit(solution)/shard_map/ppermute | solution.py:39
  50.7 0.2 collective-permute-start.24
  51.0 2.9 %collective-permute-done.19 = bf16[32,1536]{1,0:T(8,128)(2,1)S(1)} collective-permute-done((bf16[32,1536]{1,0:T(8,128)(2,1)S(1)}, bf16[32,1536]{1,0:T(8,128)(2,1)S(1)}, u32[]{:S(2)}, u32[]{:S(2)}) %collective-permute-start.19) | collective-permute-done | bytes 98336 | tf_op jit(solution)/shard_map/ppermute | solution.py:39
  53.9 2.5 %collective-permute-start.20 = (bf16[32,1536]{1,0:T(8,128)(2,1)S(1)}, bf16[32,1536]{1,0:T(8,128)(2,1)S(1)}, u32[]{:S(2)}, u32[]{:S(2)}) collective-permute-start(bf16[32,1536]{1,0:T(8,128)(2,1)S(1)} %add_convert_fusion.7), channel_id=1, source_target_pairs={{0,2},{1,3},{2,0},{3,1},{4,6},{5,7},{6,4},{7,5},{8,10},{9,11},{10,... | collective-permute-start | bytes 294920 | tf_op jit(solution)/shard_map/ppermute | solution.py:39
  56.5 0.9 %collective-permute-start.25 = (bf16[32,1024]{1,0:T(8,128)(2,1)S(1)}, bf16[32,1024]{1,0:T(8,128)(2,1)S(1)}, u32[]{:S(2)}, u32[]{:S(2)}) collective-permute-start(bf16[32,1024]{1,0:T(8,128)(2,1)S(1)} %add_convert_fusion.9), channel_id=1, source_target_pairs={{0,2},{1,3},{2,0},{3,1},{4,6},{5,7},{6,4},{7,5},{8,10},{9,11},{10,... | collective-permute-start | bytes 196616 | tf_op jit(solution)/shard_map/ppermute | solution.py:39
  57.3 3.7 %collective-permute-done.20 = bf16[32,1536]{1,0:T(8,128)(2,1)S(1)} collective-permute-done((bf16[32,1536]{1,0:T(8,128)(2,1)S(1)}, bf16[32,1536]{1,0:T(8,128)(2,1)S(1)}, u32[]{:S(2)}, u32[]{:S(2)}) %collective-permute-start.20) | collective-permute-done | bytes 98336 | tf_op jit(solution)/shard_map/ppermute | solution.py:39
  61.2 1.3 %collective-permute-done.25 = bf16[32,1024]{1,0:T(8,128)(2,1)S(1)} collective-permute-done((bf16[32,1024]{1,0:T(8,128)(2,1)S(1)}, bf16[32,1024]{1,0:T(8,128)(2,1)S(1)}, u32[]{:S(2)}, u32[]{:S(2)}) %collective-permute-start.25) | collective-permute-done | bytes 65568 | tf_op jit(solution)/shard_map/ppermute | solution.py:39
  62.5 0.8 %collective-permute-start.26 = (bf16[32,1024]{1,0:T(8,128)(2,1)S(1)}, bf16[32,1024]{1,0:T(8,128)(2,1)S(1)}, u32[]{:S(2)}, u32[]{:S(2)}) collective-permute-start(bf16[32,1024]{1,0:T(8,128)(2,1)S(1)} %add_convert_fusion.8.late_own), channel_id=1, source_target_pairs={{0,1},{1,0},{2,3},{3,2},{4,5},{5,4},{6,7},{7,6},{8,9},{9,8},{10,11... | collective-permute-start | bytes 196616 | tf_op jit(solution)/shard_map/ppermute | solution.py:39
  63.3 1.2 %post.1 = (bf16[256,512]{1,0:T(8,128)(2,1)}, bf16[256,512]{1,0:T(8,128)(2,1)}) custom-call(s32[1,32]{1,0:T(1,128)S(1)} %bitcast.9, bf16[2,64,512]{2,1,0:T(8,128)(2,1)S(1)} %get-tuple-element.116.refs_0_, bf16[2,64,512]{2,1,0:T(8,128)(2,1)S(1)} %collective-permute-done.15.refs_1_, bf16[2,64,512]{2,1,0:T(8,128)(2,1)S(1)} %collective-permute-done.17.refs_2_, ...), custom_call_target="tpu_custom_call" | custom-call | tf_op jit(solution)/shard_map/post/pallas_call | solution.py:490
  64.5 2.3 %collective-permute-done.26.late_other = bf16[32,1024]{1,0:T(8,128)(2,1)S(1)} collective-permute-done((bf16[32,1024]{1,0:T(8,128)(2,1)S(1)}, bf16[32,1024]{1,0:T(8,128)(2,1)S(1)}, u32[]{:S(2)}, u32[]{:S(2)}) %collective-permute-start.26) | collective-permute-done | bytes 65568 | tf_op jit(solution)/shard_map/ppermute | solution.py:39
  66.8 0.9 %finish.1 = (f32[64,2048]{1,0:T(8,128)}, f32[64,512]{1,0:T(8,128)}) custom-call(bf16[32,1536]{1,0:T(8,128)(2,1)S(1)} %add_convert_fusion.6.early_own, bf16[32,1536]{1,0:T(8,128)(2,1)S(1)} %collective-permute-done.21.early_other, bf16[32,1024]{1,0:T(8,128)(2,1)S(1)} %add_convert_fusion.8.late_own, bf16[32,1024]{1,0:T(8,128)(2,1)S(1)} %collective-permute-done.26.late_other), custom_call_target="tpu_custom_call" | custom-call | tf_op jit(solution)/shard_map/finish/pallas_call | solution.py:502
  (40 shorter events, 0.8 us)
Async XLA Ops:
  2.9 12.2 %collective-permute-start = (bf16[64,2560]{1,0:T(8,128)(2,1)}, bf16[64,2560]{1,0:T(8,128)(2,1)S(1)}, u32[]{:S(2)}, u32[]{:S(2)}) collective-permute-start(bf16[64,2560]{1,0:T(8,128)(2,1)} %get-tuple-element.66.w_ref), channel_id=1, source_target_pairs={{0,8},{4,12},{8,0},{12,4},{16,24},{20,28},{24,16},{28,20},{1,9},{5... | collective-permute-start | bytes 983048 | tf_op jit(solution)/shard_map/ppermute | solution.py:39
  5.9 9.4 %collective-permute-start.1 = (bf16[64,2560]{1,0:T(8,128)(2,1)}, bf16[64,2560]{1,0:T(8,128)(2,1)S(1)}, u32[]{:S(2)}, u32[]{:S(2)}) collective-permute-start(bf16[64,2560]{1,0:T(8,128)(2,1)} %get-tuple-element.66.w_ref), channel_id=1, source_target_pairs={{0,16},{4,20},{8,24},{12,28},{16,0},{20,4},{24,8},{28,12},{1,17},{... | collective-permute-start | bytes 983048 | tf_op jit(solution)/shard_map/ppermute | solution.py:39
  7.5 7.7 %collective-permute-start.2 = (bf16[2,64,512]{2,1,0:T(8,128)(2,1)}, bf16[2,64,512]{2,1,0:T(8,128)(2,1)S(1)}, u32[]{:S(2)}, u32[]{:S(2)}) collective-permute-start(bf16[2,64,512]{2,1,0:T(8,128)(2,1)} %get-tuple-element.69), channel_id=1, source_target_pairs={{0,1},{1,0},{2,3},{3,2},{4,5},{5,4},{6,7},{7,6},{8,9},{9,8},{10,11... | collective-permute-start | bytes 393224 | tf_op jit(solution)/shard_map/ppermute | solution.py:39
  9.0 12.6 %collective-permute-start.5 = (bf16[2,64,512]{2,1,0:T(8,128)(2,1)}, bf16[2,64,512]{2,1,0:T(8,128)(2,1)S(1)}, u32[]{:S(2)}, u32[]{:S(2)}) collective-permute-start(bf16[2,64,512]{2,1,0:T(8,128)(2,1)} %get-tuple-element.76), channel_id=1, source_target_pairs={{0,2},{1,3},{2,0},{3,1},{4,6},{5,7},{6,4},{7,5},{8,10},{9,11},{10,... | collective-permute-start | bytes 393224 | tf_op jit(solution)/shard_map/ppermute | solution.py:39
  11.6 10.0 %collective-permute-start.6 = (bf16[2,64,512]{2,1,0:T(8,128)(2,1)}, bf16[2,64,512]{2,1,0:T(8,128)(2,1)S(1)}, u32[]{:S(2)}, u32[]{:S(2)}) collective-permute-start(bf16[2,64,512]{2,1,0:T(8,128)(2,1)} %get-tuple-element.77), channel_id=1, source_target_pairs={{0,3},{1,2},{2,1},{3,0},{4,7},{5,6},{6,5},{7,4},{8,11},{9,10},{10,... | collective-permute-start | bytes 393224 | tf_op jit(solution)/shard_map/ppermute | solution.py:39
  11.8 1.0 %copy-start = (bf16[64,2560]{1,0:T(8,128)(2,1)S(1)}, bf16[64,2560]{1,0:T(8,128)(2,1)}, u32[]{:S(2)}) copy-start(bf16[64,2560]{1,0:T(8,128)(2,1)} %get-tuple-element.66.w_ref) | copy-start | bytes 983044
  12.8 0.9 %copy-start.1 = (bf16[2,64,512]{2,1,0:T(8,128)(2,1)S(1)}, bf16[2,64,512]{2,1,0:T(8,128)(2,1)}, u32[]{:S(2)}) copy-start(bf16[2,64,512]{2,1,0:T(8,128)(2,1)} %get-tuple-element.67.own_ref) | copy-start | bytes 393220
  13.7 0.7 copy-start.2
  15.3 6.8 %collective-permute-start.3 = (bf16[64,1280]{1,0:T(8,128)(2,1)S(1)}, bf16[64,1280]{1,0:T(8,128)(2,1)S(1)}, u32[]{:S(2)}, u32[]{:S(2)}) collective-permute-start(bf16[64,1280]{1,0:T(8,128)(2,1)S(1)} %slice.40), channel_id=1, source_target_pairs={{0,8},{4,12},{8,0},{12,4},{16,24},{20,28},{24,16},{28,20},{1,9},{5... | collective-permute-start | bytes 491528 | tf_op jit(solution)/shard_map/ppermute | solution.py:39
  15.8 6.3 %collective-permute-start.4 = (bf16[64,1280]{1,0:T(8,128)(2,1)S(1)}, bf16[64,1280]{1,0:T(8,128)(2,1)S(1)}, u32[]{:S(2)}, u32[]{:S(2)}) collective-permute-start(bf16[64,1280]{1,0:T(8,128)(2,1)S(1)} %slice.41), channel_id=1, source_target_pairs={{0,16},{4,20},{8,24},{12,28},{16,0},{20,4},{24,8},{28,12},{1,17},{... | collective-permute-start | bytes 491528 | tf_op jit(solution)/shard_map/ppermute | solution.py:39
  17.5 5.6 %collective-permute-start.7 = (bf16[64,2560]{1,0:T(8,128)(2,1)S(1)}, bf16[64,2560]{1,0:T(8,128)(2,1)S(1)}, u32[]{:S(2)}, u32[]{:S(2)}) collective-permute-start(bf16[64,2560]{1,0:T(8,128)(2,1)S(1)} %get-tuple-element.84.refs_0_), channel_id=1, source_target_pairs={{0,4},{4,0},{8,12},{12,8},{16,20},{20,16},{24,28},{28,24},{1,5},{5... | collective-permute-start | bytes 983048 | tf_op jit(solution)/shard_map/ppermute | solution.py:39
  21.6 1.6 %collective-permute-start.8 = (bf16[64,2560]{1,0:T(8,128)(2,1)S(1)}, bf16[64,2560]{1,0:T(8,128)(2,1)S(1)}, u32[]{:S(2)}, u32[]{:S(2)}) collective-permute-start(bf16[64,2560]{1,0:T(8,128)(2,1)S(1)} %collective-permute-done.refs_2_), channel_id=1, source_target_pairs={{0,4},{4,0},{8,12},{12,8},{16,20},{20,16},{24,28},{28,24},{1,5},{5... | collective-permute-start | bytes 983048 | tf_op jit(solution)/shard_map/ppermute | solution.py:39
  21.6 2.1 %collective-permute-start.9 = (bf16[64,2560]{1,0:T(8,128)(2,1)S(1)}, bf16[64,2560]{1,0:T(8,128)(2,1)S(1)}, u32[]{:S(2)}, u32[]{:S(2)}) collective-permute-start(bf16[64,2560]{1,0:T(8,128)(2,1)S(1)} %collective-permute-done.1.refs_4_), channel_id=1, source_target_pairs={{0,4},{4,0},{8,12},{12,8},{16,20},{20,16},{24,28},{28,24},{1,5},{5... | collective-permute-start | bytes 983048 | tf_op jit(solution)/shard_map/ppermute | solution.py:39
  22.1 1.8 %collective-permute-start.10 = (bf16[64,1280]{1,0:T(8,128)(2,1)S(1)}, bf16[64,1280]{1,0:T(8,128)(2,1)S(1)}, u32[]{:S(2)}, u32[]{:S(2)}) collective-permute-start(bf16[64,1280]{1,0:T(8,128)(2,1)S(1)} %collective-permute-done.3.refs_6_), channel_id=1, source_target_pairs={{0,4},{4,0},{8,12},{12,8},{16,20},{20,16},{24,28},{28,24},{1,5},{5... | collective-permute-start | bytes 491528 | tf_op jit(solution)/shard_map/ppermute | solution.py:39
  22.2 2.0 %collective-permute-start.11 = (bf16[64,1280]{1,0:T(8,128)(2,1)S(1)}, bf16[64,1280]{1,0:T(8,128)(2,1)S(1)}, u32[]{:S(2)}, u32[]{:S(2)}) collective-permute-start(bf16[64,1280]{1,0:T(8,128)(2,1)S(1)} %collective-permute-done.4.refs_7_), channel_id=1, source_target_pairs={{0,4},{4,0},{8,12},{12,8},{16,20},{20,16},{24,28},{28,24},{1,5},{5... | collective-permute-start | bytes 491528 | tf_op jit(solution)/shard_map/ppermute | solution.py:39
  28.1 2.4 %collective-permute-start.12 = (bf16[256,1536]{1,0:T(8,128)(2,1)S(1)}, bf16[256,1536]{1,0:T(8,128)(2,1)S(1)}, u32[]{:S(2)}, u32[]{:S(2)}) collective-permute-start(bf16[256,1536]{1,0:T(8,128)(2,1)S(1)} %get-tuple-element.90), channel_id=1, source_target_pairs={{0,4},{4,0},{8,12},{12,8},{16,20},{20,16},{24,28},{28,24},{1,5},{5... | collective-permute-start | bytes 2359304 | tf_op jit(solution)/shard_map/ppermute | solution.py:39
  30.5 2.2 %collective-permute-start.14 = (bf16[256,1024]{1,0:T(8,128)(2,1)S(1)}, bf16[256,1024]{1,0:T(8,128)(2,1)S(1)}, u32[]{:S(2)}, u32[]{:S(2)}) collective-permute-start(bf16[256,1024]{1,0:T(8,128)(2,1)S(1)} %get-tuple-element.101), channel_id=1, source_target_pairs={{0,4},{4,0},{8,12},{12,8},{16,20},{20,16},{24,28},{28,24},{1,5},{5... | collective-permute-start | bytes 1572872 | tf_op jit(solution)/shard_map/ppermute | solution.py:39
  31.0 11.3 %collective-permute-start.13 = (bf16[128,1536]{1,0:T(8,128)(2,1)S(1)}, bf16[128,1536]{1,0:T(8,128)(2,1)S(1)}, u32[]{:S(2)}, u32[]{:S(2)}) collective-permute-start(bf16[128,1536]{1,0:T(8,128)(2,1)S(1)} %slice.33), channel_id=1, source_target_pairs={{0,8},{4,12},{8,0},{12,4},{16,24},{20,28},{24,16},{28,20},{1,9},{5... | collective-permute-start | bytes 1179656 | tf_op jit(solution)/shard_map/ppermute | solution.py:39
  32.9 9.4 %collective-permute-start.15 = (bf16[2,64,512]{2,1,0:T(8,128)(2,1)S(1)}, bf16[2,64,512]{2,1,0:T(8,128)(2,1)S(1)}, u32[]{:S(2)}, u32[]{:S(2)}) collective-permute-start(bf16[2,64,512]{2,1,0:T(8,128)(2,1)S(1)} %get-tuple-element.110), channel_id=1, source_target_pairs={{0,1},{1,0},{2,3},{3,2},{4,5},{5,4},{6,7},{7,6},{8,9},{9,8},{10,11... | collective-permute-start | bytes 393224 | tf_op jit(solution)/shard_map/ppermute | solution.py:39
  34.5 8.5 %collective-permute-start.22 = (bf16[128,1024]{1,0:T(8,128)(2,1)S(1)}, bf16[128,1024]{1,0:T(8,128)(2,1)S(1)}, u32[]{:S(2)}, u32[]{:S(2)}) collective-permute-start(bf16[128,1024]{1,0:T(8,128)(2,1)S(1)} %slice.37), channel_id=1, source_target_pairs={{0,16},{4,20},{8,24},{12,28},{16,0},{20,4},{24,8},{28,12},{1,17},{... | collective-permute-start | bytes 786440 | tf_op jit(solution)/shard_map/ppermute | solution.py:39
  35.9 12.8 %collective-permute-start.17 = (bf16[2,64,512]{2,1,0:T(8,128)(2,1)S(1)}, bf16[2,64,512]{2,1,0:T(8,128)(2,1)S(1)}, u32[]{:S(2)}, u32[]{:S(2)}) collective-permute-start(bf16[2,64,512]{2,1,0:T(8,128)(2,1)S(1)} %get-tuple-element.114), channel_id=1, source_target_pairs={{0,2},{1,3},{2,0},{3,1},{4,6},{5,7},{6,4},{7,5},{8,10},{9,11},{10,... | collective-permute-start | bytes 393224 | tf_op jit(solution)/shard_map/ppermute | solution.py:39
  38.5 10.3 %collective-permute-start.18 = (bf16[2,64,512]{2,1,0:T(8,128)(2,1)S(1)}, bf16[2,64,512]{2,1,0:T(8,128)(2,1)S(1)}, u32[]{:S(2)}, u32[]{:S(2)}) collective-permute-start(bf16[2,64,512]{2,1,0:T(8,128)(2,1)S(1)} %get-tuple-element.115), channel_id=1, source_target_pairs={{0,3},{1,2},{2,1},{3,0},{4,7},{5,6},{6,5},{7,4},{8,11},{9,10},{10,... | collective-permute-start | bytes 393224 | tf_op jit(solution)/shard_map/ppermute | solution.py:39
  42.4 20.9 %copy-start.3 = (s32[1,1,32]{2,1,0:T(1,128)S(1)}, s32[1,1,32]{2,1,0:T(1,128)}, u32[]{:S(2)}) copy-start(s32[1,1,32]{2,1,0:T(1,128)} %param.12) | copy-start | bytes 388
  42.4 6.2 %collective-permute-start.16 = (bf16[64,1536]{1,0:T(8,128)(2,1)S(1)}, bf16[64,1536]{1,0:T(8,128)(2,1)S(1)}, u32[]{:S(2)}, u32[]{:S(2)}) collective-permute-start(bf16[64,1536]{1,0:T(8,128)(2,1)S(1)} %slice.43), channel_id=1, source_target_pairs={{0,16},{4,20},{8,24},{12,28},{16,0},{20,4},{24,8},{28,12},{1,17},{... | collective-permute-start | bytes 589832 | tf_op jit(solution)/shard_map/ppermute | solution.py:39
  43.1 7.6 %collective-permute-start.23 = (bf16[64,1024]{1,0:T(8,128)(2,1)S(1)}, bf16[64,1024]{1,0:T(8,128)(2,1)S(1)}, u32[]{:S(2)}, u32[]{:S(2)}) collective-permute-start(bf16[64,1024]{1,0:T(8,128)(2,1)S(1)} %slice.45), channel_id=1, source_target_pairs={{0,8},{4,12},{8,0},{12,4},{16,24},{20,28},{24,16},{28,20},{1,9},{5... | collective-permute-start | bytes 393224 | tf_op jit(solution)/shard_map/ppermute | solution.py:39
  48.8 5.2 %collective-permute-start.19 = (bf16[32,1536]{1,0:T(8,128)(2,1)S(1)}, bf16[32,1536]{1,0:T(8,128)(2,1)S(1)}, u32[]{:S(2)}, u32[]{:S(2)}) collective-permute-start(bf16[32,1536]{1,0:T(8,128)(2,1)S(1)} %constant_dynamic-slice_fusion.1), channel_id=1, source_target_pairs={{0,1},{1,0},{2,3},{3,2},{4,5},{5,4},{6,7},{7,6},{8,9},{9,8},{10,11... | collective-permute-start | bytes 294920 | tf_op jit(solution)/shard_map/ppermute | solution.py:39
  50.7 5.7 %collective-permute-start.24 = (bf16[32,1024]{1,0:T(8,128)(2,1)S(1)}, bf16[32,1024]{1,0:T(8,128)(2,1)S(1)}, u32[]{:S(2)}, u32[]{:S(2)}) collective-permute-start(bf16[32,1024]{1,0:T(8,128)(2,1)S(1)} %constant_dynamic-slice_fusion), channel_id=1, source_target_pairs={{0,1},{1,0},{2,3},{3,2},{4,5},{5,4},{6,7},{7,6},{8,9},{9,8},{10,11... | collective-permute-start | bytes 196616 | tf_op jit(solution)/shard_map/ppermute | solution.py:39
  53.9 7.1 %collective-permute-start.20 = (bf16[32,1536]{1,0:T(8,128)(2,1)S(1)}, bf16[32,1536]{1,0:T(8,128)(2,1)S(1)}, u32[]{:S(2)}, u32[]{:S(2)}) collective-permute-start(bf16[32,1536]{1,0:T(8,128)(2,1)S(1)} %add_convert_fusion.7), channel_id=1, source_target_pairs={{0,2},{1,3},{2,0},{3,1},{4,6},{5,7},{6,4},{7,5},{8,10},{9,11},{10,... | collective-permute-start | bytes 294920 | tf_op jit(solution)/shard_map/ppermute | solution.py:39
  56.5 6.0 %collective-permute-start.25 = (bf16[32,1024]{1,0:T(8,128)(2,1)S(1)}, bf16[32,1024]{1,0:T(8,128)(2,1)S(1)}, u32[]{:S(2)}, u32[]{:S(2)}) collective-permute-start(bf16[32,1024]{1,0:T(8,128)(2,1)S(1)} %add_convert_fusion.9), channel_id=1, source_target_pairs={{0,2},{1,3},{2,0},{3,1},{4,6},{5,7},{6,4},{7,5},{8,10},{9,11},{10,... | collective-permute-start | bytes 196616 | tf_op jit(solution)/shard_map/ppermute | solution.py:39
  61.1 5.7 %collective-permute-start.21 = (bf16[32,1536]{1,0:T(8,128)(2,1)S(1)}, bf16[32,1536]{1,0:T(8,128)(2,1)S(1)}, u32[]{:S(2)}, u32[]{:S(2)}) collective-permute-start(bf16[32,1536]{1,0:T(8,128)(2,1)S(1)} %add_convert_fusion.6.early_own), channel_id=1, source_target_pairs={{0,1},{1,0},{2,3},{3,2},{4,5},{5,4},{6,7},{7,6},{8,9},{9,8},{10,11... | collective-permute-start | bytes 294920 | tf_op jit(solution)/shard_map/ppermute | solution.py:39
  62.5 4.3 %collective-permute-start.26 = (bf16[32,1024]{1,0:T(8,128)(2,1)S(1)}, bf16[32,1024]{1,0:T(8,128)(2,1)S(1)}, u32[]{:S(2)}, u32[]{:S(2)}) collective-permute-start(bf16[32,1024]{1,0:T(8,128)(2,1)S(1)} %add_convert_fusion.8.late_own), channel_id=1, source_target_pairs={{0,1},{1,0},{2,3},{3,2},{4,5},{5,4},{6,7},{7,6},{8,9},{9,8},{10,11... | collective-permute-start | bytes 196616 | tf_op jit(solution)/shard_map/ppermute | solution.py:39

commit v6 on v5

--- a/solution.py
+++ b/solution.py
@@ -164,6 +164,10 @@
     return jnp.where(place == h, value, jnp.zeros_like(value))
 
 
+def apart(value, per, head_width):
+    return jnp.concatenate([only(value, h, head_width) for h in range(per)], axis=0)
+
+
 def blocks_of(width):
     head_width = width // HEADS
     per = max(1, 128 // head_width)
@@ -232,18 +236,19 @@
 
     scale = scale_ref[...]
     head_width, per, wide = blocks_of(width)
+    rows = scale.shape[0]
     for g in range(HEADS // per):
         v, q, k = (act_ref[:, c * width + g * wide : c * width + (g + 1) * wide] for c in (1, 2, 3))
-        mixed = 0.0
+        both = dot(apart(q, per, head_width), k, NT)
+        heads = []
         for h in range(per):
-            scores = dot(only(q, h, head_width), k, NT)
+            scores = both[h * rows : (h + 1) * rows]
             s = sigmoid(scores)
             value = scores * s
-            weights = (value * scale).astype(BF16)
-            weights_ref[g * per + h] = weights
+            heads.append((value * scale).astype(BF16))
+            weights_ref[(g * per + h) * rows : (g * per + h + 1) * rows, :] = heads[h]
             bend_ref[g * per + h] = (s + value * (1.0 - s)) * scale
-            mixed = mixed + dot(weights, only(v, h, head_width))
-        mix_ref[:, g * wide : (g + 1) * wide] = mixed
+        mix_ref[:, g * wide : (g + 1) * wide] = dot(jnp.concatenate(heads, axis=1), apart(v, per, head_width))
 
     normed, mix_inv = normalize(mix_ref[...])
     gate = act_ref[:, :width].astype(F32)
@@ -265,10 +270,8 @@
     ).astype(BF16)
     gmix_ref[...] = g_mixed
     for g in range(HEADS // per):
-        mine = g_mixed[:, g * wide : (g + 1) * wide]
-        g_v = 0.0
-        for h in range(per):
-            g_v = g_v + dot(weights_ref[g * per + h], only(mine, h, head_width), TN)
+        mine = apart(g_mixed[:, g * wide : (g + 1) * wide], per, head_width)
+        g_v = dot(mine, weights_ref[g * per * rows : (g + 1) * per * rows, :], TN).T
         at = slice(width + g * wide, width + (g + 1) * wide)
         gproj_ref[:, at] = (g_v.astype(BF16).astype(F32) * slope_ref[:, at]).astype(BF16)
     early = gproj_ref[:, : keep_ref.shape[1] - width]
@@ -285,12 +288,11 @@
     for g in range(HEADS // per):
         v, q, k = (act_ref[:, c * width + g * wide : c * width + (g + 1) * wide] for c in (1, 2, 3))
         g_mix = gmix_ref[:, g * wide : (g + 1) * wide]
-        g_q = g_k = 0.0
-        for h in range(per):
-            g_weights = dot(only(g_mix, h, head_width), v, NT).astype(BF16).astype(F32)
-            g_scores = (g_weights * bend_ref[g * per + h]).astype(BF16)
-            g_q = g_q + dot(g_scores, only(k, h, head_width))
-            g_k = g_k + dot(g_scores, only(q, h, head_width), TN)
+        both = dot(apart(g_mix, per, head_width), v, NT).astype(BF16).astype(F32)
+        rows = v.shape[0]
+        heads = [(both[h * rows : (h + 1) * rows] * bend_ref[g * per + h]).astype(BF16) for h in range(per)]
+        g_q = dot(jnp.concatenate(heads, axis=1), apart(k, per, head_width))
+        g_k = dot(apart(q, per, head_width), jnp.concatenate(heads, axis=0), TN).T
         for c, value in ((2, g_q), (3, g_k)):
             at = slice(c * width + g * wide, c * width + (g + 1) * wide)
             gproj_ref[:, at] = (value.astype(BF16).astype(F32) * slope_ref[:, at]).astype(BF16)
@@ -427,7 +429,7 @@
         in_specs=[VMEM] * (5 + len(shards)),
         out_specs=[VMEM] * 9,
         scratch_shapes=[
-            pltpu.VMEM((HEADS, rows, rows), BF16),
+            pltpu.VMEM((HEADS * rows, rows), BF16),
             pltpu.VMEM((width, rows), BF16),
             pltpu.VMEM((rows, width), F32),
             pltpu.VMEM((rows, width), BF16),

time: 67.9 us -> 67.4 us (level)
  Pallas kernels: 12.6 us -> 11.8 us
where the time goes in v6:
time: 67.4 us; the launch traced here: 67.2 us
  starting transfers between devices  27.5 us (41%)
  waiting for transfers between devices  23.6 us (35%)
  Pallas kernels  11.8 us (18%)
  local copies, waits for them, and re-layouts  2.68 us (4%)
  between operations  0.85 us (1%)
  other arithmetic  0.72 us (1%)
    ppermute x27, starting transfers between devices, exchange(): return lax.ppermute(value, axis, [(i, i ^ mask) for i in range(size)])  27.5 us
    ppermute x27, waiting for transfers between devices, exchange(): return lax.ppermute(value, axis, [(i, i ^ mask) for i in range(size)])  23.6 us
    pallas_call x1, Pallas kernels, on_device(): pl.pallas_call(partial(forward_kernel, groups, chips, places), out_shape=...  3.46 us
    unnamed x8, local copies, waits for them, and re-layouts  2.56 us
    pallas_call x1, Pallas kernels, on_device(): pl.pallas_call(partial(pre_kernel, parts), out_shape=[spec((shard, column...  2.29 us
    pallas_call x1, Pallas kernels, on_device(): pl.pallas_call(partial(backward_kernel, groups, chips[::-1]), out_shape=[...  1.68 us
  transfers between devices with their start and end apart: 27, of which 13 were waited for; matrix products, arithmetic and copies ran while one was open for 1% of the time, Pallas kernels for 8%

profile of v6, /device:TPU:0, one launch (start us, length us, event | category | flops | bytes accessed | tf_op | source)
XLA Modules:
  0.0 67.2 jit_solution(14022651977298450139)
XLA Ops:
  0.6 2.3 %pre.1 = (bf16[64,2560]{1,0:T(8,128)(2,1)}, s32[8,128]{1,0:T(8,128)}, bf16[2,64,512]{2,1,0:T(8,128)(2,1)}, bf16[2,64,512]{2,1,0:T(8,128)(2,1)}, bf16[2,64,512]{2...) custom-call(s32[1,32]{1,0:T(1,128)} %bitcast.8, s32[1,32]{1,0:T(1,128)} %bitcast.12, s32[1,8]{1,0:T(1,128)} %bitcast.13, ...), custom_call_target="tpu_custom_call" | custom-call | tf_op jit(solution)/shard_map/pre/pallas_call | solution.py:347
  2.9 3.0 %collective-permute-start = (bf16[64,2560]{1,0:T(8,128)(2,1)}, bf16[64,2560]{1,0:T(8,128)(2,1)S(1)}, u32[]{:S(2)}, u32[]{:S(2)}) collective-permute-start(bf16[64,2560]{1,0:T(8,128)(2,1)} %get-tuple-element.66.w_ref), channel_id=1, source_target_pairs={{0,8},{4,12},{8,0},{12,4},{16,24},{20,28},{24,16},{28,20},{1,9},{5... | collective-permute-start | bytes 983048 | tf_op jit(solution)/shard_map/ppermute | solution.py:39
  5.9 1.5 %collective-permute-start.1 = (bf16[64,2560]{1,0:T(8,128)(2,1)}, bf16[64,2560]{1,0:T(8,128)(2,1)S(1)}, u32[]{:S(2)}, u32[]{:S(2)}) collective-permute-start(bf16[64,2560]{1,0:T(8,128)(2,1)} %get-tuple-element.66.w_ref), channel_id=1, source_target_pairs={{0,16},{4,20},{8,24},{12,28},{16,0},{20,4},{24,8},{28,12},{1,17},{... | collective-permute-start | bytes 983048 | tf_op jit(solution)/shard_map/ppermute | solution.py:39
  7.5 1.6 %collective-permute-start.2 = (bf16[2,64,512]{2,1,0:T(8,128)(2,1)}, bf16[2,64,512]{2,1,0:T(8,128)(2,1)S(1)}, u32[]{:S(2)}, u32[]{:S(2)}) collective-permute-start(bf16[2,64,512]{2,1,0:T(8,128)(2,1)} %get-tuple-element.69), channel_id=1, source_target_pairs={{0,1},{1,0},{2,3},{3,2},{4,5},{5,4},{6,7},{7,6},{8,9},{9,8},{10,11... | collective-permute-start | bytes 393224 | tf_op jit(solution)/shard_map/ppermute | solution.py:39
  9.0 2.6 %collective-permute-start.5 = (bf16[2,64,512]{2,1,0:T(8,128)(2,1)}, bf16[2,64,512]{2,1,0:T(8,128)(2,1)S(1)}, u32[]{:S(2)}, u32[]{:S(2)}) collective-permute-start(bf16[2,64,512]{2,1,0:T(8,128)(2,1)} %get-tuple-element.76), channel_id=1, source_target_pairs={{0,2},{1,3},{2,0},{3,1},{4,6},{5,7},{6,4},{7,5},{8,10},{9,11},{10,... | collective-permute-start | bytes 393224 | tf_op jit(solution)/shard_map/ppermute | solution.py:39
  11.6 0.2 collective-permute-start.6
  11.8 1.0 %copy-done = bf16[64,2560]{1,0:T(8,128)(2,1)S(1)} copy-done((bf16[64,2560]{1,0:T(8,128)(2,1)S(1)}, bf16[64,2560]{1,0:T(8,128)(2,1)}, u32[]{:S(2)}) %copy-start) | copy-done | bytes 327704
  12.8 0.9 %copy-done.1 = bf16[2,64,512]{2,1,0:T(8,128)(2,1)S(1)} copy-done((bf16[2,64,512]{2,1,0:T(8,128)(2,1)S(1)}, bf16[2,64,512]{2,1,0:T(8,128)(2,1)}, u32[]{:S(2)}) %copy-start.1) | copy-done | bytes 131096
  13.7 0.7 %copy-done.2 = s32[8,128]{1,0:T(8,128)S(1)} copy-done((s32[8,128]{1,0:T(8,128)S(1)}, s32[8,128]{1,0:T(8,128)}, u32[]{:S(2)}) %copy-start.2) | copy-done | bytes 4120
  14.4 0.7 %plan.1 = (bf16[256,256]{1,0:T(8,128)(2,1)S(1)}, f32[256,256]{1,0:T(8,128)S(1)}, bf16[64,2560]{1,0:T(8,128)(2,1)S(1)}, bf16[2,64,512]{2,1,0:T(8,128)(2,1)S(1)}) custom-call(s32[8,128]{1,0:T(8,128)S(1)} %copy-done.2, bf16[64,2560]{1,0:T(8,128)(2,1)S(1)} %copy-done, bf16[2,64,512]{2,1,0:T(8,128)(2,1)S(1)} %copy-done.1), custom_call_target="tpu_custom_call" | custom-call | tf_op jit(solution)/shard_map/plan/pallas_call | solution.py:369
  15.2 0.2 collective-permute-done.1.refs_4_
  15.3 0.5 collective-permute-start.3
  15.8 1.7 %collective-permute-start.4 = (bf16[64,1280]{1,0:T(8,128)(2,1)S(1)}, bf16[64,1280]{1,0:T(8,128)(2,1)S(1)}, u32[]{:S(2)}, u32[]{:S(2)}) collective-permute-start(bf16[64,1280]{1,0:T(8,128)(2,1)S(1)} %slice.41), channel_id=1, source_target_pairs={{0,16},{4,20},{8,24},{12,28},{16,0},{20,4},{24,8},{28,12},{1,17},{... | collective-permute-start | bytes 491528 | tf_op jit(solution)/shard_map/ppermute | solution.py:39
  17.5 4.1 %collective-permute-done.5.refs_2_ = bf16[2,64,512]{2,1,0:T(8,128)(2,1)S(1)} collective-permute-done((bf16[2,64,512]{2,1,0:T(8,128)(2,1)}, bf16[2,64,512]{2,1,0:T(8,128)(2,1)S(1)}, u32[]{:S(2)}, u32[]{:S(2)}) %collective-permute-start.5) | collective-permute-done | bytes 131104 | tf_op jit(solution)/shard_map/ppermute | solution.py:39
  21.6 0.5 collective-permute-start.9
  22.2 0.4 collective-permute-start.11
  22.6 0.5 norm.1
  23.2 0.5 collective-permute-done.9.refs_5_
  23.7 0.2 collective-permute-done.10.refs_8_
  23.9 0.2 collective-permute-done.11.refs_9_
  24.2 3.5 %forward.1 = (bf16[256,1536]{1,0:T(8,128)(2,1)S(1)}, bf16[256,1536]{1,0:T(8,128)(2,1)S(1)}, bf16[256,512]{1,0:T(8,128)(2,1)S(1)}, bf16[512,2560]{1,0:T(8,128)(2,...) custom-call(f32[256,256]{1,0:T(8,128)S(1)} %get-tuple-element.72.sca, ...), custom_call_target="tpu_custom_call" | custom-call | tf_op jit(solution)/shard_map/forward/pallas_call | solution.py:416
  27.6 0.2 collective-permute-start.12
  27.8 1.7 %backward.1 = (bf16[256,1024]{1,0:T(8,128)(2,1)S(1)}, bf16[256,1024]{1,0:T(8,128)(2,1)S(1)}, bf16[256,2048]{1,0:T(8,128)(2,1)S(1)}) custom-call(bf16[512,256]{1,0:T(8,128)(2,1)S(1)} %get-tuple-element.83.xt_ref, bf16[256,2048]{1,0:T(8,128)(2,1)S(1)} %get-tuple-element.91.act_ref, f32[256,2048]{1,0:T(8,128)S(1)} %get-tuple-element.92.slope_ref, ...), custom_call_target="tpu_custom_call" | custom-call | tf_op jit(solution)/shard_map/backward/pallas_call | solution.py:441
  29.5 0.5 collective-permute-done.12
  30.0 0.1 collective-permute-start.14
  30.1 0.2 add_convert_fusion
  30.3 0.6 collective-permute-start.13
  31.0 1.1 %rows.1 = (bf16[2,64,512]{2,1,0:T(8,128)(2,1)S(1)}, bf16[2,64,512]{2,1,0:T(8,128)(2,1)S(1)}, bf16[2,64,512]{2,1,0:T(8,128)(2,1)S(1)}, bf16[2,64,512]{2,1,0:T(8,128)(2,1)S(1)}) custom-call(bf16[256,256]{1,0:T(8,128)(2,1)S(1)} %get-tuple-element.73.matrix_ref, bf16[256,2048]{1,0:T(8,128)(2,1)S(1)} %get-tuple-element.102.gproj_ref, ...), custom_call_target="tpu_custom_call" | custom-call | tf_op jit(solution)/shard_map/rows/pallas_call | solution.py:480
  32.1 0.2 add_convert_fusion.1
  32.3 1.6 %collective-permute-start.15 = (bf16[2,64,512]{2,1,0:T(8,128)(2,1)S(1)}, bf16[2,64,512]{2,1,0:T(8,128)(2,1)S(1)}, u32[]{:S(2)}, u32[]{:S(2)}) collective-permute-start(bf16[2,64,512]{2,1,0:T(8,128)(2,1)S(1)} %get-tuple-element.110), channel_id=1, source_target_pairs={{0,1},{1,0},{2,3},{3,2},{4,5},{5,4},{6,7},{7,6},{8,9},{9,8},{10,11... | collective-permute-start | bytes 393224 | tf_op jit(solution)/shard_map/ppermute | solution.py:39
  33.9 1.5 %collective-permute-start.22 = (bf16[128,1024]{1,0:T(8,128)(2,1)S(1)}, bf16[128,1024]{1,0:T(8,128)(2,1)S(1)}, u32[]{:S(2)}, u32[]{:S(2)}) collective-permute-start(bf16[128,1024]{1,0:T(8,128)(2,1)S(1)} %slice.37), channel_id=1, source_target_pairs={{0,16},{4,20},{8,24},{12,28},{16,0},{20,4},{24,8},{28,12},{1,17},{... | collective-permute-start | bytes 786440 | tf_op jit(solution)/shard_map/ppermute | solution.py:39
  35.4 2.6 %collective-permute-start.17 = (bf16[2,64,512]{2,1,0:T(8,128)(2,1)S(1)}, bf16[2,64,512]{2,1,0:T(8,128)(2,1)S(1)}, u32[]{:S(2)}, u32[]{:S(2)}) collective-permute-start(bf16[2,64,512]{2,1,0:T(8,128)(2,1)S(1)} %get-tuple-element.114), channel_id=1, source_target_pairs={{0,2},{1,3},{2,0},{3,1},{4,6},{5,7},{6,4},{7,5},{8,10},{9,11},{10,... | collective-permute-start | bytes 393224 | tf_op jit(solution)/shard_map/ppermute | solution.py:39
  38.0 0.2 collective-permute-start.18
  38.2 3.6 %collective-permute-done.13 = bf16[128,1536]{1,0:T(8,128)(2,1)S(1)} collective-permute-done((bf16[128,1536]{1,0:T(8,128)(2,1)S(1)}, bf16[128,1536]{1,0:T(8,128)(2,1)S(1)}, u32[]{:S(2)}, u32[]{:S(2)}) %collective-permute-start.13) | collective-permute-done | bytes 393248 | tf_op jit(solution)/shard_map/ppermute | solution.py:39
  41.9 0.6 collective-permute-start.16
  42.6 1.4 %collective-permute-start.23 = (bf16[64,1024]{1,0:T(8,128)(2,1)S(1)}, bf16[64,1024]{1,0:T(8,128)(2,1)S(1)}, u32[]{:S(2)}, u32[]{:S(2)}) collective-permute-start(bf16[64,1024]{1,0:T(8,128)(2,1)S(1)} %slice.45), channel_id=1, source_target_pairs={{0,8},{4,12},{8,0},{12,4},{16,24},{20,28},{24,16},{28,20},{1,9},{5... | collective-permute-start | bytes 393224 | tf_op jit(solution)/shard_map/ppermute | solution.py:39
  44.0 4.4 %collective-permute-done.16 = bf16[64,1536]{1,0:T(8,128)(2,1)S(1)} collective-permute-done((bf16[64,1536]{1,0:T(8,128)(2,1)S(1)}, bf16[64,1536]{1,0:T(8,128)(2,1)S(1)}, u32[]{:S(2)}, u32[]{:S(2)}) %collective-permute-start.16) | collective-permute-done | bytes 196640 | tf_op jit(solution)/shard_map/ppermute | solution.py:39
  48.5 1.7 %collective-permute-start.19 = (bf16[32,1536]{1,0:T(8,128)(2,1)S(1)}, bf16[32,1536]{1,0:T(8,128)(2,1)S(1)}, u32[]{:S(2)}, u32[]{:S(2)}) collective-permute-start(bf16[32,1536]{1,0:T(8,128)(2,1)S(1)} %constant_dynamic-slice_fusion.1), channel_id=1, source_target_pairs={{0,1},{1,0},{2,3},{3,2},{4,5},{5,4},{6,7},{7,6},{8,9},{9,8},{10,11... | collective-permute-start | bytes 294920 | tf_op jit(solution)/shard_map/ppermute | solution.py:39
  50.2 0.5 collective-permute-start.24
  50.7 2.6 %collective-permute-done.19 = bf16[32,1536]{1,0:T(8,128)(2,1)S(1)} collective-permute-done((bf16[32,1536]{1,0:T(8,128)(2,1)S(1)}, bf16[32,1536]{1,0:T(8,128)(2,1)S(1)}, u32[]{:S(2)}, u32[]{:S(2)}) %collective-permute-start.19) | collective-permute-done | bytes 98336 | tf_op jit(solution)/shard_map/ppermute | solution.py:39
  53.3 2.6 %collective-permute-start.20 = (bf16[32,1536]{1,0:T(8,128)(2,1)S(1)}, bf16[32,1536]{1,0:T(8,128)(2,1)S(1)}, u32[]{:S(2)}, u32[]{:S(2)}) collective-permute-start(bf16[32,1536]{1,0:T(8,128)(2,1)S(1)} %add_convert_fusion.7), channel_id=1, source_target_pairs={{0,2},{1,3},{2,0},{3,1},{4,6},{5,7},{6,4},{7,5},{8,10},{9,11},{10,... | collective-permute-start | bytes 294920 | tf_op jit(solution)/shard_map/ppermute | solution.py:39
  55.9 1.0 %collective-permute-start.25 = (bf16[32,1024]{1,0:T(8,128)(2,1)S(1)}, bf16[32,1024]{1,0:T(8,128)(2,1)S(1)}, u32[]{:S(2)}, u32[]{:S(2)}) collective-permute-start(bf16[32,1024]{1,0:T(8,128)(2,1)S(1)} %add_convert_fusion.9), channel_id=1, source_target_pairs={{0,2},{1,3},{2,0},{3,1},{4,6},{5,7},{6,4},{7,5},{8,10},{9,11},{10,... | collective-permute-start | bytes 196616 | tf_op jit(solution)/shard_map/ppermute | solution.py:39
  56.9 3.6 %collective-permute-done.20 = bf16[32,1536]{1,0:T(8,128)(2,1)S(1)} collective-permute-done((bf16[32,1536]{1,0:T(8,128)(2,1)S(1)}, bf16[32,1536]{1,0:T(8,128)(2,1)S(1)}, u32[]{:S(2)}, u32[]{:S(2)}) %collective-permute-start.20) | collective-permute-done | bytes 98336 | tf_op jit(solution)/shard_map/ppermute | solution.py:39
  60.6 1.3 %collective-permute-done.25 = bf16[32,1024]{1,0:T(8,128)(2,1)S(1)} collective-permute-done((bf16[32,1024]{1,0:T(8,128)(2,1)S(1)}, bf16[32,1024]{1,0:T(8,128)(2,1)S(1)}, u32[]{:S(2)}, u32[]{:S(2)}) %collective-permute-start.25) | collective-permute-done | bytes 65568 | tf_op jit(solution)/shard_map/ppermute | solution.py:39
  61.9 0.8 %collective-permute-start.26 = (bf16[32,1024]{1,0:T(8,128)(2,1)S(1)}, bf16[32,1024]{1,0:T(8,128)(2,1)S(1)}, u32[]{:S(2)}, u32[]{:S(2)}) collective-permute-start(bf16[32,1024]{1,0:T(8,128)(2,1)S(1)} %add_convert_fusion.8.late_own), channel_id=1, source_target_pairs={{0,1},{1,0},{2,3},{3,2},{4,5},{5,4},{6,7},{7,6},{8,9},{9,8},{10,11... | collective-permute-start | bytes 196616 | tf_op jit(solution)/shard_map/ppermute | solution.py:39
  62.8 1.2 %post.1 = (bf16[256,512]{1,0:T(8,128)(2,1)}, bf16[256,512]{1,0:T(8,128)(2,1)}) custom-call(s32[1,32]{1,0:T(1,128)S(1)} %bitcast.9, bf16[2,64,512]{2,1,0:T(8,128)(2,1)S(1)} %get-tuple-element.116.refs_0_, bf16[2,64,512]{2,1,0:T(8,128)(2,1)S(1)} %collective-permute-done.15.refs_1_, bf16[2,64,512]{2,1,0:T(8,128)(2,1)S(1)} %collective-permute-done.17.refs_2_, ...), custom_call_target="tpu_custom_call" | custom-call | tf_op jit(solution)/shard_map/post/pallas_call | solution.py:492
  63.9 2.3 %collective-permute-done.26.late_other = bf16[32,1024]{1,0:T(8,128)(2,1)S(1)} collective-permute-done((bf16[32,1024]{1,0:T(8,128)(2,1)S(1)}, bf16[32,1024]{1,0:T(8,128)(2,1)S(1)}, u32[]{:S(2)}, u32[]{:S(2)}) %collective-permute-start.26) | collective-permute-done | bytes 65568 | tf_op jit(solution)/shard_map/ppermute | solution.py:39
  66.3 0.9 %finish.1 = (f32[64,2048]{1,0:T(8,128)}, f32[64,512]{1,0:T(8,128)}) custom-call(bf16[32,1536]{1,0:T(8,128)(2,1)S(1)} %add_convert_fusion.6.early_own, bf16[32,1536]{1,0:T(8,128)(2,1)S(1)} %collective-permute-done.21.early_other, bf16[32,1024]{1,0:T(8,128)(2,1)S(1)} %add_convert_fusion.8.late_own, bf16[32,1024]{1,0:T(8,128)(2,1)S(1)} %collective-permute-done.26.late_other), custom_call_target="tpu_custom_call" | custom-call | tf_op jit(solution)/shard_map/finish/pallas_call | solution.py:504
  (40 shorter events, 0.8 us)
Async XLA Ops:
  2.9 12.2 %collective-permute-start = (bf16[64,2560]{1,0:T(8,128)(2,1)}, bf16[64,2560]{1,0:T(8,128)(2,1)S(1)}, u32[]{:S(2)}, u32[]{:S(2)}) collective-permute-start(bf16[64,2560]{1,0:T(8,128)(2,1)} %get-tuple-element.66.w_ref), channel_id=1, source_target_pairs={{0,8},{4,12},{8,0},{12,4},{16,24},{20,28},{24,16},{28,20},{1,9},{5... | collective-permute-start | bytes 983048 | tf_op jit(solution)/shard_map/ppermute | solution.py:39
  5.9 9.4 %collective-permute-start.1 = (bf16[64,2560]{1,0:T(8,128)(2,1)}, bf16[64,2560]{1,0:T(8,128)(2,1)S(1)}, u32[]{:S(2)}, u32[]{:S(2)}) collective-permute-start(bf16[64,2560]{1,0:T(8,128)(2,1)} %get-tuple-element.66.w_ref), channel_id=1, source_target_pairs={{0,16},{4,20},{8,24},{12,28},{16,0},{20,4},{24,8},{28,12},{1,17},{... | collective-permute-start | bytes 983048 | tf_op jit(solution)/shard_map/ppermute | solution.py:39
  7.5 7.7 %collective-permute-start.2 = (bf16[2,64,512]{2,1,0:T(8,128)(2,1)}, bf16[2,64,512]{2,1,0:T(8,128)(2,1)S(1)}, u32[]{:S(2)}, u32[]{:S(2)}) collective-permute-start(bf16[2,64,512]{2,1,0:T(8,128)(2,1)} %get-tuple-element.69), channel_id=1, source_target_pairs={{0,1},{1,0},{2,3},{3,2},{4,5},{5,4},{6,7},{7,6},{8,9},{9,8},{10,11... | collective-permute-start | bytes 393224 | tf_op jit(solution)/shard_map/ppermute | solution.py:39
  9.0 12.6 %collective-permute-start.5 = (bf16[2,64,512]{2,1,0:T(8,128)(2,1)}, bf16[2,64,512]{2,1,0:T(8,128)(2,1)S(1)}, u32[]{:S(2)}, u32[]{:S(2)}) collective-permute-start(bf16[2,64,512]{2,1,0:T(8,128)(2,1)} %get-tuple-element.76), channel_id=1, source_target_pairs={{0,2},{1,3},{2,0},{3,1},{4,6},{5,7},{6,4},{7,5},{8,10},{9,11},{10,... | collective-permute-start | bytes 393224 | tf_op jit(solution)/shard_map/ppermute | solution.py:39
  11.6 10.0 %collective-permute-start.6 = (bf16[2,64,512]{2,1,0:T(8,128)(2,1)}, bf16[2,64,512]{2,1,0:T(8,128)(2,1)S(1)}, u32[]{:S(2)}, u32[]{:S(2)}) collective-permute-start(bf16[2,64,512]{2,1,0:T(8,128)(2,1)} %get-tuple-element.77), channel_id=1, source_target_pairs={{0,3},{1,2},{2,1},{3,0},{4,7},{5,6},{6,5},{7,4},{8,11},{9,10},{10,... | collective-permute-start | bytes 393224 | tf_op jit(solution)/shard_map/ppermute | solution.py:39
  11.8 1.0 %copy-start = (bf16[64,2560]{1,0:T(8,128)(2,1)S(1)}, bf16[64,2560]{1,0:T(8,128)(2,1)}, u32[]{:S(2)}) copy-start(bf16[64,2560]{1,0:T(8,128)(2,1)} %get-tuple-element.66.w_ref) | copy-start | bytes 983044
  12.8 0.9 %copy-start.1 = (bf16[2,64,512]{2,1,0:T(8,128)(2,1)S(1)}, bf16[2,64,512]{2,1,0:T(8,128)(2,1)}, u32[]{:S(2)}) copy-start(bf16[2,64,512]{2,1,0:T(8,128)(2,1)} %get-tuple-element.67.own_ref) | copy-start | bytes 393220
  13.7 0.7 %copy-start.2 = (s32[8,128]{1,0:T(8,128)S(1)}, s32[8,128]{1,0:T(8,128)}, u32[]{:S(2)}) copy-start(s32[8,128]{1,0:T(8,128)} %get-tuple-element.65.small_ref) | copy-start | bytes 12292
  15.3 6.8 %collective-permute-start.3 = (bf16[64,1280]{1,0:T(8,128)(2,1)S(1)}, bf16[64,1280]{1,0:T(8,128)(2,1)S(1)}, u32[]{:S(2)}, u32[]{:S(2)}) collective-permute-start(bf16[64,1280]{1,0:T(8,128)(2,1)S(1)} %slice.40), channel_id=1, source_target_pairs={{0,8},{4,12},{8,0},{12,4},{16,24},{20,28},{24,16},{28,20},{1,9},{5... | collective-permute-start | bytes 491528 | tf_op jit(solution)/shard_map/ppermute | solution.py:39
  15.8 6.3 %collective-permute-start.4 = (bf16[64,1280]{1,0:T(8,128)(2,1)S(1)}, bf16[64,1280]{1,0:T(8,128)(2,1)S(1)}, u32[]{:S(2)}, u32[]{:S(2)}) collective-permute-start(bf16[64,1280]{1,0:T(8,128)(2,1)S(1)} %slice.41), channel_id=1, source_target_pairs={{0,16},{4,20},{8,24},{12,28},{16,0},{20,4},{24,8},{28,12},{1,17},{... | collective-permute-start | bytes 491528 | tf_op jit(solution)/shard_map/ppermute | solution.py:39
  17.5 5.6 %collective-permute-start.7 = (bf16[64,2560]{1,0:T(8,128)(2,1)S(1)}, bf16[64,2560]{1,0:T(8,128)(2,1)S(1)}, u32[]{:S(2)}, u32[]{:S(2)}) collective-permute-start(bf16[64,2560]{1,0:T(8,128)(2,1)S(1)} %get-tuple-element.84.refs_0_), channel_id=1, source_target_pairs={{0,4},{4,0},{8,12},{12,8},{16,20},{20,16},{24,28},{28,24},{1,5},{5... | collective-permute-start | bytes 983048 | tf_op jit(solution)/shard_map/ppermute | solution.py:39
  21.6 1.6 %collective-permute-start.8 = (bf16[64,2560]{1,0:T(8,128)(2,1)S(1)}, bf16[64,2560]{1,0:T(8,128)(2,1)S(1)}, u32[]{:S(2)}, u32[]{:S(2)}) collective-permute-start(bf16[64,2560]{1,0:T(8,128)(2,1)S(1)} %collective-permute-done.refs_2_), channel_id=1, source_target_pairs={{0,4},{4,0},{8,12},{12,8},{16,20},{20,16},{24,28},{28,24},{1,5},{5... | collective-permute-start | bytes 983048 | tf_op jit(solution)/shard_map/ppermute | solution.py:39
  21.6 2.1 %collective-permute-start.9 = (bf16[64,2560]{1,0:T(8,128)(2,1)S(1)}, bf16[64,2560]{1,0:T(8,128)(2,1)S(1)}, u32[]{:S(2)}, u32[]{:S(2)}) collective-permute-start(bf16[64,2560]{1,0:T(8,128)(2,1)S(1)} %collective-permute-done.1.refs_4_), channel_id=1, source_target_pairs={{0,4},{4,0},{8,12},{12,8},{16,20},{20,16},{24,28},{28,24},{1,5},{5... | collective-permute-start | bytes 983048 | tf_op jit(solution)/shard_map/ppermute | solution.py:39
  22.1 1.8 %collective-permute-start.10 = (bf16[64,1280]{1,0:T(8,128)(2,1)S(1)}, bf16[64,1280]{1,0:T(8,128)(2,1)S(1)}, u32[]{:S(2)}, u32[]{:S(2)}) collective-permute-start(bf16[64,1280]{1,0:T(8,128)(2,1)S(1)} %collective-permute-done.3.refs_6_), channel_id=1, source_target_pairs={{0,4},{4,0},{8,12},{12,8},{16,20},{20,16},{24,28},{28,24},{1,5},{5... | collective-permute-start | bytes 491528 | tf_op jit(solution)/shard_map/ppermute | solution.py:39
  22.2 2.0 %collective-permute-start.11 = (bf16[64,1280]{1,0:T(8,128)(2,1)S(1)}, bf16[64,1280]{1,0:T(8,128)(2,1)S(1)}, u32[]{:S(2)}, u32[]{:S(2)}) collective-permute-start(bf16[64,1280]{1,0:T(8,128)(2,1)S(1)} %collective-permute-done.4.refs_7_), channel_id=1, source_target_pairs={{0,4},{4,0},{8,12},{12,8},{16,20},{20,16},{24,28},{28,24},{1,5},{5... | collective-permute-start | bytes 491528 | tf_op jit(solution)/shard_map/ppermute | solution.py:39
  27.6 2.4 %collective-permute-start.12 = (bf16[256,1536]{1,0:T(8,128)(2,1)S(1)}, bf16[256,1536]{1,0:T(8,128)(2,1)S(1)}, u32[]{:S(2)}, u32[]{:S(2)}) collective-permute-start(bf16[256,1536]{1,0:T(8,128)(2,1)S(1)} %get-tuple-element.90), channel_id=1, source_target_pairs={{0,4},{4,0},{8,12},{12,8},{16,20},{20,16},{24,28},{28,24},{1,5},{5... | collective-permute-start | bytes 2359304 | tf_op jit(solution)/shard_map/ppermute | solution.py:39
  30.0 2.1 %collective-permute-start.14 = (bf16[256,1024]{1,0:T(8,128)(2,1)S(1)}, bf16[256,1024]{1,0:T(8,128)(2,1)S(1)}, u32[]{:S(2)}, u32[]{:S(2)}) collective-permute-start(bf16[256,1024]{1,0:T(8,128)(2,1)S(1)} %get-tuple-element.101), channel_id=1, source_target_pairs={{0,4},{4,0},{8,12},{12,8},{16,20},{20,16},{24,28},{28,24},{1,5},{5... | collective-permute-start | bytes 1572872 | tf_op jit(solution)/shard_map/ppermute | solution.py:39
  30.3 11.5 %collective-permute-start.13 = (bf16[128,1536]{1,0:T(8,128)(2,1)S(1)}, bf16[128,1536]{1,0:T(8,128)(2,1)S(1)}, u32[]{:S(2)}, u32[]{:S(2)}) collective-permute-start(bf16[128,1536]{1,0:T(8,128)(2,1)S(1)} %slice.33), channel_id=1, source_target_pairs={{0,8},{4,12},{8,0},{12,4},{16,24},{20,28},{24,16},{28,20},{1,9},{5... | collective-permute-start | bytes 1179656 | tf_op jit(solution)/shard_map/ppermute | solution.py:39
  32.3 9.5 %collective-permute-start.15 = (bf16[2,64,512]{2,1,0:T(8,128)(2,1)S(1)}, bf16[2,64,512]{2,1,0:T(8,128)(2,1)S(1)}, u32[]{:S(2)}, u32[]{:S(2)}) collective-permute-start(bf16[2,64,512]{2,1,0:T(8,128)(2,1)S(1)} %get-tuple-element.110), channel_id=1, source_target_pairs={{0,1},{1,0},{2,3},{3,2},{4,5},{5,4},{6,7},{7,6},{8,9},{9,8},{10,11... | collective-permute-start | bytes 393224 | tf_op jit(solution)/shard_map/ppermute | solution.py:39
  33.9 8.7 %collective-permute-start.22 = (bf16[128,1024]{1,0:T(8,128)(2,1)S(1)}, bf16[128,1024]{1,0:T(8,128)(2,1)S(1)}, u32[]{:S(2)}, u32[]{:S(2)}) collective-permute-start(bf16[128,1024]{1,0:T(8,128)(2,1)S(1)} %slice.37), channel_id=1, source_target_pairs={{0,16},{4,20},{8,24},{12,28},{16,0},{20,4},{24,8},{28,12},{1,17},{... | collective-permute-start | bytes 786440 | tf_op jit(solution)/shard_map/ppermute | solution.py:39
  35.4 13.0 %collective-permute-start.17 = (bf16[2,64,512]{2,1,0:T(8,128)(2,1)S(1)}, bf16[2,64,512]{2,1,0:T(8,128)(2,1)S(1)}, u32[]{:S(2)}, u32[]{:S(2)}) collective-permute-start(bf16[2,64,512]{2,1,0:T(8,128)(2,1)S(1)} %get-tuple-element.114), channel_id=1, source_target_pairs={{0,2},{1,3},{2,0},{3,1},{4,6},{5,7},{6,4},{7,5},{8,10},{9,11},{10,... | collective-permute-start | bytes 393224 | tf_op jit(solution)/shard_map/ppermute | solution.py:39
  38.0 10.5 %collective-permute-start.18 = (bf16[2,64,512]{2,1,0:T(8,128)(2,1)S(1)}, bf16[2,64,512]{2,1,0:T(8,128)(2,1)S(1)}, u32[]{:S(2)}, u32[]{:S(2)}) collective-permute-start(bf16[2,64,512]{2,1,0:T(8,128)(2,1)S(1)} %get-tuple-element.115), channel_id=1, source_target_pairs={{0,3},{1,2},{2,1},{3,0},{4,7},{5,6},{6,5},{7,4},{8,11},{9,10},{10,... | collective-permute-start | bytes 393224 | tf_op jit(solution)/shard_map/ppermute | solution.py:39
  41.9 20.8 %copy-start.3 = (s32[1,1,32]{2,1,0:T(1,128)S(1)}, s32[1,1,32]{2,1,0:T(1,128)}, u32[]{:S(2)}) copy-start(s32[1,1,32]{2,1,0:T(1,128)} %param.12) | copy-start | bytes 388
  41.9 6.4 %collective-permute-start.16 = (bf16[64,1536]{1,0:T(8,128)(2,1)S(1)}, bf16[64,1536]{1,0:T(8,128)(2,1)S(1)}, u32[]{:S(2)}, u32[]{:S(2)}) collective-permute-start(bf16[64,1536]{1,0:T(8,128)(2,1)S(1)} %slice.43), channel_id=1, source_target_pairs={{0,16},{4,20},{8,24},{12,28},{16,0},{20,4},{24,8},{28,12},{1,17},{... | collective-permute-start | bytes 589832 | tf_op jit(solution)/shard_map/ppermute | solution.py:39
  42.6 7.5 %collective-permute-start.23 = (bf16[64,1024]{1,0:T(8,128)(2,1)S(1)}, bf16[64,1024]{1,0:T(8,128)(2,1)S(1)}, u32[]{:S(2)}, u32[]{:S(2)}) collective-permute-start(bf16[64,1024]{1,0:T(8,128)(2,1)S(1)} %slice.45), channel_id=1, source_target_pairs={{0,8},{4,12},{8,0},{12,4},{16,24},{20,28},{24,16},{28,20},{1,9},{5... | collective-permute-start | bytes 393224 | tf_op jit(solution)/shard_map/ppermute | solution.py:39
  48.5 4.8 %collective-permute-start.19 = (bf16[32,1536]{1,0:T(8,128)(2,1)S(1)}, bf16[32,1536]{1,0:T(8,128)(2,1)S(1)}, u32[]{:S(2)}, u32[]{:S(2)}) collective-permute-start(bf16[32,1536]{1,0:T(8,128)(2,1)S(1)} %constant_dynamic-slice_fusion.1), channel_id=1, source_target_pairs={{0,1},{1,0},{2,3},{3,2},{4,5},{5,4},{6,7},{7,6},{8,9},{9,8},{10,11... | collective-permute-start | bytes 294920 | tf_op jit(solution)/shard_map/ppermute | solution.py:39
  50.2 5.7 %collective-permute-start.24 = (bf16[32,1024]{1,0:T(8,128)(2,1)S(1)}, bf16[32,1024]{1,0:T(8,128)(2,1)S(1)}, u32[]{:S(2)}, u32[]{:S(2)}) collective-permute-start(bf16[32,1024]{1,0:T(8,128)(2,1)S(1)} %constant_dynamic-slice_fusion), channel_id=1, source_target_pairs={{0,1},{1,0},{2,3},{3,2},{4,5},{5,4},{6,7},{7,6},{8,9},{9,8},{10,11... | collective-permute-start | bytes 196616 | tf_op jit(solution)/shard_map/ppermute | solution.py:39
  53.3 7.2 %collective-permute-start.20 = (bf16[32,1536]{1,0:T(8,128)(2,1)S(1)}, bf16[32,1536]{1,0:T(8,128)(2,1)S(1)}, u32[]{:S(2)}, u32[]{:S(2)}) collective-permute-start(bf16[32,1536]{1,0:T(8,128)(2,1)S(1)} %add_convert_fusion.7), channel_id=1, source_target_pairs={{0,2},{1,3},{2,0},{3,1},{4,6},{5,7},{6,4},{7,5},{8,10},{9,11},{10,... | collective-permute-start | bytes 294920 | tf_op jit(solution)/shard_map/ppermute | solution.py:39
  55.9 6.0 %collective-permute-start.25 = (bf16[32,1024]{1,0:T(8,128)(2,1)S(1)}, bf16[32,1024]{1,0:T(8,128)(2,1)S(1)}, u32[]{:S(2)}, u32[]{:S(2)}) collective-permute-start(bf16[32,1024]{1,0:T(8,128)(2,1)S(1)} %add_convert_fusion.9), channel_id=1, source_target_pairs={{0,2},{1,3},{2,0},{3,1},{4,6},{5,7},{6,4},{7,5},{8,10},{9,11},{10,... | collective-permute-start | bytes 196616 | tf_op jit(solution)/shard_map/ppermute | solution.py:39
  60.6 5.7 %collective-permute-start.21 = (bf16[32,1536]{1,0:T(8,128)(2,1)S(1)}, bf16[32,1536]{1,0:T(8,128)(2,1)S(1)}, u32[]{:S(2)}, u32[]{:S(2)}) collective-permute-start(bf16[32,1536]{1,0:T(8,128)(2,1)S(1)} %add_convert_fusion.6.early_own), channel_id=1, source_target_pairs={{0,1},{1,0},{2,3},{3,2},{4,5},{5,4},{6,7},{7,6},{8,9},{9,8},{10,11... | collective-permute-start | bytes 294920 | tf_op jit(solution)/shard_map/ppermute | solution.py:39
  61.9 4.3 %collective-permute-start.26 = (bf16[32,1024]{1,0:T(8,128)(2,1)S(1)}, bf16[32,1024]{1,0:T(8,128)(2,1)S(1)}, u32[]{:S(2)}, u32[]{:S(2)}) collective-permute-start(bf16[32,1024]{1,0:T(8,128)(2,1)S(1)} %add_convert_fusion.8.late_own), channel_id=1, source_target_pairs={{0,1},{1,0},{2,3},{3,2},{4,5},{5,4},{6,7},{7,6},{8,9},{9,8},{10,11... | collective-permute-start | bytes 196616 | tf_op jit(solution)/shard_map/ppermute | solution.py:39

commit v7 on v6

--- a/solution.py
+++ b/solution.py
@@ -398,7 +398,7 @@
     shards = [pieces[place] for place in places]
 
     half = groups // 2 * shard
-    early_width = 3 * width
+    early_width = 3 * width - 128
     x, cot, z, inv_scale, xt = pl.pallas_call(
         norm_kernel,
         out_shape=[
@@ -488,7 +488,6 @@
     late, returning = both_cores(keep_late, taken_late, returning)
     returned = swap_rows(returning[0], returning[1:])
     early, returned[1:2] = over_chips(early, chips, returned[1:2])
-    early, returned = lax.optimization_barrier((early, returned))
     owner = pl.pallas_call(
         partial(post_kernel, parts),
         out_shape=[spec((rows, width))] * 2,
@@ -498,7 +497,7 @@
         name="post",
     )(send_order, *returned)
     owner_out, owner_grad = owner
-    early = over_shuf(early)
+    early, owner_out, owner_grad = lax.optimization_barrier((over_shuf(early), owner_out, owner_grad))
     late, _ = over_chips(late, chips[::-1])
     late = over_shuf(late)
     grad_uvqk, grad_wout = pl.pallas_call(

time: 67.4 us -> 66.1 us (0.981)
  waiting for transfers between devices: 23.6 us -> 21.8 us
  starting transfers between devices: 27.5 us -> 28.2 us
    ppermute x27, waiting for transfers between devices: 23.6 us -> 21.8 us  [exchange(): return lax.ppermute(value, axis, [(i, i ^ mask) for i in range(size)])]
    ppermute x27, starting transfers between devices: 27.5 us -> 28.2 us  [exchange(): return lax.ppermute(value, axis, [(i, i ^ mask) for i in range(size)])]
  transfers between devices with their start and end apart: 27 -> 27, of which waited for: 13 -> 15; matrix products, arithmetic and copies ran while one was open for 1% -> 1% of each run, Pallas kernels for 8% -> 8%
where the time goes in v7:
time: 66.1 us; the launch traced here: 65.9 us
  starting transfers between devices  28.2 us (43%)
  waiting for transfers between devices  21.8 us (33%)
  Pallas kernels  11.8 us (18%)
  local copies, waits for them, and re-layouts  2.69 us (4%)
  between operations  0.84 us (1%)
    ppermute x27, starting transfers between devices, exchange(): return lax.ppermute(value, axis, [(i, i ^ mask) for i in range(size)])  28.2 us
    ppermute x27, waiting for transfers between devices, exchange(): return lax.ppermute(value, axis, [(i, i ^ mask) for i in range(size)])  21.8 us
    pallas_call x1, Pallas kernels, on_device(): pl.pallas_call(partial(forward_kernel, groups, chips, places), out_shape=...  3.45 us
    unnamed x8, local copies, waits for them, and re-layouts  2.56 us
    pallas_call x1, Pallas kernels, on_device(): pl.pallas_call(partial(pre_kernel, parts), out_shape=[spec((shard, column...  2.29 us
    pallas_call x1, Pallas kernels, on_device(): pl.pallas_call(partial(backward_kernel, groups, chips[::-1]), out_shape=[...  1.66 us
  transfers between devices with their start and end apart: 27, of which 15 were waited for; matrix products, arithmetic and copies ran while one was open for 1% of the time, Pallas kernels for 8%

profile of v7, /device:TPU:0, one launch (start us, length us, event | category | flops | bytes accessed | tf_op | source)
XLA Modules:
  0.0 65.9 jit_solution(10698922974126739897)
XLA Ops:
  0.6 2.3 %pre.1 = (bf16[64,2560]{1,0:T(8,128)(2,1)}, s32[8,128]{1,0:T(8,128)}, bf16[2,64,512]{2,1,0:T(8,128)(2,1)}, bf16[2,64,512]{2,1,0:T(8,128)(2,1)}, bf16[2,64,512]{2...) custom-call(s32[1,32]{1,0:T(1,128)} %bitcast.8, s32[1,32]{1,0:T(1,128)} %bitcast.12, s32[1,8]{1,0:T(1,128)} %bitcast.13, ...), custom_call_target="tpu_custom_call" | custom-call | tf_op jit(solution)/shard_map/pre/pallas_call | solution.py:347
  2.9 3.0 %collective-permute-start = (bf16[64,2560]{1,0:T(8,128)(2,1)}, bf16[64,2560]{1,0:T(8,128)(2,1)S(1)}, u32[]{:S(2)}, u32[]{:S(2)}) collective-permute-start(bf16[64,2560]{1,0:T(8,128)(2,1)} %get-tuple-element.65.w_ref), channel_id=1, source_target_pairs={{0,8},{4,12},{8,0},{12,4},{16,24},{20,28},{24,16},{28,20},{1,9},{5... | collective-permute-start | bytes 983048 | tf_op jit(solution)/shard_map/ppermute | solution.py:39
  5.9 1.5 %collective-permute-start.1 = (bf16[64,2560]{1,0:T(8,128)(2,1)}, bf16[64,2560]{1,0:T(8,128)(2,1)S(1)}, u32[]{:S(2)}, u32[]{:S(2)}) collective-permute-start(bf16[64,2560]{1,0:T(8,128)(2,1)} %get-tuple-element.65.w_ref), channel_id=1, source_target_pairs={{0,16},{4,20},{8,24},{12,28},{16,0},{20,4},{24,8},{28,12},{1,17},{... | collective-permute-start | bytes 983048 | tf_op jit(solution)/shard_map/ppermute | solution.py:39
  7.5 1.6 %collective-permute-start.2 = (bf16[2,64,512]{2,1,0:T(8,128)(2,1)}, bf16[2,64,512]{2,1,0:T(8,128)(2,1)S(1)}, u32[]{:S(2)}, u32[]{:S(2)}) collective-permute-start(bf16[2,64,512]{2,1,0:T(8,128)(2,1)} %get-tuple-element.68), channel_id=1, source_target_pairs={{0,1},{1,0},{2,3},{3,2},{4,5},{5,4},{6,7},{7,6},{8,9},{9,8},{10,11... | collective-permute-start | bytes 393224 | tf_op jit(solution)/shard_map/ppermute | solution.py:39
  9.0 2.6 %collective-permute-start.5 = (bf16[2,64,512]{2,1,0:T(8,128)(2,1)}, bf16[2,64,512]{2,1,0:T(8,128)(2,1)S(1)}, u32[]{:S(2)}, u32[]{:S(2)}) collective-permute-start(bf16[2,64,512]{2,1,0:T(8,128)(2,1)} %get-tuple-element.75), channel_id=1, source_target_pairs={{0,2},{1,3},{2,0},{3,1},{4,6},{5,7},{6,4},{7,5},{8,10},{9,11},{10,... | collective-permute-start | bytes 393224 | tf_op jit(solution)/shard_map/ppermute | solution.py:39
  11.6 0.2 collective-permute-start.6
  11.8 1.0 %copy-done = bf16[64,2560]{1,0:T(8,128)(2,1)S(1)} copy-done((bf16[64,2560]{1,0:T(8,128)(2,1)S(1)}, bf16[64,2560]{1,0:T(8,128)(2,1)}, u32[]{:S(2)}) %copy-start) | copy-done | bytes 327704
  12.8 0.9 %copy-done.1 = bf16[2,64,512]{2,1,0:T(8,128)(2,1)S(1)} copy-done((bf16[2,64,512]{2,1,0:T(8,128)(2,1)S(1)}, bf16[2,64,512]{2,1,0:T(8,128)(2,1)}, u32[]{:S(2)}) %copy-start.1) | copy-done | bytes 131096
  13.7 0.7 %copy-done.2 = s32[8,128]{1,0:T(8,128)S(1)} copy-done((s32[8,128]{1,0:T(8,128)S(1)}, s32[8,128]{1,0:T(8,128)}, u32[]{:S(2)}) %copy-start.2) | copy-done | bytes 4120
  14.4 0.7 %plan.1 = (bf16[256,256]{1,0:T(8,128)(2,1)S(1)}, f32[256,256]{1,0:T(8,128)S(1)}, bf16[64,2560]{1,0:T(8,128)(2,1)S(1)}, bf16[2,64,512]{2,1,0:T(8,128)(2,1)S(1)}) custom-call(s32[8,128]{1,0:T(8,128)S(1)} %copy-done.2, bf16[64,2560]{1,0:T(8,128)(2,1)S(1)} %copy-done, bf16[2,64,512]{2,1,0:T(8,128)(2,1)S(1)} %copy-done.1), custom_call_target="tpu_custom_call" | custom-call | tf_op jit(solution)/shard_map/plan/pallas_call | solution.py:369
  15.2 0.2 collective-permute-done.1.refs_4_
  15.3 0.5 collective-permute-start.3
  15.8 1.7 %collective-permute-start.4 = (bf16[64,1280]{1,0:T(8,128)(2,1)S(1)}, bf16[64,1280]{1,0:T(8,128)(2,1)S(1)}, u32[]{:S(2)}, u32[]{:S(2)}) collective-permute-start(bf16[64,1280]{1,0:T(8,128)(2,1)S(1)} %slice.41), channel_id=1, source_target_pairs={{0,16},{4,20},{8,24},{12,28},{16,0},{20,4},{24,8},{28,12},{1,17},{... | collective-permute-start | bytes 491528 | tf_op jit(solution)/shard_map/ppermute | solution.py:39
  17.5 4.1 %collective-permute-done.5.refs_2_ = bf16[2,64,512]{2,1,0:T(8,128)(2,1)S(1)} collective-permute-done((bf16[2,64,512]{2,1,0:T(8,128)(2,1)}, bf16[2,64,512]{2,1,0:T(8,128)(2,1)S(1)}, u32[]{:S(2)}, u32[]{:S(2)}) %collective-permute-start.5) | collective-permute-done | bytes 131104 | tf_op jit(solution)/shard_map/ppermute | solution.py:39
  21.6 0.5 collective-permute-start.9
  22.2 0.4 collective-permute-start.11
  22.6 0.5 norm.1
  23.2 0.5 collective-permute-done.9.refs_5_
  23.7 0.2 collective-permute-done.10.refs_8_
  23.9 0.2 collective-permute-done.11.refs_9_
  24.2 3.4 %forward.1 = (bf16[256,1408]{1,0:T(8,128)(2,1)S(1)}, bf16[256,1408]{1,0:T(8,128)(2,1)S(1)}, bf16[256,512]{1,0:T(8,128)(2,1)S(1)}, bf16[512,2560]{1,0:T(8,128)(2,...) custom-call(f32[256,256]{1,0:T(8,128)S(1)} %get-tuple-element.71.sca, ...), custom_call_target="tpu_custom_call" | custom-call | tf_op jit(solution)/shard_map/forward/pallas_call | solution.py:416
  27.6 0.2 collective-permute-start.12
  27.8 1.7 %backward.1 = (bf16[256,1152]{1,0:T(8,128)(2,1)S(1)}, bf16[256,1152]{1,0:T(8,128)(2,1)S(1)}, bf16[256,2048]{1,0:T(8,128)(2,1)S(1)}) custom-call(bf16[512,256]{1,0:T(8,128)(2,1)S(1)} %get-tuple-element.82.xt_ref, bf16[256,2048]{1,0:T(8,128)(2,1)S(1)} %get-tuple-element.90.act_ref, f32[256,2048]{1,0:T(8,128)S(1)} %get-tuple-element.91.slope_ref, ...), custom_call_target="tpu_custom_call" | custom-call | tf_op jit(solution)/shard_map/backward/pallas_call | solution.py:441
  29.5 0.4 collective-permute-done.12
  30.0 0.2 add_convert_fusion
  30.2 0.6 collective-permute-start.13
  30.8 1.1 %rows.1 = (bf16[2,64,512]{2,1,0:T(8,128)(2,1)S(1)}, bf16[2,64,512]{2,1,0:T(8,128)(2,1)S(1)}, bf16[2,64,512]{2,1,0:T(8,128)(2,1)S(1)}, bf16[2,64,512]{2,1,0:T(8,128)(2,1)S(1)}) custom-call(bf16[256,256]{1,0:T(8,128)(2,1)S(1)} %get-tuple-element.72.matrix_ref, bf16[256,2048]{1,0:T(8,128)(2,1)S(1)} %get-tuple-element.101.gproj_ref, ...), custom_call_target="tpu_custom_call" | custom-call | tf_op jit(solution)/shard_map/rows/pallas_call | solution.py:480
  32.1 1.6 %collective-permute-start.15 = (bf16[2,64,512]{2,1,0:T(8,128)(2,1)S(1)}, bf16[2,64,512]{2,1,0:T(8,128)(2,1)S(1)}, u32[]{:S(2)}, u32[]{:S(2)}) collective-permute-start(bf16[2,64,512]{2,1,0:T(8,128)(2,1)S(1)} %get-tuple-element.109), channel_id=1, source_target_pairs={{0,1},{1,0},{2,3},{3,2},{4,5},{5,4},{6,7},{7,6},{8,9},{9,8},{10,11... | collective-permute-start | bytes 393224 | tf_op jit(solution)/shard_map/ppermute | solution.py:39
  33.7 1.5 %collective-permute-start.22 = (bf16[128,1152]{1,0:T(8,128)(2,1)S(1)}, bf16[128,1152]{1,0:T(8,128)(2,1)S(1)}, u32[]{:S(2)}, u32[]{:S(2)}) collective-permute-start(bf16[128,1152]{1,0:T(8,128)(2,1)S(1)} %slice.37), channel_id=1, source_target_pairs={{0,16},{4,20},{8,24},{12,28},{16,0},{20,4},{24,8},{28,12},{1,17},{... | collective-permute-start | bytes 884744 | tf_op jit(solution)/shard_map/ppermute | solution.py:39
  35.2 2.6 %collective-permute-start.20 = (bf16[2,64,512]{2,1,0:T(8,128)(2,1)S(1)}, bf16[2,64,512]{2,1,0:T(8,128)(2,1)S(1)}, u32[]{:S(2)}, u32[]{:S(2)}) collective-permute-start(bf16[2,64,512]{2,1,0:T(8,128)(2,1)S(1)} %get-tuple-element.113), channel_id=1, source_target_pairs={{0,2},{1,3},{2,0},{3,1},{4,6},{5,7},{6,4},{7,5},{8,10},{9,11},{10,... | collective-permute-start | bytes 393224 | tf_op jit(solution)/shard_map/ppermute | solution.py:39
  37.8 0.2 collective-permute-start.21
  38.0 3.0 %collective-permute-done.13 = bf16[128,1408]{1,0:T(8,128)(2,1)S(1)} collective-permute-done((bf16[128,1408]{1,0:T(8,128)(2,1)S(1)}, bf16[128,1408]{1,0:T(8,128)(2,1)S(1)}, u32[]{:S(2)}, u32[]{:S(2)}) %collective-permute-start.13) | collective-permute-done | bytes 360480 | tf_op jit(solution)/shard_map/ppermute | solution.py:39
  41.1 0.6 collective-permute-start.16
  41.7 0.8 %collective-permute-done.22 = bf16[128,1152]{1,0:T(8,128)(2,1)S(1)} collective-permute-done((bf16[128,1152]{1,0:T(8,128)(2,1)S(1)}, bf16[128,1152]{1,0:T(8,128)(2,1)S(1)}, u32[]{:S(2)}, u32[]{:S(2)}) %collective-permute-start.22) | collective-permute-done | bytes 294944 | tf_op jit(solution)/shard_map/ppermute | solution.py:39
  42.6 1.6 %collective-permute-start.23 = (bf16[64,1152]{1,0:T(8,128)(2,1)S(1)}, bf16[64,1152]{1,0:T(8,128)(2,1)S(1)}, u32[]{:S(2)}, u32[]{:S(2)}) collective-permute-start(bf16[64,1152]{1,0:T(8,128)(2,1)S(1)} %slice.45), channel_id=1, source_target_pairs={{0,8},{4,12},{8,0},{12,4},{16,24},{20,28},{24,16},{28,20},{1,9},{5... | collective-permute-start | bytes 442376 | tf_op jit(solution)/shard_map/ppermute | solution.py:39
  44.1 3.0 %collective-permute-done.16 = bf16[64,1408]{1,0:T(8,128)(2,1)S(1)} collective-permute-done((bf16[64,1408]{1,0:T(8,128)(2,1)S(1)}, bf16[64,1408]{1,0:T(8,128)(2,1)S(1)}, u32[]{:S(2)}, u32[]{:S(2)}) %collective-permute-start.16) | collective-permute-done | bytes 180256 | tf_op jit(solution)/shard_map/ppermute | solution.py:39
  47.2 1.6 %collective-permute-start.17 = (bf16[32,1408]{1,0:T(8,128)(2,1)S(1)}, bf16[32,1408]{1,0:T(8,128)(2,1)S(1)}, u32[]{:S(2)}, u32[]{:S(2)}) collective-permute-start(bf16[32,1408]{1,0:T(8,128)(2,1)S(1)} %constant_dynamic-slice_fusion.1), channel_id=1, source_target_pairs={{0,1},{1,0},{2,3},{3,2},{4,5},{5,4},{6,7},{7,6},{8,9},{9,8},{10,11... | collective-permute-start | bytes 270344 | tf_op jit(solution)/shard_map/ppermute | solution.py:39
  48.9 0.6 collective-permute-start.24
  49.5 2.4 %collective-permute-done.17 = bf16[32,1408]{1,0:T(8,128)(2,1)S(1)} collective-permute-done((bf16[32,1408]{1,0:T(8,128)(2,1)S(1)}, bf16[32,1408]{1,0:T(8,128)(2,1)S(1)}, u32[]{:S(2)}, u32[]{:S(2)}) %collective-permute-start.17) | collective-permute-done | bytes 90144 | tf_op jit(solution)/shard_map/ppermute | solution.py:39
  51.9 2.6 %collective-permute-start.18 = (bf16[32,1408]{1,0:T(8,128)(2,1)S(1)}, bf16[32,1408]{1,0:T(8,128)(2,1)S(1)}, u32[]{:S(2)}, u32[]{:S(2)}) collective-permute-start(bf16[32,1408]{1,0:T(8,128)(2,1)S(1)} %add_convert_fusion.7), channel_id=1, source_target_pairs={{0,2},{1,3},{2,0},{3,1},{4,6},{5,7},{6,4},{7,5},{8,10},{9,11},{10,... | collective-permute-start | bytes 270344 | tf_op jit(solution)/shard_map/ppermute | solution.py:39
  54.5 1.5 %collective-permute-start.25 = (bf16[32,1152]{1,0:T(8,128)(2,1)S(1)}, bf16[32,1152]{1,0:T(8,128)(2,1)S(1)}, u32[]{:S(2)}, u32[]{:S(2)}) collective-permute-start(bf16[32,1152]{1,0:T(8,128)(2,1)S(1)} %add_convert_fusion.9), channel_id=1, source_target_pairs={{0,2},{1,3},{2,0},{3,1},{4,6},{5,7},{6,4},{7,5},{8,10},{9,11},{10,... | collective-permute-start | bytes 221192 | tf_op jit(solution)/shard_map/ppermute | solution.py:39
  55.9 3.3 %collective-permute-done.18 = bf16[32,1408]{1,0:T(8,128)(2,1)S(1)} collective-permute-done((bf16[32,1408]{1,0:T(8,128)(2,1)S(1)}, bf16[32,1408]{1,0:T(8,128)(2,1)S(1)}, u32[]{:S(2)}, u32[]{:S(2)}) %collective-permute-start.18) | collective-permute-done | bytes 90144 | tf_op jit(solution)/shard_map/ppermute | solution.py:39
  59.3 1.3 %collective-permute-done.25 = bf16[32,1152]{1,0:T(8,128)(2,1)S(1)} collective-permute-done((bf16[32,1152]{1,0:T(8,128)(2,1)S(1)}, bf16[32,1152]{1,0:T(8,128)(2,1)S(1)}, u32[]{:S(2)}, u32[]{:S(2)}) %collective-permute-start.25) | collective-permute-done | bytes 73760 | tf_op jit(solution)/shard_map/ppermute | solution.py:39
  60.6 0.8 %collective-permute-start.26 = (bf16[32,1152]{1,0:T(8,128)(2,1)S(1)}, bf16[32,1152]{1,0:T(8,128)(2,1)S(1)}, u32[]{:S(2)}, u32[]{:S(2)}) collective-permute-start(bf16[32,1152]{1,0:T(8,128)(2,1)S(1)} %add_convert_fusion.8.late_own), channel_id=1, source_target_pairs={{0,1},{1,0},{2,3},{3,2},{4,5},{5,4},{6,7},{7,6},{8,9},{9,8},{10,11... | collective-permute-start | bytes 221192 | tf_op jit(solution)/shard_map/ppermute | solution.py:39
  61.4 1.2 %post.1 = (bf16[256,512]{1,0:T(8,128)(2,1)}, bf16[256,512]{1,0:T(8,128)(2,1)}) custom-call(s32[1,32]{1,0:T(1,128)S(1)} %bitcast.9, bf16[2,64,512]{2,1,0:T(8,128)(2,1)S(1)} %get-tuple-element.111.refs_0_, bf16[2,64,512]{2,1,0:T(8,128)(2,1)S(1)} %collective-permute-done.15.refs_1_, bf16[2,64,512]{2,1,0:T(8,128)(2,1)S(1)} %collective-permute-done.20.refs_2_, ...), custom_call_target="tpu_custom_call" | custom-call | tf_op jit(solution)/shard_map/post/pallas_call | solution.py:491
  62.6 1.2 %collective-permute-done.19.early_other = bf16[32,1408]{1,0:T(8,128)(2,1)S(1)} collective-permute-done((bf16[32,1408]{1,0:T(8,128)(2,1)S(1)}, bf16[32,1408]{1,0:T(8,128)(2,1)S(1)}, u32[]{:S(2)}, u32[]{:S(2)}) %collective-permute-start.19) | collective-permute-done | bytes 90144 | tf_op jit(solution)/shard_map/ppermute | solution.py:39
  63.8 1.2 %collective-permute-done.26.late_other = bf16[32,1152]{1,0:T(8,128)(2,1)S(1)} collective-permute-done((bf16[32,1152]{1,0:T(8,128)(2,1)S(1)}, bf16[32,1152]{1,0:T(8,128)(2,1)S(1)}, u32[]{:S(2)}, u32[]{:S(2)}) %collective-permute-start.26) | collective-permute-done | bytes 73760 | tf_op jit(solution)/shard_map/ppermute | solution.py:39
  65.0 0.9 %finish.1 = (f32[64,2048]{1,0:T(8,128)}, f32[64,512]{1,0:T(8,128)}) custom-call(bf16[32,1408]{1,0:T(8,128)(2,1)S(1)} %add_convert_fusion.6.early_own, bf16[32,1408]{1,0:T(8,128)(2,1)S(1)} %collective-permute-done.19.early_other, bf16[32,1152]{1,0:T(8,128)(2,1)S(1)} %add_convert_fusion.8.late_own, bf16[32,1152]{1,0:T(8,128)(2,1)S(1)} %collective-permute-done.26.late_other), custom_call_target="tpu_custom_call" | custom-call | tf_op jit(solution)/shard_map/finish/pallas_call | solution.py:503
  (40 shorter events, 1.0 us)
Async XLA Ops:
  2.9 12.2 %collective-permute-start = (bf16[64,2560]{1,0:T(8,128)(2,1)}, bf16[64,2560]{1,0:T(8,128)(2,1)S(1)}, u32[]{:S(2)}, u32[]{:S(2)}) collective-permute-start(bf16[64,2560]{1,0:T(8,128)(2,1)} %get-tuple-element.65.w_ref), channel_id=1, source_target_pairs={{0,8},{4,12},{8,0},{12,4},{16,24},{20,28},{24,16},{28,20},{1,9},{5... | collective-permute-start | bytes 983048 | tf_op jit(solution)/shard_map/ppermute | solution.py:39
  5.9 9.4 %collective-permute-start.1 = (bf16[64,2560]{1,0:T(8,128)(2,1)}, bf16[64,2560]{1,0:T(8,128)(2,1)S(1)}, u32[]{:S(2)}, u32[]{:S(2)}) collective-permute-start(bf16[64,2560]{1,0:T(8,128)(2,1)} %get-tuple-element.65.w_ref), channel_id=1, source_target_pairs={{0,16},{4,20},{8,24},{12,28},{16,0},{20,4},{24,8},{28,12},{1,17},{... | collective-permute-start | bytes 983048 | tf_op jit(solution)/shard_map/ppermute | solution.py:39
  7.5 7.7 %collective-permute-start.2 = (bf16[2,64,512]{2,1,0:T(8,128)(2,1)}, bf16[2,64,512]{2,1,0:T(8,128)(2,1)S(1)}, u32[]{:S(2)}, u32[]{:S(2)}) collective-permute-start(bf16[2,64,512]{2,1,0:T(8,128)(2,1)} %get-tuple-element.68), channel_id=1, source_target_pairs={{0,1},{1,0},{2,3},{3,2},{4,5},{5,4},{6,7},{7,6},{8,9},{9,8},{10,11... | collective-permute-start | bytes 393224 | tf_op jit(solution)/shard_map/ppermute | solution.py:39
  9.0 12.6 %collective-permute-start.5 = (bf16[2,64,512]{2,1,0:T(8,128)(2,1)}, bf16[2,64,512]{2,1,0:T(8,128)(2,1)S(1)}, u32[]{:S(2)}, u32[]{:S(2)}) collective-permute-start(bf16[2,64,512]{2,1,0:T(8,128)(2,1)} %get-tuple-element.75), channel_id=1, source_target_pairs={{0,2},{1,3},{2,0},{3,1},{4,6},{5,7},{6,4},{7,5},{8,10},{9,11},{10,... | collective-permute-start | bytes 393224 | tf_op jit(solution)/shard_map/ppermute | solution.py:39
  11.6 10.0 %collective-permute-start.6 = (bf16[2,64,512]{2,1,0:T(8,128)(2,1)}, bf16[2,64,512]{2,1,0:T(8,128)(2,1)S(1)}, u32[]{:S(2)}, u32[]{:S(2)}) collective-permute-start(bf16[2,64,512]{2,1,0:T(8,128)(2,1)} %get-tuple-element.76), channel_id=1, source_target_pairs={{0,3},{1,2},{2,1},{3,0},{4,7},{5,6},{6,5},{7,4},{8,11},{9,10},{10,... | collective-permute-start | bytes 393224 | tf_op jit(solution)/shard_map/ppermute | solution.py:39
  11.8 1.0 %copy-start = (bf16[64,2560]{1,0:T(8,128)(2,1)S(1)}, bf16[64,2560]{1,0:T(8,128)(2,1)}, u32[]{:S(2)}) copy-start(bf16[64,2560]{1,0:T(8,128)(2,1)} %get-tuple-element.65.w_ref) | copy-start | bytes 983044
  12.8 0.9 %copy-start.1 = (bf16[2,64,512]{2,1,0:T(8,128)(2,1)S(1)}, bf16[2,64,512]{2,1,0:T(8,128)(2,1)}, u32[]{:S(2)}) copy-start(bf16[2,64,512]{2,1,0:T(8,128)(2,1)} %get-tuple-element.66.own_ref) | copy-start | bytes 393220
  13.7 0.7 %copy-start.2 = (s32[8,128]{1,0:T(8,128)S(1)}, s32[8,128]{1,0:T(8,128)}, u32[]{:S(2)}) copy-start(s32[8,128]{1,0:T(8,128)} %get-tuple-element.64.small_ref) | copy-start | bytes 12292
  15.3 6.8 %collective-permute-start.3 = (bf16[64,1280]{1,0:T(8,128)(2,1)S(1)}, bf16[64,1280]{1,0:T(8,128)(2,1)S(1)}, u32[]{:S(2)}, u32[]{:S(2)}) collective-permute-start(bf16[64,1280]{1,0:T(8,128)(2,1)S(1)} %slice.40), channel_id=1, source_target_pairs={{0,8},{4,12},{8,0},{12,4},{16,24},{20,28},{24,16},{28,20},{1,9},{5... | collective-permute-start | bytes 491528 | tf_op jit(solution)/shard_map/ppermute | solution.py:39
  15.8 6.3 %collective-permute-start.4 = (bf16[64,1280]{1,0:T(8,128)(2,1)S(1)}, bf16[64,1280]{1,0:T(8,128)(2,1)S(1)}, u32[]{:S(2)}, u32[]{:S(2)}) collective-permute-start(bf16[64,1280]{1,0:T(8,128)(2,1)S(1)} %slice.41), channel_id=1, source_target_pairs={{0,16},{4,20},{8,24},{12,28},{16,0},{20,4},{24,8},{28,12},{1,17},{... | collective-permute-start | bytes 491528 | tf_op jit(solution)/shard_map/ppermute | solution.py:39
  17.5 5.6 %collective-permute-start.7 = (bf16[64,2560]{1,0:T(8,128)(2,1)S(1)}, bf16[64,2560]{1,0:T(8,128)(2,1)S(1)}, u32[]{:S(2)}, u32[]{:S(2)}) collective-permute-start(bf16[64,2560]{1,0:T(8,128)(2,1)S(1)} %get-tuple-element.83.refs_0_), channel_id=1, source_target_pairs={{0,4},{4,0},{8,12},{12,8},{16,20},{20,16},{24,28},{28,24},{1,5},{5... | collective-permute-start | bytes 983048 | tf_op jit(solution)/shard_map/ppermute | solution.py:39
  21.6 1.6 %collective-permute-start.8 = (bf16[64,2560]{1,0:T(8,128)(2,1)S(1)}, bf16[64,2560]{1,0:T(8,128)(2,1)S(1)}, u32[]{:S(2)}, u32[]{:S(2)}) collective-permute-start(bf16[64,2560]{1,0:T(8,128)(2,1)S(1)} %collective-permute-done.refs_2_), channel_id=1, source_target_pairs={{0,4},{4,0},{8,12},{12,8},{16,20},{20,16},{24,28},{28,24},{1,5},{5... | collective-permute-start | bytes 983048 | tf_op jit(solution)/shard_map/ppermute | solution.py:39
  21.6 2.1 %collective-permute-start.9 = (bf16[64,2560]{1,0:T(8,128)(2,1)S(1)}, bf16[64,2560]{1,0:T(8,128)(2,1)S(1)}, u32[]{:S(2)}, u32[]{:S(2)}) collective-permute-start(bf16[64,2560]{1,0:T(8,128)(2,1)S(1)} %collective-permute-done.1.refs_4_), channel_id=1, source_target_pairs={{0,4},{4,0},{8,12},{12,8},{16,20},{20,16},{24,28},{28,24},{1,5},{5... | collective-permute-start | bytes 983048 | tf_op jit(solution)/shard_map/ppermute | solution.py:39
  22.1 1.8 %collective-permute-start.10 = (bf16[64,1280]{1,0:T(8,128)(2,1)S(1)}, bf16[64,1280]{1,0:T(8,128)(2,1)S(1)}, u32[]{:S(2)}, u32[]{:S(2)}) collective-permute-start(bf16[64,1280]{1,0:T(8,128)(2,1)S(1)} %collective-permute-done.3.refs_6_), channel_id=1, source_target_pairs={{0,4},{4,0},{8,12},{12,8},{16,20},{20,16},{24,28},{28,24},{1,5},{5... | collective-permute-start | bytes 491528 | tf_op jit(solution)/shard_map/ppermute | solution.py:39
  22.2 2.0 %collective-permute-start.11 = (bf16[64,1280]{1,0:T(8,128)(2,1)S(1)}, bf16[64,1280]{1,0:T(8,128)(2,1)S(1)}, u32[]{:S(2)}, u32[]{:S(2)}) collective-permute-start(bf16[64,1280]{1,0:T(8,128)(2,1)S(1)} %collective-permute-done.4.refs_7_), channel_id=1, source_target_pairs={{0,4},{4,0},{8,12},{12,8},{16,20},{20,16},{24,28},{28,24},{1,5},{5... | collective-permute-start | bytes 491528 | tf_op jit(solution)/shard_map/ppermute | solution.py:39
  27.6 2.3 %collective-permute-start.12 = (bf16[256,1408]{1,0:T(8,128)(2,1)S(1)}, bf16[256,1408]{1,0:T(8,128)(2,1)S(1)}, u32[]{:S(2)}, u32[]{:S(2)}) collective-permute-start(bf16[256,1408]{1,0:T(8,128)(2,1)S(1)} %get-tuple-element.89), channel_id=1, source_target_pairs={{0,4},{4,0},{8,12},{12,8},{16,20},{20,16},{24,28},{28,24},{1,5},{5... | collective-permute-start | bytes 2162696 | tf_op jit(solution)/shard_map/ppermute | solution.py:39
  29.9 2.1 %collective-permute-start.14 = (bf16[256,1152]{1,0:T(8,128)(2,1)S(1)}, bf16[256,1152]{1,0:T(8,128)(2,1)S(1)}, u32[]{:S(2)}, u32[]{:S(2)}) collective-permute-start(bf16[256,1152]{1,0:T(8,128)(2,1)S(1)} %get-tuple-element.100), channel_id=1, source_target_pairs={{0,4},{4,0},{8,12},{12,8},{16,20},{20,16},{24,28},{28,24},{1,5},{5... | collective-permute-start | bytes 1769480 | tf_op jit(solution)/shard_map/ppermute | solution.py:39
  30.2 10.8 %collective-permute-start.13 = (bf16[128,1408]{1,0:T(8,128)(2,1)S(1)}, bf16[128,1408]{1,0:T(8,128)(2,1)S(1)}, u32[]{:S(2)}, u32[]{:S(2)}) collective-permute-start(bf16[128,1408]{1,0:T(8,128)(2,1)S(1)} %slice.33), channel_id=1, source_target_pairs={{0,8},{4,12},{8,0},{12,4},{16,24},{20,28},{24,16},{28,20},{1,9},{5... | collective-permute-start | bytes 1081352 | tf_op jit(solution)/shard_map/ppermute | solution.py:39
  32.1 8.9 %collective-permute-start.15 = (bf16[2,64,512]{2,1,0:T(8,128)(2,1)S(1)}, bf16[2,64,512]{2,1,0:T(8,128)(2,1)S(1)}, u32[]{:S(2)}, u32[]{:S(2)}) collective-permute-start(bf16[2,64,512]{2,1,0:T(8,128)(2,1)S(1)} %get-tuple-element.109), channel_id=1, source_target_pairs={{0,1},{1,0},{2,3},{3,2},{4,5},{5,4},{6,7},{7,6},{8,9},{9,8},{10,11... | collective-permute-start | bytes 393224 | tf_op jit(solution)/shard_map/ppermute | solution.py:39
  33.7 8.8 %collective-permute-start.22 = (bf16[128,1152]{1,0:T(8,128)(2,1)S(1)}, bf16[128,1152]{1,0:T(8,128)(2,1)S(1)}, u32[]{:S(2)}, u32[]{:S(2)}) collective-permute-start(bf16[128,1152]{1,0:T(8,128)(2,1)S(1)} %slice.37), channel_id=1, source_target_pairs={{0,16},{4,20},{8,24},{12,28},{16,0},{20,4},{24,8},{28,12},{1,17},{... | collective-permute-start | bytes 884744 | tf_op jit(solution)/shard_map/ppermute | solution.py:39
  35.2 26.2 %collective-permute-start.20 = (bf16[2,64,512]{2,1,0:T(8,128)(2,1)S(1)}, bf16[2,64,512]{2,1,0:T(8,128)(2,1)S(1)}, u32[]{:S(2)}, u32[]{:S(2)}) collective-permute-start(bf16[2,64,512]{2,1,0:T(8,128)(2,1)S(1)} %get-tuple-element.113), channel_id=1, source_target_pairs={{0,2},{1,3},{2,0},{3,1},{4,6},{5,7},{6,4},{7,5},{8,10},{9,11},{10,... | collective-permute-start | bytes 393224 | tf_op jit(solution)/shard_map/ppermute | solution.py:39
  37.8 23.6 %collective-permute-start.21 = (bf16[2,64,512]{2,1,0:T(8,128)(2,1)S(1)}, bf16[2,64,512]{2,1,0:T(8,128)(2,1)S(1)}, u32[]{:S(2)}, u32[]{:S(2)}) collective-permute-start(bf16[2,64,512]{2,1,0:T(8,128)(2,1)S(1)} %get-tuple-element.114), channel_id=1, source_target_pairs={{0,3},{1,2},{2,1},{3,0},{4,7},{5,6},{6,5},{7,4},{8,11},{9,10},{10,... | collective-permute-start | bytes 393224 | tf_op jit(solution)/shard_map/ppermute | solution.py:39
  41.1 6.1 %collective-permute-start.16 = (bf16[64,1408]{1,0:T(8,128)(2,1)S(1)}, bf16[64,1408]{1,0:T(8,128)(2,1)S(1)}, u32[]{:S(2)}, u32[]{:S(2)}) collective-permute-start(bf16[64,1408]{1,0:T(8,128)(2,1)S(1)} %slice.43), channel_id=1, source_target_pairs={{0,16},{4,20},{8,24},{12,28},{16,0},{20,4},{24,8},{28,12},{1,17},{... | collective-permute-start | bytes 540680 | tf_op jit(solution)/shard_map/ppermute | solution.py:39
  42.5 18.9 %copy-start.3 = (s32[1,1,32]{2,1,0:T(1,128)S(1)}, s32[1,1,32]{2,1,0:T(1,128)}, u32[]{:S(2)}) copy-start(s32[1,1,32]{2,1,0:T(1,128)} %param.12) | copy-start | bytes 388
  42.6 6.2 %collective-permute-start.23 = (bf16[64,1152]{1,0:T(8,128)(2,1)S(1)}, bf16[64,1152]{1,0:T(8,128)(2,1)S(1)}, u32[]{:S(2)}, u32[]{:S(2)}) collective-permute-start(bf16[64,1152]{1,0:T(8,128)(2,1)S(1)} %slice.45), channel_id=1, source_target_pairs={{0,8},{4,12},{8,0},{12,4},{16,24},{20,28},{24,16},{28,20},{1,9},{5... | collective-permute-start | bytes 442376 | tf_op jit(solution)/shard_map/ppermute | solution.py:39
  47.2 4.6 %collective-permute-start.17 = (bf16[32,1408]{1,0:T(8,128)(2,1)S(1)}, bf16[32,1408]{1,0:T(8,128)(2,1)S(1)}, u32[]{:S(2)}, u32[]{:S(2)}) collective-permute-start(bf16[32,1408]{1,0:T(8,128)(2,1)S(1)} %constant_dynamic-slice_fusion.1), channel_id=1, source_target_pairs={{0,1},{1,0},{2,3},{3,2},{4,5},{5,4},{6,7},{7,6},{8,9},{9,8},{10,11... | collective-permute-start | bytes 270344 | tf_op jit(solution)/shard_map/ppermute | solution.py:39
  48.9 5.6 %collective-permute-start.24 = (bf16[32,1152]{1,0:T(8,128)(2,1)S(1)}, bf16[32,1152]{1,0:T(8,128)(2,1)S(1)}, u32[]{:S(2)}, u32[]{:S(2)}) collective-permute-start(bf16[32,1152]{1,0:T(8,128)(2,1)S(1)} %constant_dynamic-slice_fusion), channel_id=1, source_target_pairs={{0,1},{1,0},{2,3},{3,2},{4,5},{5,4},{6,7},{7,6},{8,9},{9,8},{10,11... | collective-permute-start | bytes 221192 | tf_op jit(solution)/shard_map/ppermute | solution.py:39
  51.9 7.3 %collective-permute-start.18 = (bf16[32,1408]{1,0:T(8,128)(2,1)S(1)}, bf16[32,1408]{1,0:T(8,128)(2,1)S(1)}, u32[]{:S(2)}, u32[]{:S(2)}) collective-permute-start(bf16[32,1408]{1,0:T(8,128)(2,1)S(1)} %add_convert_fusion.7), channel_id=1, source_target_pairs={{0,2},{1,3},{2,0},{3,1},{4,6},{5,7},{6,4},{7,5},{8,10},{9,11},{10,... | collective-permute-start | bytes 270344 | tf_op jit(solution)/shard_map/ppermute | solution.py:39
  54.5 6.1 %collective-permute-start.25 = (bf16[32,1152]{1,0:T(8,128)(2,1)S(1)}, bf16[32,1152]{1,0:T(8,128)(2,1)S(1)}, u32[]{:S(2)}, u32[]{:S(2)}) collective-permute-start(bf16[32,1152]{1,0:T(8,128)(2,1)S(1)} %add_convert_fusion.9), channel_id=1, source_target_pairs={{0,2},{1,3},{2,0},{3,1},{4,6},{5,7},{6,4},{7,5},{8,10},{9,11},{10,... | collective-permute-start | bytes 221192 | tf_op jit(solution)/shard_map/ppermute | solution.py:39
  59.2 4.6 %collective-permute-start.19 = (bf16[32,1408]{1,0:T(8,128)(2,1)S(1)}, bf16[32,1408]{1,0:T(8,128)(2,1)S(1)}, u32[]{:S(2)}, u32[]{:S(2)}) collective-permute-start(bf16[32,1408]{1,0:T(8,128)(2,1)S(1)} %add_convert_fusion.6.early_own), channel_id=1, source_target_pairs={{0,1},{1,0},{2,3},{3,2},{4,5},{5,4},{6,7},{7,6},{8,9},{9,8},{10,11... | collective-permute-start | bytes 270344 | tf_op jit(solution)/shard_map/ppermute | solution.py:39
  60.6 4.4 %collective-permute-start.26 = (bf16[32,1152]{1,0:T(8,128)(2,1)S(1)}, bf16[32,1152]{1,0:T(8,128)(2,1)S(1)}, u32[]{:S(2)}, u32[]{:S(2)}) collective-permute-start(bf16[32,1152]{1,0:T(8,128)(2,1)S(1)} %add_convert_fusion.8.late_own), channel_id=1, source_target_pairs={{0,1},{1,0},{2,3},{3,2},{4,5},{5,4},{6,7},{7,6},{8,9},{9,8},{10,11... | collective-permute-start | bytes 221192 | tf_op jit(solution)/shard_map/ppermute | solution.py:39

commit v8 on v7

--- a/solution.py
+++ b/solution.py
@@ -381,7 +381,7 @@
     near = list(pieces)
     for k in range(2, groups, 2):
         if k not in chips:
-            for at, mask in ((0, k & -k), (middle, 2 ** (k.bit_length() - 1))):
+            for at, mask in ((0, 2 ** (k.bit_length() - 1)), (middle, k & -k)):
                 source = pieces.get((k ^ mask, at))
                 if (k ^ mask) in chips:
                     source = pieces[k ^ mask, 0][:, at : at + middle]

time: 66.1 us -> 65.4 us (0.989)
  waiting for transfers between devices: 21.8 us -> 20.2 us
  starting transfers between devices: 28.2 us -> 29 us
    ppermute x27, waiting for transfers between devices: 21.8 us -> 20.2 us  [exchange(): return lax.ppermute(value, axis, [(i, i ^ mask) for i in range(size)])]
    ppermute x27, starting transfers between devices: 28.2 us -> 29 us  [exchange(): return lax.ppermute(value, axis, [(i, i ^ mask) for i in range(size)])]
where the time goes in v8:
time: 65.4 us; the launch traced here: 65.2 us
  starting transfers between devices  29 us (44%)
  waiting for transfers between devices  20.2 us (31%)
  Pallas kernels  11.8 us (18%)
  local copies, waits for them, and re-layouts  2.69 us (4%)
  between operations  0.84 us (1%)
  other arithmetic  0.66 us (1%)
    ppermute x27, starting transfers between devices, exchange(): return lax.ppermute(value, axis, [(i, i ^ mask) for i in range(size)])  29 us
    ppermute x27, waiting for transfers between devices, exchange(): return lax.ppermute(value, axis, [(i, i ^ mask) for i in range(size)])  20.2 us
    pallas_call x1, Pallas kernels, on_device(): pl.pallas_call(partial(forward_kernel, groups, chips, places), out_shape=...  3.45 us
    unnamed x8, local copies, waits for them, and re-layouts  2.56 us
    pallas_call x1, Pallas kernels, on_device(): pl.pallas_call(partial(pre_kernel, parts), out_shape=[spec((shard, column...  2.29 us
    pallas_call x1, Pallas kernels, on_device(): pl.pallas_call(partial(backward_kernel, groups, chips[::-1]), out_shape=[...  1.66 us
  transfers between devices with their start and end apart: 27, of which 15 were waited for; matrix products, arithmetic and copies ran while one was open for 1% of the time, Pallas kernels for 8%

profile of v8, /device:TPU:0, one launch (start us, length us, event | category | flops | bytes accessed | tf_op | source)
XLA Modules:
  0.0 65.2 jit_solution(14689606254021377374)
XLA Ops:
  0.6 2.3 %pre.1 = (bf16[64,2560]{1,0:T(8,128)(2,1)}, s32[8,128]{1,0:T(8,128)}, bf16[2,64,512]{2,1,0:T(8,128)(2,1)}, bf16[2,64,512]{2,1,0:T(8,128)(2,1)}, bf16[2,64,512]{2...) custom-call(s32[1,32]{1,0:T(1,128)} %bitcast.8, s32[1,32]{1,0:T(1,128)} %bitcast.12, s32[1,8]{1,0:T(1,128)} %bitcast.13, ...), custom_call_target="tpu_custom_call" | custom-call | tf_op jit(solution)/shard_map/pre/pallas_call | solution.py:347
  2.9 3.0 %collective-permute-start = (bf16[64,2560]{1,0:T(8,128)(2,1)}, bf16[64,2560]{1,0:T(8,128)(2,1)S(1)}, u32[]{:S(2)}, u32[]{:S(2)}) collective-permute-start(bf16[64,2560]{1,0:T(8,128)(2,1)} %get-tuple-element.65.w_ref), channel_id=1, source_target_pairs={{0,8},{4,12},{8,0},{12,4},{16,24},{20,28},{24,16},{28,20},{1,9},{5... | collective-permute-start | bytes 983048 | tf_op jit(solution)/shard_map/ppermute | solution.py:39
  5.9 1.5 %collective-permute-start.1 = (bf16[64,2560]{1,0:T(8,128)(2,1)}, bf16[64,2560]{1,0:T(8,128)(2,1)S(1)}, u32[]{:S(2)}, u32[]{:S(2)}) collective-permute-start(bf16[64,2560]{1,0:T(8,128)(2,1)} %get-tuple-element.65.w_ref), channel_id=1, source_target_pairs={{0,16},{4,20},{8,24},{12,28},{16,0},{20,4},{24,8},{28,12},{1,17},{... | collective-permute-start | bytes 983048 | tf_op jit(solution)/shard_map/ppermute | solution.py:39
  7.5 1.6 %collective-permute-start.2 = (bf16[2,64,512]{2,1,0:T(8,128)(2,1)}, bf16[2,64,512]{2,1,0:T(8,128)(2,1)S(1)}, u32[]{:S(2)}, u32[]{:S(2)}) collective-permute-start(bf16[2,64,512]{2,1,0:T(8,128)(2,1)} %get-tuple-element.68), channel_id=1, source_target_pairs={{0,1},{1,0},{2,3},{3,2},{4,5},{5,4},{6,7},{7,6},{8,9},{9,8},{10,11... | collective-permute-start | bytes 393224 | tf_op jit(solution)/shard_map/ppermute | solution.py:39
  9.0 2.6 %collective-permute-start.5 = (bf16[2,64,512]{2,1,0:T(8,128)(2,1)}, bf16[2,64,512]{2,1,0:T(8,128)(2,1)S(1)}, u32[]{:S(2)}, u32[]{:S(2)}) collective-permute-start(bf16[2,64,512]{2,1,0:T(8,128)(2,1)} %get-tuple-element.75), channel_id=1, source_target_pairs={{0,2},{1,3},{2,0},{3,1},{4,6},{5,7},{6,4},{7,5},{8,10},{9,11},{10,... | collective-permute-start | bytes 393224 | tf_op jit(solution)/shard_map/ppermute | solution.py:39
  11.6 0.2 collective-permute-start.6
  11.8 1.0 %copy-done = bf16[64,2560]{1,0:T(8,128)(2,1)S(1)} copy-done((bf16[64,2560]{1,0:T(8,128)(2,1)S(1)}, bf16[64,2560]{1,0:T(8,128)(2,1)}, u32[]{:S(2)}) %copy-start) | copy-done | bytes 327704
  12.8 0.9 %copy-done.1 = bf16[2,64,512]{2,1,0:T(8,128)(2,1)S(1)} copy-done((bf16[2,64,512]{2,1,0:T(8,128)(2,1)S(1)}, bf16[2,64,512]{2,1,0:T(8,128)(2,1)}, u32[]{:S(2)}) %copy-start.1) | copy-done | bytes 131096
  13.7 0.7 %copy-done.2 = s32[8,128]{1,0:T(8,128)S(1)} copy-done((s32[8,128]{1,0:T(8,128)S(1)}, s32[8,128]{1,0:T(8,128)}, u32[]{:S(2)}) %copy-start.2) | copy-done | bytes 4120
  14.4 0.7 %plan.1 = (bf16[256,256]{1,0:T(8,128)(2,1)S(1)}, f32[256,256]{1,0:T(8,128)S(1)}, bf16[64,2560]{1,0:T(8,128)(2,1)S(1)}, bf16[2,64,512]{2,1,0:T(8,128)(2,1)S(1)}) custom-call(s32[8,128]{1,0:T(8,128)S(1)} %copy-done.2, bf16[64,2560]{1,0:T(8,128)(2,1)S(1)} %copy-done, bf16[2,64,512]{2,1,0:T(8,128)(2,1)S(1)} %copy-done.1), custom_call_target="tpu_custom_call" | custom-call | tf_op jit(solution)/shard_map/plan/pallas_call | solution.py:369
  15.3 1.6 %collective-permute-start.3 = (bf16[64,1280]{1,0:T(8,128)(2,1)S(1)}, bf16[64,1280]{1,0:T(8,128)(2,1)S(1)}, u32[]{:S(2)}, u32[]{:S(2)}) collective-permute-start(bf16[64,1280]{1,0:T(8,128)(2,1)S(1)} %slice.40), channel_id=1, source_target_pairs={{0,16},{4,20},{8,24},{12,28},{16,0},{20,4},{24,8},{28,12},{1,17},{... | collective-permute-start | bytes 491528 | tf_op jit(solution)/shard_map/ppermute | solution.py:39
  16.9 0.6 collective-permute-start.4
  17.5 4.1 %collective-permute-done.5.refs_2_ = bf16[2,64,512]{2,1,0:T(8,128)(2,1)S(1)} collective-permute-done((bf16[2,64,512]{2,1,0:T(8,128)(2,1)}, bf16[2,64,512]{2,1,0:T(8,128)(2,1)S(1)}, u32[]{:S(2)}, u32[]{:S(2)}) %collective-permute-start.5) | collective-permute-done | bytes 131104 | tf_op jit(solution)/shard_map/ppermute | solution.py:39
  21.6 0.5 collective-permute-start.9
  22.1 0.2 collective-permute-done.4.refs_7_
  22.3 0.5 collective-permute-start.11
  22.8 0.5 norm.1
  23.3 0.3 collective-permute-done.9.refs_5_
  23.7 0.2 collective-permute-done.10.refs_8_
  23.9 0.2 collective-permute-done.11.refs_9_
  24.2 3.4 %forward.1 = (bf16[256,1408]{1,0:T(8,128)(2,1)S(1)}, bf16[256,1408]{1,0:T(8,128)(2,1)S(1)}, bf16[256,512]{1,0:T(8,128)(2,1)S(1)}, bf16[512,2560]{1,0:T(8,128)(2,...) custom-call(f32[256,256]{1,0:T(8,128)S(1)} %get-tuple-element.71.sca, ...), custom_call_target="tpu_custom_call" | custom-call | tf_op jit(solution)/shard_map/forward/pallas_call | solution.py:416
  27.6 0.2 collective-permute-start.12
  27.8 1.7 %backward.1 = (bf16[256,1152]{1,0:T(8,128)(2,1)S(1)}, bf16[256,1152]{1,0:T(8,128)(2,1)S(1)}, bf16[256,2048]{1,0:T(8,128)(2,1)S(1)}) custom-call(bf16[512,256]{1,0:T(8,128)(2,1)S(1)} %get-tuple-element.82.xt_ref, bf16[256,2048]{1,0:T(8,128)(2,1)S(1)} %get-tuple-element.90.act_ref, f32[256,2048]{1,0:T(8,128)S(1)} %get-tuple-element.91.slope_ref, ...), custom_call_target="tpu_custom_call" | custom-call | tf_op jit(solution)/shard_map/backward/pallas_call | solution.py:441
  29.5 0.4 collective-permute-done.12
  30.0 0.2 add_convert_fusion
  30.2 0.6 collective-permute-start.13
  30.8 1.1 %rows.1 = (bf16[2,64,512]{2,1,0:T(8,128)(2,1)S(1)}, bf16[2,64,512]{2,1,0:T(8,128)(2,1)S(1)}, bf16[2,64,512]{2,1,0:T(8,128)(2,1)S(1)}, bf16[2,64,512]{2,1,0:T(8,128)(2,1)S(1)}) custom-call(bf16[256,256]{1,0:T(8,128)(2,1)S(1)} %get-tuple-element.72.matrix_ref, bf16[256,2048]{1,0:T(8,128)(2,1)S(1)} %get-tuple-element.101.gproj_ref, ...), custom_call_target="tpu_custom_call" | custom-call | tf_op jit(solution)/shard_map/rows/pallas_call | solution.py:480
  32.1 1.6 %collective-permute-start.15 = (bf16[2,64,512]{2,1,0:T(8,128)(2,1)S(1)}, bf16[2,64,512]{2,1,0:T(8,128)(2,1)S(1)}, u32[]{:S(2)}, u32[]{:S(2)}) collective-permute-start(bf16[2,64,512]{2,1,0:T(8,128)(2,1)S(1)} %get-tuple-element.109), channel_id=1, source_target_pairs={{0,1},{1,0},{2,3},{3,2},{4,5},{5,4},{6,7},{7,6},{8,9},{9,8},{10,11... | collective-permute-start | bytes 393224 | tf_op jit(solution)/shard_map/ppermute | solution.py:39
  33.7 0.6 collective-permute-start.22
  34.2 2.6 %collective-permute-start.20 = (bf16[2,64,512]{2,1,0:T(8,128)(2,1)S(1)}, bf16[2,64,512]{2,1,0:T(8,128)(2,1)S(1)}, u32[]{:S(2)}, u32[]{:S(2)}) collective-permute-start(bf16[2,64,512]{2,1,0:T(8,128)(2,1)S(1)} %get-tuple-element.113), channel_id=1, source_target_pairs={{0,2},{1,3},{2,0},{3,1},{4,6},{5,7},{6,4},{7,5},{8,10},{9,11},{10,... | collective-permute-start | bytes 393224 | tf_op jit(solution)/shard_map/ppermute | solution.py:39
  36.8 0.3 collective-permute-start.21
  37.1 3.8 %collective-permute-done.13 = bf16[128,1408]{1,0:T(8,128)(2,1)S(1)} collective-permute-done((bf16[128,1408]{1,0:T(8,128)(2,1)S(1)}, bf16[128,1408]{1,0:T(8,128)(2,1)S(1)}, u32[]{:S(2)}, u32[]{:S(2)}) %collective-permute-start.13) | collective-permute-done | bytes 360480 | tf_op jit(solution)/shard_map/ppermute | solution.py:39
  41.1 0.6 collective-permute-start.16
  41.7 0.8 %collective-permute-done.22 = bf16[128,1152]{1,0:T(8,128)(2,1)S(1)} collective-permute-done((bf16[128,1152]{1,0:T(8,128)(2,1)S(1)}, bf16[128,1152]{1,0:T(8,128)(2,1)S(1)}, u32[]{:S(2)}, u32[]{:S(2)}) %collective-permute-start.22) | collective-permute-done | bytes 294944 | tf_op jit(solution)/shard_map/ppermute | solution.py:39
  42.6 1.6 %collective-permute-start.23 = (bf16[64,1152]{1,0:T(8,128)(2,1)S(1)}, bf16[64,1152]{1,0:T(8,128)(2,1)S(1)}, u32[]{:S(2)}, u32[]{:S(2)}) collective-permute-start(bf16[64,1152]{1,0:T(8,128)(2,1)S(1)} %slice.45), channel_id=1, source_target_pairs={{0,8},{4,12},{8,0},{12,4},{16,24},{20,28},{24,16},{28,20},{1,9},{5... | collective-permute-start | bytes 442376 | tf_op jit(solution)/shard_map/ppermute | solution.py:39
  44.1 3.0 %collective-permute-done.16 = bf16[64,1408]{1,0:T(8,128)(2,1)S(1)} collective-permute-done((bf16[64,1408]{1,0:T(8,128)(2,1)S(1)}, bf16[64,1408]{1,0:T(8,128)(2,1)S(1)}, u32[]{:S(2)}, u32[]{:S(2)}) %collective-permute-start.16) | collective-permute-done | bytes 180256 | tf_op jit(solution)/shard_map/ppermute | solution.py:39
  47.2 1.6 %collective-permute-start.17 = (bf16[32,1408]{1,0:T(8,128)(2,1)S(1)}, bf16[32,1408]{1,0:T(8,128)(2,1)S(1)}, u32[]{:S(2)}, u32[]{:S(2)}) collective-permute-start(bf16[32,1408]{1,0:T(8,128)(2,1)S(1)} %constant_dynamic-slice_fusion.1), channel_id=1, source_target_pairs={{0,1},{1,0},{2,3},{3,2},{4,5},{5,4},{6,7},{7,6},{8,9},{9,8},{10,11... | collective-permute-start | bytes 270344 | tf_op jit(solution)/shard_map/ppermute | solution.py:39
  48.9 0.6 collective-permute-start.24
  49.5 2.4 %collective-permute-done.17 = bf16[32,1408]{1,0:T(8,128)(2,1)S(1)} collective-permute-done((bf16[32,1408]{1,0:T(8,128)(2,1)S(1)}, bf16[32,1408]{1,0:T(8,128)(2,1)S(1)}, u32[]{:S(2)}, u32[]{:S(2)}) %collective-permute-start.17) | collective-permute-done | bytes 90144 | tf_op jit(solution)/shard_map/ppermute | solution.py:39
  51.9 2.6 %collective-permute-start.18 = (bf16[32,1408]{1,0:T(8,128)(2,1)S(1)}, bf16[32,1408]{1,0:T(8,128)(2,1)S(1)}, u32[]{:S(2)}, u32[]{:S(2)}) collective-permute-start(bf16[32,1408]{1,0:T(8,128)(2,1)S(1)} %add_convert_fusion.7), channel_id=1, source_target_pairs={{0,2},{1,3},{2,0},{3,1},{4,6},{5,7},{6,4},{7,5},{8,10},{9,11},{10,... | collective-permute-start | bytes 270344 | tf_op jit(solution)/shard_map/ppermute | solution.py:39
  54.5 1.8 %collective-permute-start.25 = (bf16[32,1152]{1,0:T(8,128)(2,1)S(1)}, bf16[32,1152]{1,0:T(8,128)(2,1)S(1)}, u32[]{:S(2)}, u32[]{:S(2)}) collective-permute-start(bf16[32,1152]{1,0:T(8,128)(2,1)S(1)} %add_convert_fusion.9), channel_id=1, source_target_pairs={{0,2},{1,3},{2,0},{3,1},{4,6},{5,7},{6,4},{7,5},{8,10},{9,11},{10,... | collective-permute-start | bytes 221192 | tf_op jit(solution)/shard_map/ppermute | solution.py:39
  56.3 2.6 %collective-permute-done.18 = bf16[32,1408]{1,0:T(8,128)(2,1)S(1)} collective-permute-done((bf16[32,1408]{1,0:T(8,128)(2,1)S(1)}, bf16[32,1408]{1,0:T(8,128)(2,1)S(1)}, u32[]{:S(2)}, u32[]{:S(2)}) %collective-permute-start.18) | collective-permute-done | bytes 90144 | tf_op jit(solution)/shard_map/ppermute | solution.py:39
  59.1 0.8 %collective-permute-done.25 = bf16[32,1152]{1,0:T(8,128)(2,1)S(1)} collective-permute-done((bf16[32,1152]{1,0:T(8,128)(2,1)S(1)}, bf16[32,1152]{1,0:T(8,128)(2,1)S(1)}, u32[]{:S(2)}, u32[]{:S(2)}) %collective-permute-start.25) | collective-permute-done | bytes 73760 | tf_op jit(solution)/shard_map/ppermute | solution.py:39
  59.9 2.1 %collective-permute-start.26 = (bf16[32,1152]{1,0:T(8,128)(2,1)S(1)}, bf16[32,1152]{1,0:T(8,128)(2,1)S(1)}, u32[]{:S(2)}, u32[]{:S(2)}) collective-permute-start(bf16[32,1152]{1,0:T(8,128)(2,1)S(1)} %add_convert_fusion.8.late_own), channel_id=1, source_target_pairs={{0,1},{1,0},{2,3},{3,2},{4,5},{5,4},{6,7},{7,6},{8,9},{9,8},{10,11... | collective-permute-start | bytes 221192 | tf_op jit(solution)/shard_map/ppermute | solution.py:39
  62.0 1.2 %post.1 = (bf16[256,512]{1,0:T(8,128)(2,1)}, bf16[256,512]{1,0:T(8,128)(2,1)}) custom-call(s32[1,32]{1,0:T(1,128)S(1)} %bitcast.9, bf16[2,64,512]{2,1,0:T(8,128)(2,1)S(1)} %get-tuple-element.111.refs_0_, bf16[2,64,512]{2,1,0:T(8,128)(2,1)S(1)} %collective-permute-done.15.refs_1_, bf16[2,64,512]{2,1,0:T(8,128)(2,1)S(1)} %collective-permute-done.20.refs_2_, ...), custom_call_target="tpu_custom_call" | custom-call | tf_op jit(solution)/shard_map/post/pallas_call | solution.py:491
  63.2 0.3 collective-permute-done.19.early_other
  63.5 0.8 %collective-permute-done.26.late_other = bf16[32,1152]{1,0:T(8,128)(2,1)S(1)} collective-permute-done((bf16[32,1152]{1,0:T(8,128)(2,1)S(1)}, bf16[32,1152]{1,0:T(8,128)(2,1)S(1)}, u32[]{:S(2)}, u32[]{:S(2)}) %collective-permute-start.26) | collective-permute-done | bytes 73760 | tf_op jit(solution)/shard_map/ppermute | solution.py:39
  64.3 0.9 %finish.1 = (f32[64,2048]{1,0:T(8,128)}, f32[64,512]{1,0:T(8,128)}) custom-call(bf16[32,1408]{1,0:T(8,128)(2,1)S(1)} %add_convert_fusion.6.early_own, bf16[32,1408]{1,0:T(8,128)(2,1)S(1)} %collective-permute-done.19.early_other, bf16[32,1152]{1,0:T(8,128)(2,1)S(1)} %add_convert_fusion.8.late_own, bf16[32,1152]{1,0:T(8,128)(2,1)S(1)} %collective-permute-done.26.late_other), custom_call_target="tpu_custom_call" | custom-call | tf_op jit(solution)/shard_map/finish/pallas_call | solution.py:503
  (40 shorter events, 1.1 us)
Async XLA Ops:
  2.9 12.2 %collective-permute-start = (bf16[64,2560]{1,0:T(8,128)(2,1)}, bf16[64,2560]{1,0:T(8,128)(2,1)S(1)}, u32[]{:S(2)}, u32[]{:S(2)}) collective-permute-start(bf16[64,2560]{1,0:T(8,128)(2,1)} %get-tuple-element.65.w_ref), channel_id=1, source_target_pairs={{0,8},{4,12},{8,0},{12,4},{16,24},{20,28},{24,16},{28,20},{1,9},{5... | collective-permute-start | bytes 983048 | tf_op jit(solution)/shard_map/ppermute | solution.py:39
  5.9 9.4 %collective-permute-start.1 = (bf16[64,2560]{1,0:T(8,128)(2,1)}, bf16[64,2560]{1,0:T(8,128)(2,1)S(1)}, u32[]{:S(2)}, u32[]{:S(2)}) collective-permute-start(bf16[64,2560]{1,0:T(8,128)(2,1)} %get-tuple-element.65.w_ref), channel_id=1, source_target_pairs={{0,16},{4,20},{8,24},{12,28},{16,0},{20,4},{24,8},{28,12},{1,17},{... | collective-permute-start | bytes 983048 | tf_op jit(solution)/shard_map/ppermute | solution.py:39
  7.5 7.7 %collective-permute-start.2 = (bf16[2,64,512]{2,1,0:T(8,128)(2,1)}, bf16[2,64,512]{2,1,0:T(8,128)(2,1)S(1)}, u32[]{:S(2)}, u32[]{:S(2)}) collective-permute-start(bf16[2,64,512]{2,1,0:T(8,128)(2,1)} %get-tuple-element.68), channel_id=1, source_target_pairs={{0,1},{1,0},{2,3},{3,2},{4,5},{5,4},{6,7},{7,6},{8,9},{9,8},{10,11... | collective-permute-start | bytes 393224 | tf_op jit(solution)/shard_map/ppermute | solution.py:39
  9.0 12.6 %collective-permute-start.5 = (bf16[2,64,512]{2,1,0:T(8,128)(2,1)}, bf16[2,64,512]{2,1,0:T(8,128)(2,1)S(1)}, u32[]{:S(2)}, u32[]{:S(2)}) collective-permute-start(bf16[2,64,512]{2,1,0:T(8,128)(2,1)} %get-tuple-element.75), channel_id=1, source_target_pairs={{0,2},{1,3},{2,0},{3,1},{4,6},{5,7},{6,4},{7,5},{8,10},{9,11},{10,... | collective-permute-start | bytes 393224 | tf_op jit(solution)/shard_map/ppermute | solution.py:39
  11.6 10.0 %collective-permute-start.6 = (bf16[2,64,512]{2,1,0:T(8,128)(2,1)}, bf16[2,64,512]{2,1,0:T(8,128)(2,1)S(1)}, u32[]{:S(2)}, u32[]{:S(2)}) collective-permute-start(bf16[2,64,512]{2,1,0:T(8,128)(2,1)} %get-tuple-element.76), channel_id=1, source_target_pairs={{0,3},{1,2},{2,1},{3,0},{4,7},{5,6},{6,5},{7,4},{8,11},{9,10},{10,... | collective-permute-start | bytes 393224 | tf_op jit(solution)/shard_map/ppermute | solution.py:39
  11.8 1.0 %copy-start = (bf16[64,2560]{1,0:T(8,128)(2,1)S(1)}, bf16[64,2560]{1,0:T(8,128)(2,1)}, u32[]{:S(2)}) copy-start(bf16[64,2560]{1,0:T(8,128)(2,1)} %get-tuple-element.65.w_ref) | copy-start | bytes 983044
  12.8 0.9 %copy-start.1 = (bf16[2,64,512]{2,1,0:T(8,128)(2,1)S(1)}, bf16[2,64,512]{2,1,0:T(8,128)(2,1)}, u32[]{:S(2)}) copy-start(bf16[2,64,512]{2,1,0:T(8,128)(2,1)} %get-tuple-element.66.own_ref) | copy-start | bytes 393220
  13.7 0.7 %copy-start.2 = (s32[8,128]{1,0:T(8,128)S(1)}, s32[8,128]{1,0:T(8,128)}, u32[]{:S(2)}) copy-start(s32[8,128]{1,0:T(8,128)} %get-tuple-element.64.small_ref) | copy-start | bytes 12292
  15.3 6.8 %collective-permute-start.3 = (bf16[64,1280]{1,0:T(8,128)(2,1)S(1)}, bf16[64,1280]{1,0:T(8,128)(2,1)S(1)}, u32[]{:S(2)}, u32[]{:S(2)}) collective-permute-start(bf16[64,1280]{1,0:T(8,128)(2,1)S(1)} %slice.40), channel_id=1, source_target_pairs={{0,16},{4,20},{8,24},{12,28},{16,0},{20,4},{24,8},{28,12},{1,17},{... | collective-permute-start | bytes 491528 | tf_op jit(solution)/shard_map/ppermute | solution.py:39
  16.9 5.4 %collective-permute-start.4 = (bf16[64,1280]{1,0:T(8,128)(2,1)S(1)}, bf16[64,1280]{1,0:T(8,128)(2,1)S(1)}, u32[]{:S(2)}, u32[]{:S(2)}) collective-permute-start(bf16[64,1280]{1,0:T(8,128)(2,1)S(1)} %slice.41), channel_id=1, source_target_pairs={{0,8},{4,12},{8,0},{12,4},{16,24},{20,28},{24,16},{28,20},{1,9},{5... | collective-permute-start | bytes 491528 | tf_op jit(solution)/shard_map/ppermute | solution.py:39
  17.5 5.8 %collective-permute-start.7 = (bf16[64,2560]{1,0:T(8,128)(2,1)S(1)}, bf16[64,2560]{1,0:T(8,128)(2,1)S(1)}, u32[]{:S(2)}, u32[]{:S(2)}) collective-permute-start(bf16[64,2560]{1,0:T(8,128)(2,1)S(1)} %get-tuple-element.83.refs_0_), channel_id=1, source_target_pairs={{0,4},{4,0},{8,12},{12,8},{16,20},{20,16},{24,28},{28,24},{1,5},{5... | collective-permute-start | bytes 983048 | tf_op jit(solution)/shard_map/ppermute | solution.py:39
  21.6 1.7 %collective-permute-start.8 = (bf16[64,2560]{1,0:T(8,128)(2,1)S(1)}, bf16[64,2560]{1,0:T(8,128)(2,1)S(1)}, u32[]{:S(2)}, u32[]{:S(2)}) collective-permute-start(bf16[64,2560]{1,0:T(8,128)(2,1)S(1)} %collective-permute-done.refs_2_), channel_id=1, source_target_pairs={{0,4},{4,0},{8,12},{12,8},{16,20},{20,16},{24,28},{28,24},{1,5},{5... | collective-permute-start | bytes 983048 | tf_op jit(solution)/shard_map/ppermute | solution.py:39
  21.6 2.1 %collective-permute-start.9 = (bf16[64,2560]{1,0:T(8,128)(2,1)S(1)}, bf16[64,2560]{1,0:T(8,128)(2,1)S(1)}, u32[]{:S(2)}, u32[]{:S(2)}) collective-permute-start(bf16[64,2560]{1,0:T(8,128)(2,1)S(1)} %collective-permute-done.1.refs_4_), channel_id=1, source_target_pairs={{0,4},{4,0},{8,12},{12,8},{16,20},{20,16},{24,28},{28,24},{1,5},{5... | collective-permute-start | bytes 983048 | tf_op jit(solution)/shard_map/ppermute | solution.py:39
  22.3 1.6 %collective-permute-start.10 = (bf16[64,1280]{1,0:T(8,128)(2,1)S(1)}, bf16[64,1280]{1,0:T(8,128)(2,1)S(1)}, u32[]{:S(2)}, u32[]{:S(2)}) collective-permute-start(bf16[64,1280]{1,0:T(8,128)(2,1)S(1)} %collective-permute-done.3.refs_6_), channel_id=1, source_target_pairs={{0,4},{4,0},{8,12},{12,8},{16,20},{20,16},{24,28},{28,24},{1,5},{5... | collective-permute-start | bytes 491528 | tf_op jit(solution)/shard_map/ppermute | solution.py:39
  22.3 1.8 %collective-permute-start.11 = (bf16[64,1280]{1,0:T(8,128)(2,1)S(1)}, bf16[64,1280]{1,0:T(8,128)(2,1)S(1)}, u32[]{:S(2)}, u32[]{:S(2)}) collective-permute-start(bf16[64,1280]{1,0:T(8,128)(2,1)S(1)} %collective-permute-done.4.refs_7_), channel_id=1, source_target_pairs={{0,4},{4,0},{8,12},{12,8},{16,20},{20,16},{24,28},{28,24},{1,5},{5... | collective-permute-start | bytes 491528 | tf_op jit(solution)/shard_map/ppermute | solution.py:39
  27.6 2.3 %collective-permute-start.12 = (bf16[256,1408]{1,0:T(8,128)(2,1)S(1)}, bf16[256,1408]{1,0:T(8,128)(2,1)S(1)}, u32[]{:S(2)}, u32[]{:S(2)}) collective-permute-start(bf16[256,1408]{1,0:T(8,128)(2,1)S(1)} %get-tuple-element.89), channel_id=1, source_target_pairs={{0,4},{4,0},{8,12},{12,8},{16,20},{20,16},{24,28},{28,24},{1,5},{5... | collective-permute-start | bytes 2162696 | tf_op jit(solution)/shard_map/ppermute | solution.py:39
  29.9 2.1 %collective-permute-start.14 = (bf16[256,1152]{1,0:T(8,128)(2,1)S(1)}, bf16[256,1152]{1,0:T(8,128)(2,1)S(1)}, u32[]{:S(2)}, u32[]{:S(2)}) collective-permute-start(bf16[256,1152]{1,0:T(8,128)(2,1)S(1)} %get-tuple-element.100), channel_id=1, source_target_pairs={{0,4},{4,0},{8,12},{12,8},{16,20},{20,16},{24,28},{28,24},{1,5},{5... | collective-permute-start | bytes 1769480 | tf_op jit(solution)/shard_map/ppermute | solution.py:39
  30.2 10.8 %collective-permute-start.13 = (bf16[128,1408]{1,0:T(8,128)(2,1)S(1)}, bf16[128,1408]{1,0:T(8,128)(2,1)S(1)}, u32[]{:S(2)}, u32[]{:S(2)}) collective-permute-start(bf16[128,1408]{1,0:T(8,128)(2,1)S(1)} %slice.33), channel_id=1, source_target_pairs={{0,8},{4,12},{8,0},{12,4},{16,24},{20,28},{24,16},{28,20},{1,9},{5... | collective-permute-start | bytes 1081352 | tf_op jit(solution)/shard_map/ppermute | solution.py:39
  32.1 8.9 %collective-permute-start.15 = (bf16[2,64,512]{2,1,0:T(8,128)(2,1)S(1)}, bf16[2,64,512]{2,1,0:T(8,128)(2,1)S(1)}, u32[]{:S(2)}, u32[]{:S(2)}) collective-permute-start(bf16[2,64,512]{2,1,0:T(8,128)(2,1)S(1)} %get-tuple-element.109), channel_id=1, source_target_pairs={{0,1},{1,0},{2,3},{3,2},{4,5},{5,4},{6,7},{7,6},{8,9},{9,8},{10,11... | collective-permute-start | bytes 393224 | tf_op jit(solution)/shard_map/ppermute | solution.py:39
  33.7 8.8 %collective-permute-start.22 = (bf16[128,1152]{1,0:T(8,128)(2,1)S(1)}, bf16[128,1152]{1,0:T(8,128)(2,1)S(1)}, u32[]{:S(2)}, u32[]{:S(2)}) collective-permute-start(bf16[128,1152]{1,0:T(8,128)(2,1)S(1)} %slice.37), channel_id=1, source_target_pairs={{0,16},{4,20},{8,24},{12,28},{16,0},{20,4},{24,8},{28,12},{1,17},{... | collective-permute-start | bytes 884744 | tf_op jit(solution)/shard_map/ppermute | solution.py:39
  34.2 27.7 %collective-permute-start.20 = (bf16[2,64,512]{2,1,0:T(8,128)(2,1)S(1)}, bf16[2,64,512]{2,1,0:T(8,128)(2,1)S(1)}, u32[]{:S(2)}, u32[]{:S(2)}) collective-permute-start(bf16[2,64,512]{2,1,0:T(8,128)(2,1)S(1)} %get-tuple-element.113), channel_id=1, source_target_pairs={{0,2},{1,3},{2,0},{3,1},{4,6},{5,7},{6,4},{7,5},{8,10},{9,11},{10,... | collective-permute-start | bytes 393224 | tf_op jit(solution)/shard_map/ppermute | solution.py:39
  36.8 25.1 %collective-permute-start.21 = (bf16[2,64,512]{2,1,0:T(8,128)(2,1)S(1)}, bf16[2,64,512]{2,1,0:T(8,128)(2,1)S(1)}, u32[]{:S(2)}, u32[]{:S(2)}) collective-permute-start(bf16[2,64,512]{2,1,0:T(8,128)(2,1)S(1)} %get-tuple-element.114), channel_id=1, source_target_pairs={{0,3},{1,2},{2,1},{3,0},{4,7},{5,6},{6,5},{7,4},{8,11},{9,10},{10,... | collective-permute-start | bytes 393224 | tf_op jit(solution)/shard_map/ppermute | solution.py:39
  41.1 6.1 %collective-permute-start.16 = (bf16[64,1408]{1,0:T(8,128)(2,1)S(1)}, bf16[64,1408]{1,0:T(8,128)(2,1)S(1)}, u32[]{:S(2)}, u32[]{:S(2)}) collective-permute-start(bf16[64,1408]{1,0:T(8,128)(2,1)S(1)} %slice.43), channel_id=1, source_target_pairs={{0,16},{4,20},{8,24},{12,28},{16,0},{20,4},{24,8},{28,12},{1,17},{... | collective-permute-start | bytes 540680 | tf_op jit(solution)/shard_map/ppermute | solution.py:39
  42.5 19.4 %copy-start.3 = (s32[1,1,32]{2,1,0:T(1,128)S(1)}, s32[1,1,32]{2,1,0:T(1,128)}, u32[]{:S(2)}) copy-start(s32[1,1,32]{2,1,0:T(1,128)} %param.12) | copy-start | bytes 388
  42.6 6.2 %collective-permute-start.23 = (bf16[64,1152]{1,0:T(8,128)(2,1)S(1)}, bf16[64,1152]{1,0:T(8,128)(2,1)S(1)}, u32[]{:S(2)}, u32[]{:S(2)}) collective-permute-start(bf16[64,1152]{1,0:T(8,128)(2,1)S(1)} %slice.45), channel_id=1, source_target_pairs={{0,8},{4,12},{8,0},{12,4},{16,24},{20,28},{24,16},{28,20},{1,9},{5... | collective-permute-start | bytes 442376 | tf_op jit(solution)/shard_map/ppermute | solution.py:39
  47.2 4.6 %collective-permute-start.17 = (bf16[32,1408]{1,0:T(8,128)(2,1)S(1)}, bf16[32,1408]{1,0:T(8,128)(2,1)S(1)}, u32[]{:S(2)}, u32[]{:S(2)}) collective-permute-start(bf16[32,1408]{1,0:T(8,128)(2,1)S(1)} %constant_dynamic-slice_fusion.1), channel_id=1, source_target_pairs={{0,1},{1,0},{2,3},{3,2},{4,5},{5,4},{6,7},{7,6},{8,9},{9,8},{10,11... | collective-permute-start | bytes 270344 | tf_op jit(solution)/shard_map/ppermute | solution.py:39
  48.9 5.6 %collective-permute-start.24 = (bf16[32,1152]{1,0:T(8,128)(2,1)S(1)}, bf16[32,1152]{1,0:T(8,128)(2,1)S(1)}, u32[]{:S(2)}, u32[]{:S(2)}) collective-permute-start(bf16[32,1152]{1,0:T(8,128)(2,1)S(1)} %constant_dynamic-slice_fusion), channel_id=1, source_target_pairs={{0,1},{1,0},{2,3},{3,2},{4,5},{5,4},{6,7},{7,6},{8,9},{9,8},{10,11... | collective-permute-start | bytes 221192 | tf_op jit(solution)/shard_map/ppermute | solution.py:39
  51.9 7.0 %collective-permute-start.18 = (bf16[32,1408]{1,0:T(8,128)(2,1)S(1)}, bf16[32,1408]{1,0:T(8,128)(2,1)S(1)}, u32[]{:S(2)}, u32[]{:S(2)}) collective-permute-start(bf16[32,1408]{1,0:T(8,128)(2,1)S(1)} %add_convert_fusion.7), channel_id=1, source_target_pairs={{0,2},{1,3},{2,0},{3,1},{4,6},{5,7},{6,4},{7,5},{8,10},{9,11},{10,... | collective-permute-start | bytes 270344 | tf_op jit(solution)/shard_map/ppermute | solution.py:39
  54.5 5.4 %collective-permute-start.25 = (bf16[32,1152]{1,0:T(8,128)(2,1)S(1)}, bf16[32,1152]{1,0:T(8,128)(2,1)S(1)}, u32[]{:S(2)}, u32[]{:S(2)}) collective-permute-start(bf16[32,1152]{1,0:T(8,128)(2,1)S(1)} %add_convert_fusion.9), channel_id=1, source_target_pairs={{0,2},{1,3},{2,0},{3,1},{4,6},{5,7},{6,4},{7,5},{8,10},{9,11},{10,... | collective-permute-start | bytes 221192 | tf_op jit(solution)/shard_map/ppermute | solution.py:39
  58.9 4.6 %collective-permute-start.19 = (bf16[32,1408]{1,0:T(8,128)(2,1)S(1)}, bf16[32,1408]{1,0:T(8,128)(2,1)S(1)}, u32[]{:S(2)}, u32[]{:S(2)}) collective-permute-start(bf16[32,1408]{1,0:T(8,128)(2,1)S(1)} %add_convert_fusion.6.early_own), channel_id=1, source_target_pairs={{0,1},{1,0},{2,3},{3,2},{4,5},{5,4},{6,7},{7,6},{8,9},{9,8},{10,11... | collective-permute-start | bytes 270344 | tf_op jit(solution)/shard_map/ppermute | solution.py:39
  59.9 4.4 %collective-permute-start.26 = (bf16[32,1152]{1,0:T(8,128)(2,1)S(1)}, bf16[32,1152]{1,0:T(8,128)(2,1)S(1)}, u32[]{:S(2)}, u32[]{:S(2)}) collective-permute-start(bf16[32,1152]{1,0:T(8,128)(2,1)S(1)} %add_convert_fusion.8.late_own), channel_id=1, source_target_pairs={{0,1},{1,0},{2,3},{3,2},{4,5},{5,4},{6,7},{7,6},{8,9},{9,8},{10,11... | collective-permute-start | bytes 221192 | tf_op jit(solution)/shard_map/ppermute | solution.py:39

commit v9 on v8

--- a/solution.py
+++ b/solution.py
@@ -147,16 +147,20 @@
         ref[...] = dot(matrix, stacked(back_refs, which), TN).astype(BF16)
 
 
-def finish_kernel(early_own, early_other, late_own, late_other, uvqk_ref, out_ref):
+def finish_kernel(early_own, early_other, late_own, late_other, uvqk_out, wout_out, uvqk_ref, wout_ref, sem):
     rows = early_own.shape[0]
-    width = out_ref.shape[1]
+    width = wout_ref.shape[2]
     split = early_own.shape[1] - width
     side = lax.axis_index("shuf") & 1
-    for place, early, late in ((side, early_own, late_own), (1 - side, early_other, late_other)):
+    copies = []
+    for n, place, early, late in ((0, side, early_own, late_own), (1, 1 - side, early_other, late_other)):
         at = pl.ds(pl.multiple_of(place * rows, rows), rows)
-        out_ref[at, :] = early[:, :width].astype(F32)
-        uvqk_ref[at, :split] = early[:, width:].astype(F32)
-        uvqk_ref[at, split:] = late[...].astype(F32)
+        uvqk_ref[n, :, :split] = early[:, width:].astype(F32)
+        uvqk_ref[n, :, split:] = late[...].astype(F32)
+        wout_ref[n] = early[:, :width].astype(F32)
+        copies += copy_all(((uvqk_ref.at[n], uvqk_out.at[at]), (wout_ref.at[n], wout_out.at[at])), sem.at[n])
+    for copy in copies:
+        copy.wait()
 
 
 def only(value, h, head_width):
@@ -504,7 +508,12 @@
         finish_kernel,
         out_shape=[spec((shard, 4 * width), F32), spec((shard, width), F32)],
         in_specs=[VMEM] * 4,
-        out_specs=[VMEM] * 2,
+        out_specs=[HBM] * 2,
+        scratch_shapes=[
+            pltpu.VMEM((2, shard // 2, 4 * width), F32),
+            pltpu.VMEM((2, shard // 2, width), F32),
+            pltpu.SemaphoreType.DMA((2, 2)),
+        ],
         compiler_params=limit,
         name="finish",
     )(*early, *late)

time: 65.4 us -> 65.4 us (level)
  no operation moved by 1% of the time
where the time goes in v9:
time: 65.4 us; the launch traced here: 65.2 us
  starting transfers between devices  29 us (44%)
  waiting for transfers between devices  20.2 us (31%)
  Pallas kernels  11.8 us (18%)
  local copies, waits for them, and re-layouts  2.69 us (4%)
  between operations  0.84 us (1%)
  other arithmetic  0.66 us (1%)
    ppermute x27, starting transfers between devices, exchange(): return lax.ppermute(value, axis, [(i, i ^ mask) for i in range(size)])  29 us
    ppermute x27, waiting for transfers between devices, exchange(): return lax.ppermute(value, axis, [(i, i ^ mask) for i in range(size)])  20.2 us
    pallas_call x1, Pallas kernels, on_device(): pl.pallas_call(partial(forward_kernel, groups, chips, places), out_shape=...  3.45 us
    unnamed x8, local copies, waits for them, and re-layouts  2.56 us
    pallas_call x1, Pallas kernels, on_device(): pl.pallas_call(partial(pre_kernel, parts), out_shape=[spec((shard, column...  2.29 us
    pallas_call x1, Pallas kernels, on_device(): pl.pallas_call(partial(backward_kernel, groups, chips[::-1]), out_shape=[...  1.66 us
  transfers between devices with their start and end apart: 27, of which 15 were waited for; matrix products, arithmetic and copies ran while one was open for 1% of the time, Pallas kernels for 8%

profile of v9, /device:TPU:0, one launch (start us, length us, event | category | flops | bytes accessed | tf_op | source)
XLA Modules:
  0.0 65.2 jit_solution(4070881634119770703)
XLA Ops:
  0.6 2.3 %pre.1 = (bf16[64,2560]{1,0:T(8,128)(2,1)}, s32[8,128]{1,0:T(8,128)}, bf16[2,64,512]{2,1,0:T(8,128)(2,1)}, bf16[2,64,512]{2,1,0:T(8,128)(2,1)}, bf16[2,64,512]{2...) custom-call(s32[1,32]{1,0:T(1,128)} %bitcast.8, s32[1,32]{1,0:T(1,128)} %bitcast.12, s32[1,8]{1,0:T(1,128)} %bitcast.13, ...), custom_call_target="tpu_custom_call" | custom-call | tf_op jit(solution)/shard_map/pre/pallas_call | solution.py:351
  2.9 3.0 %collective-permute-start = (bf16[64,2560]{1,0:T(8,128)(2,1)}, bf16[64,2560]{1,0:T(8,128)(2,1)S(1)}, u32[]{:S(2)}, u32[]{:S(2)}) collective-permute-start(bf16[64,2560]{1,0:T(8,128)(2,1)} %get-tuple-element.65.w_ref), channel_id=1, source_target_pairs={{0,8},{4,12},{8,0},{12,4},{16,24},{20,28},{24,16},{28,20},{1,9},{5... | collective-permute-start | bytes 983048 | tf_op jit(solution)/shard_map/ppermute | solution.py:39
  5.9 1.5 %collective-permute-start.1 = (bf16[64,2560]{1,0:T(8,128)(2,1)}, bf16[64,2560]{1,0:T(8,128)(2,1)S(1)}, u32[]{:S(2)}, u32[]{:S(2)}) collective-permute-start(bf16[64,2560]{1,0:T(8,128)(2,1)} %get-tuple-element.65.w_ref), channel_id=1, source_target_pairs={{0,16},{4,20},{8,24},{12,28},{16,0},{20,4},{24,8},{28,12},{1,17},{... | collective-permute-start | bytes 983048 | tf_op jit(solution)/shard_map/ppermute | solution.py:39
  7.5 1.6 %collective-permute-start.2 = (bf16[2,64,512]{2,1,0:T(8,128)(2,1)}, bf16[2,64,512]{2,1,0:T(8,128)(2,1)S(1)}, u32[]{:S(2)}, u32[]{:S(2)}) collective-permute-start(bf16[2,64,512]{2,1,0:T(8,128)(2,1)} %get-tuple-element.68), channel_id=1, source_target_pairs={{0,1},{1,0},{2,3},{3,2},{4,5},{5,4},{6,7},{7,6},{8,9},{9,8},{10,11... | collective-permute-start | bytes 393224 | tf_op jit(solution)/shard_map/ppermute | solution.py:39
  9.0 2.6 %collective-permute-start.5 = (bf16[2,64,512]{2,1,0:T(8,128)(2,1)}, bf16[2,64,512]{2,1,0:T(8,128)(2,1)S(1)}, u32[]{:S(2)}, u32[]{:S(2)}) collective-permute-start(bf16[2,64,512]{2,1,0:T(8,128)(2,1)} %get-tuple-element.75), channel_id=1, source_target_pairs={{0,2},{1,3},{2,0},{3,1},{4,6},{5,7},{6,4},{7,5},{8,10},{9,11},{10,... | collective-permute-start | bytes 393224 | tf_op jit(solution)/shard_map/ppermute | solution.py:39
  11.6 0.2 collective-permute-start.6
  11.8 1.0 %copy-done = bf16[64,2560]{1,0:T(8,128)(2,1)S(1)} copy-done((bf16[64,2560]{1,0:T(8,128)(2,1)S(1)}, bf16[64,2560]{1,0:T(8,128)(2,1)}, u32[]{:S(2)}) %copy-start) | copy-done | bytes 327704
  12.8 0.9 %copy-done.1 = bf16[2,64,512]{2,1,0:T(8,128)(2,1)S(1)} copy-done((bf16[2,64,512]{2,1,0:T(8,128)(2,1)S(1)}, bf16[2,64,512]{2,1,0:T(8,128)(2,1)}, u32[]{:S(2)}) %copy-start.1) | copy-done | bytes 131096
  13.7 0.7 %copy-done.2 = s32[8,128]{1,0:T(8,128)S(1)} copy-done((s32[8,128]{1,0:T(8,128)S(1)}, s32[8,128]{1,0:T(8,128)}, u32[]{:S(2)}) %copy-start.2) | copy-done | bytes 4120
  14.4 0.7 %plan.1 = (bf16[256,256]{1,0:T(8,128)(2,1)S(1)}, f32[256,256]{1,0:T(8,128)S(1)}, bf16[64,2560]{1,0:T(8,128)(2,1)S(1)}, bf16[2,64,512]{2,1,0:T(8,128)(2,1)S(1)}) custom-call(s32[8,128]{1,0:T(8,128)S(1)} %copy-done.2, bf16[64,2560]{1,0:T(8,128)(2,1)S(1)} %copy-done, bf16[2,64,512]{2,1,0:T(8,128)(2,1)S(1)} %copy-done.1), custom_call_target="tpu_custom_call" | custom-call | tf_op jit(solution)/shard_map/plan/pallas_call | solution.py:373
  15.3 1.6 %collective-permute-start.3 = (bf16[64,1280]{1,0:T(8,128)(2,1)S(1)}, bf16[64,1280]{1,0:T(8,128)(2,1)S(1)}, u32[]{:S(2)}, u32[]{:S(2)}) collective-permute-start(bf16[64,1280]{1,0:T(8,128)(2,1)S(1)} %slice.40), channel_id=1, source_target_pairs={{0,16},{4,20},{8,24},{12,28},{16,0},{20,4},{24,8},{28,12},{1,17},{... | collective-permute-start | bytes 491528 | tf_op jit(solution)/shard_map/ppermute | solution.py:39
  16.9 0.6 collective-permute-start.4
  17.5 4.1 %collective-permute-done.5.refs_2_ = bf16[2,64,512]{2,1,0:T(8,128)(2,1)S(1)} collective-permute-done((bf16[2,64,512]{2,1,0:T(8,128)(2,1)}, bf16[2,64,512]{2,1,0:T(8,128)(2,1)S(1)}, u32[]{:S(2)}, u32[]{:S(2)}) %collective-permute-start.5) | collective-permute-done | bytes 131104 | tf_op jit(solution)/shard_map/ppermute | solution.py:39
  21.6 0.5 collective-permute-start.9
  22.1 0.2 collective-permute-done.4.refs_7_
  22.3 0.5 collective-permute-start.11
  22.8 0.5 norm.1
  23.3 0.3 collective-permute-done.9.refs_5_
  23.7 0.2 collective-permute-done.10.refs_8_
  23.9 0.2 collective-permute-done.11.refs_9_
  24.2 3.4 %forward.1 = (bf16[256,1408]{1,0:T(8,128)(2,1)S(1)}, bf16[256,1408]{1,0:T(8,128)(2,1)S(1)}, bf16[256,512]{1,0:T(8,128)(2,1)S(1)}, bf16[512,2560]{1,0:T(8,128)(2,...) custom-call(f32[256,256]{1,0:T(8,128)S(1)} %get-tuple-element.71.sca, ...), custom_call_target="tpu_custom_call" | custom-call | tf_op jit(solution)/shard_map/forward/pallas_call | solution.py:420
  27.6 0.2 collective-permute-start.12
  27.8 1.7 %backward.1 = (bf16[256,1152]{1,0:T(8,128)(2,1)S(1)}, bf16[256,1152]{1,0:T(8,128)(2,1)S(1)}, bf16[256,2048]{1,0:T(8,128)(2,1)S(1)}) custom-call(bf16[512,256]{1,0:T(8,128)(2,1)S(1)} %get-tuple-element.82.xt_ref, bf16[256,2048]{1,0:T(8,128)(2,1)S(1)} %get-tuple-element.90.act_ref, f32[256,2048]{1,0:T(8,128)S(1)} %get-tuple-element.91.slope_ref, ...), custom_call_target="tpu_custom_call" | custom-call | tf_op jit(solution)/shard_map/backward/pallas_call | solution.py:445
  29.5 0.4 collective-permute-done.12
  30.0 0.2 add_convert_fusion
  30.2 0.6 collective-permute-start.13
  30.8 1.1 %rows.1 = (bf16[2,64,512]{2,1,0:T(8,128)(2,1)S(1)}, bf16[2,64,512]{2,1,0:T(8,128)(2,1)S(1)}, bf16[2,64,512]{2,1,0:T(8,128)(2,1)S(1)}, bf16[2,64,512]{2,1,0:T(8,128)(2,1)S(1)}) custom-call(bf16[256,256]{1,0:T(8,128)(2,1)S(1)} %get-tuple-element.72.matrix_ref, bf16[256,2048]{1,0:T(8,128)(2,1)S(1)} %get-tuple-element.101.gproj_ref, ...), custom_call_target="tpu_custom_call" | custom-call | tf_op jit(solution)/shard_map/rows/pallas_call | solution.py:484
  32.1 1.6 %collective-permute-start.15 = (bf16[2,64,512]{2,1,0:T(8,128)(2,1)S(1)}, bf16[2,64,512]{2,1,0:T(8,128)(2,1)S(1)}, u32[]{:S(2)}, u32[]{:S(2)}) collective-permute-start(bf16[2,64,512]{2,1,0:T(8,128)(2,1)S(1)} %get-tuple-element.109), channel_id=1, source_target_pairs={{0,1},{1,0},{2,3},{3,2},{4,5},{5,4},{6,7},{7,6},{8,9},{9,8},{10,11... | collective-permute-start | bytes 393224 | tf_op jit(solution)/shard_map/ppermute | solution.py:39
  33.7 0.6 collective-permute-start.22
  34.2 2.6 %collective-permute-start.20 = (bf16[2,64,512]{2,1,0:T(8,128)(2,1)S(1)}, bf16[2,64,512]{2,1,0:T(8,128)(2,1)S(1)}, u32[]{:S(2)}, u32[]{:S(2)}) collective-permute-start(bf16[2,64,512]{2,1,0:T(8,128)(2,1)S(1)} %get-tuple-element.113), channel_id=1, source_target_pairs={{0,2},{1,3},{2,0},{3,1},{4,6},{5,7},{6,4},{7,5},{8,10},{9,11},{10,... | collective-permute-start | bytes 393224 | tf_op jit(solution)/shard_map/ppermute | solution.py:39
  36.8 0.3 collective-permute-start.21
  37.1 3.8 %collective-permute-done.13 = bf16[128,1408]{1,0:T(8,128)(2,1)S(1)} collective-permute-done((bf16[128,1408]{1,0:T(8,128)(2,1)S(1)}, bf16[128,1408]{1,0:T(8,128)(2,1)S(1)}, u32[]{:S(2)}, u32[]{:S(2)}) %collective-permute-start.13) | collective-permute-done | bytes 360480 | tf_op jit(solution)/shard_map/ppermute | solution.py:39
  41.1 0.6 collective-permute-start.16
  41.7 0.8 %collective-permute-done.22 = bf16[128,1152]{1,0:T(8,128)(2,1)S(1)} collective-permute-done((bf16[128,1152]{1,0:T(8,128)(2,1)S(1)}, bf16[128,1152]{1,0:T(8,128)(2,1)S(1)}, u32[]{:S(2)}, u32[]{:S(2)}) %collective-permute-start.22) | collective-permute-done | bytes 294944 | tf_op jit(solution)/shard_map/ppermute | solution.py:39
  42.6 1.6 %collective-permute-start.23 = (bf16[64,1152]{1,0:T(8,128)(2,1)S(1)}, bf16[64,1152]{1,0:T(8,128)(2,1)S(1)}, u32[]{:S(2)}, u32[]{:S(2)}) collective-permute-start(bf16[64,1152]{1,0:T(8,128)(2,1)S(1)} %slice.45), channel_id=1, source_target_pairs={{0,8},{4,12},{8,0},{12,4},{16,24},{20,28},{24,16},{28,20},{1,9},{5... | collective-permute-start | bytes 442376 | tf_op jit(solution)/shard_map/ppermute | solution.py:39
  44.1 3.0 %collective-permute-done.16 = bf16[64,1408]{1,0:T(8,128)(2,1)S(1)} collective-permute-done((bf16[64,1408]{1,0:T(8,128)(2,1)S(1)}, bf16[64,1408]{1,0:T(8,128)(2,1)S(1)}, u32[]{:S(2)}, u32[]{:S(2)}) %collective-permute-start.16) | collective-permute-done | bytes 180256 | tf_op jit(solution)/shard_map/ppermute | solution.py:39
  47.2 1.6 %collective-permute-start.17 = (bf16[32,1408]{1,0:T(8,128)(2,1)S(1)}, bf16[32,1408]{1,0:T(8,128)(2,1)S(1)}, u32[]{:S(2)}, u32[]{:S(2)}) collective-permute-start(bf16[32,1408]{1,0:T(8,128)(2,1)S(1)} %constant_dynamic-slice_fusion.1), channel_id=1, source_target_pairs={{0,1},{1,0},{2,3},{3,2},{4,5},{5,4},{6,7},{7,6},{8,9},{9,8},{10,11... | collective-permute-start | bytes 270344 | tf_op jit(solution)/shard_map/ppermute | solution.py:39
  48.9 0.6 collective-permute-start.24
  49.5 2.4 %collective-permute-done.17 = bf16[32,1408]{1,0:T(8,128)(2,1)S(1)} collective-permute-done((bf16[32,1408]{1,0:T(8,128)(2,1)S(1)}, bf16[32,1408]{1,0:T(8,128)(2,1)S(1)}, u32[]{:S(2)}, u32[]{:S(2)}) %collective-permute-start.17) | collective-permute-done | bytes 90144 | tf_op jit(solution)/shard_map/ppermute | solution.py:39
  51.9 2.6 %collective-permute-start.18 = (bf16[32,1408]{1,0:T(8,128)(2,1)S(1)}, bf16[32,1408]{1,0:T(8,128)(2,1)S(1)}, u32[]{:S(2)}, u32[]{:S(2)}) collective-permute-start(bf16[32,1408]{1,0:T(8,128)(2,1)S(1)} %add_convert_fusion.7), channel_id=1, source_target_pairs={{0,2},{1,3},{2,0},{3,1},{4,6},{5,7},{6,4},{7,5},{8,10},{9,11},{10,... | collective-permute-start | bytes 270344 | tf_op jit(solution)/shard_map/ppermute | solution.py:39
  54.5 1.8 %collective-permute-start.25 = (bf16[32,1152]{1,0:T(8,128)(2,1)S(1)}, bf16[32,1152]{1,0:T(8,128)(2,1)S(1)}, u32[]{:S(2)}, u32[]{:S(2)}) collective-permute-start(bf16[32,1152]{1,0:T(8,128)(2,1)S(1)} %add_convert_fusion.9), channel_id=1, source_target_pairs={{0,2},{1,3},{2,0},{3,1},{4,6},{5,7},{6,4},{7,5},{8,10},{9,11},{10,... | collective-permute-start | bytes 221192 | tf_op jit(solution)/shard_map/ppermute | solution.py:39
  56.3 2.6 %collective-permute-done.18 = bf16[32,1408]{1,0:T(8,128)(2,1)S(1)} collective-permute-done((bf16[32,1408]{1,0:T(8,128)(2,1)S(1)}, bf16[32,1408]{1,0:T(8,128)(2,1)S(1)}, u32[]{:S(2)}, u32[]{:S(2)}) %collective-permute-start.18) | collective-permute-done | bytes 90144 | tf_op jit(solution)/shard_map/ppermute | solution.py:39
  59.1 0.8 %collective-permute-done.25 = bf16[32,1152]{1,0:T(8,128)(2,1)S(1)} collective-permute-done((bf16[32,1152]{1,0:T(8,128)(2,1)S(1)}, bf16[32,1152]{1,0:T(8,128)(2,1)S(1)}, u32[]{:S(2)}, u32[]{:S(2)}) %collective-permute-start.25) | collective-permute-done | bytes 73760 | tf_op jit(solution)/shard_map/ppermute | solution.py:39
  59.9 2.1 %collective-permute-start.26 = (bf16[32,1152]{1,0:T(8,128)(2,1)S(1)}, bf16[32,1152]{1,0:T(8,128)(2,1)S(1)}, u32[]{:S(2)}, u32[]{:S(2)}) collective-permute-start(bf16[32,1152]{1,0:T(8,128)(2,1)S(1)} %add_convert_fusion.8.late_own), channel_id=1, source_target_pairs={{0,1},{1,0},{2,3},{3,2},{4,5},{5,4},{6,7},{7,6},{8,9},{9,8},{10,11... | collective-permute-start | bytes 221192 | tf_op jit(solution)/shard_map/ppermute | solution.py:39
  62.0 1.2 %post.1 = (bf16[256,512]{1,0:T(8,128)(2,1)}, bf16[256,512]{1,0:T(8,128)(2,1)}) custom-call(s32[1,32]{1,0:T(1,128)S(1)} %bitcast.9, bf16[2,64,512]{2,1,0:T(8,128)(2,1)S(1)} %get-tuple-element.111.refs_0_, bf16[2,64,512]{2,1,0:T(8,128)(2,1)S(1)} %collective-permute-done.15.refs_1_, bf16[2,64,512]{2,1,0:T(8,128)(2,1)S(1)} %collective-permute-done.20.refs_2_, ...), custom_call_target="tpu_custom_call" | custom-call | tf_op jit(solution)/shard_map/post/pallas_call | solution.py:495
  63.2 0.3 collective-permute-done.19.early_other
  63.5 0.8 %collective-permute-done.26.late_other = bf16[32,1152]{1,0:T(8,128)(2,1)S(1)} collective-permute-done((bf16[32,1152]{1,0:T(8,128)(2,1)S(1)}, bf16[32,1152]{1,0:T(8,128)(2,1)S(1)}, u32[]{:S(2)}, u32[]{:S(2)}) %collective-permute-start.26) | collective-permute-done | bytes 73760 | tf_op jit(solution)/shard_map/ppermute | solution.py:39
  64.3 0.9 %finish.1 = (f32[64,2048]{1,0:T(8,128)}, f32[64,512]{1,0:T(8,128)}) custom-call(bf16[32,1408]{1,0:T(8,128)(2,1)S(1)} %add_convert_fusion.6.early_own, bf16[32,1408]{1,0:T(8,128)(2,1)S(1)} %collective-permute-done.19.early_other, bf16[32,1152]{1,0:T(8,128)(2,1)S(1)} %add_convert_fusion.8.late_own, bf16[32,1152]{1,0:T(8,128)(2,1)S(1)} %collective-permute-done.26.late_other), custom_call_target="tpu_custom_call" | custom-call | tf_op jit(solution)/shard_map/finish/pallas_call | solution.py:507
  (40 shorter events, 1.1 us)
Async XLA Ops:
  2.9 12.2 %collective-permute-start = (bf16[64,2560]{1,0:T(8,128)(2,1)}, bf16[64,2560]{1,0:T(8,128)(2,1)S(1)}, u32[]{:S(2)}, u32[]{:S(2)}) collective-permute-start(bf16[64,2560]{1,0:T(8,128)(2,1)} %get-tuple-element.65.w_ref), channel_id=1, source_target_pairs={{0,8},{4,12},{8,0},{12,4},{16,24},{20,28},{24,16},{28,20},{1,9},{5... | collective-permute-start | bytes 983048 | tf_op jit(solution)/shard_map/ppermute | solution.py:39
  5.9 9.4 %collective-permute-start.1 = (bf16[64,2560]{1,0:T(8,128)(2,1)}, bf16[64,2560]{1,0:T(8,128)(2,1)S(1)}, u32[]{:S(2)}, u32[]{:S(2)}) collective-permute-start(bf16[64,2560]{1,0:T(8,128)(2,1)} %get-tuple-element.65.w_ref), channel_id=1, source_target_pairs={{0,16},{4,20},{8,24},{12,28},{16,0},{20,4},{24,8},{28,12},{1,17},{... | collective-permute-start | bytes 983048 | tf_op jit(solution)/shard_map/ppermute | solution.py:39
  7.5 7.7 %collective-permute-start.2 = (bf16[2,64,512]{2,1,0:T(8,128)(2,1)}, bf16[2,64,512]{2,1,0:T(8,128)(2,1)S(1)}, u32[]{:S(2)}, u32[]{:S(2)}) collective-permute-start(bf16[2,64,512]{2,1,0:T(8,128)(2,1)} %get-tuple-element.68), channel_id=1, source_target_pairs={{0,1},{1,0},{2,3},{3,2},{4,5},{5,4},{6,7},{7,6},{8,9},{9,8},{10,11... | collective-permute-start | bytes 393224 | tf_op jit(solution)/shard_map/ppermute | solution.py:39
  9.0 12.6 %collective-permute-start.5 = (bf16[2,64,512]{2,1,0:T(8,128)(2,1)}, bf16[2,64,512]{2,1,0:T(8,128)(2,1)S(1)}, u32[]{:S(2)}, u32[]{:S(2)}) collective-permute-start(bf16[2,64,512]{2,1,0:T(8,128)(2,1)} %get-tuple-element.75), channel_id=1, source_target_pairs={{0,2},{1,3},{2,0},{3,1},{4,6},{5,7},{6,4},{7,5},{8,10},{9,11},{10,... | collective-permute-start | bytes 393224 | tf_op jit(solution)/shard_map/ppermute | solution.py:39
  11.6 10.0 %collective-permute-start.6 = (bf16[2,64,512]{2,1,0:T(8,128)(2,1)}, bf16[2,64,512]{2,1,0:T(8,128)(2,1)S(1)}, u32[]{:S(2)}, u32[]{:S(2)}) collective-permute-start(bf16[2,64,512]{2,1,0:T(8,128)(2,1)} %get-tuple-element.76), channel_id=1, source_target_pairs={{0,3},{1,2},{2,1},{3,0},{4,7},{5,6},{6,5},{7,4},{8,11},{9,10},{10,... | collective-permute-start | bytes 393224 | tf_op jit(solution)/shard_map/ppermute | solution.py:39
  11.8 1.0 %copy-start = (bf16[64,2560]{1,0:T(8,128)(2,1)S(1)}, bf16[64,2560]{1,0:T(8,128)(2,1)}, u32[]{:S(2)}) copy-start(bf16[64,2560]{1,0:T(8,128)(2,1)} %get-tuple-element.65.w_ref) | copy-start | bytes 983044
  12.8 0.9 %copy-start.1 = (bf16[2,64,512]{2,1,0:T(8,128)(2,1)S(1)}, bf16[2,64,512]{2,1,0:T(8,128)(2,1)}, u32[]{:S(2)}) copy-start(bf16[2,64,512]{2,1,0:T(8,128)(2,1)} %get-tuple-element.66.own_ref) | copy-start | bytes 393220
  13.7 0.7 %copy-start.2 = (s32[8,128]{1,0:T(8,128)S(1)}, s32[8,128]{1,0:T(8,128)}, u32[]{:S(2)}) copy-start(s32[8,128]{1,0:T(8,128)} %get-tuple-element.64.small_ref) | copy-start | bytes 12292
  15.3 6.8 %collective-permute-start.3 = (bf16[64,1280]{1,0:T(8,128)(2,1)S(1)}, bf16[64,1280]{1,0:T(8,128)(2,1)S(1)}, u32[]{:S(2)}, u32[]{:S(2)}) collective-permute-start(bf16[64,1280]{1,0:T(8,128)(2,1)S(1)} %slice.40), channel_id=1, source_target_pairs={{0,16},{4,20},{8,24},{12,28},{16,0},{20,4},{24,8},{28,12},{1,17},{... | collective-permute-start | bytes 491528 | tf_op jit(solution)/shard_map/ppermute | solution.py:39
  16.9 5.4 %collective-permute-start.4 = (bf16[64,1280]{1,0:T(8,128)(2,1)S(1)}, bf16[64,1280]{1,0:T(8,128)(2,1)S(1)}, u32[]{:S(2)}, u32[]{:S(2)}) collective-permute-start(bf16[64,1280]{1,0:T(8,128)(2,1)S(1)} %slice.41), channel_id=1, source_target_pairs={{0,8},{4,12},{8,0},{12,4},{16,24},{20,28},{24,16},{28,20},{1,9},{5... | collective-permute-start | bytes 491528 | tf_op jit(solution)/shard_map/ppermute | solution.py:39
  17.5 5.8 %collective-permute-start.7 = (bf16[64,2560]{1,0:T(8,128)(2,1)S(1)}, bf16[64,2560]{1,0:T(8,128)(2,1)S(1)}, u32[]{:S(2)}, u32[]{:S(2)}) collective-permute-start(bf16[64,2560]{1,0:T(8,128)(2,1)S(1)} %get-tuple-element.83.refs_0_), channel_id=1, source_target_pairs={{0,4},{4,0},{8,12},{12,8},{16,20},{20,16},{24,28},{28,24},{1,5},{5... | collective-permute-start | bytes 983048 | tf_op jit(solution)/shard_map/ppermute | solution.py:39
  21.6 1.7 %collective-permute-start.8 = (bf16[64,2560]{1,0:T(8,128)(2,1)S(1)}, bf16[64,2560]{1,0:T(8,128)(2,1)S(1)}, u32[]{:S(2)}, u32[]{:S(2)}) collective-permute-start(bf16[64,2560]{1,0:T(8,128)(2,1)S(1)} %collective-permute-done.refs_2_), channel_id=1, source_target_pairs={{0,4},{4,0},{8,12},{12,8},{16,20},{20,16},{24,28},{28,24},{1,5},{5... | collective-permute-start | bytes 983048 | tf_op jit(solution)/shard_map/ppermute | solution.py:39
  21.6 2.1 %collective-permute-start.9 = (bf16[64,2560]{1,0:T(8,128)(2,1)S(1)}, bf16[64,2560]{1,0:T(8,128)(2,1)S(1)}, u32[]{:S(2)}, u32[]{:S(2)}) collective-permute-start(bf16[64,2560]{1,0:T(8,128)(2,1)S(1)} %collective-permute-done.1.refs_4_), channel_id=1, source_target_pairs={{0,4},{4,0},{8,12},{12,8},{16,20},{20,16},{24,28},{28,24},{1,5},{5... | collective-permute-start | bytes 983048 | tf_op jit(solution)/shard_map/ppermute | solution.py:39
  22.3 1.6 %collective-permute-start.10 = (bf16[64,1280]{1,0:T(8,128)(2,1)S(1)}, bf16[64,1280]{1,0:T(8,128)(2,1)S(1)}, u32[]{:S(2)}, u32[]{:S(2)}) collective-permute-start(bf16[64,1280]{1,0:T(8,128)(2,1)S(1)} %collective-permute-done.3.refs_6_), channel_id=1, source_target_pairs={{0,4},{4,0},{8,12},{12,8},{16,20},{20,16},{24,28},{28,24},{1,5},{5... | collective-permute-start | bytes 491528 | tf_op jit(solution)/shard_map/ppermute | solution.py:39
  22.3 1.8 %collective-permute-start.11 = (bf16[64,1280]{1,0:T(8,128)(2,1)S(1)}, bf16[64,1280]{1,0:T(8,128)(2,1)S(1)}, u32[]{:S(2)}, u32[]{:S(2)}) collective-permute-start(bf16[64,1280]{1,0:T(8,128)(2,1)S(1)} %collective-permute-done.4.refs_7_), channel_id=1, source_target_pairs={{0,4},{4,0},{8,12},{12,8},{16,20},{20,16},{24,28},{28,24},{1,5},{5... | collective-permute-start | bytes 491528 | tf_op jit(solution)/shard_map/ppermute | solution.py:39
  27.6 2.3 %collective-permute-start.12 = (bf16[256,1408]{1,0:T(8,128)(2,1)S(1)}, bf16[256,1408]{1,0:T(8,128)(2,1)S(1)}, u32[]{:S(2)}, u32[]{:S(2)}) collective-permute-start(bf16[256,1408]{1,0:T(8,128)(2,1)S(1)} %get-tuple-element.89), channel_id=1, source_target_pairs={{0,4},{4,0},{8,12},{12,8},{16,20},{20,16},{24,28},{28,24},{1,5},{5... | collective-permute-start | bytes 2162696 | tf_op jit(solution)/shard_map/ppermute | solution.py:39
  29.9 2.1 %collective-permute-start.14 = (bf16[256,1152]{1,0:T(8,128)(2,1)S(1)}, bf16[256,1152]{1,0:T(8,128)(2,1)S(1)}, u32[]{:S(2)}, u32[]{:S(2)}) collective-permute-start(bf16[256,1152]{1,0:T(8,128)(2,1)S(1)} %get-tuple-element.100), channel_id=1, source_target_pairs={{0,4},{4,0},{8,12},{12,8},{16,20},{20,16},{24,28},{28,24},{1,5},{5... | collective-permute-start | bytes 1769480 | tf_op jit(solution)/shard_map/ppermute | solution.py:39
  30.2 10.8 %collective-permute-start.13 = (bf16[128,1408]{1,0:T(8,128)(2,1)S(1)}, bf16[128,1408]{1,0:T(8,128)(2,1)S(1)}, u32[]{:S(2)}, u32[]{:S(2)}) collective-permute-start(bf16[128,1408]{1,0:T(8,128)(2,1)S(1)} %slice.33), channel_id=1, source_target_pairs={{0,8},{4,12},{8,0},{12,4},{16,24},{20,28},{24,16},{28,20},{1,9},{5... | collective-permute-start | bytes 1081352 | tf_op jit(solution)/shard_map/ppermute | solution.py:39
  32.1 8.9 %collective-permute-start.15 = (bf16[2,64,512]{2,1,0:T(8,128)(2,1)S(1)}, bf16[2,64,512]{2,1,0:T(8,128)(2,1)S(1)}, u32[]{:S(2)}, u32[]{:S(2)}) collective-permute-start(bf16[2,64,512]{2,1,0:T(8,128)(2,1)S(1)} %get-tuple-element.109), channel_id=1, source_target_pairs={{0,1},{1,0},{2,3},{3,2},{4,5},{5,4},{6,7},{7,6},{8,9},{9,8},{10,11... | collective-permute-start | bytes 393224 | tf_op jit(solution)/shard_map/ppermute | solution.py:39
  33.7 8.8 %collective-permute-start.22 = (bf16[128,1152]{1,0:T(8,128)(2,1)S(1)}, bf16[128,1152]{1,0:T(8,128)(2,1)S(1)}, u32[]{:S(2)}, u32[]{:S(2)}) collective-permute-start(bf16[128,1152]{1,0:T(8,128)(2,1)S(1)} %slice.37), channel_id=1, source_target_pairs={{0,16},{4,20},{8,24},{12,28},{16,0},{20,4},{24,8},{28,12},{1,17},{... | collective-permute-start | bytes 884744 | tf_op jit(solution)/shard_map/ppermute | solution.py:39
  34.2 27.7 %collective-permute-start.20 = (bf16[2,64,512]{2,1,0:T(8,128)(2,1)S(1)}, bf16[2,64,512]{2,1,0:T(8,128)(2,1)S(1)}, u32[]{:S(2)}, u32[]{:S(2)}) collective-permute-start(bf16[2,64,512]{2,1,0:T(8,128)(2,1)S(1)} %get-tuple-element.113), channel_id=1, source_target_pairs={{0,2},{1,3},{2,0},{3,1},{4,6},{5,7},{6,4},{7,5},{8,10},{9,11},{10,... | collective-permute-start | bytes 393224 | tf_op jit(solution)/shard_map/ppermute | solution.py:39
  36.8 25.1 %collective-permute-start.21 = (bf16[2,64,512]{2,1,0:T(8,128)(2,1)S(1)}, bf16[2,64,512]{2,1,0:T(8,128)(2,1)S(1)}, u32[]{:S(2)}, u32[]{:S(2)}) collective-permute-start(bf16[2,64,512]{2,1,0:T(8,128)(2,1)S(1)} %get-tuple-element.114), channel_id=1, source_target_pairs={{0,3},{1,2},{2,1},{3,0},{4,7},{5,6},{6,5},{7,4},{8,11},{9,10},{10,... | collective-permute-start | bytes 393224 | tf_op jit(solution)/shard_map/ppermute | solution.py:39
  41.1 6.1 %collective-permute-start.16 = (bf16[64,1408]{1,0:T(8,128)(2,1)S(1)}, bf16[64,1408]{1,0:T(8,128)(2,1)S(1)}, u32[]{:S(2)}, u32[]{:S(2)}) collective-permute-start(bf16[64,1408]{1,0:T(8,128)(2,1)S(1)} %slice.43), channel_id=1, source_target_pairs={{0,16},{4,20},{8,24},{12,28},{16,0},{20,4},{24,8},{28,12},{1,17},{... | collective-permute-start | bytes 540680 | tf_op jit(solution)/shard_map/ppermute | solution.py:39
  42.5 19.4 %copy-start.3 = (s32[1,1,32]{2,1,0:T(1,128)S(1)}, s32[1,1,32]{2,1,0:T(1,128)}, u32[]{:S(2)}) copy-start(s32[1,1,32]{2,1,0:T(1,128)} %param.12) | copy-start | bytes 388
  42.6 6.2 %collective-permute-start.23 = (bf16[64,1152]{1,0:T(8,128)(2,1)S(1)}, bf16[64,1152]{1,0:T(8,128)(2,1)S(1)}, u32[]{:S(2)}, u32[]{:S(2)}) collective-permute-start(bf16[64,1152]{1,0:T(8,128)(2,1)S(1)} %slice.45), channel_id=1, source_target_pairs={{0,8},{4,12},{8,0},{12,4},{16,24},{20,28},{24,16},{28,20},{1,9},{5... | collective-permute-start | bytes 442376 | tf_op jit(solution)/shard_map/ppermute | solution.py:39
  47.2 4.6 %collective-permute-start.17 = (bf16[32,1408]{1,0:T(8,128)(2,1)S(1)}, bf16[32,1408]{1,0:T(8,128)(2,1)S(1)}, u32[]{:S(2)}, u32[]{:S(2)}) collective-permute-start(bf16[32,1408]{1,0:T(8,128)(2,1)S(1)} %constant_dynamic-slice_fusion.1), channel_id=1, source_target_pairs={{0,1},{1,0},{2,3},{3,2},{4,5},{5,4},{6,7},{7,6},{8,9},{9,8},{10,11... | collective-permute-start | bytes 270344 | tf_op jit(solution)/shard_map/ppermute | solution.py:39
  48.9 5.6 %collective-permute-start.24 = (bf16[32,1152]{1,0:T(8,128)(2,1)S(1)}, bf16[32,1152]{1,0:T(8,128)(2,1)S(1)}, u32[]{:S(2)}, u32[]{:S(2)}) collective-permute-start(bf16[32,1152]{1,0:T(8,128)(2,1)S(1)} %constant_dynamic-slice_fusion), channel_id=1, source_target_pairs={{0,1},{1,0},{2,3},{3,2},{4,5},{5,4},{6,7},{7,6},{8,9},{9,8},{10,11... | collective-permute-start | bytes 221192 | tf_op jit(solution)/shard_map/ppermute | solution.py:39
  51.9 7.0 %collective-permute-start.18 = (bf16[32,1408]{1,0:T(8,128)(2,1)S(1)}, bf16[32,1408]{1,0:T(8,128)(2,1)S(1)}, u32[]{:S(2)}, u32[]{:S(2)}) collective-permute-start(bf16[32,1408]{1,0:T(8,128)(2,1)S(1)} %add_convert_fusion.7), channel_id=1, source_target_pairs={{0,2},{1,3},{2,0},{3,1},{4,6},{5,7},{6,4},{7,5},{8,10},{9,11},{10,... | collective-permute-start | bytes 270344 | tf_op jit(solution)/shard_map/ppermute | solution.py:39
  54.5 5.4 %collective-permute-start.25 = (bf16[32,1152]{1,0:T(8,128)(2,1)S(1)}, bf16[32,1152]{1,0:T(8,128)(2,1)S(1)}, u32[]{:S(2)}, u32[]{:S(2)}) collective-permute-start(bf16[32,1152]{1,0:T(8,128)(2,1)S(1)} %add_convert_fusion.9), channel_id=1, source_target_pairs={{0,2},{1,3},{2,0},{3,1},{4,6},{5,7},{6,4},{7,5},{8,10},{9,11},{10,... | collective-permute-start | bytes 221192 | tf_op jit(solution)/shard_map/ppermute | solution.py:39
  58.9 4.6 %collective-permute-start.19 = (bf16[32,1408]{1,0:T(8,128)(2,1)S(1)}, bf16[32,1408]{1,0:T(8,128)(2,1)S(1)}, u32[]{:S(2)}, u32[]{:S(2)}) collective-permute-start(bf16[32,1408]{1,0:T(8,128)(2,1)S(1)} %add_convert_fusion.6.early_own), channel_id=1, source_target_pairs={{0,1},{1,0},{2,3},{3,2},{4,5},{5,4},{6,7},{7,6},{8,9},{9,8},{10,11... | collective-permute-start | bytes 270344 | tf_op jit(solution)/shard_map/ppermute | solution.py:39
  59.9 4.4 %collective-permute-start.26 = (bf16[32,1152]{1,0:T(8,128)(2,1)S(1)}, bf16[32,1152]{1,0:T(8,128)(2,1)S(1)}, u32[]{:S(2)}, u32[]{:S(2)}) collective-permute-start(bf16[32,1152]{1,0:T(8,128)(2,1)S(1)} %add_convert_fusion.8.late_own), channel_id=1, source_target_pairs={{0,1},{1,0},{2,3},{3,2},{4,5},{5,4},{6,7},{7,6},{8,9},{9,8},{10,11... | collective-permute-start | bytes 221192 | tf_op jit(solution)/shard_map/ppermute | solution.py:39
